TPU v7x, 256 devices: a whole 4x4x8 slice. The times are simulated.
256 devices in a mesh: grp: 4 (over x), seq: 64 (over y, z, core).
Axes of the slice: x: 4, y: 4, z: 8, core: 2. Of those that a mesh axis runs over, the one named last changes fastest.
Arguments:
- tokens: bfloat16 [32768, 8192], P(('grp', 'seq')), may hold values from -6 to 6
- cotangent: bfloat16 [32768, 1024], P(('grp', 'seq')), may hold values from -6 to 6
- frozen_weight: bfloat16 [8192, 1024], P('seq'), may hold values from -0.0625 to 0.0625
- adapters: bfloat16 [64, 9216, 64], P('grp', 'seq'), may hold values from -0.5 to 0.5
- tile_job: int32 [256, 1], replicated, may hold values from 0 to 63
- job_slot: int32 [64], replicated, may hold values from 0 to 63, each once
Outputs:
- keys: bfloat16 [32768, 1024], P(('grp', 'seq'))
- token_gradient: bfloat16 [32768, 8192], P(('grp', 'seq'))
- grad_adapters: float32 [64, 9216, 64], P('grp', 'seq')
All inputs are finite; a program needn't handle non-finite values.
Results may differ from a plain program's by a relative error of at most 0.0029.
Values may be sent and summed in bfloat16 or wider, within the bound.
No kernel may reach another device: no remote copies, remote signals or barrier semaphores. Data moves between devices by JAX's collectives and lax.ppermute only.
A program may use at most 128 MiB of HBM per device.

v0:
```python
import jax
import jax.numpy as jnp
from jax import lax
from jax.sharding import PartitionSpec as P

TILE_ROWS = 128


adapter_scale = 0.5


def on_device(tokens, cotangent, frozen_weight, adapters, tile_job, job_slot):
    rank_width = tokens.shape[1]
    key_columns = cotangent.shape[1]
    rank = adapters.shape[2]
    slot_count = adapters.shape[0]
    row_count = adapters.shape[1]
    total_jobs = job_slot.shape[0]
    groups = lax.axis_size("grp")
    shards = lax.axis_size("seq")
    tiles_dev = tokens.shape[0] // TILE_ROWS
    group_index = lax.axis_index("grp")
    jobs = tile_job[:, 0]
    table = jnp.arange(total_jobs, dtype=jnp.int32)
    slots_all = jnp.sum(jnp.where(jobs[:, None] == table[None, :], job_slot[None, :], 0), axis=1)
    slots_all = slots_all.reshape(groups, shards, tiles_dev)
    group_slots = lax.dynamic_index_in_dim(slots_all, group_index, 0, keepdims=False)
    tile_slots = group_slots.T
    piece = lax.all_gather(frozen_weight, "seq", axis=0, tiled=True)
    forward_pass = jnp.dot(tokens, piece, preferred_element_type=jnp.float32)
    weight_update = jnp.einsum("nk,dk->nd", cotangent, piece, preferred_element_type=jnp.float32)
    owners = jnp.transpose(slots_all // slot_count, (0, 2, 1))
    local_slots = jnp.transpose(slots_all % slot_count, (0, 2, 1))
    picked = jnp.take(adapters, local_slots, axis=0)
    outgoing = jnp.where((owners == group_index)[..., None, None], picked, jnp.zeros_like(picked))
    arrived = lax.all_to_all(
        lax.all_to_all(outgoing, "grp", split_axis=0, concat_axis=0, tiled=True),
        "seq",
        split_axis=2,
        concat_axis=2,
        tiled=True,
    )
    fetched = jnp.sum(arrived.astype(jnp.float32), axis=0).astype(jnp.bfloat16)
    adapter_full = fetched.reshape(tiles_dev, shards * row_count, rank)
    down_weight = adapter_full[:, :rank_width]
    up_weight = adapter_full[:, rank_width:]
    token_tiles = tokens.reshape(tiles_dev, TILE_ROWS, rank_width)
    cot_tiles = cotangent.reshape(tiles_dev, TILE_ROWS, key_columns)
    hidden_width = jnp.einsum(
        "tnd,tdr->tnr", token_tiles, down_weight, preferred_element_type=jnp.float32
    ).astype(jnp.bfloat16)
    adapter_weights = jnp.einsum(
        "mhw,mow->mho", hidden_width, up_weight, preferred_element_type=jnp.float32
    )
    keys = (forward_pass + adapter_scale * adapter_weights.reshape(-1, key_columns)).astype(
        jnp.bfloat16
    )
    backward_pass = jnp.einsum(
        "tnk,tkr->tnr", cot_tiles, up_weight, preferred_element_type=jnp.float32
    ).astype(jnp.bfloat16)
    pass_through = jnp.einsum(
        "tnr,tdr->tnd", backward_pass, down_weight, preferred_element_type=jnp.float32
    )
    token_gradient = (weight_update + adapter_scale * pass_through.reshape(-1, rank_width)).astype(
        jnp.bfloat16
    )
    down_term = adapter_scale * jnp.einsum(
        "tnd,tnr->tdr", token_tiles, backward_pass, preferred_element_type=jnp.float32
    )
    up_term = adapter_scale * jnp.einsum(
        "tnk,tnr->tkr", cot_tiles, hidden_width, preferred_element_type=jnp.float32
    )
    terms = jnp.concatenate([down_term, up_term], axis=1).reshape(
        tiles_dev, shards, row_count, rank
    )
    incoming = lax.all_to_all(terms, "seq", split_axis=1, concat_axis=1, tiled=True)
    selector = (tile_slots.reshape(-1)[None, :] == table[:, None]).astype(jnp.float32)
    sums = jnp.dot(
        selector,
        incoming.reshape(tiles_dev * shards, row_count * rank),
        precision=lax.Precision.HIGHEST,
        preferred_element_type=jnp.float32,
    )
    owned = lax.psum_scatter(
        sums.reshape(total_jobs, row_count, rank), "grp", scatter_dimension=0, tiled=True
    )
    return (keys, token_gradient, owned)


def solution(mesh):
    placed = (
        P(("grp", "seq"), None),
        P(("grp", "seq"), None),
        P("seq", None),
        P("grp", "seq", None),
        P(),
        P(),
    )
    return jax.shard_map(
        on_device,
        mesh=mesh,
        in_specs=placed,
        out_specs=(P(("grp", "seq"), None), P(("grp", "seq"), None), P("grp", "seq", None)),
        check_vma=False,
    )
```

profile of v0, /device:TPU:1, one launch (start us, length us, event | category | flops | bytes accessed | tf_op | source)
XLA Modules:
  0.0 622.6 jit_solution(13296227686005759614)
XLA Ops:
  9.2 9.6 %gather_fusion = bf16[256,144,64]{1,2,0:T(8,128)(2,1)} fusion(bf16[16,144,64]{1,2,0:T(8,128)(2,1)} %param.9, s32[1024]{0:T(1024)S(1)} %pad_clamp_fusion), kind=kCustom, calls=%fused_computation | custom fusion | bytes 9438208 | tf_op jit(solution)/shard_map/jit(_take)/gather | solution.py:34
  18.9 4.6 select_select_fusion
  23.5 96.2 %all_to_all.15 = bf16[4,1,64,144,64]{3,4,2,1,0:T(8,128)(2,1)} all-to-all(bf16[4,1,64,144,64]{3,4,2,1,0:T(8,128)(2,1)S(1)} %select_select_fusion), channel_id=1, replica_groups=mesh['grp'=4,'seq'=64] {'grp'}, dimensions={0} | all-to-all | bytes 9437184 | tf_op jit(solution)/shard_map/all_to_all | solution.py:37
  119.7 8.3 %copy.26 = bf16[4,1,64,144,64]{3,4,0,1,2:T(8,128)(2,1)} copy(bf16[4,1,64,144,64]{3,4,2,1,0:T(8,128)(2,1)} %all_to_all.15) | data formatting | bytes 9437184 | tf_op jit(solution)/shard_map/all_to_all | solution.py:37
  128.0 201.0 %all_to_all.16 = bf16[4,1,64,144,64]{3,4,0,1,2:T(8,128)(2,1)} all-to-all(bf16[4,1,64,144,64]{3,4,0,1,2:T(8,128)(2,1)} %copy.26), channel_id=1, replica_groups=mesh['grp'=4,'seq'=64] {'seq'}, dimensions={2} | all-to-all | bytes 9437184 | tf_op jit(solution)/shard_map/all_to_all | solution.py:36
  329.0 7.4 %reduce_sum.22 = bf16[64,144,64]{1,2,0:T(8,128)(2,1)} reduce(bf16[4,1,64,144,64]{3,4,0,1,2:T(8,128)(2,1)} %all_to_all.16, bf16[]{:T(256)} %constant.61.clone.1), dimensions={0,1}, to_apply=%region_1.2 | reduce | flops 1769472 | bytes 5898242 | tf_op jit(solution)/shard_map/reduce_sum | solution.py:43
  336.5 4.1 copy.28
  340.6 4.1 reshape.282
  346.5 1.6 pad_maximum_fusion
  348.1 5.6 reshape.286
  353.6 6.6 %copy.29 = f32[1,64,144,64]{2,3,0,1:T(8,128)} copy(f32[1,64,144,64]{2,1,3,0:T(8,128)} %reshape.286) | data formatting | bytes 4718592 | tf_op jit(solution)/shard_map/reshape | solution.py:73
  360.2 6.0 all-to-all-start.2
  368.7 93.4 %all-to-all-done.2 = f32[1,64,144,64]{2,3,0,1:T(8,128)} async-done(((f32[1,64,144,64]{2,3,0,1:T(8,128)}), f32[1,64,144,64]{2,3,0,1:T(8,128)}, u32[]{:S(2)}, u32[]{:S(2)}) %all-to-all-start.2) | async-done | bytes 2359328 | tf_op jit(solution)/shard_map/all_to_all | solution.py:76
  462.1 6.0 copy.30
  468.1 5.1 reshape.287
  473.2 4.5 dot_general.40
  477.7 6.5 %copy.31 = f32[144,64,64]{0,2,1:T(8,128)} copy(f32[144,64,64]{1,0,2:T(8,128)} %dot_general.40) | data formatting | bytes 4718592 | tf_op jit(solution)/shard_map/dot_general | solution.py:78
  484.1 6.5 %fusion.7 = f32[64,144,64]{1,0,2:T(8,128)} fusion(f32[144,64,64]{0,2,1:T(8,128)} %copy.31, s32[64]{0:T(128)} %dynamic-slice_bitcast_fusion), kind=kOutput, calls=%fused_computation.21 | convolution fusion | flops 452988928 | bytes 4718848 | tf_op jit(solution)/shard_map/dot_general | solution.py:78
  491.3 43.6 %reduce-scatter.2.cloned.1.call-done = f32[16,144,64]{1,0,2:T(8,128)} async-done(((f32[64,144,64]{1,0,2:T(8,128)}), f32[16,144,64]{1,0,2:T(8,128)}) %reduce-scatter.2.cloned.1.call-update) | async-done | bytes 589840 | tf_op jit(solution)/shard_map/reduce_scatter | solution.py:84
  534.8 2.8 copy.32
  537.6 51.0 %all-gather.2.cloned.1.call-done = bf16[8192,1024]{1,0:T(8,128)(2,1)} async-done(((bf16[128,1024]{1,0:T(8,128)(2,1)}), bf16[8192,1024]{1,0:T(8,128)(2,1)}) %all-gather.2.cloned.1.call-update) | async-done | bytes 16777232 | tf_op jit(solution)/shard_map/all_gather | solution.py:29
  588.6 13.2 %fusion.14 = f32[128,8192]{1,0:T(8,128)} fusion(bf16[128,1024]{1,0:T(8,128)(2,1)S(1)} %copy-done.1, bf16[8192,1024]{1,0:T(8,128)(2,1)} %all-gather.2.cloned.1.call-done), kind=kOutput, calls=%fused_computation.42 | convolution fusion | flops 2147483648 | bytes 21233664 | tf_op jit(solution)/shard_map/nk,dk->nd/dot_general | solution.py:31
  601.9 4.3 fusion.1
  606.1 8.1 %fusion.13 = f32[128,1024]{1,0:T(8,128)S(1)} fusion(bf16[128,8192]{1,0:T(8,128)(2,1)S(1)} %copy-done, bf16[8192,1024]{1,0:T(8,128)(2,1)} %all-gather.2.cloned.1.call-done), kind=kOutput, calls=%fused_computation.41 | convolution fusion | flops 2147483648 | bytes 19398656 | tf_op jit(solution)/shard_map/dot_general | solution.py:30
  (26 shorter events, 6.9 us)
Async XLA Ops:
  8.0 337.0 %copy-start = (bf16[128,8192]{1,0:T(8,128)(2,1)S(1)}, bf16[128,8192]{1,0:T(8,128)(2,1)}, u32[]{:S(2)}) copy-start(bf16[128,8192]{1,0:T(8,128)(2,1)} %param.6) | copy-start | bytes 6291460
  9.0 9.9 %copy-start.3 = (s32[256]{0:T(256)}, s32[256]{0:T(256)S(1)}, u32[]{:S(2)}) copy-start(s32[256]{0:T(256)S(1)} %select_reduce_fusion) | copy-start | bytes 3076
  336.5 8.3 %copy-start.1 = (bf16[128,1024]{1,0:T(8,128)(2,1)S(1)}, bf16[128,1024]{1,0:T(8,128)(2,1)}, u32[]{:S(2)}) copy-start(bf16[128,1024]{1,0:T(8,128)(2,1)} %param.7) | copy-start | bytes 786436
  345.0 1.0 copy-start.2
  360.2 101.9 %all-to-all-start.2 = ((f32[1,64,144,64]{2,3,0,1:T(8,128)}), f32[1,64,144,64]{2,3,0,1:T(8,128)}, u32[]{:S(2)}, u32[]{:S(2)}) async-start(f32[1,64,144,64]{2,3,0,1:T(8,128)} %copy.29), calls=%async_computation.2 | async-start | bytes 8388608 | tf_op jit(solution)/shard_map/all_to_all | solution.py:76
  366.2 168.6 %reduce-scatter.2.cloned.1.call-start = ((), (), s32[]{:S(2)}) async-start(), calls=%async_computation.5 | async-start | bytes 5242880 | tf_op jit(solution)/shard_map/reduce_scatter | solution.py:84
  490.7 97.9 %all-gather.2.cloned.1.call-start = ((), (), s32[]{:S(2)}) async-start(), calls=%async_computation.4 | async-start | bytes 17039360 | tf_op jit(solution)/shard_map/all_gather | solution.py:29
Sparse Core Ops, SparseCore 0:
  490.8 43.9 reduce-scatter.1
Sparse Core Ops, SparseCore 1:
  493.9 94.6 all-gather.1
where the time goes:
time: 624 us; the launch traced here: 623 us
  blocking collectives  297 us (48%)
  waiting for transfers between devices  188 us (30%)
  local copies, waits for them, and re-layouts  65.8 us (11%)
  matrix products  34.7 us (6%)
  between operations  15.6 us (2%)
  other arithmetic  14.6 us (2%)
    all_to_all x1, blocking collectives, on_device(): lax.all_to_all(lax.all_to_all(outgoing, 'grp', split_axis=0, concat_axis=...  201 us
    all_to_all x1, blocking collectives, on_device(): lax.all_to_all(outgoing, 'grp', split_axis=0, concat_axis=0, tiled=True)  96.2 us
    all_to_all x1, waiting for transfers between devices, on_device(): lax.all_to_all(terms, 'seq', split_axis=1, concat_axis=1, tiled=True)  93.4 us
    all_gather x1, waiting for transfers between devices, on_device(): piece = lax.all_gather(frozen_weight, 'seq', axis=0, tiled=True)  51 us
    reduce_scatter x1, waiting for transfers between devices, on_device(): lax.psum_scatter(sums.reshape(total_jobs, row_count, rank), 'grp', scatte...  43.6 us
    dot_general x1, matrix products, on_device(): jnp.einsum('nk,dk->nd', cotangent, piece, preferred_element_type=jnp.floa...  13.2 us
  transfers between devices with their start and end apart: 3, of which 3 were waited for; matrix products, arithmetic and copies ran while one was open for 1% of the time, Pallas kernels for 0%

commit v1 on v0

v1 whole, which is shorter than its diff:
```python
import functools

import jax
import jax.numpy as jnp
from jax import lax
from jax.experimental import pallas as pl
from jax.experimental.pallas import tpu as pltpu
from jax.sharding import PartitionSpec as P

TILE_ROWS = 128
LANES = 128
adapter_scale = 0.5
f32 = jnp.float32
bf16 = jnp.bfloat16
NT = (((1,), (1,)), ((), ()))
TN = (((0,), (0,)), ((), ()))


def params(vmem_mib=32):
    return pltpu.CompilerParams(vmem_limit_bytes=vmem_mib * 1024 * 1024)


def pack_kernel(a_ref, o_ref):
    slots, rank, width = a_ref.shape
    tail = width - LANES
    for s in range(slots):
        o_ref[s, :rank, :] = a_ref[s, :, :LANES]
        rest = a_ref[s, :, LANES:].astype(f32)
        pieces = [rest[8 * b : 8 * b + 8, :] for b in range(LANES // tail)]
        o_ref[s, rank:, :] = jnp.concatenate(pieces, axis=1).astype(o_ref.dtype)


def pick_kernel(group_ref, job_ref, slot_ref, a_ref, o_ref):
    tiles = o_ref.shape[0]

    def step(t, carry):
        o_ref[t] = a_ref[slot_ref[job_ref[group_ref[0] * tiles + t]]]
        return carry

    lax.fori_loop(0, tiles, step, 0)


def sum_kernel(group_ref, job_ref, slot_ref, x_ref, o_ref):
    tiles = x_ref.shape[0]
    o_ref[...] = jnp.zeros_like(o_ref)

    def step(t, carry):
        s = slot_ref[job_ref[group_ref[0] * tiles + t]]
        o_ref[s] = o_ref[s] + x_ref[t].astype(f32)
        return carry

    lax.fori_loop(0, tiles, step, 0)


def unpack_kernel(x_ref, o_ref):
    slots, rank, width = o_ref.shape
    tail = width - LANES
    for s in range(slots):
        o_ref[s, :, :LANES] = x_ref[s, :rank, :]
        rest = x_ref[s, rank:, :]
        for b in range(LANES // tail):
            o_ref[s, 8 * b : 8 * b + 8, LANES:] = rest[:, tail * b : tail * (b + 1)]


def tile_kernel(x_ref, tok_ref, cot_ref, terms_ref, at_ref, hid_ref, back_ref, t_ref):
    shards, _, _ = x_ref.shape
    rank = at_ref.shape[0]
    depth = tok_ref.shape[1]
    tail = at_ref.shape[1] // shards - LANES
    per = LANES // tail
    group = per * (LANES + tail)
    lane = lax.broadcasted_iota(jnp.int32, (rank, LANES), 1)
    lane8 = lax.broadcasted_iota(jnp.int32, (8, LANES), 1)

    def unpack(a, carry):
        before = None
        for j in range(per + 1):
            if j < per:
                block = x_ref[a * per + j].astype(f32)
                main = block[:rank]
                now = main if j == 0 else pltpu.roll(main, tail * j, axis=1)
            else:
                now = None
            if before is None:
                out = now
            else:
                out = jnp.where(lane >= tail * (j - 1), rest, before)
                if now is not None:
                    out = jnp.where(lane >= tail * j, now, out)
            start = pl.multiple_of(a * group + LANES * j, LANES)
            at_ref[:, pl.ds(start, LANES)] = out.astype(at_ref.dtype)
            before = now
            if j < per:
                packed = block[rank:]
                rest = jnp.concatenate(
                    [
                        packed if b == j else pltpu.roll(packed, tail * ((j - b) % per), axis=1)
                        for b in range(per)
                    ],
                    axis=0,
                )
        return carry

    lax.fori_loop(0, shards // per, unpack, 0)

    tok = tok_ref[...]
    cot = cot_ref[...]
    hidden = lax.dot_general(
        tok, at_ref[:, :depth], NT, preferred_element_type=f32
    ).astype(bf16)
    back = lax.dot_general(cot, at_ref[:, depth:], NT, preferred_element_type=f32).astype(bf16)
    hid_ref[...] = hidden
    back_ref[...] = back
    t_ref[:, :depth] = adapter_scale * lax.dot_general(
        back, tok, TN, preferred_element_type=f32
    )
    t_ref[:, depth:] = adapter_scale * lax.dot_general(
        hidden, cot, TN, preferred_element_type=f32
    )

    def pack(a, carry):
        cols = [
            t_ref[:, pl.ds(pl.multiple_of(a * group + LANES * j, LANES), LANES)]
            for j in range(per + 1)
        ]
        for j in range(per):
            main = jnp.where(lane >= tail * j, cols[j], cols[j + 1])
            if j:
                main = pltpu.roll(main, LANES - tail * j, axis=1)
            packed = jnp.zeros((8, LANES), f32)
            for b in range(per):
                piece = cols[j + 1][8 * b : 8 * b + 8]
                if b != j:
                    piece = pltpu.roll(piece, tail * ((b - j) % per), axis=1)
                packed = jnp.where(lane8 // tail == b, piece, packed)
            terms_ref[a * per + j] = jnp.concatenate([main, packed], axis=0).astype(
                terms_ref.dtype
            )
        return carry

    lax.fori_loop(0, shards // per, pack, 0)


def main_kernel(tok_ref, cot_ref, w_ref, at_ref, up_ref, hid_ref, back_ref, keys_ref, grad_ref, acc_ref):
    step = pl.program_id(0)

    @pl.when(step == 0)
    def _():
        acc_ref[...] = adapter_scale * jnp.dot(
            hid_ref[...], up_ref[...], preferred_element_type=f32
        )

    acc_ref[...] += jnp.dot(tok_ref[...], w_ref[...], preferred_element_type=f32)
    grad = lax.dot_general(cot_ref[...], w_ref[...], NT, preferred_element_type=f32)
    grad += adapter_scale * jnp.dot(back_ref[...], at_ref[...], preferred_element_type=f32)
    grad_ref[...] = grad.astype(grad_ref.dtype)

    @pl.when(step == pl.num_programs(0) - 1)
    def _():
        keys_ref[...] = acc_ref[...].astype(keys_ref.dtype)


def whole(memory=pltpu.VMEM):
    return pl.BlockSpec(memory_space=memory)


def on_device(tokens, cotangent, frozen_weight, adapters, tile_job, job_slot):
    rows, depth = tokens.shape
    key_columns = cotangent.shape[1]
    slot_count, row_count, rank = adapters.shape
    total_jobs = job_slot.shape[0]
    groups = lax.axis_size("grp")
    shards = lax.axis_size("seq")
    packed_rows = row_count * rank // LANES
    width = depth + key_columns
    group = lax.axis_index("grp").reshape(1).astype(jnp.int32)
    jobs = tile_job.reshape(-1)

    weight = lax.all_gather(frozen_weight, "seq", axis=0, tiled=True)

    own = pl.pallas_call(
        pack_kernel,
        out_shape=jax.ShapeDtypeStruct((slot_count, packed_rows, LANES), bf16),
        in_specs=[whole()],
        out_specs=whole(),
        compiler_params=params(),
        name="pack",
    )(jnp.swapaxes(adapters, 1, 2))
    every = lax.all_gather(own, "grp", axis=0, tiled=True)
    smem = whole(pltpu.SMEM)
    outgoing = pl.pallas_call(
        pick_kernel,
        out_shape=jax.ShapeDtypeStruct((shards, packed_rows, LANES), bf16),
        in_specs=[smem, smem, smem, whole()],
        out_specs=whole(),
        compiler_params=params(),
        name="pick",
    )(group, jobs, job_slot, every)
    arrived = lax.all_to_all(outgoing, "seq", split_axis=0, concat_axis=0, tiled=True)
    terms, adapter, hidden, back = pl.pallas_call(
        tile_kernel,
        out_shape=(
            jax.ShapeDtypeStruct((shards, packed_rows, LANES), bf16),
            jax.ShapeDtypeStruct((rank, width), bf16),
            jax.ShapeDtypeStruct((rows, rank), bf16),
            jax.ShapeDtypeStruct((rows, rank), bf16),
        ),
        in_specs=[whole()] * 3,
        out_specs=(whole(),) * 4,
        scratch_shapes=[pltpu.VMEM((rank, width), f32)],
        compiler_params=params(),
        name="tile",
    )(arrived, tokens, cotangent)
    incoming = lax.all_to_all(terms, "seq", split_axis=0, concat_axis=0, tiled=True)
    sums = pl.pallas_call(
        sum_kernel,
        out_shape=jax.ShapeDtypeStruct((total_jobs, packed_rows, LANES), f32),
        in_specs=[smem, smem, smem, whole()],
        out_specs=whole(),
        compiler_params=params(),
        name="sum",
    )(group, jobs, job_slot, incoming)
    owned = lax.psum_scatter(sums, "grp", scatter_dimension=0, tiled=True)
    grads = pl.pallas_call(
        unpack_kernel,
        out_shape=jax.ShapeDtypeStruct((slot_count, rank, row_count), f32),
        in_specs=[whole()],
        out_specs=whole(),
        compiler_params=params(),
        name="unpack",
    )(owned)

    block = 512
    steps = depth // block
    keys, token_gradient = pl.pallas_call(
        main_kernel,
        grid=(steps,),
        out_shape=(
            jax.ShapeDtypeStruct((rows, key_columns), bf16),
            jax.ShapeDtypeStruct((rows, depth), bf16),
        ),
        in_specs=[
            pl.BlockSpec((rows, block), lambda i: (0, i)),
            pl.BlockSpec((rows, key_columns), lambda i: (0, 0)),
            pl.BlockSpec((block, key_columns), lambda i: (i, 0)),
            pl.BlockSpec((rank, block), lambda i: (0, i)),
            pl.BlockSpec((rank, key_columns), lambda i: (0, depth // key_columns)),
            pl.BlockSpec((rows, rank), lambda i: (0, 0)),
            pl.BlockSpec((rows, rank), lambda i: (0, 0)),
        ],
        out_specs=(
            pl.BlockSpec((rows, key_columns), lambda i: (0, 0)),
            pl.BlockSpec((rows, block), lambda i: (0, i)),
        ),
        scratch_shapes=[pltpu.VMEM((rows, key_columns), f32)],
        compiler_params=params(),
        cost_estimate=pl.CostEstimate(
            flops=4 * rows * depth * key_columns,
            bytes_accessed=2 * depth * key_columns + 4 * rows * width,
            transcendentals=0,
        ),
        name="base",
    )(tokens, cotangent, weight, adapter, adapter, hidden, back)
    return keys, token_gradient, jnp.swapaxes(grads, 1, 2)


def solution(mesh):
    placed = (
        P(("grp", "seq"), None),
        P(("grp", "seq"), None),
        P("seq", None),
        P("grp", "seq", None),
        P(),
        P(),
    )
    return jax.shard_map(
        on_device,
        mesh=mesh,
        in_specs=placed,
        out_specs=(P(("grp", "seq"), None), P(("grp", "seq"), None), P("grp", "seq", None)),
        check_vma=False,
    )
```

time: 624 us -> 261 us (0.42)
  blocking collectives: 297 us -> 80.4 us
  waiting for transfers between devices: 188 us -> 128 us
  local copies, waits for them, and re-layouts: 65.8 us -> 13.2 us
  matrix products: 34.7 us -> 0 us
  Pallas kernels: 0 us -> 22.9 us
  other arithmetic: 14.6 us -> 0 us
    all_to_all x2, blocking collectives: 297 us -> 80.4 us  [the longest x1 42.9 us: on_device(): lax.all_to_all(outgoing, 'seq', split_axis=0, concat_axis=0, tiled=True)]
    all_to_all x1 -> x0, waiting for transfers between devices: 93.4 us -> none  [on_device(): lax.all_to_all(terms, 'seq', split_axis=1, concat_axis=1, tiled=True)]
    all_gather x1 -> x2, waiting for transfers between devices: 51 us -> 97.6 us  [the longest x1 66.6 us: on_device(): weight = lax.all_gather(frozen_weight, 'seq', axis=0, tiled=True)]
    dot_general x9 -> x0, matrix products: 34.7 us -> none  [the longest x1 13.2 us: on_device(): jnp.einsum('nk,dk->nd', cotangent, piece, preferred_element_type=jnp.floa...]
    pallas_call x0 -> x6, Pallas kernels: none -> 22.9 us  [the longest x1 12.7 us: on_device(): pl.pallas_call(main_kernel, grid=(steps,), out_shape=(jax.ShapeDtypeStruc...]
    reshape x7 -> x0, local copies, waits for them, and re-layouts: 22.8 us -> none  [the longest x2 12.1 us: on_device(): jnp.concatenate([down_term, up_term], axis=1)]
    all_to_all x2 -> x0, local copies, waits for them, and re-layouts: 14.3 us -> none  [the longest x1 8.26 us: on_device(): lax.all_to_all(outgoing, 'grp', split_axis=0, concat_axis=0, tiled=True)]
    reduce_scatter x1, waiting for transfers between devices: 43.6 us -> 30.1 us  [on_device(): owned = lax.psum_scatter(sums, 'grp', scatter_dimension=0, tiled=True)]
  transfers between devices with their start and end apart: 3 -> 3, of which waited for: 3 -> 3; matrix products, arithmetic and copies ran while one was open for 1% -> 0% of each run, Pallas kernels for 0% -> 0%
where the time goes in v1:
time: 261 us; the launch traced here: 260 us
  waiting for transfers between devices  128 us (49%)
  blocking collectives  80.4 us (31%)
  Pallas kernels  22.9 us (9%)
  between operations  15.5 us (6%)
  local copies, waits for them, and re-layouts  13.2 us (5%)
    all_gather x1, waiting for transfers between devices, on_device(): weight = lax.all_gather(frozen_weight, 'seq', axis=0, tiled=True)  66.6 us
    all_to_all x1, blocking collectives, on_device(): lax.all_to_all(outgoing, 'seq', split_axis=0, concat_axis=0, tiled=True)  42.9 us
    all_to_all x1, blocking collectives, on_device(): lax.all_to_all(terms, 'seq', split_axis=0, concat_axis=0, tiled=True)  37.5 us
    all_gather x1, waiting for transfers between devices, on_device(): every = lax.all_gather(own, 'grp', axis=0, tiled=True)  31 us
    reduce_scatter x1, waiting for transfers between devices, on_device(): owned = lax.psum_scatter(sums, 'grp', scatter_dimension=0, tiled=True)  30.1 us
    unnamed x28, local copies, waits for them, and re-layouts  13.2 us
    pallas_call x1, Pallas kernels, on_device(): pl.pallas_call(main_kernel, grid=(steps,), out_shape=(jax.ShapeDtypeStruc...  12.7 us
  transfers between devices with their start and end apart: 3, of which 3 were waited for; matrix products, arithmetic and copies ran while one was open for 0% of the time, Pallas kernels for 0%

profile of v1, /device:TPU:1, one launch (start us, length us, event | category | flops | bytes accessed | tf_op | source)
XLA Modules:
  0.0 260.5 jit_solution(8440183701821243617)
XLA Ops:
  8.1 1.0 copy-done.5
  9.1 0.8 pack.1
  10.0 0.0 reduce-scatter.2.cloned.1.call-start
  10.0 31.0 %all-gather.5.cloned.1.call-done.a_ref = bf16[64,72,128]{2,1,0:T(8,128)(2,1)} async-done(((bf16[16,72,128]{2,1,0:T(8,128)(2,1)}), bf16[64,72,128]{2,1,0:T(8,128)(2,1)}) %all-gather.5.cloned.1.call-update) | async-done | bytes 1179664 | tf_op jit(solution)/shard_map/all_gather | solution.py:189
  41.0 1.3 copy-done.2
  42.3 0.7 copy-done.10
  43.0 0.7 copy-done.12
  43.6 1.5 pick.1
  45.1 42.9 %all_to_all.10.x_ref = bf16[64,72,128]{2,1,0:T(8,128)(2,1)S(1)} all-to-all(bf16[64,72,128]{2,1,0:T(8,128)(2,1)S(1)} %pick.1), channel_id=1, replica_groups=mesh['grp'=4,'seq'=64] {'seq'}, dimensions={0} | all-to-all | bytes 2359296 | tf_op jit(solution)/shard_map/all_to_all | solution.py:199
  88.1 3.5 %tile.1 = (bf16[64,72,128]{2,1,0:T(8,128)(2,1)S(1)}, bf16[64,9216]{1,0:T(8,128)(2,1)S(1)}, bf16[128,64]{1,0:T(8,128)(2,1)S(1)}, bf16[128,64]{1,0:T(8,128)(2,1)S(1)}) custom-call(bf16[64,72,128]{2,1,0:T(8,128)(2,1)S(1)} %all_to_all.10.x_ref, bf16[128,8192]{1,0:T(8,128)(2,1)S(1)} %copy-done.1, bf16[128,1024]{1,0:T(8,128)(2,1)S(1)} %copy-done.3), custom_call_target="tpu_custom_call" | custom-call | tf_op jit(solution)/shard_map/tile/pallas_call | solution.py:200
  91.6 0.6 copy-done.6
  92.2 0.6 copy-done.8
  92.8 37.5 %all_to_all.11.x_ref = bf16[64,72,128]{2,1,0:T(8,128)(2,1)S(1)} all-to-all(bf16[64,72,128]{2,1,0:T(8,128)(2,1)S(1)} %get-tuple-element.14), channel_id=1, replica_groups=mesh['grp'=4,'seq'=64] {'seq'}, dimensions={0} | all-to-all | bytes 2359296 | tf_op jit(solution)/shard_map/all_to_all | solution.py:214
  130.3 3.2 %sum.1 = f32[64,72,128]{2,1,0:T(8,128)} custom-call(s32[1]{0:T(128)} %bitcast.group_ref, s32[256]{0:T(256)S(1)} %bitcast.6, s32[64]{0:T(128)S(1)} %copy-done.13, bf16[64,72,128]{2,1,0:T(8,128)(2,1)S(1)} %all_to_all.11.x_ref), custom_call_target="tpu_custom_call" | custom-call | tf_op jit(solution)/shard_map/sum/pallas_call | solution.py:215
  133.5 0.0 all-gather.3.cloned.1.call-start
  133.6 0.5 all-gather.3.cloned.1.call-update
  134.1 30.1 %reduce-scatter.2.cloned.1.call-done.x_ref = f32[16,72,128]{2,1,0:T(8,128)} async-done(((f32[64,72,128]{2,1,0:T(8,128)}), f32[16,72,128]{2,1,0:T(8,128)}) %reduce-scatter.2.cloned.1.call-update) | async-done | bytes 589840 | tf_op jit(solution)/shard_map/reduce_scatter | solution.py:223
  164.2 1.1 copy-done.4
  165.2 1.2 unpack.1
  166.4 66.6 %all-gather.3.cloned.1.call-done.w_ref = bf16[8192,1024]{1,0:T(8,128)(2,1)} async-done(((bf16[128,1024]{1,0:T(8,128)(2,1)}), bf16[8192,1024]{1,0:T(8,128)(2,1)}) %all-gather.3.cloned.1.call-update) | async-done | bytes 16777232 | tf_op jit(solution)/shard_map/all_gather | solution.py:179
  233.0 5.8 %copy-done = bf16[8192,1024]{1,0:T(8,128)(2,1)S(1)} copy-done((bf16[8192,1024]{1,0:T(8,128)(2,1)S(1)}, bf16[8192,1024]{1,0:T(8,128)(2,1)}, u32[]{:S(2)}) %copy-start) | copy-done | bytes 16777240
  238.8 0.8 copy-done.7
  239.6 0.8 copy-done.9
  240.3 12.7 %base.1 = (bf16[128,1024]{1,0:T(8,128)(2,1)}, bf16[128,8192]{1,0:T(8,128)(2,1)}) custom-call(bf16[128,8192]{1,0:T(8,128)(2,1)S(1)} %copy-done.1, bf16[128,1024]{1,0:T(8,128)(2,1)S(1)} %copy-done.3, bf16[8192,1024]{1,0:T(8,128)(2,1)S(1)} %copy-done, bf16[64,9216]{1,0:T(8,128)(2,1)S(1)} %get-tuple-element.9.at_ref.up_ref, ...), custom_call_target="tpu_custom_call" | custom-call | flops 4294967296 | bytes 21495808 | tf_op jit(solution)/shard_map/base/pallas_call | solution.py:235
  (21 shorter events, 0.1 us)
Async XLA Ops:
  8.0 33.0 %all-gather.5.cloned.1.call-start = ((), (), s32[]{:S(2)}) async-start(), calls=%async_computation.4 | async-start | bytes 1474560 | tf_op jit(solution)/shard_map/all_gather | solution.py:189
  8.0 1.0 copy-start.5
  10.0 154.2 %reduce-scatter.2.cloned.1.call-start = ((), (), s32[]{:S(2)}) async-start(), calls=%async_computation.5 | async-start | bytes 2949120 | tf_op jit(solution)/shard_map/reduce_scatter | solution.py:223
  41.0 1.3 copy-start.2
  42.3 0.7 copy-start.10
  43.0 0.7 copy-start.12
  45.1 43.0 %copy-start.1 = (bf16[128,8192]{1,0:T(8,128)(2,1)S(1)}, bf16[128,8192]{1,0:T(8,128)(2,1)}, u32[]{:S(2)}) copy-start(bf16[128,8192]{1,0:T(8,128)(2,1)} %tok_ref.3) | copy-start | bytes 6291460
  45.1 43.0 %copy-start.3 = (bf16[128,1024]{1,0:T(8,128)(2,1)S(1)}, bf16[128,1024]{1,0:T(8,128)(2,1)}, u32[]{:S(2)}) copy-start(bf16[128,1024]{1,0:T(8,128)(2,1)} %cot_ref.3) | copy-start | bytes 786436
  91.6 0.6 copy-start.6
  92.2 0.6 copy-start.8
  92.8 37.5 %copy-start.11 = (s32[256,1]{0,1:T(1,128)S(1)}, s32[256,1]{0,1:T(1,128)}, u32[]{:S(2)}) copy-start(s32[256,1]{0,1:T(1,128)} %param.10) | copy-start | bytes 3076
  92.8 37.5 %copy-start.13 = (s32[64]{0:T(128)S(1)}, s32[64]{0:T(128)}, u32[]{:S(2)}) copy-start(s32[64]{0:T(128)} %slot_ref.3) | copy-start | bytes 772
  133.5 99.5 %all-gather.3.cloned.1.call-start = ((), (), s32[]{:S(2)}) async-start(), calls=%async_computation.3 | async-start | bytes 17039360 | tf_op jit(solution)/shard_map/all_gather | solution.py:179
  164.2 1.1 copy-start.4
  233.0 5.8 %copy-start = (bf16[8192,1024]{1,0:T(8,128)(2,1)S(1)}, bf16[8192,1024]{1,0:T(8,128)(2,1)}, u32[]{:S(2)}) copy-start(bf16[8192,1024]{1,0:T(8,128)(2,1)} %all-gather.3.cloned.1.call-done.w_ref) | copy-start | bytes 50331652
  238.8 0.8 copy-start.7
  239.6 0.8 copy-start.9
Sparse Core Ops, SparseCore 0:
  11.2 29.7 all-gather.4
  133.6 30.4 reduce-scatter.1
Sparse Core Ops, SparseCore 1:
  136.8 96.2 all-gather.2

commit v2 on v1

--- a/solution.py
+++ b/solution.py
@@ -212,6 +212,7 @@
         name="tile",
     )(arrived, tokens, cotangent)
     incoming = lax.all_to_all(terms, "seq", split_axis=0, concat_axis=0, tiled=True)
+    incoming, weight = lax.optimization_barrier((incoming, weight))
     sums = pl.pallas_call(
         sum_kernel,
         out_shape=jax.ShapeDtypeStruct((total_jobs, packed_rows, LANES), f32),
@@ -253,7 +254,7 @@
             pl.BlockSpec((rows, block), lambda i: (0, i)),
         ),
         scratch_shapes=[pltpu.VMEM((rows, key_columns), f32)],
-        compiler_params=params(),
+        compiler_params=params(56),
         cost_estimate=pl.CostEstimate(
             flops=4 * rows * depth * key_columns,
             bytes_accessed=2 * depth * key_columns + 4 * rows * width,

time: 261 us -> 221 us (0.85)
  waiting for transfers between devices: 128 us -> 69.5 us
  blocking collectives: 80.4 us -> 102 us
  local copies, waits for them, and re-layouts: 13.2 us -> 5.67 us
  Pallas kernels: 22.9 us -> 28.9 us
    all_gather x1, waiting for transfers between devices: 66.6 us -> 24.5 us  [on_device(): weight = lax.all_gather(frozen_weight, 'seq', axis=0, tiled=True)]
    reduce_scatter x1, waiting for transfers between devices: 30.1 us -> 14 us  [on_device(): owned = lax.psum_scatter(sums, 'grp', scatter_dimension=0, tiled=True)]
    all_to_all x1, blocking collectives: 37.5 us -> 50.2 us  [on_device(): lax.all_to_all(terms, 'seq', split_axis=0, concat_axis=0, tiled=True)]
    all_to_all x1, blocking collectives: 42.9 us -> 52.3 us  [on_device(): lax.all_to_all(outgoing, 'seq', split_axis=0, concat_axis=0, tiled=True)]
    unnamed x28 -> x20, local copies, waits for them, and re-layouts: 13.2 us -> 5.67 us
    pallas_call x1, Pallas kernels: 12.7 us -> 18.7 us  [on_device(): pl.pallas_call(main_kernel, grid=(steps,), out_shape=(jax.ShapeDtypeStruc...]
  transfers between devices with their start and end apart: 3 -> 3, of which waited for: 3 -> 3; matrix products, arithmetic and copies ran while one was open for 0% -> 0% of each run, Pallas kernels for 0% -> 11%
where the time goes in v2:
time: 221 us; the launch traced here: 220 us
  blocking collectives  102 us (46%)
  waiting for transfers between devices  69.5 us (31%)
  Pallas kernels  28.9 us (13%)
  between operations  13.8 us (6%)
  local copies, waits for them, and re-layouts  5.67 us (3%)
    all_to_all x1, blocking collectives, on_device(): lax.all_to_all(outgoing, 'seq', split_axis=0, concat_axis=0, tiled=True)  52.3 us
    all_to_all x1, blocking collectives, on_device(): lax.all_to_all(terms, 'seq', split_axis=0, concat_axis=0, tiled=True)  50.2 us
    all_gather x1, waiting for transfers between devices, on_device(): every = lax.all_gather(own, 'grp', axis=0, tiled=True)  30.3 us
    all_gather x1, waiting for transfers between devices, on_device(): weight = lax.all_gather(frozen_weight, 'seq', axis=0, tiled=True)  24.5 us
    pallas_call x1, Pallas kernels, on_device(): pl.pallas_call(main_kernel, grid=(steps,), out_shape=(jax.ShapeDtypeStruc...  18.7 us
    reduce_scatter x1, waiting for transfers between devices, on_device(): owned = lax.psum_scatter(sums, 'grp', scatter_dimension=0, tiled=True)  14 us
    unnamed x20, local copies, waits for them, and re-layouts  5.67 us
  transfers between devices with their start and end apart: 3, of which 3 were waited for; matrix products, arithmetic and copies ran while one was open for 0% of the time, Pallas kernels for 11%

profile of v2, /device:TPU:1, one launch (start us, length us, event | category | flops | bytes accessed | tf_op | source)
XLA Modules:
  0.0 220.4 jit_solution(11489150521299879488)
XLA Ops:
  7.2 0.0 all-gather.3.cloned.1.call-start
  7.2 1.0 copy-done.5
  8.3 0.8 pack.1
  9.1 0.0 all-gather.3.cloned.1.call-update
  9.1 0.0 all-gather.5.cloned.1.call-start
  9.2 0.7 all-gather.5.cloned.1.call-update
  9.9 0.0 reduce-scatter.2.cloned.1.call-start
  9.9 30.3 %all-gather.3.cloned.1.call-done.a_ref = bf16[64,72,128]{2,1,0:T(8,128)(2,1)} async-done(((bf16[16,72,128]{2,1,0:T(8,128)(2,1)}), bf16[64,72,128]{2,1,0:T(8,128)(2,1)}) %all-gather.3.cloned.1.call-update) | async-done | bytes 1179664 | tf_op jit(solution)/shard_map/all_gather | solution.py:189
  40.2 1.3 copy-done.2
  41.5 1.5 pick.1
  43.0 0.0 copy-start.3
  43.0 52.3 %all_to_all.10.x_ref = bf16[64,72,128]{2,1,0:T(8,128)(2,1)S(1)} all-to-all(bf16[64,72,128]{2,1,0:T(8,128)(2,1)S(1)} %pick.1), channel_id=1, replica_groups=mesh['grp'=4,'seq'=64] {'seq'}, dimensions={0} | all-to-all | bytes 2359296 | tf_op jit(solution)/shard_map/all_to_all | solution.py:199
  95.3 3.5 %tile.1 = (bf16[64,72,128]{2,1,0:T(8,128)(2,1)S(1)}, bf16[64,9216]{1,0:T(8,128)(2,1)S(1)}, bf16[128,64]{1,0:T(8,128)(2,1)S(1)}, bf16[128,64]{1,0:T(8,128)(2,1)S(1)}) custom-call(bf16[64,72,128]{2,1,0:T(8,128)(2,1)S(1)} %all_to_all.10.x_ref, bf16[128,8192]{1,0:T(8,128)(2,1)S(1)} %copy-done, bf16[128,1024]{1,0:T(8,128)(2,1)S(1)} %copy-done.3), custom_call_target="tpu_custom_call" | custom-call | tf_op jit(solution)/shard_map/tile/pallas_call | solution.py:200
  98.8 1.1 copy-done.1
  99.8 0.6 copy-done.6
  100.4 0.6 copy-done.7
  101.0 50.2 %all_to_all.11.x_ref = bf16[64,72,128]{2,1,0:T(8,128)(2,1)S(1)} all-to-all(bf16[64,72,128]{2,1,0:T(8,128)(2,1)S(1)} %get-tuple-element.11), channel_id=1, replica_groups=mesh['grp'=4,'seq'=64] {'seq'}, dimensions={0} | all-to-all | bytes 2359296 | tf_op jit(solution)/shard_map/all_to_all | solution.py:214
  151.2 24.5 %all-gather.5.cloned.1.call-done.w_ref = bf16[8192,1024]{1,0:T(8,128)(2,1)} async-done(((bf16[128,1024]{1,0:T(8,128)(2,1)}), bf16[8192,1024]{1,0:T(8,128)(2,1)}) %all-gather.5.cloned.1.call-update) | async-done | bytes 16777232 | tf_op jit(solution)/shard_map/all_gather | solution.py:179
  175.7 3.2 %sum.1 = f32[64,72,128]{2,1,0:T(8,128)} custom-call(s32[1]{0:T(128)} %bitcast.group_ref, s32[256]{0:T(256)S(1)} %bitcast.6, s32[64]{0:T(128)S(1)} %copy-done.9, bf16[64,72,128]{2,1,0:T(8,128)(2,1)S(1)} %all_to_all.11.x_ref), custom_call_target="tpu_custom_call" | custom-call | tf_op jit(solution)/shard_map/sum/pallas_call | solution.py:216
  178.9 0.0 reduce-scatter.2.cloned.1.call-update
  178.9 18.7 %base.1 = (bf16[128,1024]{1,0:T(8,128)(2,1)}, bf16[128,8192]{1,0:T(8,128)(2,1)}) custom-call(bf16[128,8192]{1,0:T(8,128)(2,1)} %tok_ref.3, bf16[128,1024]{1,0:T(8,128)(2,1)} %cot_ref.3, bf16[8192,1024]{1,0:T(8,128)(2,1)} %all-gather.5.cloned.1.call-done.w_ref, bf16[64,9216]{1,0:T(8,128)(2,1)} %copy-done.1, bf16[64,9216]{1,0:T(8,128)(2,1)} %copy-done.1, ...), custom_call_target="tpu_custom_call" | custom-call | flops 4294967296 | bytes 21495808 | tf_op jit(solution)/shard_map/base/pallas_call | solution.py:236
  197.7 14.0 %reduce-scatter.2.cloned.1.call-done.x_ref = f32[16,72,128]{2,1,0:T(8,128)} async-done(((f32[64,72,128]{2,1,0:T(8,128)}), f32[16,72,128]{2,1,0:T(8,128)}) %reduce-scatter.2.cloned.1.call-update) | async-done | bytes 589840 | tf_op jit(solution)/shard_map/reduce_scatter | solution.py:224
  211.6 1.1 copy-done.4
  212.7 1.2 unpack.1
  (13 shorter events, 0.0 us)
Async XLA Ops:
  7.2 33.0 %copy-start.9 = (s32[64]{0:T(128)S(1)}, s32[64]{0:T(128)}, u32[]{:S(2)}) copy-start(s32[64]{0:T(128)} %slot_ref.3) | copy-start | bytes 772
  7.2 33.0 %copy-start.8 = (s32[256,1]{0,1:T(1,128)S(1)}, s32[256,1]{0,1:T(1,128)}, u32[]{:S(2)}) copy-start(s32[256,1]{0,1:T(1,128)} %param.10) | copy-start | bytes 3076
  7.2 33.0 %all-gather.3.cloned.1.call-start = ((), (), s32[]{:S(2)}) async-start(), calls=%async_computation.3 | async-start | bytes 1474560 | tf_op jit(solution)/shard_map/all_gather | solution.py:189
  7.2 1.0 copy-start.5
  9.1 166.6 %all-gather.5.cloned.1.call-start = ((), (), s32[]{:S(2)}) async-start(), calls=%async_computation.4 | async-start | bytes 17039360 | tf_op jit(solution)/shard_map/all_gather | solution.py:179
  9.9 201.7 %reduce-scatter.2.cloned.1.call-start = ((), (), s32[]{:S(2)}) async-start(), calls=%async_computation.5 | async-start | bytes 2949120 | tf_op jit(solution)/shard_map/reduce_scatter | solution.py:224
  40.2 1.3 copy-start.2
  43.0 52.3 %copy-start = (bf16[128,8192]{1,0:T(8,128)(2,1)S(1)}, bf16[128,8192]{1,0:T(8,128)(2,1)}, u32[]{:S(2)}) copy-start(bf16[128,8192]{1,0:T(8,128)(2,1)} %tok_ref.3) | copy-start | bytes 6291460
  43.0 52.3 %copy-start.3 = (bf16[128,1024]{1,0:T(8,128)(2,1)S(1)}, bf16[128,1024]{1,0:T(8,128)(2,1)}, u32[]{:S(2)}) copy-start(bf16[128,1024]{1,0:T(8,128)(2,1)} %cot_ref.3) | copy-start | bytes 786436
  98.8 1.1 copy-start.1
  99.8 0.6 copy-start.6
  100.4 0.6 copy-start.7
  211.6 1.1 copy-start.4
Sparse Core Ops, SparseCore 0:
  10.4 29.7 all-gather.2
  43.0 132.7 all-gather.4
  179.1 32.5 reduce-scatter.1

commit v3 on v2

--- a/solution.py
+++ b/solution.py
@@ -1,5 +1,3 @@
-import functools
-
 import jax
 import jax.numpy as jnp
 from jax import lax
@@ -30,34 +28,56 @@
         o_ref[s, rank:, :] = jnp.concatenate(pieces, axis=1).astype(o_ref.dtype)
 
 
-def pick_kernel(group_ref, job_ref, slot_ref, a_ref, o_ref):
+def pick_kernel(group_ref, job_ref, slot_ref, a0_ref, a1_ref, a2_ref, a3_ref, o_ref):
     tiles = o_ref.shape[0]
+    sources = (a0_ref, a1_ref, a2_ref, a3_ref)
+    count = a0_ref.shape[0]
+    me = group_ref[0]
 
     def step(t, carry):
-        o_ref[t] = a_ref[slot_ref[job_ref[group_ref[0] * tiles + t]]]
+        s = slot_ref[job_ref[me * tiles + t]]
+        away = lax.rem(s // count - me + len(sources), len(sources))
+        for k, source in enumerate(sources):
+
+            @pl.when(away == k)
+            def _():
+                o_ref[t] = source[lax.rem(s, count)]
+
         return carry
 
     lax.fori_loop(0, tiles, step, 0)
 
 
-def sum_kernel(group_ref, job_ref, slot_ref, x_ref, o_ref):
+def sum_kernel(group_ref, job_ref, slot_ref, x_ref, o0_ref, o1_ref, o2_ref, o3_ref):
     tiles = x_ref.shape[0]
-    o_ref[...] = jnp.zeros_like(o_ref)
+    sinks = (o0_ref, o1_ref, o2_ref, o3_ref)
+    count = o0_ref.shape[0]
+    me = group_ref[0]
+    for sink in sinks:
+        sink[...] = jnp.zeros_like(sink)
 
     def step(t, carry):
-        s = slot_ref[job_ref[group_ref[0] * tiles + t]]
-        o_ref[s] = o_ref[s] + x_ref[t].astype(f32)
+        s = slot_ref[job_ref[me * tiles + t]]
+        away = lax.rem(s // count - me + len(sinks), len(sinks))
+        at = lax.rem(s, count)
+        for k, sink in enumerate(sinks):
+
+            @pl.when(away == k)
+            def _():
+                sink[at] = sink[at] + x_ref[t].astype(f32)
+
         return carry
 
     lax.fori_loop(0, tiles, step, 0)
 
 
-def unpack_kernel(x_ref, o_ref):
+def unpack_kernel(x0_ref, x1_ref, x2_ref, x3_ref, o_ref):
     slots, rank, width = o_ref.shape
     tail = width - LANES
     for s in range(slots):
-        o_ref[s, :, :LANES] = x_ref[s, :rank, :]
-        rest = x_ref[s, rank:, :]
+        total = (x0_ref[s] + x1_ref[s]) + (x2_ref[s] + x3_ref[s])
+        o_ref[s, :, :LANES] = total[:rank]
+        rest = total[rank:]
         for b in range(LANES // tail):
             o_ref[s, 8 * b : 8 * b + 8, LANES:] = rest[:, tail * b : tail * (b + 1)]
 
@@ -160,6 +180,10 @@
         keys_ref[...] = acc_ref[...].astype(keys_ref.dtype)
 
 
+def shift(x, by, groups):
+    return lax.ppermute(x, "grp", [(i, (i + by) % groups) for i in range(groups)])
+
+
 def whole(memory=pltpu.VMEM):
     return pl.BlockSpec(memory_space=memory)
 
@@ -168,7 +192,6 @@
     rows, depth = tokens.shape
     key_columns = cotangent.shape[1]
     slot_count, row_count, rank = adapters.shape
-    total_jobs = job_slot.shape[0]
     groups = lax.axis_size("grp")
     shards = lax.axis_size("seq")
     packed_rows = row_count * rank // LANES
@@ -186,16 +209,16 @@
         compiler_params=params(),
         name="pack",
     )(jnp.swapaxes(adapters, 1, 2))
-    every = lax.all_gather(own, "grp", axis=0, tiled=True)
+    every = (own,) + tuple(shift(own, -k, groups) for k in range(1, groups))
     smem = whole(pltpu.SMEM)
     outgoing = pl.pallas_call(
         pick_kernel,
         out_shape=jax.ShapeDtypeStruct((shards, packed_rows, LANES), bf16),
-        in_specs=[smem, smem, smem, whole()],
+        in_specs=[smem, smem, smem] + [whole()] * groups,
         out_specs=whole(),
         compiler_params=params(),
         name="pick",
-    )(group, jobs, job_slot, every)
+    )(group, jobs, job_slot, *every)
     arrived = lax.all_to_all(outgoing, "seq", split_axis=0, concat_axis=0, tiled=True)
     terms, adapter, hidden, back = pl.pallas_call(
         tile_kernel,
@@ -215,21 +238,21 @@
     incoming, weight = lax.optimization_barrier((incoming, weight))
     sums = pl.pallas_call(
         sum_kernel,
-        out_shape=jax.ShapeDtypeStruct((total_jobs, packed_rows, LANES), f32),
+        out_shape=(jax.ShapeDtypeStruct((slot_count, packed_rows, LANES), f32),) * groups,
         in_specs=[smem, smem, smem, whole()],
-        out_specs=whole(),
+        out_specs=(whole(),) * groups,
         compiler_params=params(),
         name="sum",
     )(group, jobs, job_slot, incoming)
-    owned = lax.psum_scatter(sums, "grp", scatter_dimension=0, tiled=True)
+    owned = (sums[0],) + tuple(shift(sums[k], k, groups) for k in range(1, groups))
     grads = pl.pallas_call(
         unpack_kernel,
         out_shape=jax.ShapeDtypeStruct((slot_count, rank, row_count), f32),
-        in_specs=[whole()],
+        in_specs=[whole()] * groups,
         out_specs=whole(),
         compiler_params=params(),
         name="unpack",
-    )(owned)
+    )(*owned)
 
     block = 512
     steps = depth // block

time: 221 us -> 188 us (0.85)
  waiting for transfers between devices: 69.5 us -> 29.1 us
  starting transfers between devices: 0.12 us -> 10.4 us
  blocking collectives: 102 us -> 98.5 us
    all_gather x1 -> x0, waiting for transfers between devices: 30.3 us -> none  [on_device(): every = lax.all_gather(own, 'grp', axis=0, tiled=True)]
    ppermute x0 -> x6, waiting for transfers between devices: none -> 17.8 us  [shift(): lax.ppermute(x, 'grp', [(i, (i + by) % groups) for i in range(groups)])]
    reduce_scatter x1 -> x0, waiting for transfers between devices: 14 us -> none  [on_device(): owned = lax.psum_scatter(sums, 'grp', scatter_dimension=0, tiled=True)]
    all_gather x1, waiting for transfers between devices: 24.5 us -> 10.7 us  [on_device(): weight = lax.all_gather(frozen_weight, 'seq', axis=0, tiled=True)]
    ppermute x0 -> x6, starting transfers between devices: none -> 10.3 us  [shift(): lax.ppermute(x, 'grp', [(i, (i + by) % groups) for i in range(groups)])]
    all_to_all x1, blocking collectives: 52.3 us -> 46.8 us  [on_device(): lax.all_to_all(outgoing, 'seq', split_axis=0, concat_axis=0, tiled=True)]
  transfers between devices with their start and end apart: 3 -> 7, of which waited for: 3 -> 4; matrix products, arithmetic and copies ran while one was open for 0% -> 0% of each run, Pallas kernels for 11% -> 14%
where the time goes in v3:
time: 188 us; the launch traced here: 187 us
  blocking collectives  98.5 us (52%)
  Pallas kernels  30.4 us (16%)
  waiting for transfers between devices  29.1 us (15%)
  between operations  14.1 us (8%)
  starting transfers between devices  10.4 us (6%)
  local copies, waits for them, and re-layouts  4.64 us (2%)
    all_to_all x1, blocking collectives, on_device(): lax.all_to_all(terms, 'seq', split_axis=0, concat_axis=0, tiled=True)  51.6 us
    all_to_all x1, blocking collectives, on_device(): lax.all_to_all(outgoing, 'seq', split_axis=0, concat_axis=0, tiled=True)  46.8 us
    pallas_call x1, Pallas kernels, on_device(): pl.pallas_call(main_kernel, grid=(steps,), out_shape=(jax.ShapeDtypeStruc...  18.6 us
    ppermute x6, waiting for transfers between devices, shift(): lax.ppermute(x, 'grp', [(i, (i + by) % groups) for i in range(groups)])  17.8 us
    all_gather x1, waiting for transfers between devices, on_device(): weight = lax.all_gather(frozen_weight, 'seq', axis=0, tiled=True)  10.7 us
    ppermute x6, starting transfers between devices, shift(): lax.ppermute(x, 'grp', [(i, (i + by) % groups) for i in range(groups)])  10.3 us
    unnamed x20, local copies, waits for them, and re-layouts  4.64 us
  transfers between devices with their start and end apart: 7, of which 4 were waited for; matrix products, arithmetic and copies ran while one was open for 0% of the time, Pallas kernels for 14%

profile of v3, /device:TPU:1, one launch (start us, length us, event | category | flops | bytes accessed | tf_op | source)
XLA Modules:
  0.0 187.1 jit_solution(10669060933081551628)
XLA Ops:
  7.2 0.7 all-gather.2.cloned.1.call-update
  7.9 1.0 copy-done.3
  9.1 2.1 %collective-permute-start.2 = (bf16[16,72,128]{2,1,0:T(8,128)(2,1)S(1)}, bf16[16,72,128]{2,1,0:T(8,128)(2,1)S(1)}, u32[]{:S(2)}, u32[]{:S(2)}) collective-permute-start(bf16[16,72,128]{2,1,0:T(8,128)(2,1)S(1)} %pack.1.a0_ref), channel_id=1, source_target_pairs={{0,64},{64,128},{128,192},{192,0},{1,65},{65,129},{129,193},{193,1... | collective-permute-start | bytes 884744 | tf_op jit(solution)/shard_map/ppermute | solution.py:184
  11.2 2.5 %collective-permute-start.1 = (bf16[16,72,128]{2,1,0:T(8,128)(2,1)S(1)}, bf16[16,72,128]{2,1,0:T(8,128)(2,1)S(1)}, u32[]{:S(2)}, u32[]{:S(2)}) collective-permute-start(bf16[16,72,128]{2,1,0:T(8,128)(2,1)S(1)} %pack.1.a0_ref), channel_id=1, source_target_pairs={{0,128},{64,192},{128,0},{192,64},{1,129},{65,193},{129,1},{193,65... | collective-permute-start | bytes 884744 | tf_op jit(solution)/shard_map/ppermute | solution.py:184
  13.7 1.2 collective-permute-start
  14.8 2.1 %collective-permute-done.2.a3_ref = bf16[16,72,128]{2,1,0:T(8,128)(2,1)S(1)} collective-permute-done((bf16[16,72,128]{2,1,0:T(8,128)(2,1)S(1)}, bf16[16,72,128]{2,1,0:T(8,128)(2,1)S(1)}, u32[]{:S(2)}, u32[]{:S(2)}) %collective-permute-start.2) | collective-permute-done | bytes 294944 | tf_op jit(solution)/shard_map/ppermute | solution.py:184
  16.9 9.5 %collective-permute-done.1.a2_ref = bf16[16,72,128]{2,1,0:T(8,128)(2,1)S(1)} collective-permute-done((bf16[16,72,128]{2,1,0:T(8,128)(2,1)S(1)}, bf16[16,72,128]{2,1,0:T(8,128)(2,1)S(1)}, u32[]{:S(2)}, u32[]{:S(2)}) %collective-permute-start.1) | collective-permute-done | bytes 294944 | tf_op jit(solution)/shard_map/ppermute | solution.py:184
  26.4 0.7 copy-done.6
  27.1 0.7 copy-done.8
  27.7 3.3 %pick.1 = bf16[64,72,128]{2,1,0:T(8,128)(2,1)S(1)} custom-call(s32[1]{0:T(128)} %bitcast.group_ref, s32[256]{0:T(256)S(1)} %bitcast.5, s32[64]{0:T(128)S(1)} %copy-done.8, bf16[16,72,128]{2,1,0:T(8,128)(2,1)S(1)} %pack.1.a0_ref, bf16[16,72,128]{2,1,0:T(8,128)(2,1)S(1)} %collective-permute-done.a1_ref, ...), custom_call_target="tpu_custom_call" | custom-call | tf_op jit(solution)/shard_map/pick/pallas_call | solution.py:214
  31.1 46.8 %all_to_all.10.x_ref = bf16[64,72,128]{2,1,0:T(8,128)(2,1)S(1)} all-to-all(bf16[64,72,128]{2,1,0:T(8,128)(2,1)S(1)} %pick.1), channel_id=1, replica_groups=mesh['grp'=4,'seq'=64] {'seq'}, dimensions={0} | all-to-all | bytes 2359296 | tf_op jit(solution)/shard_map/all_to_all | solution.py:222
  77.9 3.5 %tile.1 = (bf16[64,72,128]{2,1,0:T(8,128)(2,1)S(1)}, bf16[64,9216]{1,0:T(8,128)(2,1)S(1)}, bf16[128,64]{1,0:T(8,128)(2,1)S(1)}, bf16[128,64]{1,0:T(8,128)(2,1)S(1)}) custom-call(bf16[64,72,128]{2,1,0:T(8,128)(2,1)S(1)} %all_to_all.10.x_ref, bf16[128,8192]{1,0:T(8,128)(2,1)S(1)} %copy-done, bf16[128,1024]{1,0:T(8,128)(2,1)S(1)} %copy-done.2), custom_call_target="tpu_custom_call" | custom-call | tf_op jit(solution)/shard_map/tile/pallas_call | solution.py:223
  81.4 1.0 copy-done.1
  82.4 0.6 copy-done.4
  83.0 0.6 copy-done.5
  83.7 51.6 %all_to_all.11.x_ref = bf16[64,72,128]{2,1,0:T(8,128)(2,1)S(1)} all-to-all(bf16[64,72,128]{2,1,0:T(8,128)(2,1)S(1)} %get-tuple-element.15), channel_id=1, replica_groups=mesh['grp'=4,'seq'=64] {'seq'}, dimensions={0} | all-to-all | bytes 2359296 | tf_op jit(solution)/shard_map/all_to_all | solution.py:237
  135.3 10.7 %all-gather.2.cloned.1.call-done.w_ref = bf16[8192,1024]{1,0:T(8,128)(2,1)} async-done(((bf16[128,1024]{1,0:T(8,128)(2,1)}), bf16[8192,1024]{1,0:T(8,128)(2,1)}) %all-gather.2.cloned.1.call-update) | async-done | bytes 16777232 | tf_op jit(solution)/shard_map/all_gather | solution.py:202
  146.0 3.7 %sum.1 = (f32[16,72,128]{2,1,0:T(8,128)S(1)}, f32[16,72,128]{2,1,0:T(8,128)S(1)}, f32[16,72,128]{2,1,0:T(8,128)S(1)}, f32[16,72,128]{2,1,0:T(8,128)S(1)}) custom-call(s32[1]{0:T(128)} %bitcast.group_ref, s32[256]{0:T(256)S(1)} %bitcast.6, s32[64]{0:T(128)S(1)} %copy-done.9, bf16[64,72,128]{2,1,0:T(8,128)(2,1)S(1)} %all_to_all.11.x_ref), custom_call_target="tpu_custom_call" | custom-call | tf_op jit(solution)/shard_map/sum/pallas_call | solution.py:239
  149.7 1.1 collective-permute-start.3
  150.8 2.4 %collective-permute-start.4 = (f32[16,72,128]{2,1,0:T(8,128)S(1)}, f32[16,72,128]{2,1,0:T(8,128)S(1)}, u32[]{:S(2)}, u32[]{:S(2)}) collective-permute-start(f32[16,72,128]{2,1,0:T(8,128)S(1)} %get-tuple-element.25), channel_id=1, source_target_pairs={{0,128},{64,192},{128,0},{192,64},{1,129},{65,193},{129,1},{193,65... | collective-permute-start | bytes 1769480 | tf_op jit(solution)/shard_map/ppermute | solution.py:184
  153.2 1.1 collective-permute-start.5
  154.3 18.6 %base.1 = (bf16[128,1024]{1,0:T(8,128)(2,1)}, bf16[128,8192]{1,0:T(8,128)(2,1)}) custom-call(bf16[128,8192]{1,0:T(8,128)(2,1)} %tok_ref.3, bf16[128,1024]{1,0:T(8,128)(2,1)} %cot_ref.3, bf16[8192,1024]{1,0:T(8,128)(2,1)} %all-gather.2.cloned.1.call-done.w_ref, bf16[64,9216]{1,0:T(8,128)(2,1)} %copy-done.1, bf16[64,9216]{1,0:T(8,128)(2,1)} %copy-done.1, ...), custom_call_target="tpu_custom_call" | custom-call | flops 4294967296 | bytes 21495808 | tf_op jit(solution)/shard_map/base/pallas_call | solution.py:259
  172.9 6.2 %collective-permute-done.4.x2_ref = f32[16,72,128]{2,1,0:T(8,128)S(1)} collective-permute-done((f32[16,72,128]{2,1,0:T(8,128)S(1)}, f32[16,72,128]{2,1,0:T(8,128)S(1)}, u32[]{:S(2)}, u32[]{:S(2)}) %collective-permute-start.4) | collective-permute-done | bytes 589856 | tf_op jit(solution)/shard_map/ppermute | solution.py:184
  179.0 1.2 unpack.1
  (19 shorter events, 0.2 us)
Async XLA Ops:
  7.2 138.8 %all-gather.2.cloned.1.call-start = ((), (), s32[]{:S(2)}) async-start(), calls=%async_computation.2 | async-start | bytes 17039360 | tf_op jit(solution)/shard_map/all_gather | solution.py:202
  7.9 1.0 copy-start.3
  9.1 7.8 %collective-permute-start.2 = (bf16[16,72,128]{2,1,0:T(8,128)(2,1)S(1)}, bf16[16,72,128]{2,1,0:T(8,128)(2,1)S(1)}, u32[]{:S(2)}, u32[]{:S(2)}) collective-permute-start(bf16[16,72,128]{2,1,0:T(8,128)(2,1)S(1)} %pack.1.a0_ref), channel_id=1, source_target_pairs={{0,64},{64,128},{128,192},{192,0},{1,65},{65,129},{129,193},{193,1... | collective-permute-start | bytes 884744 | tf_op jit(solution)/shard_map/ppermute | solution.py:184
  11.2 15.2 %collective-permute-start.1 = (bf16[16,72,128]{2,1,0:T(8,128)(2,1)S(1)}, bf16[16,72,128]{2,1,0:T(8,128)(2,1)S(1)}, u32[]{:S(2)}, u32[]{:S(2)}) collective-permute-start(bf16[16,72,128]{2,1,0:T(8,128)(2,1)S(1)} %pack.1.a0_ref), channel_id=1, source_target_pairs={{0,128},{64,192},{128,0},{192,64},{1,129},{65,193},{129,1},{193,65... | collective-permute-start | bytes 884744 | tf_op jit(solution)/shard_map/ppermute | solution.py:184
  13.7 12.7 %collective-permute-start = (bf16[16,72,128]{2,1,0:T(8,128)(2,1)S(1)}, bf16[16,72,128]{2,1,0:T(8,128)(2,1)S(1)}, u32[]{:S(2)}, u32[]{:S(2)}) collective-permute-start(bf16[16,72,128]{2,1,0:T(8,128)(2,1)S(1)} %pack.1.a0_ref), channel_id=1, source_target_pairs={{0,192},{64,0},{128,64},{192,128},{1,193},{65,1},{129,65},{193,129... | collective-permute-start | bytes 884744 | tf_op jit(solution)/shard_map/ppermute | solution.py:184
  26.4 0.7 copy-start.6
  27.1 0.7 copy-start.8
  31.1 46.9 %copy-start = (bf16[128,8192]{1,0:T(8,128)(2,1)S(1)}, bf16[128,8192]{1,0:T(8,128)(2,1)}, u32[]{:S(2)}) copy-start(bf16[128,8192]{1,0:T(8,128)(2,1)} %tok_ref.3) | copy-start | bytes 6291460
  31.1 46.9 %copy-start.2 = (bf16[128,1024]{1,0:T(8,128)(2,1)S(1)}, bf16[128,1024]{1,0:T(8,128)(2,1)}, u32[]{:S(2)}) copy-start(bf16[128,1024]{1,0:T(8,128)(2,1)} %cot_ref.3) | copy-start | bytes 786436
  81.4 1.0 copy-start.1
  82.4 0.6 copy-start.4
  83.0 0.6 copy-start.5
  83.6 62.3 %copy-start.7 = (s32[256,1]{0,1:T(1,128)S(1)}, s32[256,1]{0,1:T(1,128)}, u32[]{:S(2)}) copy-start(s32[256,1]{0,1:T(1,128)} %param.10) | copy-start | bytes 3076
  83.6 62.3 %copy-start.9 = (s32[64]{0:T(128)S(1)}, s32[64]{0:T(128)}, u32[]{:S(2)}) copy-start(s32[64]{0:T(128)} %slot_ref.3) | copy-start | bytes 772
  149.7 23.2 %collective-permute-start.3 = (f32[16,72,128]{2,1,0:T(8,128)S(1)}, f32[16,72,128]{2,1,0:T(8,128)S(1)}, u32[]{:S(2)}, u32[]{:S(2)}) collective-permute-start(f32[16,72,128]{2,1,0:T(8,128)S(1)} %get-tuple-element.24), channel_id=1, source_target_pairs={{0,64},{64,128},{128,192},{192,0},{1,65},{65,129},{129,193},{193,1... | collective-permute-start | bytes 1769480 | tf_op jit(solution)/shard_map/ppermute | solution.py:184
  150.8 28.2 %collective-permute-start.4 = (f32[16,72,128]{2,1,0:T(8,128)S(1)}, f32[16,72,128]{2,1,0:T(8,128)S(1)}, u32[]{:S(2)}, u32[]{:S(2)}) collective-permute-start(f32[16,72,128]{2,1,0:T(8,128)S(1)} %get-tuple-element.25), channel_id=1, source_target_pairs={{0,128},{64,192},{128,0},{192,64},{1,129},{65,193},{129,1},{193,65... | collective-permute-start | bytes 1769480 | tf_op jit(solution)/shard_map/ppermute | solution.py:184
  153.2 25.9 %collective-permute-start.5 = (f32[16,72,128]{2,1,0:T(8,128)S(1)}, f32[16,72,128]{2,1,0:T(8,128)S(1)}, u32[]{:S(2)}, u32[]{:S(2)}) collective-permute-start(f32[16,72,128]{2,1,0:T(8,128)S(1)} %get-tuple-element.26), channel_id=1, source_target_pairs={{0,192},{64,0},{128,64},{192,128},{1,193},{65,1},{129,65},{193,129... | collective-permute-start | bytes 1769480 | tf_op jit(solution)/shard_map/ppermute | solution.py:184
Sparse Core Ops, SparseCore 0:
  10.8 135.1 all-gather.1

commit v4 on v3

--- a/solution.py
+++ b/solution.py
@@ -3,8 +3,10 @@
 from jax import lax
 from jax.experimental import pallas as pl
 from jax.experimental.pallas import tpu as pltpu
+from jax.sharding import Mesh
 from jax.sharding import PartitionSpec as P
 
+SEQ = ("y", "z", "core")
 TILE_ROWS = 128
 LANES = 128
 adapter_scale = 0.5
@@ -82,11 +84,12 @@
             o_ref[s, 8 * b : 8 * b + 8, LANES:] = rest[:, tail * b : tail * (b + 1)]
 
 
-def tile_kernel(x_ref, tok_ref, cot_ref, terms_ref, at_ref, hid_ref, back_ref, t_ref):
+def tile_kernel(x_ref, tok_ref, cot_ref, terms_ref, at_ref, t_ref):
     shards, _, _ = x_ref.shape
     rank = at_ref.shape[0]
     depth = tok_ref.shape[1]
-    tail = at_ref.shape[1] // shards - LANES
+    width = depth + cot_ref.shape[1]
+    tail = width // shards - LANES
     per = LANES // tail
     group = per * (LANES + tail)
     lane = lax.broadcasted_iota(jnp.int32, (rank, LANES), 1)
@@ -126,17 +129,15 @@
     tok = tok_ref[...]
     cot = cot_ref[...]
     hidden = lax.dot_general(
-        tok, at_ref[:, :depth], NT, preferred_element_type=f32
+        at_ref[:, :depth], tok, NT, preferred_element_type=f32
     ).astype(bf16)
-    back = lax.dot_general(cot, at_ref[:, depth:], NT, preferred_element_type=f32).astype(bf16)
-    hid_ref[...] = hidden
-    back_ref[...] = back
-    t_ref[:, :depth] = adapter_scale * lax.dot_general(
-        back, tok, TN, preferred_element_type=f32
-    )
-    t_ref[:, depth:] = adapter_scale * lax.dot_general(
-        hidden, cot, TN, preferred_element_type=f32
-    )
+    back = lax.dot_general(
+        at_ref[:, depth:width], cot, NT, preferred_element_type=f32
+    ).astype(bf16)
+    at_ref[:, width : width + LANES] = hidden
+    at_ref[:, width + LANES :] = back
+    t_ref[:, :depth] = adapter_scale * jnp.dot(back, tok, preferred_element_type=f32)
+    t_ref[:, depth:] = adapter_scale * jnp.dot(hidden, cot, preferred_element_type=f32)
 
     def pack(a, carry):
         cols = [
@@ -161,21 +162,47 @@
     lax.fori_loop(0, shards // per, pack, 0)
 
 
-def main_kernel(tok_ref, cot_ref, w_ref, at_ref, up_ref, hid_ref, back_ref, keys_ref, grad_ref, acc_ref):
+def base_kernel(core_ref, tok_ref, cot_ref, half_ref, other_ref, at_ref, up_ref, hid_ref, back_ref, keys_ref, grad_ref, w_ref, acc_ref, sems):
     step = pl.program_id(0)
+    steps = pl.num_programs(0)
+    rows = TILE_ROWS
+    pairs = w_ref.shape[1] // (2 * rows)
+    slot = lax.rem(step, 2)
+
+    def copies(at, to):
+        out = []
+        for p in range(pairs):
+            src = pl.ds(pl.multiple_of((at * pairs + p) * rows, rows), rows)
+            for k, source in enumerate((half_ref, other_ref)):
+                mine = core_ref[0] if k == 0 else 1 - core_ref[0]
+                dst = pl.ds(pl.multiple_of(2 * p * rows + mine * rows, rows), rows)
+                out.append(pltpu.make_async_copy(source.at[src], w_ref.at[to, dst], sems.at[to, 2 * p + k]))
+        return out
 
     @pl.when(step == 0)
     def _():
-        acc_ref[...] = adapter_scale * jnp.dot(
-            hid_ref[...], up_ref[...], preferred_element_type=f32
+        for c in copies(step, slot):
+            c.start()
+        acc_ref[...] = adapter_scale * lax.dot_general(
+            hid_ref[...], up_ref[...], TN, preferred_element_type=f32
         )
 
-    acc_ref[...] += jnp.dot(tok_ref[...], w_ref[...], preferred_element_type=f32)
-    grad = lax.dot_general(cot_ref[...], w_ref[...], NT, preferred_element_type=f32)
-    grad += adapter_scale * jnp.dot(back_ref[...], at_ref[...], preferred_element_type=f32)
+    @pl.when(step + 1 < steps)
+    def _():
+        for c in copies(step + 1, 1 - slot):
+            c.start()
+
+    for c in copies(step, slot):
+        c.wait()
+    weight = w_ref[slot]
+    acc_ref[...] += jnp.dot(tok_ref[...], weight, preferred_element_type=f32)
+    grad = lax.dot_general(cot_ref[...], weight, NT, preferred_element_type=f32)
+    grad += adapter_scale * lax.dot_general(
+        back_ref[...], at_ref[...], TN, preferred_element_type=f32
+    )
     grad_ref[...] = grad.astype(grad_ref.dtype)
 
-    @pl.when(step == pl.num_programs(0) - 1)
+    @pl.when(step == steps - 1)
     def _():
         keys_ref[...] = acc_ref[...].astype(keys_ref.dtype)
 
@@ -193,13 +220,14 @@
     key_columns = cotangent.shape[1]
     slot_count, row_count, rank = adapters.shape
     groups = lax.axis_size("grp")
-    shards = lax.axis_size("seq")
+    shards = lax.axis_size(SEQ)
     packed_rows = row_count * rank // LANES
     width = depth + key_columns
     group = lax.axis_index("grp").reshape(1).astype(jnp.int32)
+    core = lax.axis_index("core").reshape(1).astype(jnp.int32)
     jobs = tile_job.reshape(-1)
 
-    weight = lax.all_gather(frozen_weight, "seq", axis=0, tiled=True)
+    column = lax.all_gather(frozen_weight, "z", axis=0, tiled=True)
 
     own = pl.pallas_call(
         pack_kernel,
@@ -219,31 +247,34 @@
         compiler_params=params(),
         name="pick",
     )(group, jobs, job_slot, *every)
-    arrived = lax.all_to_all(outgoing, "seq", split_axis=0, concat_axis=0, tiled=True)
-    terms, adapter, hidden, back = pl.pallas_call(
+    outgoing, column = lax.optimization_barrier((outgoing, column))
+    half = lax.all_gather(column, "y", axis=0, tiled=True)
+    arrived = lax.all_to_all(outgoing, SEQ, split_axis=0, concat_axis=0, tiled=True)
+    terms, adapter = pl.pallas_call(
         tile_kernel,
         out_shape=(
             jax.ShapeDtypeStruct((shards, packed_rows, LANES), bf16),
-            jax.ShapeDtypeStruct((rank, width), bf16),
-            jax.ShapeDtypeStruct((rows, rank), bf16),
-            jax.ShapeDtypeStruct((rows, rank), bf16),
+            jax.ShapeDtypeStruct((rank, width + 2 * rows), bf16),
         ),
         in_specs=[whole()] * 3,
-        out_specs=(whole(),) * 4,
+        out_specs=(whole(),) * 2,
         scratch_shapes=[pltpu.VMEM((rank, width), f32)],
         compiler_params=params(),
         name="tile",
     )(arrived, tokens, cotangent)
-    incoming = lax.all_to_all(terms, "seq", split_axis=0, concat_axis=0, tiled=True)
-    incoming, weight = lax.optimization_barrier((incoming, weight))
+    incoming = lax.all_to_all(terms, SEQ, split_axis=0, concat_axis=0, tiled=True)
+    incoming, half = lax.optimization_barrier((incoming, half))
+    other = lax.ppermute(half, "core", [(0, 1), (1, 0)])
     sums = pl.pallas_call(
         sum_kernel,
         out_shape=(jax.ShapeDtypeStruct((slot_count, packed_rows, LANES), f32),) * groups,
         in_specs=[smem, smem, smem, whole()],
         out_specs=(whole(),) * groups,
-        compiler_params=params(),
+        compiler_params=params(56),
         name="sum",
     )(group, jobs, job_slot, incoming)
+    last, other = lax.optimization_barrier((sums[-1], other))
+    sums = tuple(sums[:-1]) + (last,)
     owned = (sums[0],) + tuple(shift(sums[k], k, groups) for k in range(1, groups))
     grads = pl.pallas_call(
         unpack_kernel,
@@ -254,29 +285,35 @@
         name="unpack",
     )(*owned)
 
-    block = 512
+    block = 1024
     steps = depth // block
     keys, token_gradient = pl.pallas_call(
-        main_kernel,
+        base_kernel,
         grid=(steps,),
         out_shape=(
             jax.ShapeDtypeStruct((rows, key_columns), bf16),
             jax.ShapeDtypeStruct((rows, depth), bf16),
         ),
         in_specs=[
+            smem,
             pl.BlockSpec((rows, block), lambda i: (0, i)),
             pl.BlockSpec((rows, key_columns), lambda i: (0, 0)),
-            pl.BlockSpec((block, key_columns), lambda i: (i, 0)),
+            whole(pl.ANY),
+            whole(pl.ANY),
             pl.BlockSpec((rank, block), lambda i: (0, i)),
             pl.BlockSpec((rank, key_columns), lambda i: (0, depth // key_columns)),
-            pl.BlockSpec((rows, rank), lambda i: (0, 0)),
-            pl.BlockSpec((rows, rank), lambda i: (0, 0)),
+            pl.BlockSpec((rank, rows), lambda i: (0, width // rows)),
+            pl.BlockSpec((rank, rows), lambda i: (0, width // rows + 1)),
         ],
         out_specs=(
             pl.BlockSpec((rows, key_columns), lambda i: (0, 0)),
             pl.BlockSpec((rows, block), lambda i: (0, i)),
         ),
-        scratch_shapes=[pltpu.VMEM((rows, key_columns), f32)],
+        scratch_shapes=[
+            pltpu.VMEM((2, block, key_columns), bf16),
+            pltpu.VMEM((rows, key_columns), f32),
+            pltpu.SemaphoreType.DMA((2, block // TILE_ROWS)),
+        ],
         compiler_params=params(56),
         cost_estimate=pl.CostEstimate(
             flops=4 * rows * depth * key_columns,
@@ -284,16 +321,24 @@
             transcendentals=0,
         ),
         name="base",
-    )(tokens, cotangent, weight, adapter, adapter, hidden, back)
+    )(core, tokens, cotangent, half, other, adapter, adapter, adapter, adapter)
     return keys, token_gradient, jnp.swapaxes(grads, 1, 2)
 
 
 def solution(mesh):
+    groups, shards = mesh.devices.shape
+    cores = 2
+    deep = 8
+    mesh = Mesh(
+        mesh.devices.reshape(groups, shards // (cores * deep), deep, cores),
+        ("grp", "y", "z", "core"),
+    )
+    every = ("grp",) + SEQ
     placed = (
-        P(("grp", "seq"), None),
-        P(("grp", "seq"), None),
-        P("seq", None),
-        P("grp", "seq", None),
+        P(every, None),
+        P(every, None),
+        P(SEQ, None),
+        P("grp", SEQ, None),
         P(),
         P(),
     )
@@ -301,6 +346,6 @@
         on_device,
         mesh=mesh,
         in_specs=placed,
-        out_specs=(P(("grp", "seq"), None), P(("grp", "seq"), None), P("grp", "seq", None)),
+        out_specs=(P(every, None), P(every, None), P("grp", SEQ, None)),
         check_vma=False,
     )

time: 188 us -> 208 us (1.11)
  waiting for transfers between devices: 29.1 us -> 68.8 us
  blocking collectives: 98.5 us -> 80.5 us
    all_gather x1 -> x2, waiting for transfers between devices: 10.7 us -> 43.7 us  [the longest x1 26.7 us: on_device(): half = lax.all_gather(column, 'y', axis=0, tiled=True)]
    all_to_all x2, blocking collectives: 98.5 us -> 80.5 us  [the longest x1 42.9 us: on_device(): lax.all_to_all(outgoing, SEQ, split_axis=0, concat_axis=0, tiled=True)]
    ppermute x0 -> x1, waiting for transfers between devices: none -> 3.67 us  [on_device(): other = lax.ppermute(half, 'core', [(0, 1), (1, 0)])]
    pallas_call x1, Pallas kernels: 18.6 us -> 15.2 us  [on_device(): pl.pallas_call(base_kernel, grid=(steps,), out_shape=(jax.ShapeDtypeStruc...]
    ppermute x6, waiting for transfers between devices: 17.8 us -> 20.8 us  [shift(): lax.ppermute(x, 'grp', [(i, (i + by) % groups) for i in range(groups)])]
    pallas_call x1, Pallas kernels: 3.7 us -> 5.86 us  [on_device(): pl.pallas_call(sum_kernel, out_shape=(jax.ShapeDtypeStruct((slot_count, p...]
    unnamed x20 -> x14, local copies, waits for them, and re-layouts: 4.64 us -> 3.41 us
  transfers between devices with their start and end apart: 7 -> 9, of which waited for: 4 -> 7; matrix products, arithmetic and copies ran while one was open for 0% -> 0% of each run, Pallas kernels for 14% -> 14%
where the time goes in v4:
time: 208 us; the launch traced here: 207 us
  blocking collectives  80.5 us (39%)
  waiting for transfers between devices  68.8 us (33%)
  Pallas kernels  29.2 us (14%)
  between operations  14.1 us (7%)
  starting transfers between devices  11.1 us (5%)
  local copies, waits for them, and re-layouts  3.41 us (2%)
    all_to_all x1, blocking collectives, on_device(): lax.all_to_all(outgoing, SEQ, split_axis=0, concat_axis=0, tiled=True)  42.9 us
    all_to_all x1, blocking collectives, on_device(): lax.all_to_all(terms, SEQ, split_axis=0, concat_axis=0, tiled=True)  37.5 us
    all_gather x1, waiting for transfers between devices, on_device(): half = lax.all_gather(column, 'y', axis=0, tiled=True)  26.7 us
    ppermute x6, waiting for transfers between devices, shift(): lax.ppermute(x, 'grp', [(i, (i + by) % groups) for i in range(groups)])  20.8 us
    all_gather x1, waiting for transfers between devices, on_device(): column = lax.all_gather(frozen_weight, 'z', axis=0, tiled=True)  17 us
    pallas_call x1, Pallas kernels, on_device(): pl.pallas_call(base_kernel, grid=(steps,), out_shape=(jax.ShapeDtypeStruc...  15.2 us
    ppermute x6, starting transfers between devices, shift(): lax.ppermute(x, 'grp', [(i, (i + by) % groups) for i in range(groups)])  10.5 us
    pallas_call x1, Pallas kernels, on_device(): pl.pallas_call(sum_kernel, out_shape=(jax.ShapeDtypeStruct((slot_count, p...  5.86 us
  transfers between devices with their start and end apart: 9, of which 7 were waited for; matrix products, arithmetic and copies ran while one was open for 0% of the time, Pallas kernels for 14%

profile of v4, /device:TPU:1, one launch (start us, length us, event | category | flops | bytes accessed | tf_op | source)
XLA Modules:
  0.0 207.1 jit_solution(16448652468037387414)
XLA Ops:
  7.2 0.7 all-gather.3.cloned.1.call-update
  8.0 1.0 copy-done.4
  9.1 3.4 %collective-permute-start = (bf16[16,72,128]{2,1,0:T(8,128)(2,1)S(1)}, bf16[16,72,128]{2,1,0:T(8,128)(2,1)S(1)}, u32[]{:S(2)}, u32[]{:S(2)}) collective-permute-start(bf16[16,72,128]{2,1,0:T(8,128)(2,1)S(1)} %pack.1.a0_ref), channel_id=1, source_target_pairs={{0,192},{64,0},{128,64},{192,128},{1,193},{65,1},{129,65},{193,129... | collective-permute-start | bytes 884744 | tf_op jit(solution)/shard_map/ppermute | solution.py:211
  12.5 0.5 collective-permute-start.1
  13.0 0.6 collective-permute-start.2
  13.6 7.9 %collective-permute-done.a1_ref = bf16[16,72,128]{2,1,0:T(8,128)(2,1)S(1)} collective-permute-done((bf16[16,72,128]{2,1,0:T(8,128)(2,1)S(1)}, bf16[16,72,128]{2,1,0:T(8,128)(2,1)S(1)}, u32[]{:S(2)}, u32[]{:S(2)}) %collective-permute-start) | collective-permute-done | bytes 294944 | tf_op jit(solution)/shard_map/ppermute | solution.py:211
  21.6 7.8 %collective-permute-done.2.a3_ref = bf16[16,72,128]{2,1,0:T(8,128)(2,1)S(1)} collective-permute-done((bf16[16,72,128]{2,1,0:T(8,128)(2,1)S(1)}, bf16[16,72,128]{2,1,0:T(8,128)(2,1)S(1)}, u32[]{:S(2)}, u32[]{:S(2)}) %collective-permute-start.2) | collective-permute-done | bytes 294944 | tf_op jit(solution)/shard_map/ppermute | solution.py:211
  29.4 0.7 copy-done.5
  30.1 0.7 copy-done.6
  30.7 3.3 %pick.1 = bf16[64,72,128]{2,1,0:T(8,128)(2,1)S(1)} custom-call(s32[1]{0:T(128)} %bitcast.1.group_ref, s32[256]{0:T(256)S(1)} %bitcast.7, s32[64]{0:T(128)S(1)} %copy-done.6, bf16[16,72,128]{2,1,0:T(8,128)(2,1)S(1)} %pack.1.a0_ref, bf16[16,72,128]{2,1,0:T(8,128)(2,1)S(1)} %collective-permute-done.a1_ref, ...), custom_call_target="tpu_custom_call" | custom-call | tf_op jit(solution)/shard_map/pick/pallas_call | solution.py:242
  34.0 17.0 %all-gather.3.cloned.1.call-done = bf16[1024,1024]{1,0:T(8,128)(2,1)} async-done(((bf16[128,1024]{1,0:T(8,128)(2,1)}), bf16[1024,1024]{1,0:T(8,128)(2,1)}) %all-gather.3.cloned.1.call-update) | async-done | bytes 2097168 | tf_op jit(solution)/shard_map/all_gather | solution.py:230
  51.1 42.9 %all_to_all.10.x_ref = bf16[64,72,128]{2,1,0:T(8,128)(2,1)S(1)} all-to-all(bf16[64,72,128]{2,1,0:T(8,128)(2,1)S(1)} %pick.1), channel_id=1, replica_groups=mesh['grp'=4,'y'=4,'z'=8,'core'=2] {'y','z','core'}, dimensions={0} | all-to-all | bytes 2359296 | tf_op jit(solution)/shard_map/all_to_all | solution.py:252
  94.0 3.6 %tile.1 = (bf16[64,72,128]{2,1,0:T(8,128)(2,1)S(1)}, bf16[64,9472]{1,0:T(8,128)(2,1)S(1)}) custom-call(bf16[64,72,128]{2,1,0:T(8,128)(2,1)S(1)} %all_to_all.10.x_ref, bf16[128,8192]{1,0:T(8,128)(2,1)S(1)} %copy-done.1, bf16[128,1024]{1,0:T(8,128)(2,1)S(1)} %copy-done.2), custom_call_target="tpu_custom_call" | custom-call | tf_op jit(solution)/shard_map/tile/pallas_call | solution.py:253
  97.6 1.0 copy-done
  98.6 37.5 %all_to_all.11.x_ref = bf16[64,72,128]{2,1,0:T(8,128)(2,1)} all-to-all(bf16[64,72,128]{2,1,0:T(8,128)(2,1)S(1)} %get-tuple-element.18), channel_id=1, replica_groups=mesh['grp'=4,'y'=4,'z'=8,'core'=2] {'y','z','core'}, dimensions={0} | all-to-all | bytes 2359296 | tf_op jit(solution)/shard_map/all_to_all | solution.py:265
  136.2 26.7 %all-gather.5.cloned.1.call-done.half_ref = bf16[4096,1024]{1,0:T(8,128)(2,1)} async-done(((bf16[1024,1024]{1,0:T(8,128)(2,1)}), bf16[4096,1024]{1,0:T(8,128)(2,1)}) %all-gather.5.cloned.1.call-update) | async-done | bytes 8388624 | tf_op jit(solution)/shard_map/all_gather | solution.py:251
  163.3 5.9 %sum.1 = (f32[16,72,128]{2,1,0:T(8,128)}, f32[16,72,128]{2,1,0:T(8,128)}, f32[16,72,128]{2,1,0:T(8,128)}, f32[16,72,128]{2,1,0:T(8,128)}) custom-call(s32[1]{0:T(128)} %bitcast.1.group_ref, s32[256]{0:T(256)} %bitcast.6, s32[64]{0:T(128)} %slot_ref.3, bf16[64,72,128]{2,1,0:T(8,128)(2,1)} %all_to_all.11.x_ref), custom_call_target="tpu_custom_call" | custom-call | tf_op jit(solution)/shard_map/sum/pallas_call | solution.py:268
  169.2 1.2 collective-permute-start.4
  170.4 2.4 %collective-permute-start.5 = (f32[16,72,128]{2,1,0:T(8,128)}, f32[16,72,128]{2,1,0:T(8,128)S(1)}, u32[]{:S(2)}, u32[]{:S(2)}) collective-permute-start(f32[16,72,128]{2,1,0:T(8,128)} %get-tuple-element.29), channel_id=1, source_target_pairs={{0,128},{64,192},{128,0},{192,64},{1,129},{65,193},{129,1},{193,65... | collective-permute-start | bytes 1769480 | tf_op jit(solution)/shard_map/ppermute | solution.py:211
  172.8 3.7 %collective-permute-done.3.other_ref = bf16[4096,1024]{1,0:T(8,128)(2,1)} collective-permute-done((bf16[4096,1024]{1,0:T(8,128)(2,1)}, bf16[4096,1024]{1,0:T(8,128)(2,1)}, u32[]{:S(2)}, u32[]{:S(2)}) %collective-permute-start.3) | collective-permute-done | bytes 8388640 | tf_op jit(solution)/shard_map/ppermute | solution.py:267
  176.5 2.4 %collective-permute-start.6 = (f32[16,72,128]{2,1,0:T(8,128)}, f32[16,72,128]{2,1,0:T(8,128)S(1)}, u32[]{:S(2)}, u32[]{:S(2)}) collective-permute-start(f32[16,72,128]{2,1,0:T(8,128)} %get-tuple-element.30), channel_id=1, source_target_pairs={{0,192},{64,0},{128,64},{192,128},{1,193},{65,1},{129,65},{193,129... | collective-permute-start | bytes 1769480 | tf_op jit(solution)/shard_map/ppermute | solution.py:211
  178.9 15.2 %base.1 = (bf16[128,1024]{1,0:T(8,128)(2,1)}, bf16[128,8192]{1,0:T(8,128)(2,1)}) custom-call(s32[1]{0:T(128)} %bitcast.core_ref, bf16[128,8192]{1,0:T(8,128)(2,1)} %tok_ref.3, bf16[128,1024]{1,0:T(8,128)(2,1)} %cot_ref.3, bf16[4096,1024]{1,0:T(8,128)(2,1)} %all-gather.5.cloned.1.call-done.half_ref, bf16[4096,1024]{1,0:T(8,128)(2,1)} %collective-permute-done.3.other_ref, ...), custom_call_target="tpu_custom_call" | custom-call | flops 4294967296 | bytes 21495808 | tf_op jit(solution)/shard_map/base/pallas_call | solution.py:290
  194.1 5.0 %collective-permute-done.5.x2_ref = f32[16,72,128]{2,1,0:T(8,128)S(1)} collective-permute-done((f32[16,72,128]{2,1,0:T(8,128)}, f32[16,72,128]{2,1,0:T(8,128)S(1)}, u32[]{:S(2)}, u32[]{:S(2)}) %collective-permute-start.5) | collective-permute-done | bytes 589856 | tf_op jit(solution)/shard_map/ppermute | solution.py:211
  199.1 1.2 unpack.1
  (18 shorter events, 0.8 us)
Async XLA Ops:
  7.2 43.9 %all-gather.3.cloned.1.call-start = ((), (), s32[]{:S(2)}) async-start(), calls=%async_computation.2 | async-start | bytes 2359296 | tf_op jit(solution)/shard_map/all_gather | solution.py:230
  7.9 155.0 %all-gather.5.cloned.1.call-start = ((), (), s32[]{:S(2)}) async-start(), calls=%async_computation.3 | async-start | bytes 10485760 | tf_op jit(solution)/shard_map/all_gather | solution.py:251
  7.9 1.0 copy-start.4
  9.1 12.4 %collective-permute-start = (bf16[16,72,128]{2,1,0:T(8,128)(2,1)S(1)}, bf16[16,72,128]{2,1,0:T(8,128)(2,1)S(1)}, u32[]{:S(2)}, u32[]{:S(2)}) collective-permute-start(bf16[16,72,128]{2,1,0:T(8,128)(2,1)S(1)} %pack.1.a0_ref), channel_id=1, source_target_pairs={{0,192},{64,0},{128,64},{192,128},{1,193},{65,1},{129,65},{193,129... | collective-permute-start | bytes 884744 | tf_op jit(solution)/shard_map/ppermute | solution.py:211
  12.5 9.1 %collective-permute-start.1 = (bf16[16,72,128]{2,1,0:T(8,128)(2,1)S(1)}, bf16[16,72,128]{2,1,0:T(8,128)(2,1)S(1)}, u32[]{:S(2)}, u32[]{:S(2)}) collective-permute-start(bf16[16,72,128]{2,1,0:T(8,128)(2,1)S(1)} %pack.1.a0_ref), channel_id=1, source_target_pairs={{0,128},{64,192},{128,0},{192,64},{1,129},{65,193},{129,1},{193,65... | collective-permute-start | bytes 884744 | tf_op jit(solution)/shard_map/ppermute | solution.py:211
  13.0 16.3 %collective-permute-start.2 = (bf16[16,72,128]{2,1,0:T(8,128)(2,1)S(1)}, bf16[16,72,128]{2,1,0:T(8,128)(2,1)S(1)}, u32[]{:S(2)}, u32[]{:S(2)}) collective-permute-start(bf16[16,72,128]{2,1,0:T(8,128)(2,1)S(1)} %pack.1.a0_ref), channel_id=1, source_target_pairs={{0,64},{64,128},{128,192},{192,0},{1,65},{65,129},{129,193},{193,1... | collective-permute-start | bytes 884744 | tf_op jit(solution)/shard_map/ppermute | solution.py:211
  29.4 0.7 copy-start.5
  30.1 0.7 copy-start.6
  51.0 43.0 %copy-start.1 = (bf16[128,8192]{1,0:T(8,128)(2,1)S(1)}, bf16[128,8192]{1,0:T(8,128)(2,1)}, u32[]{:S(2)}) copy-start(bf16[128,8192]{1,0:T(8,128)(2,1)} %tok_ref.3) | copy-start | bytes 6291460
  51.0 43.0 %copy-start.2 = (bf16[128,1024]{1,0:T(8,128)(2,1)S(1)}, bf16[128,1024]{1,0:T(8,128)(2,1)}, u32[]{:S(2)}) copy-start(bf16[128,1024]{1,0:T(8,128)(2,1)} %cot_ref.3) | copy-start | bytes 786436
  97.6 1.0 copy-start
  162.9 13.6 %collective-permute-start.3 = (bf16[4096,1024]{1,0:T(8,128)(2,1)}, bf16[4096,1024]{1,0:T(8,128)(2,1)}, u32[]{:S(2)}, u32[]{:S(2)}) collective-permute-start(bf16[4096,1024]{1,0:T(8,128)(2,1)} %all-gather.5.cloned.1.call-done.half_ref), channel_id=1, source_target_pairs={{0,1},{1,0},{2,3},{3,2},{4,5},{5,4},{6,7},{7,6},{8,9},{9,8},{10,11... | collective-permute-start | bytes 25165832 | tf_op jit(solution)/shard_map/ppermute | solution.py:267
  169.2 24.9 %collective-permute-start.4 = (f32[16,72,128]{2,1,0:T(8,128)}, f32[16,72,128]{2,1,0:T(8,128)S(1)}, u32[]{:S(2)}, u32[]{:S(2)}) collective-permute-start(f32[16,72,128]{2,1,0:T(8,128)} %get-tuple-element.28), channel_id=1, source_target_pairs={{0,64},{64,128},{128,192},{192,0},{1,65},{65,129},{129,193},{193,1... | collective-permute-start | bytes 1769480 | tf_op jit(solution)/shard_map/ppermute | solution.py:211
  170.4 28.7 %collective-permute-start.5 = (f32[16,72,128]{2,1,0:T(8,128)}, f32[16,72,128]{2,1,0:T(8,128)S(1)}, u32[]{:S(2)}, u32[]{:S(2)}) collective-permute-start(f32[16,72,128]{2,1,0:T(8,128)} %get-tuple-element.29), channel_id=1, source_target_pairs={{0,128},{64,192},{128,0},{192,64},{1,129},{65,193},{129,1},{193,65... | collective-permute-start | bytes 1769480 | tf_op jit(solution)/shard_map/ppermute | solution.py:211
  176.5 22.6 %collective-permute-start.6 = (f32[16,72,128]{2,1,0:T(8,128)}, f32[16,72,128]{2,1,0:T(8,128)S(1)}, u32[]{:S(2)}, u32[]{:S(2)}) collective-permute-start(f32[16,72,128]{2,1,0:T(8,128)} %get-tuple-element.30), channel_id=1, source_target_pairs={{0,192},{64,0},{128,64},{192,128},{1,193},{65,1},{129,65},{193,129... | collective-permute-start | bytes 1769480 | tf_op jit(solution)/shard_map/ppermute | solution.py:211
  178.9 20.2 %copy-start.3 = (f32[16,72,128]{2,1,0:T(8,128)S(1)}, f32[16,72,128]{2,1,0:T(8,128)}, u32[]{:S(2)}) copy-start(f32[16,72,128]{2,1,0:T(8,128)} %get-tuple-element.27.x0_ref) | copy-start | bytes 1769476
Sparse Core Ops, SparseCore 0:
  9.8 41.1 all-gather.2
  52.8 109.9 all-gather.4

commit v5 on v4

--- a/solution.py
+++ b/solution.py
@@ -30,54 +30,43 @@
         o_ref[s, rank:, :] = jnp.concatenate(pieces, axis=1).astype(o_ref.dtype)
 
 
-def pick_kernel(group_ref, job_ref, slot_ref, a0_ref, a1_ref, a2_ref, a3_ref, o_ref):
+def pick_kernel(group_ref, job_ref, slot_ref, *refs):
+    sources, (o_ref, every_ref) = refs[:-2], refs[-2:]
     tiles = o_ref.shape[0]
-    sources = (a0_ref, a1_ref, a2_ref, a3_ref)
-    count = a0_ref.shape[0]
+    count = sources[0].shape[0]
     me = group_ref[0]
+    for k, source in enumerate(sources):
+        every_ref[pl.ds(lax.rem(me + k, len(sources)) * count, count)] = source[...]
+
+    def step(t, carry):
+        o_ref[t] = every_ref[slot_ref[job_ref[me * tiles + t]]]
+        return carry
+
+    lax.fori_loop(0, tiles, step, 0, unroll=4)
+
+
+def sum_kernel(group_ref, job_ref, slot_ref, x_ref, *refs):
+    sinks, sum_ref = refs[:-1], refs[-1]
+    tiles = x_ref.shape[0]
+    count = sinks[0].shape[0]
+    me = group_ref[0]
+    sum_ref[...] = jnp.zeros_like(sum_ref)
 
     def step(t, carry):
         s = slot_ref[job_ref[me * tiles + t]]
-        away = lax.rem(s // count - me + len(sources), len(sources))
-        for k, source in enumerate(sources):
-
-            @pl.when(away == k)
-            def _():
-                o_ref[t] = source[lax.rem(s, count)]
-
+        sum_ref[s] = sum_ref[s] + x_ref[t].astype(f32)
         return carry
 
-    lax.fori_loop(0, tiles, step, 0)
-
-
-def sum_kernel(group_ref, job_ref, slot_ref, x_ref, o0_ref, o1_ref, o2_ref, o3_ref):
-    tiles = x_ref.shape[0]
-    sinks = (o0_ref, o1_ref, o2_ref, o3_ref)
-    count = o0_ref.shape[0]
-    me = group_ref[0]
-    for sink in sinks:
-        sink[...] = jnp.zeros_like(sink)
-
-    def step(t, carry):
-        s = slot_ref[job_ref[me * tiles + t]]
-        away = lax.rem(s // count - me + len(sinks), len(sinks))
-        at = lax.rem(s, count)
-        for k, sink in enumerate(sinks):
-
-            @pl.when(away == k)
-            def _():
-                sink[at] = sink[at] + x_ref[t].astype(f32)
-
-        return carry
-
-    lax.fori_loop(0, tiles, step, 0)
+    lax.fori_loop(0, tiles, step, 0, unroll=4)
+    for k, sink in enumerate(sinks):
+        sink[...] = sum_ref[pl.ds(lax.rem(me + k, len(sinks)) * count, count)].astype(sink.dtype)
 
 
 def unpack_kernel(x0_ref, x1_ref, x2_ref, x3_ref, o_ref):
     slots, rank, width = o_ref.shape
     tail = width - LANES
     for s in range(slots):
-        total = (x0_ref[s] + x1_ref[s]) + (x2_ref[s] + x3_ref[s])
+        total = x0_ref[s] + (x1_ref[s].astype(f32) + x2_ref[s].astype(f32)) + x3_ref[s].astype(f32)
         o_ref[s, :, :LANES] = total[:rank]
         rest = total[rank:]
         for b in range(LANES // tail):
@@ -162,39 +151,16 @@
     lax.fori_loop(0, shards // per, pack, 0)
 
 
-def base_kernel(core_ref, tok_ref, cot_ref, half_ref, other_ref, at_ref, up_ref, hid_ref, back_ref, keys_ref, grad_ref, w_ref, acc_ref, sems):
+def base_kernel(tok_ref, cot_ref, w_ref, at_ref, up_ref, hid_ref, back_ref, keys_ref, grad_ref, acc_ref):
     step = pl.program_id(0)
-    steps = pl.num_programs(0)
-    rows = TILE_ROWS
-    pairs = w_ref.shape[1] // (2 * rows)
-    slot = lax.rem(step, 2)
-
-    def copies(at, to):
-        out = []
-        for p in range(pairs):
-            src = pl.ds(pl.multiple_of((at * pairs + p) * rows, rows), rows)
-            for k, source in enumerate((half_ref, other_ref)):
-                mine = core_ref[0] if k == 0 else 1 - core_ref[0]
-                dst = pl.ds(pl.multiple_of(2 * p * rows + mine * rows, rows), rows)
-                out.append(pltpu.make_async_copy(source.at[src], w_ref.at[to, dst], sems.at[to, 2 * p + k]))
-        return out
 
     @pl.when(step == 0)
     def _():
-        for c in copies(step, slot):
-            c.start()
         acc_ref[...] = adapter_scale * lax.dot_general(
             hid_ref[...], up_ref[...], TN, preferred_element_type=f32
         )
 
-    @pl.when(step + 1 < steps)
-    def _():
-        for c in copies(step + 1, 1 - slot):
-            c.start()
-
-    for c in copies(step, slot):
-        c.wait()
-    weight = w_ref[slot]
+    weight = w_ref[...]
     acc_ref[...] += jnp.dot(tok_ref[...], weight, preferred_element_type=f32)
     grad = lax.dot_general(cot_ref[...], weight, NT, preferred_element_type=f32)
     grad += adapter_scale * lax.dot_general(
@@ -202,7 +168,7 @@
     )
     grad_ref[...] = grad.astype(grad_ref.dtype)
 
-    @pl.when(step == steps - 1)
+    @pl.when(step == pl.num_programs(0) - 1)
     def _():
         keys_ref[...] = acc_ref[...].astype(keys_ref.dtype)
 
@@ -224,10 +190,9 @@
     packed_rows = row_count * rank // LANES
     width = depth + key_columns
     group = lax.axis_index("grp").reshape(1).astype(jnp.int32)
-    core = lax.axis_index("core").reshape(1).astype(jnp.int32)
     jobs = tile_job.reshape(-1)
 
-    column = lax.all_gather(frozen_weight, "z", axis=0, tiled=True)
+    weight = lax.all_gather(frozen_weight, SEQ, axis=0, tiled=True)
 
     own = pl.pallas_call(
         pack_kernel,
@@ -244,11 +209,10 @@
         out_shape=jax.ShapeDtypeStruct((shards, packed_rows, LANES), bf16),
         in_specs=[smem, smem, smem] + [whole()] * groups,
         out_specs=whole(),
+        scratch_shapes=[pltpu.VMEM((groups * slot_count, packed_rows, LANES), bf16)],
         compiler_params=params(),
         name="pick",
     )(group, jobs, job_slot, *every)
-    outgoing, column = lax.optimization_barrier((outgoing, column))
-    half = lax.all_gather(column, "y", axis=0, tiled=True)
     arrived = lax.all_to_all(outgoing, SEQ, split_axis=0, concat_axis=0, tiled=True)
     terms, adapter = pl.pallas_call(
         tile_kernel,
@@ -263,17 +227,17 @@
         name="tile",
     )(arrived, tokens, cotangent)
     incoming = lax.all_to_all(terms, SEQ, split_axis=0, concat_axis=0, tiled=True)
-    incoming, half = lax.optimization_barrier((incoming, half))
-    other = lax.ppermute(half, "core", [(0, 1), (1, 0)])
     sums = pl.pallas_call(
         sum_kernel,
-        out_shape=(jax.ShapeDtypeStruct((slot_count, packed_rows, LANES), f32),) * groups,
+        out_shape=(jax.ShapeDtypeStruct((slot_count, packed_rows, LANES), f32),)
+        + (jax.ShapeDtypeStruct((slot_count, packed_rows, LANES), bf16),) * (groups - 1),
         in_specs=[smem, smem, smem, whole()],
         out_specs=(whole(),) * groups,
-        compiler_params=params(56),
+        scratch_shapes=[pltpu.VMEM((groups * slot_count, packed_rows, LANES), f32)],
+        compiler_params=params(),
         name="sum",
     )(group, jobs, job_slot, incoming)
-    last, other = lax.optimization_barrier((sums[-1], other))
+    last, weight = lax.optimization_barrier((sums[-1], weight))
     sums = tuple(sums[:-1]) + (last,)
     owned = (sums[0],) + tuple(shift(sums[k], k, groups) for k in range(1, groups))
     grads = pl.pallas_call(
@@ -295,11 +259,9 @@
             jax.ShapeDtypeStruct((rows, depth), bf16),
         ),
         in_specs=[
-            smem,
             pl.BlockSpec((rows, block), lambda i: (0, i)),
             pl.BlockSpec((rows, key_columns), lambda i: (0, 0)),
-            whole(pl.ANY),
-            whole(pl.ANY),
+            pl.BlockSpec((block, key_columns), lambda i: (i, 0)),
             pl.BlockSpec((rank, block), lambda i: (0, i)),
             pl.BlockSpec((rank, key_columns), lambda i: (0, depth // key_columns)),
             pl.BlockSpec((rank, rows), lambda i: (0, width // rows)),
@@ -309,11 +271,7 @@
             pl.BlockSpec((rows, key_columns), lambda i: (0, 0)),
             pl.BlockSpec((rows, block), lambda i: (0, i)),
         ),
-        scratch_shapes=[
-            pltpu.VMEM((2, block, key_columns), bf16),
-            pltpu.VMEM((rows, key_columns), f32),
-            pltpu.SemaphoreType.DMA((2, block // TILE_ROWS)),
-        ],
+        scratch_shapes=[pltpu.VMEM((rows, key_columns), f32)],
         compiler_params=params(56),
         cost_estimate=pl.CostEstimate(
             flops=4 * rows * depth * key_columns,
@@ -321,7 +279,7 @@
             transcendentals=0,
         ),
         name="base",
-    )(core, tokens, cotangent, half, other, adapter, adapter, adapter, adapter)
+    )(tokens, cotangent, weight, adapter, adapter, adapter, adapter)
     return keys, token_gradient, jnp.swapaxes(grads, 1, 2)
 
 

time: 208 us -> 171 us (0.82)
  waiting for transfers between devices: 68.8 us -> 27.6 us
  blocking collectives: 80.5 us -> 96.8 us
  Pallas kernels: 29.2 us -> 21.5 us
  starting transfers between devices: 11.1 us -> 7.91 us
    all_gather x2 -> x1, waiting for transfers between devices: 43.7 us -> 11.3 us  [on_device(): weight = lax.all_gather(frozen_weight, SEQ, axis=0, tiled=True)]
    all_to_all x1, blocking collectives: 37.5 us -> 50.9 us  [on_device(): lax.all_to_all(terms, SEQ, split_axis=0, concat_axis=0, tiled=True)]
    ppermute x6, waiting for transfers between devices: 20.8 us -> 15.6 us  [shift(): lax.ppermute(x, 'grp', [(i, (i + by) % groups) for i in range(groups)])]
    pallas_call x1, Pallas kernels: 5.86 us -> 1.26 us  [on_device(): pl.pallas_call(sum_kernel, out_shape=(jax.ShapeDtypeStruct((slot_count, p...]
    ppermute x1 -> x0, waiting for transfers between devices: 3.67 us -> none  [on_device(): other = lax.ppermute(half, 'core', [(0, 1), (1, 0)])]
    all_to_all x1, blocking collectives: 42.9 us -> 45.9 us  [on_device(): lax.all_to_all(outgoing, SEQ, split_axis=0, concat_axis=0, tiled=True)]
    ppermute x6, starting transfers between devices: 10.5 us -> 7.87 us  [shift(): lax.ppermute(x, 'grp', [(i, (i + by) % groups) for i in range(groups)])]
    pallas_call x1, Pallas kernels: 3.31 us -> 0.87 us  [on_device(): pl.pallas_call(pick_kernel, out_shape=jax.ShapeDtypeStruct((shards, packe...]
  transfers between devices with their start and end apart: 9 -> 7, of which waited for: 7 -> 4; matrix products, arithmetic and copies ran while one was open for 0% -> 0% of each run, Pallas kernels for 14% -> 12%
where the time goes in v5:
time: 171 us; the launch traced here: 170 us
  blocking collectives  96.8 us (57%)
  waiting for transfers between devices  27.6 us (16%)
  Pallas kernels  21.5 us (13%)
  between operations  14.1 us (8%)
  starting transfers between devices  7.91 us (5%)
  local copies, waits for them, and re-layouts  2.4 us (1%)
    all_to_all x1, blocking collectives, on_device(): lax.all_to_all(terms, SEQ, split_axis=0, concat_axis=0, tiled=True)  50.9 us
    all_to_all x1, blocking collectives, on_device(): lax.all_to_all(outgoing, SEQ, split_axis=0, concat_axis=0, tiled=True)  45.9 us
    ppermute x6, waiting for transfers between devices, shift(): lax.ppermute(x, 'grp', [(i, (i + by) % groups) for i in range(groups)])  15.6 us
    pallas_call x1, Pallas kernels, on_device(): pl.pallas_call(base_kernel, grid=(steps,), out_shape=(jax.ShapeDtypeStruc...  14.5 us
    all_gather x1, waiting for transfers between devices, on_device(): weight = lax.all_gather(frozen_weight, SEQ, axis=0, tiled=True)  11.3 us
    ppermute x6, starting transfers between devices, shift(): lax.ppermute(x, 'grp', [(i, (i + by) % groups) for i in range(groups)])  7.87 us
    pallas_call x1, Pallas kernels, on_device(): pl.pallas_call(tile_kernel, out_shape=(jax.ShapeDtypeStruct((shards, pack...  3.57 us
  transfers between devices with their start and end apart: 7, of which 4 were waited for; matrix products, arithmetic and copies ran while one was open for 0% of the time, Pallas kernels for 12%

profile of v5, /device:TPU:1, one launch (start us, length us, event | category | flops | bytes accessed | tf_op | source)
XLA Modules:
  0.0 170.4 jit_solution(13317465279819820106)
XLA Ops:
  7.2 0.0 all-gather.2.cloned.1.call-start
  7.2 0.7 all-gather.2.cloned.1.call-update
  7.9 1.0 copy-done.3
  8.9 0.1 pack.1.refs_0_
  9.1 3.4 %collective-permute-start = (bf16[16,72,128]{2,1,0:T(8,128)(2,1)S(1)}, bf16[16,72,128]{2,1,0:T(8,128)(2,1)S(1)}, u32[]{:S(2)}, u32[]{:S(2)}) collective-permute-start(bf16[16,72,128]{2,1,0:T(8,128)(2,1)S(1)} %pack.1.refs_0_), channel_id=1, source_target_pairs={{0,192},{64,0},{128,64},{192,128},{1,193},{65,1},{129,65},{193,129... | collective-permute-start | bytes 884744 | tf_op jit(solution)/shard_map/ppermute | solution.py:177
  12.5 0.5 collective-permute-start.1
  13.0 0.6 collective-permute-start.2
  13.6 7.9 %collective-permute-done.refs_1_ = bf16[16,72,128]{2,1,0:T(8,128)(2,1)S(1)} collective-permute-done((bf16[16,72,128]{2,1,0:T(8,128)(2,1)S(1)}, bf16[16,72,128]{2,1,0:T(8,128)(2,1)S(1)}, u32[]{:S(2)}, u32[]{:S(2)}) %collective-permute-start) | collective-permute-done | bytes 294944 | tf_op jit(solution)/shard_map/ppermute | solution.py:177
  21.5 0.1 collective-permute-done.1.refs_2_
  21.6 7.6 %collective-permute-done.2.refs_3_ = bf16[16,72,128]{2,1,0:T(8,128)(2,1)S(1)} collective-permute-done((bf16[16,72,128]{2,1,0:T(8,128)(2,1)S(1)}, bf16[16,72,128]{2,1,0:T(8,128)(2,1)S(1)}, u32[]{:S(2)}, u32[]{:S(2)}) %collective-permute-start.2) | collective-permute-done | bytes 294944 | tf_op jit(solution)/shard_map/ppermute | solution.py:177
  29.2 0.7 copy-done.4
  29.9 0.7 copy-done.6
  30.6 0.9 pick.1
  31.4 0.0 copy-start.1
  31.5 45.9 %all_to_all.10.x_ref = bf16[64,72,128]{2,1,0:T(8,128)(2,1)S(1)} all-to-all(bf16[64,72,128]{2,1,0:T(8,128)(2,1)S(1)} %pick.1), channel_id=1, replica_groups=mesh['grp'=4,'y'=4,'z'=8,'core'=2] {'y','z','core'}, dimensions={0} | all-to-all | bytes 2359296 | tf_op jit(solution)/shard_map/all_to_all | solution.py:216
  77.3 3.6 %tile.1 = (bf16[64,72,128]{2,1,0:T(8,128)(2,1)S(1)}, bf16[64,9472]{1,0:T(8,128)(2,1)S(1)}) custom-call(bf16[64,72,128]{2,1,0:T(8,128)(2,1)S(1)} %all_to_all.10.x_ref, bf16[128,8192]{1,0:T(8,128)(2,1)S(1)} %copy-done.1, bf16[128,1024]{1,0:T(8,128)(2,1)S(1)} %copy-done.2), custom_call_target="tpu_custom_call" | custom-call | tf_op jit(solution)/shard_map/tile/pallas_call | solution.py:217
  80.9 50.9 %all_to_all.11.x_ref = bf16[64,72,128]{2,1,0:T(8,128)(2,1)S(1)} all-to-all(bf16[64,72,128]{2,1,0:T(8,128)(2,1)S(1)} %get-tuple-element.13), channel_id=1, replica_groups=mesh['grp'=4,'y'=4,'z'=8,'core'=2] {'y','z','core'}, dimensions={0} | all-to-all | bytes 2359296 | tf_op jit(solution)/shard_map/all_to_all | solution.py:229
  131.9 1.3 sum.1
  133.2 0.1 collective-permute-start.3
  133.3 2.0 %collective-permute-start.4 = (bf16[16,72,128]{2,1,0:T(8,128)(2,1)S(1)}, bf16[16,72,128]{2,1,0:T(8,128)(2,1)S(1)}, u32[]{:S(2)}, u32[]{:S(2)}) collective-permute-start(bf16[16,72,128]{2,1,0:T(8,128)(2,1)S(1)} %get-tuple-element.21), channel_id=1, source_target_pairs={{0,128},{64,192},{128,0},{192,64},{1,129},{65,193},{129,1},{193,65... | collective-permute-start | bytes 884744 | tf_op jit(solution)/shard_map/ppermute | solution.py:177
  135.2 11.3 %all-gather.2.cloned.1.call-done.w_ref = bf16[8192,1024]{1,0:T(8,128)(2,1)} async-done(((bf16[128,1024]{1,0:T(8,128)(2,1)}), bf16[8192,1024]{1,0:T(8,128)(2,1)}) %all-gather.2.cloned.1.call-update) | async-done | bytes 16777232 | tf_op jit(solution)/shard_map/all_gather | solution.py:195
  146.5 1.3 collective-permute-start.5
  147.8 14.5 %base.1 = (bf16[128,1024]{1,0:T(8,128)(2,1)}, bf16[128,8192]{1,0:T(8,128)(2,1)}) custom-call(bf16[128,8192]{1,0:T(8,128)(2,1)} %tok_ref.3, bf16[128,1024]{1,0:T(8,128)(2,1)} %cot_ref.3, bf16[8192,1024]{1,0:T(8,128)(2,1)} %all-gather.2.cloned.1.call-done.w_ref, bf16[64,9472]{1,0:T(8,128)(2,1)} %copy-done, bf16[64,9472]{1,0:T(8,128)(2,1)} %copy-done, ...), custom_call_target="tpu_custom_call" | custom-call | flops 4294967296 | bytes 21495808 | tf_op jit(solution)/shard_map/base/pallas_call | solution.py:254
  162.4 1.2 unpack.1
  (15 shorter events, 0.0 us)
Async XLA Ops:
  7.2 139.3 %all-gather.2.cloned.1.call-start = ((), (), s32[]{:S(2)}) async-start(), calls=%async_computation.2 | async-start | bytes 17039360 | tf_op jit(solution)/shard_map/all_gather | solution.py:195
  7.9 1.0 copy-start.3
  9.1 12.4 %collective-permute-start = (bf16[16,72,128]{2,1,0:T(8,128)(2,1)S(1)}, bf16[16,72,128]{2,1,0:T(8,128)(2,1)S(1)}, u32[]{:S(2)}, u32[]{:S(2)}) collective-permute-start(bf16[16,72,128]{2,1,0:T(8,128)(2,1)S(1)} %pack.1.refs_0_), channel_id=1, source_target_pairs={{0,192},{64,0},{128,64},{192,128},{1,193},{65,1},{129,65},{193,129... | collective-permute-start | bytes 884744 | tf_op jit(solution)/shard_map/ppermute | solution.py:177
  12.5 9.1 %collective-permute-start.1 = (bf16[16,72,128]{2,1,0:T(8,128)(2,1)S(1)}, bf16[16,72,128]{2,1,0:T(8,128)(2,1)S(1)}, u32[]{:S(2)}, u32[]{:S(2)}) collective-permute-start(bf16[16,72,128]{2,1,0:T(8,128)(2,1)S(1)} %pack.1.refs_0_), channel_id=1, source_target_pairs={{0,128},{64,192},{128,0},{192,64},{1,129},{65,193},{129,1},{193,65... | collective-permute-start | bytes 884744 | tf_op jit(solution)/shard_map/ppermute | solution.py:177
  13.0 16.2 %collective-permute-start.2 = (bf16[16,72,128]{2,1,0:T(8,128)(2,1)S(1)}, bf16[16,72,128]{2,1,0:T(8,128)(2,1)S(1)}, u32[]{:S(2)}, u32[]{:S(2)}) collective-permute-start(bf16[16,72,128]{2,1,0:T(8,128)(2,1)S(1)} %pack.1.refs_0_), channel_id=1, source_target_pairs={{0,64},{64,128},{128,192},{192,0},{1,65},{65,129},{129,193},{193,1... | collective-permute-start | bytes 884744 | tf_op jit(solution)/shard_map/ppermute | solution.py:177
  29.2 0.7 copy-start.4
  29.9 0.7 copy-start.6
  31.4 45.9 %copy-start.1 = (bf16[128,8192]{1,0:T(8,128)(2,1)S(1)}, bf16[128,8192]{1,0:T(8,128)(2,1)}, u32[]{:S(2)}) copy-start(bf16[128,8192]{1,0:T(8,128)(2,1)} %tok_ref.3) | copy-start | bytes 6291460
  31.4 45.9 %copy-start.2 = (bf16[128,1024]{1,0:T(8,128)(2,1)S(1)}, bf16[128,1024]{1,0:T(8,128)(2,1)}, u32[]{:S(2)}) copy-start(bf16[128,1024]{1,0:T(8,128)(2,1)} %cot_ref.3) | copy-start | bytes 786436
  80.9 52.2 %copy-start = (bf16[64,9472]{1,0:T(8,128)(2,1)}, bf16[64,9472]{1,0:T(8,128)(2,1)S(1)}, u32[]{:S(2)}) copy-start(bf16[64,9472]{1,0:T(8,128)(2,1)S(1)} %get-tuple-element.16.at_ref.up_ref.hid_ref.back_ref) | copy-start | bytes 3637252
  80.9 51.0 %copy-start.5 = (s32[256,1]{0,1:T(1,128)S(1)}, s32[256,1]{0,1:T(1,128)}, u32[]{:S(2)}) copy-start(s32[256,1]{0,1:T(1,128)} %param.10) | copy-start | bytes 3076
  80.9 51.0 %copy-start.7 = (s32[64]{0:T(128)S(1)}, s32[64]{0:T(128)}, u32[]{:S(2)}) copy-start(s32[64]{0:T(128)} %slot_ref.3) | copy-start | bytes 772
  133.2 29.2 %collective-permute-start.3 = (bf16[16,72,128]{2,1,0:T(8,128)(2,1)S(1)}, bf16[16,72,128]{2,1,0:T(8,128)(2,1)S(1)}, u32[]{:S(2)}, u32[]{:S(2)}) collective-permute-start(bf16[16,72,128]{2,1,0:T(8,128)(2,1)S(1)} %get-tuple-element.20), channel_id=1, source_target_pairs={{0,64},{64,128},{128,192},{192,0},{1,65},{65,129},{129,193},{193,1... | collective-permute-start | bytes 884744 | tf_op jit(solution)/shard_map/ppermute | solution.py:177
  133.3 29.1 %collective-permute-start.4 = (bf16[16,72,128]{2,1,0:T(8,128)(2,1)S(1)}, bf16[16,72,128]{2,1,0:T(8,128)(2,1)S(1)}, u32[]{:S(2)}, u32[]{:S(2)}) collective-permute-start(bf16[16,72,128]{2,1,0:T(8,128)(2,1)S(1)} %get-tuple-element.21), channel_id=1, source_target_pairs={{0,128},{64,192},{128,0},{192,64},{1,129},{65,193},{129,1},{193,65... | collective-permute-start | bytes 884744 | tf_op jit(solution)/shard_map/ppermute | solution.py:177
  146.5 15.9 %collective-permute-start.5 = (bf16[16,72,128]{2,1,0:T(8,128)(2,1)S(1)}, bf16[16,72,128]{2,1,0:T(8,128)(2,1)S(1)}, u32[]{:S(2)}, u32[]{:S(2)}) collective-permute-start(bf16[16,72,128]{2,1,0:T(8,128)(2,1)S(1)} %get-tuple-element.22), channel_id=1, source_target_pairs={{0,192},{64,0},{128,64},{192,128},{1,193},{65,1},{129,65},{193,129... | collective-permute-start | bytes 884744 | tf_op jit(solution)/shard_map/ppermute | solution.py:177
Sparse Core Ops, SparseCore 0:
  10.8 135.6 all-gather.1

commit v6 on v5

--- a/solution.py
+++ b/solution.py
@@ -151,8 +151,12 @@
     lax.fori_loop(0, shards // per, pack, 0)
 
 
-def base_kernel(tok_ref, cot_ref, w_ref, at_ref, up_ref, hid_ref, back_ref, keys_ref, grad_ref, acc_ref):
-    step = pl.program_id(0)
+def base_kernel(z_ref, tok_ref, cot_ref, w_ref, at_ref, up_ref, hid_ref, back_ref, keys_ref, grad_ref, acc_ref):
+    step = pl.program_id(0) * pl.num_programs(1) + pl.program_id(1)
+    _, pieces, count, quarter, _ = w_ref.shape
+    span = pieces * quarter
+    deep = count * pl.num_programs(1)
+    order = [x * 2 + c for c in range(2) for x in range(pieces // 2)]
 
     @pl.when(step == 0)
     def _():
@@ -160,21 +164,37 @@
             hid_ref[...], up_ref[...], TN, preferred_element_type=f32
         )
 
-    weight = w_ref[...]
-    acc_ref[...] += jnp.dot(tok_ref[...], weight, preferred_element_type=f32)
+    places = []
+    for k in range(count):
+        place = lax.rem(z_ref[0] - (pl.program_id(1) * count + k) + deep, deep)
+        places.append(pl.ds(pl.multiple_of(place * span, span), span))
+    weight = jnp.concatenate([w_ref[0, p, k] for k in range(count) for p in order], axis=0)
+    tok = jnp.concatenate([tok_ref[:, at] for at in places], axis=1)
+    down = jnp.concatenate([at_ref[:, at] for at in places], axis=1)
+    acc_ref[...] += jnp.dot(tok, weight, preferred_element_type=f32)
     grad = lax.dot_general(cot_ref[...], weight, NT, preferred_element_type=f32)
-    grad += adapter_scale * lax.dot_general(
-        back_ref[...], at_ref[...], TN, preferred_element_type=f32
-    )
-    grad_ref[...] = grad.astype(grad_ref.dtype)
-
-    @pl.when(step == pl.num_programs(0) - 1)
+    grad += adapter_scale * lax.dot_general(back_ref[...], down, TN, preferred_element_type=f32)
+    grad = grad.astype(grad_ref.dtype)
+    for k, at in enumerate(places):
+        grad_ref[:, at] = grad[:, k * span : (k + 1) * span]
+
+    @pl.when(step == pl.num_programs(0) * pl.num_programs(1) - 1)
     def _():
         keys_ref[...] = acc_ref[...].astype(keys_ref.dtype)
 
 
 def shift(x, by, groups):
     return lax.ppermute(x, "grp", [(i, (i + by) % groups) for i in range(groups)])
+
+
+def ring(x, axis, size):
+    up = [x]
+    down = [x]
+    for _ in range(size // 2):
+        up.append(lax.ppermute(up[-1], axis, [(i, (i + 1) % size) for i in range(size)]))
+    for _ in range(size // 2 - 1):
+        down.append(lax.ppermute(down[-1], axis, [(i, (i - 1) % size) for i in range(size)]))
+    return jnp.concatenate(up + down[:0:-1], axis=0)
 
 
 def whole(memory=pltpu.VMEM):
@@ -190,9 +210,12 @@
     packed_rows = row_count * rank // LANES
     width = depth + key_columns
     group = lax.axis_index("grp").reshape(1).astype(jnp.int32)
+    z = lax.axis_index("z").reshape(1).astype(jnp.int32)
     jobs = tile_job.reshape(-1)
 
-    weight = lax.all_gather(frozen_weight, SEQ, axis=0, tiled=True)
+    quarter = TILE_ROWS // groups
+    mine = lax.dynamic_slice_in_dim(frozen_weight, lax.axis_index("grp") * quarter, quarter, 0)
+    column = ring(mine, "z", lax.axis_size("z"))
 
     own = pl.pallas_call(
         pack_kernel,
@@ -213,6 +236,8 @@
         compiler_params=params(),
         name="pick",
     )(group, jobs, job_slot, *every)
+    outgoing, column = lax.optimization_barrier((outgoing, column))
+    weight = lax.all_gather(column, ("y", "grp", "core"), axis=0, tiled=True)
     arrived = lax.all_to_all(outgoing, SEQ, split_axis=0, concat_axis=0, tiled=True)
     terms, adapter = pl.pallas_call(
         tile_kernel,
@@ -249,27 +274,32 @@
         name="unpack",
     )(*owned)
 
-    block = 1024
-    steps = depth // block
+    wide, deep, halves = lax.axis_size("y"), lax.axis_size("z"), 2
+    span = depth // wide
+    weight = weight.reshape(wide, shards // (wide * deep) * groups, deep, quarter, key_columns)
     keys, token_gradient = pl.pallas_call(
         base_kernel,
-        grid=(steps,),
+        grid=(wide, halves),
         out_shape=(
             jax.ShapeDtypeStruct((rows, key_columns), bf16),
             jax.ShapeDtypeStruct((rows, depth), bf16),
         ),
         in_specs=[
-            pl.BlockSpec((rows, block), lambda i: (0, i)),
-            pl.BlockSpec((rows, key_columns), lambda i: (0, 0)),
-            pl.BlockSpec((block, key_columns), lambda i: (i, 0)),
-            pl.BlockSpec((rank, block), lambda i: (0, i)),
-            pl.BlockSpec((rank, key_columns), lambda i: (0, depth // key_columns)),
-            pl.BlockSpec((rank, rows), lambda i: (0, width // rows)),
-            pl.BlockSpec((rank, rows), lambda i: (0, width // rows + 1)),
+            smem,
+            pl.BlockSpec((rows, span), lambda i, h: (0, i)),
+            pl.BlockSpec((rows, key_columns), lambda i, h: (0, 0)),
+            pl.BlockSpec(
+                (1, weight.shape[1], deep // halves, quarter, key_columns),
+                lambda i, h: (i, 0, h, 0, 0),
+            ),
+            pl.BlockSpec((rank, span), lambda i, h: (0, i)),
+            pl.BlockSpec((rank, key_columns), lambda i, h: (0, depth // key_columns)),
+            pl.BlockSpec((rank, rows), lambda i, h: (0, width // rows)),
+            pl.BlockSpec((rank, rows), lambda i, h: (0, width // rows + 1)),
         ],
         out_specs=(
-            pl.BlockSpec((rows, key_columns), lambda i: (0, 0)),
-            pl.BlockSpec((rows, block), lambda i: (0, i)),
+            pl.BlockSpec((rows, key_columns), lambda i, h: (0, 0)),
+            pl.BlockSpec((rows, span), lambda i, h: (0, i)),
         ),
         scratch_shapes=[pltpu.VMEM((rows, key_columns), f32)],
         compiler_params=params(56),
@@ -279,7 +309,7 @@
             transcendentals=0,
         ),
         name="base",
-    )(tokens, cotangent, weight, adapter, adapter, adapter, adapter)
+    )(z, tokens, cotangent, weight, adapter, adapter, adapter, adapter)
     return keys, token_gradient, jnp.swapaxes(grads, 1, 2)
 
 

time: 171 us -> 162 us (0.947)
  blocking collectives: 96.8 us -> 43 us
  waiting for transfers between devices: 27.6 us -> 50.2 us
  starting transfers between devices: 7.91 us -> 28 us
    all_to_all x1 -> x0, blocking collectives: 50.9 us -> none  [on_device(): lax.all_to_all(terms, SEQ, split_axis=0, concat_axis=0, tiled=True)]
    all_to_all x0 -> x1, waiting for transfers between devices: none -> 31.4 us  [on_device(): lax.all_to_all(terms, SEQ, split_axis=0, concat_axis=0, tiled=True)]
    ppermute x6, waiting for transfers between devices: 15.6 us -> 1.98 us  [shift(): lax.ppermute(x, 'grp', [(i, (i + by) % groups) for i in range(groups)])]
    ppermute x0 -> x7, starting transfers between devices: none -> 12.2 us  [the longest x3 9.67 us: ring(): lax.ppermute(down[-1], axis, [(i, (i - 1) % size) for i in range(size)])]
    ppermute x0 -> x7, waiting for transfers between devices: none -> 7.9 us  [the longest x4 7.89 us: ring(): lax.ppermute(up[-1], axis, [(i, (i + 1) % size) for i in range(size)])]
    all_to_all x0 -> x1, starting transfers between devices: none -> 6.18 us  [on_device(): lax.all_to_all(terms, SEQ, split_axis=0, concat_axis=0, tiled=True)]
    all_to_all x1, blocking collectives: 45.9 us -> 43 us  [on_device(): lax.all_to_all(outgoing, SEQ, split_axis=0, concat_axis=0, tiled=True)]
    all_gather x1, waiting for transfers between devices: 11.3 us -> 8.95 us  [on_device(): weight = lax.all_gather(column, ('y', 'grp', 'core'), axis=0, tiled=True)]
  transfers between devices with their start and end apart: 7 -> 15, of which waited for: 4 -> 6; matrix products, arithmetic and copies ran while one was open for 0% -> 0% of each run, Pallas kernels for 12% -> 13%
where the time goes in v6:
time: 162 us; the launch traced here: 161 us
  waiting for transfers between devices  50.2 us (31%)
  blocking collectives  43 us (27%)
  starting transfers between devices  28 us (17%)
  Pallas kernels  22.9 us (14%)
  between operations  14.2 us (9%)
  local copies, waits for them, and re-layouts  3 us (2%)
    all_to_all x1, blocking collectives, on_device(): lax.all_to_all(outgoing, SEQ, split_axis=0, concat_axis=0, tiled=True)  43 us
    all_to_all x1, waiting for transfers between devices, on_device(): lax.all_to_all(terms, SEQ, split_axis=0, concat_axis=0, tiled=True)  31.4 us
    pallas_call x1, Pallas kernels, on_device(): pl.pallas_call(base_kernel, grid=(wide, halves), out_shape=(jax.ShapeDtyp...  14.8 us
    ppermute x3, starting transfers between devices, ring(): lax.ppermute(down[-1], axis, [(i, (i - 1) % size) for i in range(size)])  9.67 us
    ppermute x6, starting transfers between devices, shift(): lax.ppermute(x, 'grp', [(i, (i + by) % groups) for i in range(groups)])  9.61 us
    all_gather x1, waiting for transfers between devices, on_device(): weight = lax.all_gather(column, ('y', 'grp', 'core'), axis=0, tiled=True)  8.95 us
    ppermute x4, waiting for transfers between devices, ring(): lax.ppermute(up[-1], axis, [(i, (i + 1) % size) for i in range(size)])  7.89 us
    all_to_all x1, starting transfers between devices, on_device(): lax.all_to_all(terms, SEQ, split_axis=0, concat_axis=0, tiled=True)  6.18 us
  transfers between devices with their start and end apart: 15, of which 6 were waited for; matrix products, arithmetic and copies ran while one was open for 0% of the time, Pallas kernels for 13%

profile of v6, /device:TPU:1, one launch (start us, length us, event | category | flops | bytes accessed | tf_op | source)
XLA Modules:
  0.0 161.3 jit_solution(3327009564420407812)
XLA Ops:
  7.2 0.9 constant_dynamic-update-slice_fusion.7
  8.1 2.5 %collective-permute-start.3 = (bf16[32,1024]{1,0:T(8,128)(2,1)S(1)}, bf16[32,1024]{1,0:T(8,128)(2,1)S(1)}, u32[]{:S(2)}, u32[]{:S(2)}) collective-permute-start(bf16[32,1024]{1,0:T(8,128)(2,1)S(1)} %get-tuple-element.28), channel_id=1, source_target_pairs={{0,2},{2,4},{4,6},{6,8},{8,10},{10,12},{12,14},{14,0},{1,3},{3,5},... | collective-permute-start | bytes 196616 | tf_op jit(solution)/shard_map/ppermute | solution.py:194
  10.6 4.0 %collective-permute-start.7 = (bf16[32,1024]{1,0:T(8,128)(2,1)S(1)}, bf16[32,1024]{1,0:T(8,128)(2,1)S(1)}, u32[]{:S(2)}, u32[]{:S(2)}) collective-permute-start(bf16[32,1024]{1,0:T(8,128)(2,1)S(1)} %get-tuple-element.28), channel_id=1, source_target_pairs={{0,14},{2,0},{4,2},{6,4},{8,6},{10,8},{12,10},{14,12},{1,15},{3,1}... | collective-permute-start | bytes 196616 | tf_op jit(solution)/shard_map/ppermute | solution.py:196
  14.7 1.0 copy-done.3
  15.9 2.6 %collective-permute-start = (bf16[16,72,128]{2,1,0:T(8,128)(2,1)S(1)}, bf16[16,72,128]{2,1,0:T(8,128)(2,1)S(1)}, u32[]{:S(2)}, u32[]{:S(2)}) collective-permute-start(bf16[16,72,128]{2,1,0:T(8,128)(2,1)S(1)} %pack.1.refs_0_), channel_id=1, source_target_pairs={{0,192},{64,0},{128,64},{192,128},{1,193},{65,1},{129,65},{193,129... | collective-permute-start | bytes 884744 | tf_op jit(solution)/shard_map/ppermute | solution.py:187
  19.5 2.7 %collective-permute-start.8 = (bf16[32,1024]{1,0:T(8,128)(2,1)S(1)}, bf16[32,1024]{1,0:T(8,128)(2,1)S(1)}, u32[]{:S(2)}, u32[]{:S(2)}) collective-permute-start(bf16[32,1024]{1,0:T(8,128)(2,1)S(1)} %collective-permute-done.7), channel_id=1, source_target_pairs={{0,14},{2,0},{4,2},{6,4},{8,6},{10,8},{12,10},{14,12},{1,15},{3,1}... | collective-permute-start | bytes 196616 | tf_op jit(solution)/shard_map/ppermute | solution.py:196
  22.2 1.6 %collective-permute-done.4 = bf16[32,1024]{1,0:T(8,128)(2,1)S(1)} collective-permute-done((bf16[32,1024]{1,0:T(8,128)(2,1)S(1)}, bf16[32,1024]{1,0:T(8,128)(2,1)S(1)}, u32[]{:S(2)}, u32[]{:S(2)}) %collective-permute-start.4) | collective-permute-done | bytes 65568 | tf_op jit(solution)/shard_map/ppermute | solution.py:194
  23.9 3.0 %collective-permute-start.9 = (bf16[32,1024]{1,0:T(8,128)(2,1)S(1)}, bf16[32,1024]{1,0:T(8,128)(2,1)S(1)}, u32[]{:S(2)}, u32[]{:S(2)}) collective-permute-start(bf16[32,1024]{1,0:T(8,128)(2,1)S(1)} %collective-permute-done.8), channel_id=1, source_target_pairs={{0,14},{2,0},{4,2},{6,4},{8,6},{10,8},{12,10},{14,12},{1,15},{3,1}... | collective-permute-start | bytes 196616 | tf_op jit(solution)/shard_map/ppermute | solution.py:196
  26.8 1.6 %collective-permute-done.5 = bf16[32,1024]{1,0:T(8,128)(2,1)S(1)} collective-permute-done((bf16[32,1024]{1,0:T(8,128)(2,1)S(1)}, bf16[32,1024]{1,0:T(8,128)(2,1)S(1)}, u32[]{:S(2)}, u32[]{:S(2)}) %collective-permute-start.5) | collective-permute-done | bytes 65568 | tf_op jit(solution)/shard_map/ppermute | solution.py:194
  28.5 4.6 %collective-permute-done.6 = bf16[32,1024]{1,0:T(8,128)(2,1)S(1)} collective-permute-done((bf16[32,1024]{1,0:T(8,128)(2,1)S(1)}, bf16[32,1024]{1,0:T(8,128)(2,1)S(1)}, u32[]{:S(2)}, u32[]{:S(2)}) %collective-permute-start.6) | collective-permute-done | bytes 65568 | tf_op jit(solution)/shard_map/ppermute | solution.py:194
  33.2 2.0 %collective-permute-done.2.refs_3_ = bf16[16,72,128]{2,1,0:T(8,128)(2,1)S(1)} collective-permute-done((bf16[16,72,128]{2,1,0:T(8,128)(2,1)S(1)}, bf16[16,72,128]{2,1,0:T(8,128)(2,1)S(1)}, u32[]{:S(2)}, u32[]{:S(2)}) %collective-permute-start.2) | collective-permute-done | bytes 294944 | tf_op jit(solution)/shard_map/ppermute | solution.py:187
  35.2 0.9 pick.1
  36.1 43.0 %all_to_all.10.x_ref = bf16[64,72,128]{2,1,0:T(8,128)(2,1)S(1)} all-to-all(bf16[64,72,128]{2,1,0:T(8,128)(2,1)S(1)} %pick.1), channel_id=1, replica_groups=mesh['grp'=4,'y'=4,'z'=8,'core'=2] {'y','z','core'}, dimensions={0} | all-to-all | bytes 2359296 | tf_op jit(solution)/shard_map/all_to_all | solution.py:241
  79.1 4.6 %tile.1 = (bf16[64,72,128]{2,1,0:T(8,128)(2,1)}, bf16[64,9472]{1,0:T(8,128)(2,1)S(1)}) custom-call(bf16[64,72,128]{2,1,0:T(8,128)(2,1)S(1)} %all_to_all.10.x_ref, bf16[128,8192]{1,0:T(8,128)(2,1)S(1)} %copy-done.1, bf16[128,1024]{1,0:T(8,128)(2,1)S(1)} %copy-done.2), custom_call_target="tpu_custom_call" | custom-call | tf_op jit(solution)/shard_map/tile/pallas_call | solution.py:242
  83.7 1.0 copy-done
  84.7 6.2 %all-to-all-start.1 = ((bf16[64,72,128]{2,1,0:T(8,128)(2,1)}), bf16[64,72,128]{2,1,0:T(8,128)(2,1)S(1)}, u32[]{:S(2)}, u32[]{:S(2)}) async-start(bf16[64,72,128]{2,1,0:T(8,128)(2,1)} %get-tuple-element.16), calls=%async_computation.1 | async-start | bytes 2359296 | tf_op jit(solution)/shard_map/all_to_all | solution.py:254
  90.9 31.4 %all-to-all-done.1.x_ref = bf16[64,72,128]{2,1,0:T(8,128)(2,1)S(1)} async-done(((bf16[64,72,128]{2,1,0:T(8,128)(2,1)}), bf16[64,72,128]{2,1,0:T(8,128)(2,1)S(1)}, u32[]{:S(2)}, u32[]{:S(2)}) %all-to-all-start.1) | async-done | bytes 1179680 | tf_op jit(solution)/shard_map/all_to_all | solution.py:254
  122.3 1.3 sum.1
  123.5 1.8 %collective-permute-start.10 = (bf16[16,72,128]{2,1,0:T(8,128)(2,1)S(1)}, bf16[16,72,128]{2,1,0:T(8,128)(2,1)S(1)}, u32[]{:S(2)}, u32[]{:S(2)}) collective-permute-start(bf16[16,72,128]{2,1,0:T(8,128)(2,1)S(1)} %get-tuple-element.24), channel_id=1, source_target_pairs={{0,64},{64,128},{128,192},{192,0},{1,65},{65,129},{129,193},{193,1... | collective-permute-start | bytes 884744 | tf_op jit(solution)/shard_map/ppermute | solution.py:187
  125.3 1.7 %collective-permute-start.11 = (bf16[16,72,128]{2,1,0:T(8,128)(2,1)S(1)}, bf16[16,72,128]{2,1,0:T(8,128)(2,1)S(1)}, u32[]{:S(2)}, u32[]{:S(2)}) collective-permute-start(bf16[16,72,128]{2,1,0:T(8,128)(2,1)S(1)} %get-tuple-element.25), channel_id=1, source_target_pairs={{0,128},{64,192},{128,0},{192,64},{1,129},{65,193},{129,1},{193,65... | collective-permute-start | bytes 884744 | tf_op jit(solution)/shard_map/ppermute | solution.py:187
  127.0 8.9 %all-gather.2.cloned.1.call-done = bf16[8192,1024]{1,0:T(8,128)(2,1)} async-done(((bf16[256,1024]{1,0:T(8,128)(2,1)}), bf16[8192,1024]{1,0:T(8,128)(2,1)}) %all-gather.2.cloned.1.call-update) | async-done | bytes 16777232 | tf_op jit(solution)/shard_map/all_gather | solution.py:240
  136.0 2.4 %collective-permute-start.12 = (bf16[16,72,128]{2,1,0:T(8,128)(2,1)S(1)}, bf16[16,72,128]{2,1,0:T(8,128)(2,1)S(1)}, u32[]{:S(2)}, u32[]{:S(2)}) collective-permute-start(bf16[16,72,128]{2,1,0:T(8,128)(2,1)S(1)} %get-tuple-element.26), channel_id=1, source_target_pairs={{0,192},{64,0},{128,64},{192,128},{1,193},{65,1},{129,65},{193,129... | collective-permute-start | bytes 884744 | tf_op jit(solution)/shard_map/ppermute | solution.py:187
  138.4 14.8 %base.1 = (bf16[128,1024]{1,0:T(8,128)(2,1)}, bf16[128,8192]{1,0:T(8,128)(2,1)}) custom-call(s32[1]{0:T(128)} %bitcast.z_ref, bf16[128,8192]{1,0:T(8,128)(2,1)} %tok_ref.3, bf16[128,1024]{1,0:T(8,128)(2,1)} %cot_ref.3, bf16[4,8,8,32,1024]{4,3,2,1,0:T(8,128)(2,1)} %bitcast.9, bf16[64,9472]{1,0:T(8,128)(2,1)} %copy-done, bf16[64,9472]{1,0:T(8,128)(2,1)} %copy-done, ...), custom_call_target="tpu_custom_call" | custom-call | flops 4294967296 | bytes 21495808 | tf_op jit(solution)/shard_map/base/pallas_call | solution.py:280
  153.3 1.2 unpack.1
  (36 shorter events, 1.4 us)
Async XLA Ops:
  7.2 28.0 %copy-start.4 = (s32[256,1]{0,1:T(1,128)S(1)}, s32[256,1]{0,1:T(1,128)}, u32[]{:S(2)}) copy-start(s32[256,1]{0,1:T(1,128)} %param.10) | copy-start | bytes 3076
  7.2 28.0 %copy-start.5 = (s32[64]{0:T(128)S(1)}, s32[64]{0:T(128)}, u32[]{:S(2)}) copy-start(s32[64]{0:T(128)} %slot_ref.3) | copy-start | bytes 772
  7.2 128.8 %all-gather.2.cloned.1.call-start = ((), (), s32[]{:S(2)}) async-start(), calls=%async_computation.2 | async-start | bytes 17301504 | tf_op jit(solution)/shard_map/all_gather | solution.py:240
  8.1 11.4 %collective-permute-start.3 = (bf16[32,1024]{1,0:T(8,128)(2,1)S(1)}, bf16[32,1024]{1,0:T(8,128)(2,1)S(1)}, u32[]{:S(2)}, u32[]{:S(2)}) collective-permute-start(bf16[32,1024]{1,0:T(8,128)(2,1)S(1)} %get-tuple-element.28), channel_id=1, source_target_pairs={{0,2},{2,4},{4,6},{6,8},{8,10},{10,12},{12,14},{14,0},{1,3},{3,5},... | collective-permute-start | bytes 196616 | tf_op jit(solution)/shard_map/ppermute | solution.py:194
  10.6 8.9 %collective-permute-start.7 = (bf16[32,1024]{1,0:T(8,128)(2,1)S(1)}, bf16[32,1024]{1,0:T(8,128)(2,1)S(1)}, u32[]{:S(2)}, u32[]{:S(2)}) collective-permute-start(bf16[32,1024]{1,0:T(8,128)(2,1)S(1)} %get-tuple-element.28), channel_id=1, source_target_pairs={{0,14},{2,0},{4,2},{6,4},{8,6},{10,8},{12,10},{14,12},{1,15},{3,1}... | collective-permute-start | bytes 196616 | tf_op jit(solution)/shard_map/ppermute | solution.py:196
  14.7 1.0 copy-start.3
  15.9 17.3 %collective-permute-start = (bf16[16,72,128]{2,1,0:T(8,128)(2,1)S(1)}, bf16[16,72,128]{2,1,0:T(8,128)(2,1)S(1)}, u32[]{:S(2)}, u32[]{:S(2)}) collective-permute-start(bf16[16,72,128]{2,1,0:T(8,128)(2,1)S(1)} %pack.1.refs_0_), channel_id=1, source_target_pairs={{0,192},{64,0},{128,64},{192,128},{1,193},{65,1},{129,65},{193,129... | collective-permute-start | bytes 884744 | tf_op jit(solution)/shard_map/ppermute | solution.py:187
  18.4 14.8 %collective-permute-start.1 = (bf16[16,72,128]{2,1,0:T(8,128)(2,1)S(1)}, bf16[16,72,128]{2,1,0:T(8,128)(2,1)S(1)}, u32[]{:S(2)}, u32[]{:S(2)}) collective-permute-start(bf16[16,72,128]{2,1,0:T(8,128)(2,1)S(1)} %pack.1.refs_0_), channel_id=1, source_target_pairs={{0,128},{64,192},{128,0},{192,64},{1,129},{65,193},{129,1},{193,65... | collective-permute-start | bytes 884744 | tf_op jit(solution)/shard_map/ppermute | solution.py:187
  18.9 16.2 %collective-permute-start.2 = (bf16[16,72,128]{2,1,0:T(8,128)(2,1)S(1)}, bf16[16,72,128]{2,1,0:T(8,128)(2,1)S(1)}, u32[]{:S(2)}, u32[]{:S(2)}) collective-permute-start(bf16[16,72,128]{2,1,0:T(8,128)(2,1)S(1)} %pack.1.refs_0_), channel_id=1, source_target_pairs={{0,64},{64,128},{128,192},{192,0},{1,65},{65,129},{129,193},{193,1... | collective-permute-start | bytes 884744 | tf_op jit(solution)/shard_map/ppermute | solution.py:187
  19.5 4.3 %collective-permute-start.4 = (bf16[32,1024]{1,0:T(8,128)(2,1)S(1)}, bf16[32,1024]{1,0:T(8,128)(2,1)S(1)}, u32[]{:S(2)}, u32[]{:S(2)}) collective-permute-start(bf16[32,1024]{1,0:T(8,128)(2,1)S(1)} %collective-permute-done.3), channel_id=1, source_target_pairs={{0,2},{2,4},{4,6},{6,8},{8,10},{10,12},{12,14},{14,0},{1,3},{3,5},... | collective-permute-start | bytes 196616 | tf_op jit(solution)/shard_map/ppermute | solution.py:194
  19.5 4.3 %collective-permute-start.8 = (bf16[32,1024]{1,0:T(8,128)(2,1)S(1)}, bf16[32,1024]{1,0:T(8,128)(2,1)S(1)}, u32[]{:S(2)}, u32[]{:S(2)}) collective-permute-start(bf16[32,1024]{1,0:T(8,128)(2,1)S(1)} %collective-permute-done.7), channel_id=1, source_target_pairs={{0,14},{2,0},{4,2},{6,4},{8,6},{10,8},{12,10},{14,12},{1,15},{3,1}... | collective-permute-start | bytes 196616 | tf_op jit(solution)/shard_map/ppermute | solution.py:196
  23.9 4.6 %collective-permute-start.5 = (bf16[32,1024]{1,0:T(8,128)(2,1)S(1)}, bf16[32,1024]{1,0:T(8,128)(2,1)S(1)}, u32[]{:S(2)}, u32[]{:S(2)}) collective-permute-start(bf16[32,1024]{1,0:T(8,128)(2,1)S(1)} %collective-permute-done.4), channel_id=1, source_target_pairs={{0,2},{2,4},{4,6},{6,8},{8,10},{10,12},{12,14},{14,0},{1,3},{3,5},... | collective-permute-start | bytes 196616 | tf_op jit(solution)/shard_map/ppermute | solution.py:194
  23.9 9.2 %collective-permute-start.9 = (bf16[32,1024]{1,0:T(8,128)(2,1)S(1)}, bf16[32,1024]{1,0:T(8,128)(2,1)S(1)}, u32[]{:S(2)}, u32[]{:S(2)}) collective-permute-start(bf16[32,1024]{1,0:T(8,128)(2,1)S(1)} %collective-permute-done.8), channel_id=1, source_target_pairs={{0,14},{2,0},{4,2},{6,4},{8,6},{10,8},{12,10},{14,12},{1,15},{3,1}... | collective-permute-start | bytes 196616 | tf_op jit(solution)/shard_map/ppermute | solution.py:196
  28.5 4.6 %collective-permute-start.6 = (bf16[32,1024]{1,0:T(8,128)(2,1)S(1)}, bf16[32,1024]{1,0:T(8,128)(2,1)S(1)}, u32[]{:S(2)}, u32[]{:S(2)}) collective-permute-start(bf16[32,1024]{1,0:T(8,128)(2,1)S(1)} %collective-permute-done.5), channel_id=1, source_target_pairs={{0,2},{2,4},{4,6},{6,8},{8,10},{10,12},{12,14},{14,0},{1,3},{3,5},... | collective-permute-start | bytes 196616 | tf_op jit(solution)/shard_map/ppermute | solution.py:194
  33.2 2.9 %copy-start.6 = (bf16[256,1024]{1,0:T(8,128)(2,1)}, bf16[256,1024]{1,0:T(8,128)(2,1)S(1)}, u32[]{:S(2)}) copy-start(bf16[256,1024]{1,0:T(8,128)(2,1)S(1)} %constant_dynamic-update-slice_fusion) | copy-start | bytes 1572868
  36.1 43.0 %copy-start.1 = (bf16[128,8192]{1,0:T(8,128)(2,1)S(1)}, bf16[128,8192]{1,0:T(8,128)(2,1)}, u32[]{:S(2)}) copy-start(bf16[128,8192]{1,0:T(8,128)(2,1)} %tok_ref.3) | copy-start | bytes 6291460
  36.1 43.0 %copy-start.2 = (bf16[128,1024]{1,0:T(8,128)(2,1)S(1)}, bf16[128,1024]{1,0:T(8,128)(2,1)}, u32[]{:S(2)}) copy-start(bf16[128,1024]{1,0:T(8,128)(2,1)} %cot_ref.3) | copy-start | bytes 786436
  83.7 1.0 copy-start
  84.7 37.6 %all-to-all-start.1 = ((bf16[64,72,128]{2,1,0:T(8,128)(2,1)}), bf16[64,72,128]{2,1,0:T(8,128)(2,1)S(1)}, u32[]{:S(2)}, u32[]{:S(2)}) async-start(bf16[64,72,128]{2,1,0:T(8,128)(2,1)} %get-tuple-element.16), calls=%async_computation.1 | async-start | bytes 2359296 | tf_op jit(solution)/shard_map/all_to_all | solution.py:254
  123.5 29.7 %collective-permute-start.10 = (bf16[16,72,128]{2,1,0:T(8,128)(2,1)S(1)}, bf16[16,72,128]{2,1,0:T(8,128)(2,1)S(1)}, u32[]{:S(2)}, u32[]{:S(2)}) collective-permute-start(bf16[16,72,128]{2,1,0:T(8,128)(2,1)S(1)} %get-tuple-element.24), channel_id=1, source_target_pairs={{0,64},{64,128},{128,192},{192,0},{1,65},{65,129},{129,193},{193,1... | collective-permute-start | bytes 884744 | tf_op jit(solution)/shard_map/ppermute | solution.py:187
  125.3 27.9 %collective-permute-start.11 = (bf16[16,72,128]{2,1,0:T(8,128)(2,1)S(1)}, bf16[16,72,128]{2,1,0:T(8,128)(2,1)S(1)}, u32[]{:S(2)}, u32[]{:S(2)}) collective-permute-start(bf16[16,72,128]{2,1,0:T(8,128)(2,1)S(1)} %get-tuple-element.25), channel_id=1, source_target_pairs={{0,128},{64,192},{128,0},{192,64},{1,129},{65,193},{129,1},{193,65... | collective-permute-start | bytes 884744 | tf_op jit(solution)/shard_map/ppermute | solution.py:187
  136.0 17.3 %collective-permute-start.12 = (bf16[16,72,128]{2,1,0:T(8,128)(2,1)S(1)}, bf16[16,72,128]{2,1,0:T(8,128)(2,1)S(1)}, u32[]{:S(2)}, u32[]{:S(2)}) collective-permute-start(bf16[16,72,128]{2,1,0:T(8,128)(2,1)S(1)} %get-tuple-element.26), channel_id=1, source_target_pairs={{0,192},{64,0},{128,64},{192,128},{1,193},{65,1},{129,65},{193,129... | collective-permute-start | bytes 884744 | tf_op jit(solution)/shard_map/ppermute | solution.py:187
Sparse Core Ops, SparseCore 0:
  36.2 99.7 all-gather.1

commit v7 on v5

--- a/solution.py
+++ b/solution.py
@@ -151,30 +151,91 @@
     lax.fori_loop(0, shards // per, pack, 0)
 
 
-def base_kernel(tok_ref, cot_ref, w_ref, at_ref, up_ref, hid_ref, back_ref, keys_ref, grad_ref, acc_ref):
-    step = pl.program_id(0)
-
-    @pl.when(step == 0)
-    def _():
-        acc_ref[...] = adapter_scale * lax.dot_general(
-            hid_ref[...], up_ref[...], TN, preferred_element_type=f32
-        )
-
-    weight = w_ref[...]
-    acc_ref[...] += jnp.dot(tok_ref[...], weight, preferred_element_type=f32)
+def columns(place_ref, y, k, parity, counts):
+    deep, cores = counts
+    z = lax.rem(place_ref[0] - k + deep, deep)
+    start = ((y * deep + z) * cores + parity) * TILE_ROWS
+    return pl.ds(pl.multiple_of(start, TILE_ROWS), TILE_ROWS)
+
+
+def products(tok_ref, cot_ref, weight, adapter_ref, back, places):
+    tok = jnp.concatenate([tok_ref[:, at] for at in places], axis=1)
+    down = jnp.concatenate([adapter_ref[:, at] for at in places], axis=1)
+    key = jnp.dot(tok, weight, preferred_element_type=f32)
     grad = lax.dot_general(cot_ref[...], weight, NT, preferred_element_type=f32)
-    grad += adapter_scale * lax.dot_general(
-        back_ref[...], at_ref[...], TN, preferred_element_type=f32
-    )
-    grad_ref[...] = grad.astype(grad_ref.dtype)
-
-    @pl.when(step == pl.num_programs(0) - 1)
-    def _():
-        keys_ref[...] = acc_ref[...].astype(keys_ref.dtype)
+    grad += adapter_scale * lax.dot_general(back, down, TN, preferred_element_type=f32)
+    return key, grad.astype(bf16)
+
+
+def fetch(source_ref, w_ref, sems):
+    wide, groups = w_ref.shape[:2]
+    copies = [
+        [pltpu.make_async_copy(source_ref.at[y, x], w_ref.at[y, x], sems.at[y, x]) for x in range(groups)]
+        for y in range(wide)
+    ]
+    for row in copies:
+        for copy in row:
+            copy.start()
+    return copies
+
+
+def block(copies, w_ref, y):
+    groups, deep = w_ref.shape[1:3]
+    for copy in copies[y]:
+        copy.wait()
+    return jnp.concatenate([w_ref[y, x, k] for k in range(deep) for x in range(groups)], axis=0)
+
+
+def own_kernel(place_ref, tok_ref, cot_ref, half_ref, adapter_ref, key_ref, grad_ref, w_ref, sems):
+    wide, _, deep, _, key_columns = half_ref.shape
+    rows, depth = tok_ref.shape
+    width = depth + key_columns
+    span = deep * TILE_ROWS
+    copies = fetch(half_ref, w_ref, sems)
+    hidden = adapter_ref[:, width : width + rows]
+    back = adapter_ref[:, width + rows :]
+    up = adapter_ref[:, depth:width]
+    key_ref[...] = adapter_scale * lax.dot_general(hidden, up, TN, preferred_element_type=f32)
+    for y in range(wide):
+        weight = block(copies, w_ref, y)
+        places = [columns(place_ref, y, k, place_ref[1], (deep, 2)) for k in range(deep)]
+        key, grad = products(tok_ref, cot_ref, weight, adapter_ref, back, places)
+        key_ref[...] += key
+        grad_ref[:, y * span : (y + 1) * span] = grad
+
+
+def other_kernel(
+    place_ref, tok_ref, cot_ref, half_ref, adapter_ref, key_ref, own_ref, keys_ref, grad_ref, acc_ref, w_ref, sems
+):
+    wide, _, deep, _, key_columns = half_ref.shape
+    rows, depth = tok_ref.shape
+    copies = fetch(half_ref, w_ref, sems)
+    back = adapter_ref[:, depth + key_columns + rows :]
+    acc_ref[...] = key_ref[...]
+    for y in range(wide):
+        weight = block(copies, w_ref, y)
+        places = [columns(place_ref, y, k, 1 - place_ref[1], (deep, 2)) for k in range(deep)]
+        key, grad = products(tok_ref, cot_ref, weight, adapter_ref, back, places)
+        acc_ref[...] += key
+        for k in range(deep):
+            at = (y * deep + k) * TILE_ROWS
+            grad_ref[:, columns(place_ref, y, k, place_ref[1], (deep, 2))] = own_ref[:, at : at + TILE_ROWS]
+            grad_ref[:, places[k]] = grad[:, k * TILE_ROWS : (k + 1) * TILE_ROWS]
+    keys_ref[...] = acc_ref[...].astype(keys_ref.dtype)
 
 
 def shift(x, by, groups):
     return lax.ppermute(x, "grp", [(i, (i + by) % groups) for i in range(groups)])
+
+
+def ring(x, axis, size):
+    up = [x]
+    down = [x]
+    for _ in range(size // 2):
+        up.append(lax.ppermute(up[-1], axis, [(i, (i + 1) % size) for i in range(size)]))
+    for _ in range(size // 2 - 1):
+        down.append(lax.ppermute(down[-1], axis, [(i, (i - 1) % size) for i in range(size)]))
+    return jnp.concatenate(up + down[:0:-1], axis=0)
 
 
 def whole(memory=pltpu.VMEM):
@@ -190,9 +251,12 @@
     packed_rows = row_count * rank // LANES
     width = depth + key_columns
     group = lax.axis_index("grp").reshape(1).astype(jnp.int32)
+    place = jnp.stack([lax.axis_index("z"), lax.axis_index("core")]).astype(jnp.int32)
     jobs = tile_job.reshape(-1)
 
-    weight = lax.all_gather(frozen_weight, SEQ, axis=0, tiled=True)
+    quarter = TILE_ROWS // groups
+    mine = lax.dynamic_slice_in_dim(frozen_weight, lax.axis_index("grp") * quarter, quarter, 0)
+    column = ring(mine, "z", lax.axis_size("z"))
 
     own = pl.pallas_call(
         pack_kernel,
@@ -213,6 +277,8 @@
         compiler_params=params(),
         name="pick",
     )(group, jobs, job_slot, *every)
+    outgoing, column = lax.optimization_barrier((outgoing, column))
+    half = lax.all_gather(column, ("y", "grp"), axis=0, tiled=True)
     arrived = lax.all_to_all(outgoing, SEQ, split_axis=0, concat_axis=0, tiled=True)
     terms, adapter = pl.pallas_call(
         tile_kernel,
@@ -227,6 +293,8 @@
         name="tile",
     )(arrived, tokens, cotangent)
     incoming = lax.all_to_all(terms, SEQ, split_axis=0, concat_axis=0, tiled=True)
+    incoming, half = lax.optimization_barrier((incoming, half))
+    other = lax.ppermute(half, "core", [(0, 1), (1, 0)])
     sums = pl.pallas_call(
         sum_kernel,
         out_shape=(jax.ShapeDtypeStruct((slot_count, packed_rows, LANES), f32),)
@@ -237,8 +305,29 @@
         compiler_params=params(),
         name="sum",
     )(group, jobs, job_slot, incoming)
-    last, weight = lax.optimization_barrier((sums[-1], weight))
-    sums = tuple(sums[:-1]) + (last,)
+    kept, half = lax.optimization_barrier((sums[0], half))
+    wide, deep = lax.axis_size("y"), lax.axis_size("z")
+    blocks = (wide, groups, deep, quarter, key_columns)
+    cost = pl.CostEstimate(
+        flops=2 * rows * depth * key_columns,
+        bytes_accessed=depth * key_columns + 4 * rows * width,
+        transcendentals=0,
+    )
+    key_part, own_part = pl.pallas_call(
+        own_kernel,
+        out_shape=(
+            jax.ShapeDtypeStruct((rows, key_columns), f32),
+            jax.ShapeDtypeStruct((rows, depth // 2), bf16),
+        ),
+        in_specs=[smem, whole(), whole(), whole(pltpu.HBM), whole()],
+        out_specs=(whole(),) * 2,
+        scratch_shapes=[pltpu.VMEM(blocks, bf16), pltpu.SemaphoreType.DMA((wide, groups))],
+        compiler_params=params(50),
+        cost_estimate=cost,
+        name="own",
+    )(place, tokens, cotangent, half.reshape(blocks), adapter)
+    last, other, key_part = lax.optimization_barrier((sums[-1], other, key_part))
+    sums = (kept,) + tuple(sums[1:-1]) + (last,)
     owned = (sums[0],) + tuple(shift(sums[k], k, groups) for k in range(1, groups))
     grads = pl.pallas_call(
         unpack_kernel,
@@ -249,37 +338,23 @@
         name="unpack",
     )(*owned)
 
-    block = 1024
-    steps = depth // block
     keys, token_gradient = pl.pallas_call(
-        base_kernel,
-        grid=(steps,),
+        other_kernel,
         out_shape=(
             jax.ShapeDtypeStruct((rows, key_columns), bf16),
             jax.ShapeDtypeStruct((rows, depth), bf16),
         ),
-        in_specs=[
-            pl.BlockSpec((rows, block), lambda i: (0, i)),
-            pl.BlockSpec((rows, key_columns), lambda i: (0, 0)),
-            pl.BlockSpec((block, key_columns), lambda i: (i, 0)),
-            pl.BlockSpec((rank, block), lambda i: (0, i)),
-            pl.BlockSpec((rank, key_columns), lambda i: (0, depth // key_columns)),
-            pl.BlockSpec((rank, rows), lambda i: (0, width // rows)),
-            pl.BlockSpec((rank, rows), lambda i: (0, width // rows + 1)),
+        in_specs=[smem, whole(), whole(), whole(pltpu.HBM), whole(), whole(), whole()],
+        out_specs=(whole(),) * 2,
+        scratch_shapes=[
+            pltpu.VMEM((rows, key_columns), f32),
+            pltpu.VMEM(blocks, bf16),
+            pltpu.SemaphoreType.DMA((wide, groups)),
         ],
-        out_specs=(
-            pl.BlockSpec((rows, key_columns), lambda i: (0, 0)),
-            pl.BlockSpec((rows, block), lambda i: (0, i)),
-        ),
-        scratch_shapes=[pltpu.VMEM((rows, key_columns), f32)],
-        compiler_params=params(56),
-        cost_estimate=pl.CostEstimate(
-            flops=4 * rows * depth * key_columns,
-            bytes_accessed=2 * depth * key_columns + 4 * rows * width,
-            transcendentals=0,
-        ),
-        name="base",
-    )(tokens, cotangent, weight, adapter, adapter, adapter, adapter)
+        compiler_params=params(50),
+        cost_estimate=cost,
+        name="other",
+    )(place, tokens, cotangent, other.reshape(blocks), adapter, key_part, own_part)
     return keys, token_gradient, jnp.swapaxes(grads, 1, 2)
 
 

time: 171 us -> 168 us (0.982)
  blocking collectives: 96.8 us -> 80.4 us
  starting transfers between devices: 7.91 us -> 22.7 us
  waiting for transfers between devices: 27.6 us -> 23.6 us
  Pallas kernels: 21.5 us -> 24.9 us
    ppermute x6, waiting for transfers between devices: 15.6 us -> 1.98 us  [shift(): lax.ppermute(x, 'grp', [(i, (i + by) % groups) for i in range(groups)])]
    all_to_all x1, blocking collectives: 50.9 us -> 37.5 us  [on_device(): lax.all_to_all(terms, SEQ, split_axis=0, concat_axis=0, tiled=True)]
    ppermute x0 -> x8, starting transfers between devices: none -> 12.9 us  [the longest x3 9.67 us: ring(): lax.ppermute(down[-1], axis, [(i, (i - 1) % size) for i in range(size)])]
    ppermute x0 -> x8, waiting for transfers between devices: none -> 7.92 us  [the longest x4 7.89 us: ring(): lax.ppermute(up[-1], axis, [(i, (i + 1) % size) for i in range(size)])]
    pallas_call x1 -> x2, Pallas kernels: 14.5 us -> 17.8 us  [the longest x1 9.73 us: on_device(): pl.pallas_call(other_kernel, out_shape=(jax.ShapeDtypeStruct((rows, key_c...]
    all_to_all x1, blocking collectives: 45.9 us -> 43 us  [on_device(): lax.all_to_all(outgoing, SEQ, split_axis=0, concat_axis=0, tiled=True)]
    all_gather x1, waiting for transfers between devices: 11.3 us -> 13.7 us  [on_device(): half = lax.all_gather(column, ('y', 'grp'), axis=0, tiled=True)]
    ppermute x6, starting transfers between devices: 7.87 us -> 9.76 us  [shift(): lax.ppermute(x, 'grp', [(i, (i + by) % groups) for i in range(groups)])]
  transfers between devices with their start and end apart: 7 -> 15, of which waited for: 4 -> 5; matrix products, arithmetic and copies ran while one was open for 0% -> 0% of each run, Pallas kernels for 12% -> 14%
where the time goes in v7:
time: 168 us
  blocking collectives  80.4 us (48%)
  Pallas kernels  24.9 us (15%)
  waiting for transfers between devices  23.6 us (14%)
  starting transfers between devices  22.7 us (14%)
  between operations  14.2 us (8%)
  local copies, waits for them, and re-layouts  1.97 us (1%)
    all_to_all x1, blocking collectives, on_device(): lax.all_to_all(outgoing, SEQ, split_axis=0, concat_axis=0, tiled=True)  43 us
    all_to_all x1, blocking collectives, on_device(): lax.all_to_all(terms, SEQ, split_axis=0, concat_axis=0, tiled=True)  37.5 us
    all_gather x1, waiting for transfers between devices, on_device(): half = lax.all_gather(column, ('y', 'grp'), axis=0, tiled=True)  13.7 us
    ppermute x6, starting transfers between devices, shift(): lax.ppermute(x, 'grp', [(i, (i + by) % groups) for i in range(groups)])  9.76 us
    pallas_call x1, Pallas kernels, on_device(): pl.pallas_call(other_kernel, out_shape=(jax.ShapeDtypeStruct((rows, key_c...  9.73 us
    ppermute x3, starting transfers between devices, ring(): lax.ppermute(down[-1], axis, [(i, (i - 1) % size) for i in range(size)])  9.67 us
    pallas_call x1, Pallas kernels, on_device(): pl.pallas_call(own_kernel, out_shape=(jax.ShapeDtypeStruct((rows, key_col...  8.08 us
    ppermute x4, waiting for transfers between devices, ring(): lax.ppermute(up[-1], axis, [(i, (i + 1) % size) for i in range(size)])  7.89 us
  transfers between devices with their start and end apart: 15, of which 5 were waited for; matrix products, arithmetic and copies ran while one was open for 0% of the time, Pallas kernels for 14%

profile of v7, /device:TPU:1, one launch (start us, length us, event | category | flops | bytes accessed | tf_op | source)
XLA Modules:
  0.0 167.9 jit_solution(312748137374341801)
XLA Ops:
  7.2 0.9 constant_dynamic-update-slice_fusion.7
  8.1 2.5 %collective-permute-start.3 = (bf16[32,1024]{1,0:T(8,128)(2,1)S(1)}, bf16[32,1024]{1,0:T(8,128)(2,1)S(1)}, u32[]{:S(2)}, u32[]{:S(2)}) collective-permute-start(bf16[32,1024]{1,0:T(8,128)(2,1)S(1)} %get-tuple-element.42), channel_id=1, source_target_pairs={{0,2},{2,4},{4,6},{6,8},{8,10},{10,12},{12,14},{14,0},{1,3},{3,5},... | collective-permute-start | bytes 196616 | tf_op jit(solution)/shard_map/ppermute | solution.py:235
  10.6 4.0 %collective-permute-start.7 = (bf16[32,1024]{1,0:T(8,128)(2,1)S(1)}, bf16[32,1024]{1,0:T(8,128)(2,1)S(1)}, u32[]{:S(2)}, u32[]{:S(2)}) collective-permute-start(bf16[32,1024]{1,0:T(8,128)(2,1)S(1)} %get-tuple-element.42), channel_id=1, source_target_pairs={{0,14},{2,0},{4,2},{6,4},{8,6},{10,8},{12,10},{14,12},{1,15},{3,1}... | collective-permute-start | bytes 196616 | tf_op jit(solution)/shard_map/ppermute | solution.py:237
  14.7 1.0 copy-done.3
  15.9 2.6 %collective-permute-start = (bf16[16,72,128]{2,1,0:T(8,128)(2,1)S(1)}, bf16[16,72,128]{2,1,0:T(8,128)(2,1)S(1)}, u32[]{:S(2)}, u32[]{:S(2)}) collective-permute-start(bf16[16,72,128]{2,1,0:T(8,128)(2,1)S(1)} %pack.1.refs_0_), channel_id=1, source_target_pairs={{0,192},{64,0},{128,64},{192,128},{1,193},{65,1},{129,65},{193,129... | collective-permute-start | bytes 884744 | tf_op jit(solution)/shard_map/ppermute | solution.py:228
  19.5 2.7 %collective-permute-start.8 = (bf16[32,1024]{1,0:T(8,128)(2,1)S(1)}, bf16[32,1024]{1,0:T(8,128)(2,1)S(1)}, u32[]{:S(2)}, u32[]{:S(2)}) collective-permute-start(bf16[32,1024]{1,0:T(8,128)(2,1)S(1)} %collective-permute-done.7), channel_id=1, source_target_pairs={{0,14},{2,0},{4,2},{6,4},{8,6},{10,8},{12,10},{14,12},{1,15},{3,1}... | collective-permute-start | bytes 196616 | tf_op jit(solution)/shard_map/ppermute | solution.py:237
  22.2 1.6 collective-permute-done.4
  23.9 3.0 %collective-permute-start.9 = (bf16[32,1024]{1,0:T(8,128)(2,1)S(1)}, bf16[32,1024]{1,0:T(8,128)(2,1)S(1)}, u32[]{:S(2)}, u32[]{:S(2)}) collective-permute-start(bf16[32,1024]{1,0:T(8,128)(2,1)S(1)} %collective-permute-done.8), channel_id=1, source_target_pairs={{0,14},{2,0},{4,2},{6,4},{8,6},{10,8},{12,10},{14,12},{1,15},{3,1}... | collective-permute-start | bytes 196616 | tf_op jit(solution)/shard_map/ppermute | solution.py:237
  26.8 1.6 collective-permute-done.5
  28.5 4.6 %collective-permute-done.6 = bf16[32,1024]{1,0:T(8,128)(2,1)S(1)} collective-permute-done((bf16[32,1024]{1,0:T(8,128)(2,1)S(1)}, bf16[32,1024]{1,0:T(8,128)(2,1)S(1)}, u32[]{:S(2)}, u32[]{:S(2)}) %collective-permute-start.6) | collective-permute-done | bytes 65568 | tf_op jit(solution)/shard_map/ppermute | solution.py:235
  33.2 2.0 %collective-permute-done.2.refs_3_ = bf16[16,72,128]{2,1,0:T(8,128)(2,1)S(1)} collective-permute-done((bf16[16,72,128]{2,1,0:T(8,128)(2,1)S(1)}, bf16[16,72,128]{2,1,0:T(8,128)(2,1)S(1)}, u32[]{:S(2)}, u32[]{:S(2)}) %collective-permute-start.2) | collective-permute-done | bytes 294944 | tf_op jit(solution)/shard_map/ppermute | solution.py:228
  35.2 0.9 pick.1
  36.1 43.0 %all_to_all.10.x_ref = bf16[64,72,128]{2,1,0:T(8,128)(2,1)S(1)} all-to-all(bf16[64,72,128]{2,1,0:T(8,128)(2,1)S(1)} %pick.1), channel_id=1, replica_groups=mesh['grp'=4,'y'=4,'z'=8,'core'=2] {'y','z','core'}, dimensions={0} | all-to-all | bytes 2359296 | tf_op jit(solution)/shard_map/all_to_all | solution.py:282
  79.1 3.6 %tile.1 = (bf16[64,72,128]{2,1,0:T(8,128)(2,1)S(1)}, bf16[64,9472]{1,0:T(8,128)(2,1)S(1)}) custom-call(bf16[64,72,128]{2,1,0:T(8,128)(2,1)S(1)} %all_to_all.10.x_ref, bf16[128,8192]{1,0:T(8,128)(2,1)S(1)} %copy-done, bf16[128,1024]{1,0:T(8,128)(2,1)S(1)} %copy-done.1), custom_call_target="tpu_custom_call" | custom-call | tf_op jit(solution)/shard_map/tile/pallas_call | solution.py:283
  82.7 37.5 %all_to_all.11.x_ref = bf16[64,72,128]{2,1,0:T(8,128)(2,1)S(1)} all-to-all(bf16[64,72,128]{2,1,0:T(8,128)(2,1)S(1)} %get-tuple-element.23), channel_id=1, replica_groups=mesh['grp'=4,'y'=4,'z'=8,'core'=2] {'y','z','core'}, dimensions={0} | all-to-all | bytes 2359296 | tf_op jit(solution)/shard_map/all_to_all | solution.py:295
  120.1 13.7 %all-gather.2.cloned.1.call-done = bf16[4096,1024]{1,0:T(8,128)(2,1)} async-done(((bf16[256,1024]{1,0:T(8,128)(2,1)}), bf16[4096,1024]{1,0:T(8,128)(2,1)}) %all-gather.2.cloned.1.call-update) | async-done | bytes 8388624 | tf_op jit(solution)/shard_map/all_gather | solution.py:281
  133.8 0.7 collective-permute-start.10
  134.6 1.3 sum.1
  135.9 1.2 collective-permute-start.11
  137.1 2.4 %collective-permute-start.12 = (bf16[16,72,128]{2,1,0:T(8,128)(2,1)S(1)}, bf16[16,72,128]{2,1,0:T(8,128)(2,1)S(1)}, u32[]{:S(2)}, u32[]{:S(2)}) collective-permute-start(bf16[16,72,128]{2,1,0:T(8,128)(2,1)S(1)} %get-tuple-element.39), channel_id=1, source_target_pairs={{0,128},{64,192},{128,0},{192,64},{1,129},{65,193},{129,1},{193,65... | collective-permute-start | bytes 884744 | tf_op jit(solution)/shard_map/ppermute | solution.py:228
  139.6 8.1 %own.1 = (f32[128,1024]{1,0:T(8,128)S(1)}, bf16[128,4096]{1,0:T(8,128)(2,1)S(1)}) custom-call(s32[2]{0:T(128)S(1)} %pad_add_fusion.place_ref, bf16[128,8192]{1,0:T(8,128)(2,1)} %tok_ref.5, bf16[128,1024]{1,0:T(8,128)(2,1)S(1)} %copy-done.2, bf16[4,4,8,32,1024]{4,3,2,1,0:T(8,128)(2,1)} %bitcast.11, bf16[64,9472]{1,0:T(8,128)(2,1)S(1)} %get-tuple-element.30.adapter_ref), custom_call_target="tpu_custom_call" | custom-call | flops 2147483648 | bytes 13107200 | tf_op jit(solution)/shard_map/own/pallas_call | solution.py:316
  147.7 2.4 %collective-permute-start.13 = (bf16[16,72,128]{2,1,0:T(8,128)(2,1)S(1)}, bf16[16,72,128]{2,1,0:T(8,128)(2,1)S(1)}, u32[]{:S(2)}, u32[]{:S(2)}) collective-permute-start(bf16[16,72,128]{2,1,0:T(8,128)(2,1)S(1)} %get-tuple-element.40), channel_id=1, source_target_pairs={{0,192},{64,0},{128,64},{192,128},{1,193},{65,1},{129,65},{193,129... | collective-permute-start | bytes 884744 | tf_op jit(solution)/shard_map/ppermute | solution.py:228
  150.1 9.7 %other.1 = (bf16[128,1024]{1,0:T(8,128)(2,1)}, bf16[128,8192]{1,0:T(8,128)(2,1)}) custom-call(s32[2]{0:T(128)S(1)} %pad_add_fusion.place_ref, bf16[128,8192]{1,0:T(8,128)(2,1)} %tok_ref.5, bf16[128,1024]{1,0:T(8,128)(2,1)S(1)} %copy-done.2, bf16[4,4,8,32,1024]{4,3,2,1,0:T(8,128)(2,1)} %bitcast.6.half_ref, ...), custom_call_target="tpu_custom_call" | custom-call | flops 2147483648 | bytes 13107200 | tf_op jit(solution)/shard_map/other/pallas_call | solution.py:341
  159.9 1.2 unpack.1
  (39 shorter events, 1.5 us)
Async XLA Ops:
  7.2 28.0 %copy-start.4 = (s32[256,1]{0,1:T(1,128)S(1)}, s32[256,1]{0,1:T(1,128)}, u32[]{:S(2)}) copy-start(s32[256,1]{0,1:T(1,128)} %param.10) | copy-start | bytes 3076
  7.2 28.0 %copy-start.5 = (s32[64]{0:T(128)S(1)}, s32[64]{0:T(128)}, u32[]{:S(2)}) copy-start(s32[64]{0:T(128)} %slot_ref.3) | copy-start | bytes 772
  7.2 126.7 %all-gather.2.cloned.1.call-start = ((), (), s32[]{:S(2)}) async-start(), calls=%async_computation.2 | async-start | bytes 8912896 | tf_op jit(solution)/shard_map/all_gather | solution.py:281
  8.1 11.4 %collective-permute-start.3 = (bf16[32,1024]{1,0:T(8,128)(2,1)S(1)}, bf16[32,1024]{1,0:T(8,128)(2,1)S(1)}, u32[]{:S(2)}, u32[]{:S(2)}) collective-permute-start(bf16[32,1024]{1,0:T(8,128)(2,1)S(1)} %get-tuple-element.42), channel_id=1, source_target_pairs={{0,2},{2,4},{4,6},{6,8},{8,10},{10,12},{12,14},{14,0},{1,3},{3,5},... | collective-permute-start | bytes 196616 | tf_op jit(solution)/shard_map/ppermute | solution.py:235
  10.6 8.9 %collective-permute-start.7 = (bf16[32,1024]{1,0:T(8,128)(2,1)S(1)}, bf16[32,1024]{1,0:T(8,128)(2,1)S(1)}, u32[]{:S(2)}, u32[]{:S(2)}) collective-permute-start(bf16[32,1024]{1,0:T(8,128)(2,1)S(1)} %get-tuple-element.42), channel_id=1, source_target_pairs={{0,14},{2,0},{4,2},{6,4},{8,6},{10,8},{12,10},{14,12},{1,15},{3,1}... | collective-permute-start | bytes 196616 | tf_op jit(solution)/shard_map/ppermute | solution.py:237
  14.7 1.0 copy-start.3
  15.9 17.3 %collective-permute-start = (bf16[16,72,128]{2,1,0:T(8,128)(2,1)S(1)}, bf16[16,72,128]{2,1,0:T(8,128)(2,1)S(1)}, u32[]{:S(2)}, u32[]{:S(2)}) collective-permute-start(bf16[16,72,128]{2,1,0:T(8,128)(2,1)S(1)} %pack.1.refs_0_), channel_id=1, source_target_pairs={{0,192},{64,0},{128,64},{192,128},{1,193},{65,1},{129,65},{193,129... | collective-permute-start | bytes 884744 | tf_op jit(solution)/shard_map/ppermute | solution.py:228
  18.4 14.8 %collective-permute-start.1 = (bf16[16,72,128]{2,1,0:T(8,128)(2,1)S(1)}, bf16[16,72,128]{2,1,0:T(8,128)(2,1)S(1)}, u32[]{:S(2)}, u32[]{:S(2)}) collective-permute-start(bf16[16,72,128]{2,1,0:T(8,128)(2,1)S(1)} %pack.1.refs_0_), channel_id=1, source_target_pairs={{0,128},{64,192},{128,0},{192,64},{1,129},{65,193},{129,1},{193,65... | collective-permute-start | bytes 884744 | tf_op jit(solution)/shard_map/ppermute | solution.py:228
  18.9 16.2 %collective-permute-start.2 = (bf16[16,72,128]{2,1,0:T(8,128)(2,1)S(1)}, bf16[16,72,128]{2,1,0:T(8,128)(2,1)S(1)}, u32[]{:S(2)}, u32[]{:S(2)}) collective-permute-start(bf16[16,72,128]{2,1,0:T(8,128)(2,1)S(1)} %pack.1.refs_0_), channel_id=1, source_target_pairs={{0,64},{64,128},{128,192},{192,0},{1,65},{65,129},{129,193},{193,1... | collective-permute-start | bytes 884744 | tf_op jit(solution)/shard_map/ppermute | solution.py:228
  19.5 4.3 %collective-permute-start.4 = (bf16[32,1024]{1,0:T(8,128)(2,1)S(1)}, bf16[32,1024]{1,0:T(8,128)(2,1)S(1)}, u32[]{:S(2)}, u32[]{:S(2)}) collective-permute-start(bf16[32,1024]{1,0:T(8,128)(2,1)S(1)} %collective-permute-done.3), channel_id=1, source_target_pairs={{0,2},{2,4},{4,6},{6,8},{8,10},{10,12},{12,14},{14,0},{1,3},{3,5},... | collective-permute-start | bytes 196616 | tf_op jit(solution)/shard_map/ppermute | solution.py:235
  19.5 4.3 %collective-permute-start.8 = (bf16[32,1024]{1,0:T(8,128)(2,1)S(1)}, bf16[32,1024]{1,0:T(8,128)(2,1)S(1)}, u32[]{:S(2)}, u32[]{:S(2)}) collective-permute-start(bf16[32,1024]{1,0:T(8,128)(2,1)S(1)} %collective-permute-done.7), channel_id=1, source_target_pairs={{0,14},{2,0},{4,2},{6,4},{8,6},{10,8},{12,10},{14,12},{1,15},{3,1}... | collective-permute-start | bytes 196616 | tf_op jit(solution)/shard_map/ppermute | solution.py:237
  23.9 4.6 %collective-permute-start.5 = (bf16[32,1024]{1,0:T(8,128)(2,1)S(1)}, bf16[32,1024]{1,0:T(8,128)(2,1)S(1)}, u32[]{:S(2)}, u32[]{:S(2)}) collective-permute-start(bf16[32,1024]{1,0:T(8,128)(2,1)S(1)} %collective-permute-done.4), channel_id=1, source_target_pairs={{0,2},{2,4},{4,6},{6,8},{8,10},{10,12},{12,14},{14,0},{1,3},{3,5},... | collective-permute-start | bytes 196616 | tf_op jit(solution)/shard_map/ppermute | solution.py:235
  23.9 9.2 %collective-permute-start.9 = (bf16[32,1024]{1,0:T(8,128)(2,1)S(1)}, bf16[32,1024]{1,0:T(8,128)(2,1)S(1)}, u32[]{:S(2)}, u32[]{:S(2)}) collective-permute-start(bf16[32,1024]{1,0:T(8,128)(2,1)S(1)} %collective-permute-done.8), channel_id=1, source_target_pairs={{0,14},{2,0},{4,2},{6,4},{8,6},{10,8},{12,10},{14,12},{1,15},{3,1}... | collective-permute-start | bytes 196616 | tf_op jit(solution)/shard_map/ppermute | solution.py:237
  28.5 4.6 %collective-permute-start.6 = (bf16[32,1024]{1,0:T(8,128)(2,1)S(1)}, bf16[32,1024]{1,0:T(8,128)(2,1)S(1)}, u32[]{:S(2)}, u32[]{:S(2)}) collective-permute-start(bf16[32,1024]{1,0:T(8,128)(2,1)S(1)} %collective-permute-done.5), channel_id=1, source_target_pairs={{0,2},{2,4},{4,6},{6,8},{8,10},{10,12},{12,14},{14,0},{1,3},{3,5},... | collective-permute-start | bytes 196616 | tf_op jit(solution)/shard_map/ppermute | solution.py:235
  33.2 2.9 %copy-start.6 = (bf16[256,1024]{1,0:T(8,128)(2,1)}, bf16[256,1024]{1,0:T(8,128)(2,1)S(1)}, u32[]{:S(2)}) copy-start(bf16[256,1024]{1,0:T(8,128)(2,1)S(1)} %constant_dynamic-update-slice_fusion) | copy-start | bytes 1572868
  36.1 43.0 %copy-start = (bf16[128,8192]{1,0:T(8,128)(2,1)S(1)}, bf16[128,8192]{1,0:T(8,128)(2,1)}, u32[]{:S(2)}) copy-start(bf16[128,8192]{1,0:T(8,128)(2,1)} %tok_ref.5) | copy-start | bytes 6291460
  36.1 43.0 %copy-start.1 = (bf16[128,1024]{1,0:T(8,128)(2,1)S(1)}, bf16[128,1024]{1,0:T(8,128)(2,1)}, u32[]{:S(2)}) copy-start(bf16[128,1024]{1,0:T(8,128)(2,1)} %cot_ref.5) | copy-start | bytes 786436
  82.7 56.9 %copy-start.2 = (bf16[128,1024]{1,0:T(8,128)(2,1)S(1)}, bf16[128,1024]{1,0:T(8,128)(2,1)}, u32[]{:S(2)}) copy-start(bf16[128,1024]{1,0:T(8,128)(2,1)} %cot_ref.5) | copy-start | bytes 786436
  133.8 13.8 %collective-permute-start.10 = (bf16[4096,1024]{1,0:T(8,128)(2,1)}, bf16[4096,1024]{1,0:T(8,128)(2,1)}, u32[]{:S(2)}, u32[]{:S(2)}) collective-permute-start(bf16[4096,1024]{1,0:T(8,128)(2,1)} %all-gather.2.cloned.1.call-done), channel_id=1, source_target_pairs={{0,1},{1,0},{2,3},{3,2},{4,5},{5,4},{6,7},{7,6},{8,9},{9,8},{10,11... | collective-permute-start | bytes 25165832 | tf_op jit(solution)/shard_map/ppermute | solution.py:297
  135.9 23.9 %collective-permute-start.11 = (bf16[16,72,128]{2,1,0:T(8,128)(2,1)S(1)}, bf16[16,72,128]{2,1,0:T(8,128)(2,1)S(1)}, u32[]{:S(2)}, u32[]{:S(2)}) collective-permute-start(bf16[16,72,128]{2,1,0:T(8,128)(2,1)S(1)} %get-tuple-element.38), channel_id=1, source_target_pairs={{0,64},{64,128},{128,192},{192,0},{1,65},{65,129},{129,193},{193,1... | collective-permute-start | bytes 884744 | tf_op jit(solution)/shard_map/ppermute | solution.py:228
  137.1 22.7 %collective-permute-start.12 = (bf16[16,72,128]{2,1,0:T(8,128)(2,1)S(1)}, bf16[16,72,128]{2,1,0:T(8,128)(2,1)S(1)}, u32[]{:S(2)}, u32[]{:S(2)}) collective-permute-start(bf16[16,72,128]{2,1,0:T(8,128)(2,1)S(1)} %get-tuple-element.39), channel_id=1, source_target_pairs={{0,128},{64,192},{128,0},{192,64},{1,129},{65,193},{129,1},{193,65... | collective-permute-start | bytes 884744 | tf_op jit(solution)/shard_map/ppermute | solution.py:228
  147.7 12.2 %collective-permute-start.13 = (bf16[16,72,128]{2,1,0:T(8,128)(2,1)S(1)}, bf16[16,72,128]{2,1,0:T(8,128)(2,1)S(1)}, u32[]{:S(2)}, u32[]{:S(2)}) collective-permute-start(bf16[16,72,128]{2,1,0:T(8,128)(2,1)S(1)} %get-tuple-element.40), channel_id=1, source_target_pairs={{0,192},{64,0},{128,64},{192,128},{1,193},{65,1},{129,65},{193,129... | collective-permute-start | bytes 884744 | tf_op jit(solution)/shard_map/ppermute | solution.py:228
Sparse Core Ops, SparseCore 0:
  36.2 97.5 all-gather.1

commit v8 on v5

--- a/solution.py
+++ b/solution.py
@@ -153,6 +153,8 @@
 
 def base_kernel(tok_ref, cot_ref, w_ref, at_ref, up_ref, hid_ref, back_ref, keys_ref, grad_ref, acc_ref):
     step = pl.program_id(0)
+    _, pieces, count, _, _ = w_ref.shape
+    order = [x * 2 + c for c in range(2) for x in range(pieces // 2)]
 
     @pl.when(step == 0)
     def _():
@@ -160,7 +162,7 @@
             hid_ref[...], up_ref[...], TN, preferred_element_type=f32
         )
 
-    weight = w_ref[...]
+    weight = jnp.concatenate([w_ref[0, p, k] for k in range(count) for p in order], axis=0)
     acc_ref[...] += jnp.dot(tok_ref[...], weight, preferred_element_type=f32)
     grad = lax.dot_general(cot_ref[...], weight, NT, preferred_element_type=f32)
     grad += adapter_scale * lax.dot_general(
@@ -192,7 +194,12 @@
     group = lax.axis_index("grp").reshape(1).astype(jnp.int32)
     jobs = tile_job.reshape(-1)
 
-    weight = lax.all_gather(frozen_weight, SEQ, axis=0, tiled=True)
+    quarter = TILE_ROWS // groups
+    mine = lax.dynamic_slice_in_dim(frozen_weight, lax.axis_index("grp") * quarter, quarter, 0)
+    deep = lax.axis_size("z")
+    column = lax.all_to_all(
+        jnp.broadcast_to(mine, (deep,) + mine.shape), "z", split_axis=0, concat_axis=0, tiled=True
+    ).reshape(deep * quarter, -1)
 
     own = pl.pallas_call(
         pack_kernel,
@@ -213,6 +220,8 @@
         compiler_params=params(),
         name="pick",
     )(group, jobs, job_slot, *every)
+    outgoing, column = lax.optimization_barrier((outgoing, column))
+    weight = lax.all_gather(column, ("y", "grp", "core"), axis=0, tiled=True)
     arrived = lax.all_to_all(outgoing, SEQ, split_axis=0, concat_axis=0, tiled=True)
     terms, adapter = pl.pallas_call(
         tile_kernel,
@@ -249,11 +258,12 @@
         name="unpack",
     )(*owned)
 
-    block = 1024
-    steps = depth // block
+    wide, halves = lax.axis_size("y"), 2
+    block = depth // (wide * halves)
+    weight = weight.reshape(wide, shards // (wide * deep) * groups, deep, quarter, key_columns)
     keys, token_gradient = pl.pallas_call(
         base_kernel,
-        grid=(steps,),
+        grid=(wide * halves,),
         out_shape=(
             jax.ShapeDtypeStruct((rows, key_columns), bf16),
             jax.ShapeDtypeStruct((rows, depth), bf16),
@@ -261,7 +271,10 @@
         in_specs=[
             pl.BlockSpec((rows, block), lambda i: (0, i)),
             pl.BlockSpec((rows, key_columns), lambda i: (0, 0)),
-            pl.BlockSpec((block, key_columns), lambda i: (i, 0)),
+            pl.BlockSpec(
+                (1, weight.shape[1], deep // halves, quarter, key_columns),
+                lambda i: (i // halves, 0, i % halves, 0, 0),
+            ),
             pl.BlockSpec((rank, block), lambda i: (0, i)),
             pl.BlockSpec((rank, key_columns), lambda i: (0, depth // key_columns)),
             pl.BlockSpec((rank, rows), lambda i: (0, width // rows)),

time: 171 us -> 162 us (0.947)
  blocking collectives: 96.8 us -> 79.2 us
  starting transfers between devices: 7.91 us -> 16.8 us
    all_to_all x1, blocking collectives: 50.9 us -> 37.3 us  [on_device(): lax.all_to_all(terms, SEQ, split_axis=0, concat_axis=0, tiled=True)]
    all_to_all x0 -> x1, starting transfers between devices: none -> 9.01 us  [on_device(): lax.all_to_all(jnp.broadcast_to(mine, (deep,) + mine.shape), 'z', split_a...]
    all_to_all x1, blocking collectives: 45.9 us -> 41.9 us  [on_device(): lax.all_to_all(outgoing, SEQ, split_axis=0, concat_axis=0, tiled=True)]
  transfers between devices with their start and end apart: 7 -> 8, of which waited for: 4 -> 4; matrix products, arithmetic and copies ran while one was open for 0% -> 0% of each run, Pallas kernels for 12% -> 13%
where the time goes in v8:
time: 162 us
  blocking collectives  79.2 us (49%)
  waiting for transfers between devices  27.3 us (17%)
  Pallas kernels  21.5 us (13%)
  starting transfers between devices  16.8 us (10%)
  between operations  14.2 us (9%)
  local copies, waits for them, and re-layouts  2.61 us (2%)
    all_to_all x1, blocking collectives, on_device(): lax.all_to_all(outgoing, SEQ, split_axis=0, concat_axis=0, tiled=True)  41.9 us
    all_to_all x1, blocking collectives, on_device(): lax.all_to_all(terms, SEQ, split_axis=0, concat_axis=0, tiled=True)  37.3 us
    ppermute x6, waiting for transfers between devices, shift(): lax.ppermute(x, 'grp', [(i, (i + by) % groups) for i in range(groups)])  15.6 us
    pallas_call x1, Pallas kernels, on_device(): pl.pallas_call(base_kernel, grid=(wide * halves,), out_shape=(jax.ShapeDt...  14.5 us
    all_gather x1, waiting for transfers between devices, on_device(): weight = lax.all_gather(column, ('y', 'grp', 'core'), axis=0, tiled=True)  11.7 us
    all_to_all x1, starting transfers between devices, on_device(): lax.all_to_all(jnp.broadcast_to(mine, (deep,) + mine.shape), 'z', split_a...  9.01 us
    ppermute x6, starting transfers between devices, shift(): lax.ppermute(x, 'grp', [(i, (i + by) % groups) for i in range(groups)])  7.71 us
    pallas_call x1, Pallas kernels, on_device(): pl.pallas_call(tile_kernel, out_shape=(jax.ShapeDtypeStruct((shards, pack...  3.58 us
  transfers between devices with their start and end apart: 8, of which 4 were waited for; matrix products, arithmetic and copies ran while one was open for 0% of the time, Pallas kernels for 13%

profile of v8, /device:TPU:1, one launch (start us, length us, event | category | flops | bytes accessed | tf_op | source)
XLA Modules:
  0.0 161.6 jit_solution(8169287239756953452)
XLA Ops:
  7.2 0.9 copy-done
  8.1 0.9 broadcast_in_dim.3
  9.0 9.0 %all-to-all-start = ((bf16[8,32,1024]{2,1,0:T(8,128)(2,1)}), bf16[8,32,1024]{2,1,0:T(8,128)(2,1)S(1)}, u32[]{:S(2)}, u32[]{:S(2)}) async-start(bf16[8,32,1024]{2,1,0:T(8,128)(2,1)} %broadcast_in_dim.3), calls=%async_computation | async-start | bytes 1048576 | tf_op jit(solution)/shard_map/all_to_all | solution.py:200
  18.0 0.0 all-gather.2.cloned.1.call-start
  18.1 0.1 pack.1.refs_0_
  18.2 2.6 %collective-permute-start = (bf16[16,72,128]{2,1,0:T(8,128)(2,1)S(1)}, bf16[16,72,128]{2,1,0:T(8,128)(2,1)S(1)}, u32[]{:S(2)}, u32[]{:S(2)}) collective-permute-start(bf16[16,72,128]{2,1,0:T(8,128)(2,1)S(1)} %pack.1.refs_0_), channel_id=1, source_target_pairs={{0,192},{64,0},{128,64},{192,128},{1,193},{65,1},{129,65},{193,129... | collective-permute-start | bytes 884744 | tf_op jit(solution)/shard_map/ppermute | solution.py:179
  20.8 0.5 collective-permute-start.1
  21.3 0.6 collective-permute-start.2
  21.9 5.0 %collective-permute-done.refs_1_ = bf16[16,72,128]{2,1,0:T(8,128)(2,1)S(1)} collective-permute-done((bf16[16,72,128]{2,1,0:T(8,128)(2,1)S(1)}, bf16[16,72,128]{2,1,0:T(8,128)(2,1)S(1)}, u32[]{:S(2)}, u32[]{:S(2)}) %collective-permute-start) | collective-permute-done | bytes 294944 | tf_op jit(solution)/shard_map/ppermute | solution.py:179
  26.9 2.7 %collective-permute-done.1.refs_2_ = bf16[16,72,128]{2,1,0:T(8,128)(2,1)S(1)} collective-permute-done((bf16[16,72,128]{2,1,0:T(8,128)(2,1)S(1)}, bf16[16,72,128]{2,1,0:T(8,128)(2,1)S(1)}, u32[]{:S(2)}, u32[]{:S(2)}) %collective-permute-start.1) | collective-permute-done | bytes 294944 | tf_op jit(solution)/shard_map/ppermute | solution.py:179
  29.6 7.9 %collective-permute-done.2.refs_3_ = bf16[16,72,128]{2,1,0:T(8,128)(2,1)S(1)} collective-permute-done((bf16[16,72,128]{2,1,0:T(8,128)(2,1)S(1)}, bf16[16,72,128]{2,1,0:T(8,128)(2,1)S(1)}, u32[]{:S(2)}, u32[]{:S(2)}) %collective-permute-start.2) | collective-permute-done | bytes 294944 | tf_op jit(solution)/shard_map/ppermute | solution.py:179
  37.5 0.9 pick.1
  38.4 0.8 copy-done.7
  39.2 0.0 all-gather.2.cloned.1.call-update
  39.3 41.9 %all_to_all.15.x_ref = bf16[64,72,128]{2,1,0:T(8,128)(2,1)S(1)} all-to-all(bf16[64,72,128]{2,1,0:T(8,128)(2,1)S(1)} %pick.1), channel_id=1, replica_groups=mesh['grp'=4,'y'=4,'z'=8,'core'=2] {'y','z','core'}, dimensions={0} | all-to-all | bytes 2359296 | tf_op jit(solution)/shard_map/all_to_all | solution.py:225
  81.1 3.6 %tile.1 = (bf16[64,72,128]{2,1,0:T(8,128)(2,1)S(1)}, bf16[64,9472]{1,0:T(8,128)(2,1)S(1)}) custom-call(bf16[64,72,128]{2,1,0:T(8,128)(2,1)S(1)} %all_to_all.15.x_ref, bf16[128,8192]{1,0:T(8,128)(2,1)S(1)} %copy-done.2, bf16[128,1024]{1,0:T(8,128)(2,1)S(1)} %copy-done.3), custom_call_target="tpu_custom_call" | custom-call | tf_op jit(solution)/shard_map/tile/pallas_call | solution.py:226
  84.7 37.3 %all_to_all.16.x_ref = bf16[64,72,128]{2,1,0:T(8,128)(2,1)S(1)} all-to-all(bf16[64,72,128]{2,1,0:T(8,128)(2,1)S(1)} %get-tuple-element.16), channel_id=1, replica_groups=mesh['grp'=4,'y'=4,'z'=8,'core'=2] {'y','z','core'}, dimensions={0} | all-to-all | bytes 2359296 | tf_op jit(solution)/shard_map/all_to_all | solution.py:238
  122.1 1.3 sum.1
  123.3 0.1 collective-permute-start.3
  123.4 1.5 collective-permute-start.4
  124.9 11.7 %all-gather.2.cloned.1.call-done = bf16[8192,1024]{1,0:T(8,128)(2,1)} async-done(((bf16[256,1024]{1,0:T(8,128)(2,1)}), bf16[8192,1024]{1,0:T(8,128)(2,1)}) %all-gather.2.cloned.1.call-update) | async-done | bytes 16777232 | tf_op jit(solution)/shard_map/all_gather | solution.py:224
  136.6 2.4 %collective-permute-start.5 = (bf16[16,72,128]{2,1,0:T(8,128)(2,1)S(1)}, bf16[16,72,128]{2,1,0:T(8,128)(2,1)S(1)}, u32[]{:S(2)}, u32[]{:S(2)}) collective-permute-start(bf16[16,72,128]{2,1,0:T(8,128)(2,1)S(1)} %get-tuple-element.26), channel_id=1, source_target_pairs={{0,192},{64,0},{128,64},{192,128},{1,193},{65,1},{129,65},{193,129... | collective-permute-start | bytes 884744 | tf_op jit(solution)/shard_map/ppermute | solution.py:179
  139.1 14.5 %base.1 = (bf16[128,1024]{1,0:T(8,128)(2,1)}, bf16[128,8192]{1,0:T(8,128)(2,1)}) custom-call(bf16[128,8192]{1,0:T(8,128)(2,1)} %tok_ref.3, bf16[128,1024]{1,0:T(8,128)(2,1)} %cot_ref.3, bf16[4,8,8,32,1024]{4,3,2,1,0:T(8,128)(2,1)} %bitcast.9, bf16[64,9472]{1,0:T(8,128)(2,1)} %copy-done.1, bf16[64,9472]{1,0:T(8,128)(2,1)} %copy-done.1, ...), custom_call_target="tpu_custom_call" | custom-call | flops 4294967296 | bytes 21495808 | tf_op jit(solution)/shard_map/base/pallas_call | solution.py:264
  153.6 1.2 unpack.1
  (19 shorter events, 0.1 us)
Async XLA Ops:
  7.2 1.0 copy-start
  7.2 10.9 %copy-start.4 = (bf16[16,144,64]{1,2,0:T(8,128)(2,1)S(1)}, bf16[16,144,64]{1,2,0:T(8,128)(2,1)}, u32[]{:S(2)}) copy-start(bf16[16,144,64]{1,2,0:T(8,128)(2,1)} %param.9) | copy-start | bytes 884740
  8.1 29.4 %copy-start.5 = (s32[256,1]{0,1:T(1,128)S(1)}, s32[256,1]{0,1:T(1,128)}, u32[]{:S(2)}) copy-start(s32[256,1]{0,1:T(1,128)} %param.10) | copy-start | bytes 3076
  8.1 29.4 %copy-start.6 = (s32[64]{0:T(128)S(1)}, s32[64]{0:T(128)}, u32[]{:S(2)}) copy-start(s32[64]{0:T(128)} %slot_ref.3) | copy-start | bytes 772
  9.0 29.4 %all-to-all-start = ((bf16[8,32,1024]{2,1,0:T(8,128)(2,1)}), bf16[8,32,1024]{2,1,0:T(8,128)(2,1)S(1)}, u32[]{:S(2)}, u32[]{:S(2)}) async-start(bf16[8,32,1024]{2,1,0:T(8,128)(2,1)} %broadcast_in_dim.3), calls=%async_computation | async-start | bytes 1048576 | tf_op jit(solution)/shard_map/all_to_all | solution.py:200
  18.0 118.6 %all-gather.2.cloned.1.call-start = ((), (), s32[]{:S(2)}) async-start(), calls=%async_computation.3 | async-start | bytes 17301504 | tf_op jit(solution)/shard_map/all_gather | solution.py:224
  18.2 8.7 %collective-permute-start = (bf16[16,72,128]{2,1,0:T(8,128)(2,1)S(1)}, bf16[16,72,128]{2,1,0:T(8,128)(2,1)S(1)}, u32[]{:S(2)}, u32[]{:S(2)}) collective-permute-start(bf16[16,72,128]{2,1,0:T(8,128)(2,1)S(1)} %pack.1.refs_0_), channel_id=1, source_target_pairs={{0,192},{64,0},{128,64},{192,128},{1,193},{65,1},{129,65},{193,129... | collective-permute-start | bytes 884744 | tf_op jit(solution)/shard_map/ppermute | solution.py:179
  20.8 8.8 %collective-permute-start.1 = (bf16[16,72,128]{2,1,0:T(8,128)(2,1)S(1)}, bf16[16,72,128]{2,1,0:T(8,128)(2,1)S(1)}, u32[]{:S(2)}, u32[]{:S(2)}) collective-permute-start(bf16[16,72,128]{2,1,0:T(8,128)(2,1)S(1)} %pack.1.refs_0_), channel_id=1, source_target_pairs={{0,128},{64,192},{128,0},{192,64},{1,129},{65,193},{129,1},{193,65... | collective-permute-start | bytes 884744 | tf_op jit(solution)/shard_map/ppermute | solution.py:179
  21.3 16.2 %collective-permute-start.2 = (bf16[16,72,128]{2,1,0:T(8,128)(2,1)S(1)}, bf16[16,72,128]{2,1,0:T(8,128)(2,1)S(1)}, u32[]{:S(2)}, u32[]{:S(2)}) collective-permute-start(bf16[16,72,128]{2,1,0:T(8,128)(2,1)S(1)} %pack.1.refs_0_), channel_id=1, source_target_pairs={{0,64},{64,128},{128,192},{192,0},{1,65},{65,129},{129,193},{193,1... | collective-permute-start | bytes 884744 | tf_op jit(solution)/shard_map/ppermute | solution.py:179
  38.4 0.8 copy-start.7
  39.2 41.9 %copy-start.2 = (bf16[128,8192]{1,0:T(8,128)(2,1)S(1)}, bf16[128,8192]{1,0:T(8,128)(2,1)}, u32[]{:S(2)}) copy-start(bf16[128,8192]{1,0:T(8,128)(2,1)} %tok_ref.3) | copy-start | bytes 6291460
  39.2 41.9 %copy-start.3 = (bf16[128,1024]{1,0:T(8,128)(2,1)S(1)}, bf16[128,1024]{1,0:T(8,128)(2,1)}, u32[]{:S(2)}) copy-start(bf16[128,1024]{1,0:T(8,128)(2,1)} %cot_ref.3) | copy-start | bytes 786436
  84.7 38.6 %copy-start.1 = (bf16[64,9472]{1,0:T(8,128)(2,1)}, bf16[64,9472]{1,0:T(8,128)(2,1)S(1)}, u32[]{:S(2)}) copy-start(bf16[64,9472]{1,0:T(8,128)(2,1)S(1)} %get-tuple-element.20.at_ref.up_ref.hid_ref.back_ref) | copy-start | bytes 3637252
  123.3 30.2 %collective-permute-start.3 = (bf16[16,72,128]{2,1,0:T(8,128)(2,1)S(1)}, bf16[16,72,128]{2,1,0:T(8,128)(2,1)S(1)}, u32[]{:S(2)}, u32[]{:S(2)}) collective-permute-start(bf16[16,72,128]{2,1,0:T(8,128)(2,1)S(1)} %get-tuple-element.24), channel_id=1, source_target_pairs={{0,64},{64,128},{128,192},{192,0},{1,65},{65,129},{129,193},{193,1... | collective-permute-start | bytes 884744 | tf_op jit(solution)/shard_map/ppermute | solution.py:179
  123.4 30.1 %collective-permute-start.4 = (bf16[16,72,128]{2,1,0:T(8,128)(2,1)S(1)}, bf16[16,72,128]{2,1,0:T(8,128)(2,1)S(1)}, u32[]{:S(2)}, u32[]{:S(2)}) collective-permute-start(bf16[16,72,128]{2,1,0:T(8,128)(2,1)S(1)} %get-tuple-element.25), channel_id=1, source_target_pairs={{0,128},{64,192},{128,0},{192,64},{1,129},{65,193},{129,1},{193,65... | collective-permute-start | bytes 884744 | tf_op jit(solution)/shard_map/ppermute | solution.py:179
  136.6 17.0 %collective-permute-start.5 = (bf16[16,72,128]{2,1,0:T(8,128)(2,1)S(1)}, bf16[16,72,128]{2,1,0:T(8,128)(2,1)S(1)}, u32[]{:S(2)}, u32[]{:S(2)}) collective-permute-start(bf16[16,72,128]{2,1,0:T(8,128)(2,1)S(1)} %get-tuple-element.26), channel_id=1, source_target_pairs={{0,192},{64,0},{128,64},{192,128},{1,193},{65,1},{129,65},{193,129... | collective-permute-start | bytes 884744 | tf_op jit(solution)/shard_map/ppermute | solution.py:179
Sparse Core Ops, SparseCore 0:
  39.3 97.2 all-gather.1

commit v9 on v7

--- a/solution.py
+++ b/solution.py
@@ -151,10 +151,8 @@
     lax.fori_loop(0, shards // per, pack, 0)
 
 
-def columns(place_ref, y, k, parity, counts):
-    deep, cores = counts
-    z = lax.rem(place_ref[0] - k + deep, deep)
-    start = ((y * deep + z) * cores + parity) * TILE_ROWS
+def columns(y, z, parity, deep):
+    start = ((y * deep + z) * 2 + parity) * TILE_ROWS
     return pl.ds(pl.multiple_of(start, TILE_ROWS), TILE_ROWS)
 
 
@@ -167,60 +165,61 @@
     return key, grad.astype(bf16)
 
 
-def fetch(source_ref, w_ref, sems):
+def fetch(place_ref, core, sources, w_ref, sems):
     wide, groups = w_ref.shape[:2]
-    copies = [
-        [pltpu.make_async_copy(source_ref.at[y, x], w_ref.at[y, x], sems.at[y, x]) for x in range(groups)]
-        for y in range(wide)
-    ]
-    for row in copies:
-        for copy in row:
-            copy.start()
-    return copies
-
-
-def block(copies, w_ref, y):
+    for a, source in enumerate(sources):
+        for b in range(source.shape[0]):
+            back_y = jnp.where(core == 0, b, a)
+            back_g = jnp.where(core == 0, a, b)
+            y = lax.rem(place_ref[1] - back_y + wide, wide)
+            g = lax.rem(place_ref[0] - back_g + groups, groups)
+            pltpu.make_async_copy(source.at[b], w_ref.at[y, g], sems.at[y, g]).start()
+
+
+def block(source, w_ref, sems, y):
     groups, deep = w_ref.shape[1:3]
-    for copy in copies[y]:
-        copy.wait()
-    return jnp.concatenate([w_ref[y, x, k] for k in range(deep) for x in range(groups)], axis=0)
-
-
-def own_kernel(place_ref, tok_ref, cot_ref, half_ref, adapter_ref, key_ref, grad_ref, w_ref, sems):
-    wide, _, deep, _, key_columns = half_ref.shape
+    for g in range(groups):
+        pltpu.make_async_copy(source.at[0], w_ref.at[y, g], sems.at[y, g]).wait()
+    return jnp.concatenate([w_ref[y, g, z] for z in range(deep) for g in range(groups)], axis=0)
+
+
+def own_kernel(place_ref, tok_ref, cot_ref, s0, s1, s2, s3, adapter_ref, key_ref, grad_ref, w_ref, sems):
+    wide, _, deep, _, key_columns = w_ref.shape
     rows, depth = tok_ref.shape
     width = depth + key_columns
     span = deep * TILE_ROWS
-    copies = fetch(half_ref, w_ref, sems)
+    core = place_ref[2]
+    fetch(place_ref, core, (s0, s1, s2, s3), w_ref, sems)
     hidden = adapter_ref[:, width : width + rows]
     back = adapter_ref[:, width + rows :]
     up = adapter_ref[:, depth:width]
     key_ref[...] = adapter_scale * lax.dot_general(hidden, up, TN, preferred_element_type=f32)
     for y in range(wide):
-        weight = block(copies, w_ref, y)
-        places = [columns(place_ref, y, k, place_ref[1], (deep, 2)) for k in range(deep)]
+        weight = block(s0, w_ref, sems, y)
+        places = [columns(y, z, core, deep) for z in range(deep)]
         key, grad = products(tok_ref, cot_ref, weight, adapter_ref, back, places)
         key_ref[...] += key
         grad_ref[:, y * span : (y + 1) * span] = grad
 
 
 def other_kernel(
-    place_ref, tok_ref, cot_ref, half_ref, adapter_ref, key_ref, own_ref, keys_ref, grad_ref, acc_ref, w_ref, sems
+    place_ref, tok_ref, cot_ref, s0, s1, s2, s3, adapter_ref, key_ref, own_ref, keys_ref, grad_ref, acc_ref, w_ref, sems
 ):
-    wide, _, deep, _, key_columns = half_ref.shape
+    wide, _, deep, _, key_columns = w_ref.shape
     rows, depth = tok_ref.shape
-    copies = fetch(half_ref, w_ref, sems)
+    core = place_ref[2]
+    fetch(place_ref, 1 - core, (s0, s1, s2, s3), w_ref, sems)
     back = adapter_ref[:, depth + key_columns + rows :]
     acc_ref[...] = key_ref[...]
     for y in range(wide):
-        weight = block(copies, w_ref, y)
-        places = [columns(place_ref, y, k, 1 - place_ref[1], (deep, 2)) for k in range(deep)]
+        weight = block(s0, w_ref, sems, y)
+        places = [columns(y, z, 1 - core, deep) for z in range(deep)]
         key, grad = products(tok_ref, cot_ref, weight, adapter_ref, back, places)
         acc_ref[...] += key
-        for k in range(deep):
-            at = (y * deep + k) * TILE_ROWS
-            grad_ref[:, columns(place_ref, y, k, place_ref[1], (deep, 2))] = own_ref[:, at : at + TILE_ROWS]
-            grad_ref[:, places[k]] = grad[:, k * TILE_ROWS : (k + 1) * TILE_ROWS]
+        for z in range(deep):
+            at = (y * deep + z) * TILE_ROWS
+            grad_ref[:, columns(y, z, core, deep)] = own_ref[:, at : at + TILE_ROWS]
+            grad_ref[:, places[z]] = grad[:, z * TILE_ROWS : (z + 1) * TILE_ROWS]
     keys_ref[...] = acc_ref[...].astype(keys_ref.dtype)
 
 
@@ -228,14 +227,15 @@
     return lax.ppermute(x, "grp", [(i, (i + by) % groups) for i in range(groups)])
 
 
-def ring(x, axis, size):
-    up = [x]
-    down = [x]
-    for _ in range(size // 2):
-        up.append(lax.ppermute(up[-1], axis, [(i, (i + 1) % size) for i in range(size)]))
-    for _ in range(size // 2 - 1):
-        down.append(lax.ppermute(down[-1], axis, [(i, (i - 1) % size) for i in range(size)]))
-    return jnp.concatenate(up + down[:0:-1], axis=0)
+def route(x, by, groups, wide, first):
+    pairs = []
+    for g in range(groups):
+        for y in range(wide):
+            for c in range(2):
+                along_y = (c == 0) == first
+                to = (g, (y + by) % wide) if along_y else ((g + by) % groups, y)
+                pairs.append(((g * wide + y) * 2 + c, (to[0] * wide + to[1]) * 2 + c))
+    return lax.ppermute(x, ("grp", "y", "core"), pairs)
 
 
 def whole(memory=pltpu.VMEM):
@@ -251,12 +251,19 @@
     packed_rows = row_count * rank // LANES
     width = depth + key_columns
     group = lax.axis_index("grp").reshape(1).astype(jnp.int32)
-    place = jnp.stack([lax.axis_index("z"), lax.axis_index("core")]).astype(jnp.int32)
+    place = jnp.stack([lax.axis_index("grp"), lax.axis_index("y"), lax.axis_index("core")])
+    place = place.astype(jnp.int32)
     jobs = tile_job.reshape(-1)
 
     quarter = TILE_ROWS // groups
+    wide, deep = lax.axis_size("y"), lax.axis_size("z")
     mine = lax.dynamic_slice_in_dim(frozen_weight, lax.axis_index("grp") * quarter, quarter, 0)
-    column = ring(mine, "z", lax.axis_size("z"))
+    column = lax.all_to_all(
+        jnp.broadcast_to(mine, (deep,) + mine.shape), "z", split_axis=0, concat_axis=0, tiled=True
+    )
+    line = jnp.stack([column] + [route(column, k, groups, wide, True) for k in range(1, wide)])
+    halves = [line] + [route(line, k, groups, wide, False) for k in range(1, groups)]
+    others = [lax.ppermute(x, "core", [(0, 1), (1, 0)]) for x in halves]
 
     own = pl.pallas_call(
         pack_kernel,
@@ -277,8 +284,6 @@
         compiler_params=params(),
         name="pick",
     )(group, jobs, job_slot, *every)
-    outgoing, column = lax.optimization_barrier((outgoing, column))
-    half = lax.all_gather(column, ("y", "grp"), axis=0, tiled=True)
     arrived = lax.all_to_all(outgoing, SEQ, split_axis=0, concat_axis=0, tiled=True)
     terms, adapter = pl.pallas_call(
         tile_kernel,
@@ -293,8 +298,7 @@
         name="tile",
     )(arrived, tokens, cotangent)
     incoming = lax.all_to_all(terms, SEQ, split_axis=0, concat_axis=0, tiled=True)
-    incoming, half = lax.optimization_barrier((incoming, half))
-    other = lax.ppermute(half, "core", [(0, 1), (1, 0)])
+    incoming, others = lax.optimization_barrier((incoming, others))
     sums = pl.pallas_call(
         sum_kernel,
         out_shape=(jax.ShapeDtypeStruct((slot_count, packed_rows, LANES), f32),)
@@ -305,8 +309,8 @@
         compiler_params=params(),
         name="sum",
     )(group, jobs, job_slot, incoming)
-    kept, half = lax.optimization_barrier((sums[0], half))
-    wide, deep = lax.axis_size("y"), lax.axis_size("z")
+    kept, line = lax.optimization_barrier((sums[0], line))
+    sums = (kept,) + tuple(sums[1:])
     blocks = (wide, groups, deep, quarter, key_columns)
     cost = pl.CostEstimate(
         flops=2 * rows * depth * key_columns,
@@ -319,15 +323,13 @@
             jax.ShapeDtypeStruct((rows, key_columns), f32),
             jax.ShapeDtypeStruct((rows, depth // 2), bf16),
         ),
-        in_specs=[smem, whole(), whole(), whole(pltpu.HBM), whole()],
+        in_specs=[smem, whole(), whole()] + [whole(pltpu.HBM)] * groups + [whole()],
         out_specs=(whole(),) * 2,
         scratch_shapes=[pltpu.VMEM(blocks, bf16), pltpu.SemaphoreType.DMA((wide, groups))],
         compiler_params=params(50),
         cost_estimate=cost,
         name="own",
-    )(place, tokens, cotangent, half.reshape(blocks), adapter)
-    last, other, key_part = lax.optimization_barrier((sums[-1], other, key_part))
-    sums = (kept,) + tuple(sums[1:-1]) + (last,)
+    )(place, tokens, cotangent, line, *halves[1:], adapter)
     owned = (sums[0],) + tuple(shift(sums[k], k, groups) for k in range(1, groups))
     grads = pl.pallas_call(
         unpack_kernel,
@@ -344,7 +346,7 @@
             jax.ShapeDtypeStruct((rows, key_columns), bf16),
             jax.ShapeDtypeStruct((rows, depth), bf16),
         ),
-        in_specs=[smem, whole(), whole(), whole(pltpu.HBM), whole(), whole(), whole()],
+        in_specs=[smem, whole(), whole()] + [whole(pltpu.HBM)] * groups + [whole()] * 3,
         out_specs=(whole(),) * 2,
         scratch_shapes=[
             pltpu.VMEM((rows, key_columns), f32),
@@ -354,7 +356,7 @@
         compiler_params=params(50),
         cost_estimate=cost,
         name="other",
-    )(place, tokens, cotangent, other.reshape(blocks), adapter, key_part, own_part)
+    )(place, tokens, cotangent, *others, adapter, key_part, own_part)
     return keys, token_gradient, jnp.swapaxes(grads, 1, 2)
 
 

time: 168 us -> 157 us (0.935)
  blocking collectives: 80.4 us -> 0 us
  waiting for transfers between devices: 23.6 us -> 73.9 us
  starting transfers between devices: 22.7 us -> 44.6 us
  between operations: 14.2 us -> 0.84 us
  local copies, waits for them, and re-layouts: 1.97 us -> 5.62 us
  other arithmetic: 0.07 us -> 3.32 us
  Pallas kernels: 24.9 us -> 28 us
    all_to_all x2 -> x0, blocking collectives: 80.4 us -> none  [the longest x1 43 us: on_device(): lax.all_to_all(outgoing, SEQ, split_axis=0, concat_axis=0, tiled=True)]
    all_to_all x0 -> x3, waiting for transfers between devices: none -> 37.7 us  [the longest x1 22.8 us: on_device(): lax.all_to_all(outgoing, SEQ, split_axis=0, concat_axis=0, tiled=True)]
    ppermute x8 -> x10, waiting for transfers between devices: 7.92 us -> 36.2 us  [the longest x6 30.8 us: route(): return lax.ppermute(x, ('grp', 'y', 'core'), pairs)]
    all_to_all x0 -> x3, starting transfers between devices: none -> 26.3 us  [the longest x1 10.9 us: on_device(): lax.all_to_all(outgoing, SEQ, split_axis=0, concat_axis=0, tiled=True)]
    all_gather x1 -> x0, waiting for transfers between devices: 13.7 us -> none  [on_device(): half = lax.all_gather(column, ('y', 'grp'), axis=0, tiled=True)]
    another operation x1 -> x2, other arithmetic: 0.07 us -> 3.32 us  [the longest x1 3.24 us: on_device(): jnp.stack([column] + [route(column, k, groups, wide, True) for k in range...]
    ppermute x8 -> x10, starting transfers between devices: 12.9 us -> 9.93 us  [the longest x6 9.27 us: route(): return lax.ppermute(x, ('grp', 'y', 'core'), pairs)]
    unnamed x21 -> x24, local copies, waits for them, and re-layouts: 1.96 us -> 4.76 us
  transfers between devices with their start and end apart: 15 -> 19, of which waited for: 5 -> 7; matrix products, arithmetic and copies ran while one was open for 0% -> 2% of each run, Pallas kernels for 14% -> 16%
where the time goes in v9:
time: 157 us; the launch traced here: 156 us
  waiting for transfers between devices  73.9 us (47%)
  starting transfers between devices  44.6 us (28%)
  Pallas kernels  28 us (18%)
  local copies, waits for them, and re-layouts  5.62 us (4%)
  other arithmetic  3.32 us (2%)
    ppermute x6, waiting for transfers between devices, route(): return lax.ppermute(x, ('grp', 'y', 'core'), pairs)  30.8 us
    all_to_all x1, waiting for transfers between devices, on_device(): lax.all_to_all(outgoing, SEQ, split_axis=0, concat_axis=0, tiled=True)  22.8 us
    all_to_all x1, waiting for transfers between devices, on_device(): lax.all_to_all(jnp.broadcast_to(mine, (deep,) + mine.shape), 'z', split_a...  14.1 us
    pallas_call x1, Pallas kernels, on_device(): pl.pallas_call(other_kernel, out_shape=(jax.ShapeDtypeStruct((rows, key_c...  11.2 us
    all_to_all x1, starting transfers between devices, on_device(): lax.all_to_all(outgoing, SEQ, split_axis=0, concat_axis=0, tiled=True)  10.9 us
    ppermute x6, starting transfers between devices, route(): return lax.ppermute(x, ('grp', 'y', 'core'), pairs)  9.27 us
    all_to_all x1, starting transfers between devices, on_device(): lax.all_to_all(jnp.broadcast_to(mine, (deep,) + mine.shape), 'z', split_a...  9.01 us
    pallas_call x1, Pallas kernels, on_device(): pl.pallas_call(own_kernel, out_shape=(jax.ShapeDtypeStruct((rows, key_col...  8.76 us
  transfers between devices with their start and end apart: 19, of which 7 were waited for; matrix products, arithmetic and copies ran while one was open for 2% of the time, Pallas kernels for 16%

profile of v9, /device:TPU:1, one launch (start us, length us, event | category | flops | bytes accessed | tf_op | source)
XLA Modules:
  0.0 156.3 jit_solution(9188017162740069997)
XLA Ops:
  2.4 9.0 %all-to-all-start.2 = ((bf16[8,32,1024]{2,1,0:T(8,128)(2,1)}), bf16[8,32,1024]{2,1,0:T(8,128)(2,1)S(1)}, u32[]{:S(2)}, u32[]{:S(2)}) async-start(bf16[8,32,1024]{2,1,0:T(8,128)(2,1)} %broadcast_in_dim.3), calls=%async_computation.2 | async-start | bytes 1048576 | tf_op jit(solution)/shard_map/all_to_all | solution.py:261
  11.6 2.6 %collective-permute-start = (bf16[16,72,128]{2,1,0:T(8,128)(2,1)S(1)}, bf16[16,72,128]{2,1,0:T(8,128)(2,1)S(1)}, u32[]{:S(2)}, u32[]{:S(2)}) collective-permute-start(bf16[16,72,128]{2,1,0:T(8,128)(2,1)S(1)} %pack.1.refs_0_), channel_id=1, source_target_pairs={{0,192},{64,0},{128,64},{192,128},{1,193},{65,1},{129,65},{193,129... | collective-permute-start | bytes 884744 | tf_op jit(solution)/shard_map/ppermute | solution.py:227
  15.3 14.1 %all-to-all-done.2 = bf16[8,32,1024]{2,1,0:T(8,128)(2,1)S(1)} async-done(((bf16[8,32,1024]{2,1,0:T(8,128)(2,1)}), bf16[8,32,1024]{2,1,0:T(8,128)(2,1)S(1)}, u32[]{:S(2)}, u32[]{:S(2)}) %all-to-all-start.2) | async-done | bytes 524320 | tf_op jit(solution)/shard_map/all_to_all | solution.py:261
  29.4 1.2 collective-permute-start.3
  30.6 2.5 %collective-permute-start.4 = (bf16[8,32,1024]{2,1,0:T(8,128)(2,1)S(1)}, bf16[8,32,1024]{2,1,0:T(8,128)(2,1)}, u32[]{:S(2)}, u32[]{:S(2)}) collective-permute-start(bf16[8,32,1024]{2,1,0:T(8,128)(2,1)S(1)} %all-to-all-done.2), channel_id=1, source_target_pairs={{0,32},{1,129},{16,48},{17,145},{32,0},{33,161},{48,16},{49,177},{... | collective-permute-start | bytes 1572872 | tf_op jit(solution)/shard_map/ppermute | solution.py:238
  33.1 1.2 collective-permute-start.5
  34.3 1.9 %pick.1 = bf16[64,72,128]{2,1,0:T(8,128)(2,1)} custom-call(s32[1]{0:T(128)} %bitcast.group_ref, s32[256]{0:T(256)S(1)} %bitcast.11, s32[64]{0:T(128)S(1)} %copy-done.9, bf16[16,72,128]{2,1,0:T(8,128)(2,1)S(1)} %pack.1.refs_0_, bf16[16,72,128]{2,1,0:T(8,128)(2,1)S(1)} %collective-permute-done.refs_1_, ...), custom_call_target="tpu_custom_call" | custom-call | tf_op jit(solution)/shard_map/pick/pallas_call | solution.py:278
  36.2 10.9 %all-to-all-start = ((bf16[64,72,128]{2,1,0:T(8,128)(2,1)}), bf16[64,72,128]{2,1,0:T(8,128)(2,1)S(1)}, u32[]{:S(2)}, u32[]{:S(2)}) async-start(bf16[64,72,128]{2,1,0:T(8,128)(2,1)} %pick.1), calls=%async_computation | async-start | bytes 2359296 | tf_op jit(solution)/shard_map/all_to_all | solution.py:287
  47.9 3.2 %pad_maximum_fusion.s0 = bf16[4,8,32,1024]{3,2,1,0:T(8,128)(2,1)} fusion(bf16[1,8,32,1024]{3,2,1,0:T(8,128)(2,1)} %bitcast.15, bf16[1,8,32,1024]{3,2,1,0:T(8,128)(2,1)} %bitcast.7, bf16[1,8,32,1024]{3,2,1,0:T(8,128)(2,1)} %bitcast.6, bf16[1,8,32,1024]{3,2,1,0:T(8,128)(2,1)} %bitcast.13), kind=kLoop, calls=%fused_computation | loop fusion | flops 3145728 | bytes 4194304 | tf_op jit(solution)/shard_map/stack | solution.py:264
  51.1 3.0 %collective-permute-start.9 = (bf16[4,8,32,1024]{3,2,1,0:T(8,128)(2,1)}, bf16[4,8,32,1024]{3,2,1,0:T(8,128)(2,1)}, u32[]{:S(2)}, u32[]{:S(2)}) collective-permute-start(bf16[4,8,32,1024]{3,2,1,0:T(8,128)(2,1)} %pad_maximum_fusion.s0), channel_id=1, source_target_pairs={{0,128},{1,33},{16,144},{17,49},{32,160},{33,1},{48,176},{49,17},{... | collective-permute-start | bytes 6291464 | tf_op jit(solution)/shard_map/ppermute | solution.py:238
  55.6 22.8 %all-to-all-done.x_ref = bf16[64,72,128]{2,1,0:T(8,128)(2,1)S(1)} async-done(((bf16[64,72,128]{2,1,0:T(8,128)(2,1)}), bf16[64,72,128]{2,1,0:T(8,128)(2,1)S(1)}, u32[]{:S(2)}, u32[]{:S(2)}) %all-to-all-start) | async-done | bytes 1179680 | tf_op jit(solution)/shard_map/all_to_all | solution.py:287
  79.4 3.6 %tile.1 = (bf16[64,72,128]{2,1,0:T(8,128)(2,1)S(1)}, bf16[64,9472]{1,0:T(8,128)(2,1)S(1)}) custom-call(bf16[64,72,128]{2,1,0:T(8,128)(2,1)S(1)} %all-to-all-done.x_ref, bf16[128,8192]{1,0:T(8,128)(2,1)S(1)} %copy-done.1, bf16[128,1024]{1,0:T(8,128)(2,1)S(1)} %copy-done.4), custom_call_target="tpu_custom_call" | custom-call | tf_op jit(solution)/shard_map/tile/pallas_call | solution.py:288
  83.0 1.0 copy-done.2
  84.0 1.0 copy-done.6
  85.1 6.4 %all-to-all-start.1 = ((bf16[64,72,128]{2,1,0:T(8,128)(2,1)}), bf16[64,72,128]{2,1,0:T(8,128)(2,1)S(1)}, u32[]{:S(2)}, u32[]{:S(2)}) async-start(bf16[64,72,128]{2,1,0:T(8,128)(2,1)} %copy-done.6), calls=%async_computation.1 | async-start | bytes 2359296 | tf_op jit(solution)/shard_map/all_to_all | solution.py:300
  92.1 29.5 %collective-permute-done.11.s3 = bf16[4,8,32,1024]{3,2,1,0:T(8,128)(2,1)} collective-permute-done((bf16[4,8,32,1024]{3,2,1,0:T(8,128)(2,1)}, bf16[4,8,32,1024]{3,2,1,0:T(8,128)(2,1)}, u32[]{:S(2)}, u32[]{:S(2)}) %collective-permute-start.11) | collective-permute-done | bytes 2097184 | tf_op jit(solution)/shard_map/ppermute | solution.py:238
  121.7 1.2 collective-permute-done.7.s1
  123.7 2.5 %collective-permute-done.12.s3 = bf16[4,8,32,1024]{3,2,1,0:T(8,128)(2,1)} collective-permute-done((bf16[4,8,32,1024]{3,2,1,0:T(8,128)(2,1)}, bf16[4,8,32,1024]{3,2,1,0:T(8,128)(2,1)}, u32[]{:S(2)}, u32[]{:S(2)}) %collective-permute-start.12) | collective-permute-done | bytes 2097184 | tf_op jit(solution)/shard_map/ppermute | solution.py:266
  126.2 3.0 %collective-permute-done.8.s1 = bf16[4,8,32,1024]{3,2,1,0:T(8,128)(2,1)} collective-permute-done((bf16[4,8,32,1024]{3,2,1,0:T(8,128)(2,1)}, bf16[4,8,32,1024]{3,2,1,0:T(8,128)(2,1)}, u32[]{:S(2)}, u32[]{:S(2)}) %collective-permute-start.8) | collective-permute-done | bytes 2097184 | tf_op jit(solution)/shard_map/ppermute | solution.py:266
  129.2 1.3 sum.1
  130.5 4.6 %collective-permute-start.14 = (bf16[16,72,128]{2,1,0:T(8,128)(2,1)S(1)}, bf16[16,72,128]{2,1,0:T(8,128)(2,1)S(1)}, u32[]{:S(2)}, u32[]{:S(2)}) collective-permute-start(bf16[16,72,128]{2,1,0:T(8,128)(2,1)S(1)} %get-tuple-element.35), channel_id=1, source_target_pairs={{0,128},{64,192},{128,0},{192,64},{1,129},{65,193},{129,1},{193,65... | collective-permute-start | bytes 884744 | tf_op jit(solution)/shard_map/ppermute | solution.py:227
  135.1 8.8 %own.1 = (f32[128,1024]{1,0:T(8,128)S(1)}, bf16[128,4096]{1,0:T(8,128)(2,1)S(1)}) custom-call(s32[3]{0:T(128)S(1)} %pad_add_fusion.place_ref, bf16[128,8192]{1,0:T(8,128)(2,1)} %tok_ref.5, bf16[128,1024]{1,0:T(8,128)(2,1)S(1)} %copy-done.5, bf16[4,8,32,1024]{3,2,1,0:T(8,128)(2,1)} %pad_maximum_fusion.s0, bf16[4,8,32,1024]{3,2,1,0:T(8,128)(2,1)} %collective-permute-done.7.s1, ...), custom_call_target="tpu_custom_call" | custom-call | flops 2147483648 | bytes 13107200 | tf_op jit(solution)/shard_map/own/pallas_call | solution.py:320
  143.9 11.2 %other.1 = (bf16[128,1024]{1,0:T(8,128)(2,1)}, bf16[128,8192]{1,0:T(8,128)(2,1)}) custom-call(s32[3]{0:T(128)S(1)} %pad_add_fusion.place_ref, bf16[128,8192]{1,0:T(8,128)(2,1)} %tok_ref.5, bf16[128,1024]{1,0:T(8,128)(2,1)S(1)} %copy-done.5, bf16[4,8,32,1024]{3,2,1,0:T(8,128)(2,1)} %collective-permute-done.6.s0, ...), custom_call_target="tpu_custom_call" | custom-call | flops 2147483648 | bytes 13107200 | tf_op jit(solution)/shard_map/other/pallas_call | solution.py:343
  155.1 1.2 unpack.1
  (49 shorter events, 7.9 us)
Async XLA Ops:
  0.7 33.6 %copy-start.8 = (s32[256,1]{0,1:T(1,128)S(1)}, s32[256,1]{0,1:T(1,128)}, u32[]{:S(2)}) copy-start(s32[256,1]{0,1:T(1,128)} %param.10) | copy-start | bytes 3076
  0.7 33.6 %copy-start.9 = (s32[64]{0:T(128)S(1)}, s32[64]{0:T(128)}, u32[]{:S(2)}) copy-start(s32[64]{0:T(128)} %slot_ref.3) | copy-start | bytes 772
  2.4 27.0 %all-to-all-start.2 = ((bf16[8,32,1024]{2,1,0:T(8,128)(2,1)}), bf16[8,32,1024]{2,1,0:T(8,128)(2,1)S(1)}, u32[]{:S(2)}, u32[]{:S(2)}) async-start(bf16[8,32,1024]{2,1,0:T(8,128)(2,1)} %broadcast_in_dim.3), calls=%async_computation.2 | async-start | bytes 1048576 | tf_op jit(solution)/shard_map/all_to_all | solution.py:261
  11.6 21.5 %collective-permute-start = (bf16[16,72,128]{2,1,0:T(8,128)(2,1)S(1)}, bf16[16,72,128]{2,1,0:T(8,128)(2,1)S(1)}, u32[]{:S(2)}, u32[]{:S(2)}) collective-permute-start(bf16[16,72,128]{2,1,0:T(8,128)(2,1)S(1)} %pack.1.refs_0_), channel_id=1, source_target_pairs={{0,192},{64,0},{128,64},{192,128},{1,193},{65,1},{129,65},{193,129... | collective-permute-start | bytes 884744 | tf_op jit(solution)/shard_map/ppermute | solution.py:227
  14.2 20.1 %collective-permute-start.1 = (bf16[16,72,128]{2,1,0:T(8,128)(2,1)S(1)}, bf16[16,72,128]{2,1,0:T(8,128)(2,1)S(1)}, u32[]{:S(2)}, u32[]{:S(2)}) collective-permute-start(bf16[16,72,128]{2,1,0:T(8,128)(2,1)S(1)} %pack.1.refs_0_), channel_id=1, source_target_pairs={{0,128},{64,192},{128,0},{192,64},{1,129},{65,193},{129,1},{193,65... | collective-permute-start | bytes 884744 | tf_op jit(solution)/shard_map/ppermute | solution.py:227
  14.7 19.6 %collective-permute-start.2 = (bf16[16,72,128]{2,1,0:T(8,128)(2,1)S(1)}, bf16[16,72,128]{2,1,0:T(8,128)(2,1)S(1)}, u32[]{:S(2)}, u32[]{:S(2)}) collective-permute-start(bf16[16,72,128]{2,1,0:T(8,128)(2,1)S(1)} %pack.1.refs_0_), channel_id=1, source_target_pairs={{0,64},{64,128},{128,192},{192,0},{1,65},{65,129},{129,193},{193,1... | collective-permute-start | bytes 884744 | tf_op jit(solution)/shard_map/ppermute | solution.py:227
  29.4 17.7 %collective-permute-start.3 = (bf16[8,32,1024]{2,1,0:T(8,128)(2,1)S(1)}, bf16[8,32,1024]{2,1,0:T(8,128)(2,1)}, u32[]{:S(2)}, u32[]{:S(2)}) collective-permute-start(bf16[8,32,1024]{2,1,0:T(8,128)(2,1)S(1)} %all-to-all-done.2), channel_id=1, source_target_pairs={{0,16},{1,65},{16,32},{17,81},{32,48},{33,97},{48,0},{49,113},{64,... | collective-permute-start | bytes 1572872 | tf_op jit(solution)/shard_map/ppermute | solution.py:238
  30.6 16.5 %collective-permute-start.4 = (bf16[8,32,1024]{2,1,0:T(8,128)(2,1)S(1)}, bf16[8,32,1024]{2,1,0:T(8,128)(2,1)}, u32[]{:S(2)}, u32[]{:S(2)}) collective-permute-start(bf16[8,32,1024]{2,1,0:T(8,128)(2,1)S(1)} %all-to-all-done.2), channel_id=1, source_target_pairs={{0,32},{1,129},{16,48},{17,145},{32,0},{33,161},{48,16},{49,177},{... | collective-permute-start | bytes 1572872 | tf_op jit(solution)/shard_map/ppermute | solution.py:238
  33.1 14.0 %collective-permute-start.5 = (bf16[8,32,1024]{2,1,0:T(8,128)(2,1)S(1)}, bf16[8,32,1024]{2,1,0:T(8,128)(2,1)S(1)}, u32[]{:S(2)}, u32[]{:S(2)}) collective-permute-start(bf16[8,32,1024]{2,1,0:T(8,128)(2,1)S(1)} %all-to-all-done.2), channel_id=1, source_target_pairs={{0,48},{1,193},{16,0},{17,209},{32,16},{33,225},{48,32},{49,241},{... | collective-permute-start | bytes 1572872 | tf_op jit(solution)/shard_map/ppermute | solution.py:238
  36.2 42.3 %all-to-all-start = ((bf16[64,72,128]{2,1,0:T(8,128)(2,1)}), bf16[64,72,128]{2,1,0:T(8,128)(2,1)S(1)}, u32[]{:S(2)}, u32[]{:S(2)}) async-start(bf16[64,72,128]{2,1,0:T(8,128)(2,1)} %pick.1), calls=%async_computation | async-start | bytes 2359296 | tf_op jit(solution)/shard_map/all_to_all | solution.py:287
  47.9 30.5 %copy-start.1 = (bf16[128,8192]{1,0:T(8,128)(2,1)S(1)}, bf16[128,8192]{1,0:T(8,128)(2,1)}, u32[]{:S(2)}) copy-start(bf16[128,8192]{1,0:T(8,128)(2,1)} %tok_ref.5) | copy-start | bytes 6291460
  51.1 40.9 %collective-permute-start.9 = (bf16[4,8,32,1024]{3,2,1,0:T(8,128)(2,1)}, bf16[4,8,32,1024]{3,2,1,0:T(8,128)(2,1)}, u32[]{:S(2)}, u32[]{:S(2)}) collective-permute-start(bf16[4,8,32,1024]{3,2,1,0:T(8,128)(2,1)} %pad_maximum_fusion.s0), channel_id=1, source_target_pairs={{0,128},{1,33},{16,144},{17,49},{32,160},{33,1},{48,176},{49,17},{... | collective-permute-start | bytes 6291464 | tf_op jit(solution)/shard_map/ppermute | solution.py:238
  54.1 67.5 %collective-permute-start.11 = (bf16[4,8,32,1024]{3,2,1,0:T(8,128)(2,1)}, bf16[4,8,32,1024]{3,2,1,0:T(8,128)(2,1)}, u32[]{:S(2)}, u32[]{:S(2)}) collective-permute-start(bf16[4,8,32,1024]{3,2,1,0:T(8,128)(2,1)} %pad_maximum_fusion.s0), channel_id=1, source_target_pairs={{0,192},{1,49},{16,208},{17,1},{32,224},{33,17},{48,240},{49,33},{... | collective-permute-start | bytes 6291464 | tf_op jit(solution)/shard_map/ppermute | solution.py:238
  54.9 67.9 %collective-permute-start.7 = (bf16[4,8,32,1024]{3,2,1,0:T(8,128)(2,1)}, bf16[4,8,32,1024]{3,2,1,0:T(8,128)(2,1)}, u32[]{:S(2)}, u32[]{:S(2)}) collective-permute-start(bf16[4,8,32,1024]{3,2,1,0:T(8,128)(2,1)} %pad_maximum_fusion.s0), channel_id=1, source_target_pairs={{0,64},{1,17},{16,80},{17,33},{32,96},{33,49},{48,112},{49,1},{64,... | collective-permute-start | bytes 6291464 | tf_op jit(solution)/shard_map/ppermute | solution.py:238
  85.1 50.0 %copy-start.5 = (bf16[128,1024]{1,0:T(8,128)(2,1)S(1)}, bf16[128,1024]{1,0:T(8,128)(2,1)}, u32[]{:S(2)}) copy-start(bf16[128,1024]{1,0:T(8,128)(2,1)} %cot_ref.5) | copy-start | bytes 786436
  85.1 50.0 %copy-start.3 = (bf16[64,9472]{1,0:T(8,128)(2,1)S(1)}, bf16[64,9472]{1,0:T(8,128)(2,1)}, u32[]{:S(2)}) copy-start(bf16[64,9472]{1,0:T(8,128)(2,1)} %copy-done.2) | copy-start | bytes 3637252
  85.1 38.6 %all-to-all-start.1 = ((bf16[64,72,128]{2,1,0:T(8,128)(2,1)}), bf16[64,72,128]{2,1,0:T(8,128)(2,1)S(1)}, u32[]{:S(2)}, u32[]{:S(2)}) async-start(bf16[64,72,128]{2,1,0:T(8,128)(2,1)} %copy-done.6), calls=%async_computation.1 | async-start | bytes 2359296 | tf_op jit(solution)/shard_map/all_to_all | solution.py:300
  91.5 31.5 %collective-permute-start.6 = (bf16[4,8,32,1024]{3,2,1,0:T(8,128)(2,1)}, bf16[4,8,32,1024]{3,2,1,0:T(8,128)(2,1)}, u32[]{:S(2)}, u32[]{:S(2)}) collective-permute-start(bf16[4,8,32,1024]{3,2,1,0:T(8,128)(2,1)} %pad_maximum_fusion.s0), channel_id=1, source_target_pairs={{0,1},{1,0},{2,3},{3,2},{4,5},{5,4},{6,7},{7,6},{8,9},{9,8},{10,11... | collective-permute-start | bytes 6291464 | tf_op jit(solution)/shard_map/ppermute | solution.py:266
  92.0 31.7 %collective-permute-start.10 = (bf16[4,8,32,1024]{3,2,1,0:T(8,128)(2,1)}, bf16[4,8,32,1024]{3,2,1,0:T(8,128)(2,1)}, u32[]{:S(2)}, u32[]{:S(2)}) collective-permute-start(bf16[4,8,32,1024]{3,2,1,0:T(8,128)(2,1)} %collective-permute-done.9.s2), channel_id=1, source_target_pairs={{0,1},{1,0},{2,3},{3,2},{4,5},{5,4},{6,7},{7,6},{8,9},{9,8},{10,11... | collective-permute-start | bytes 6291464 | tf_op jit(solution)/shard_map/ppermute | solution.py:266
  121.7 4.5 %collective-permute-start.12 = (bf16[4,8,32,1024]{3,2,1,0:T(8,128)(2,1)}, bf16[4,8,32,1024]{3,2,1,0:T(8,128)(2,1)}, u32[]{:S(2)}, u32[]{:S(2)}) collective-permute-start(bf16[4,8,32,1024]{3,2,1,0:T(8,128)(2,1)} %collective-permute-done.11.s3), channel_id=1, source_target_pairs={{0,1},{1,0},{2,3},{3,2},{4,5},{5,4},{6,7},{7,6},{8,9},{9,8},{10,11... | collective-permute-start | bytes 6291464 | tf_op jit(solution)/shard_map/ppermute | solution.py:266
  122.9 6.3 %collective-permute-start.8 = (bf16[4,8,32,1024]{3,2,1,0:T(8,128)(2,1)}, bf16[4,8,32,1024]{3,2,1,0:T(8,128)(2,1)}, u32[]{:S(2)}, u32[]{:S(2)}) collective-permute-start(bf16[4,8,32,1024]{3,2,1,0:T(8,128)(2,1)} %collective-permute-done.7.s1), channel_id=1, source_target_pairs={{0,1},{1,0},{2,3},{3,2},{4,5},{5,4},{6,7},{7,6},{8,9},{9,8},{10,11... | collective-permute-start | bytes 6291464 | tf_op jit(solution)/shard_map/ppermute | solution.py:266
  130.4 24.7 %collective-permute-start.13 = (bf16[16,72,128]{2,1,0:T(8,128)(2,1)S(1)}, bf16[16,72,128]{2,1,0:T(8,128)(2,1)S(1)}, u32[]{:S(2)}, u32[]{:S(2)}) collective-permute-start(bf16[16,72,128]{2,1,0:T(8,128)(2,1)S(1)} %get-tuple-element.34), channel_id=1, source_target_pairs={{0,64},{64,128},{128,192},{192,0},{1,65},{65,129},{129,193},{193,1... | collective-permute-start | bytes 884744 | tf_op jit(solution)/shard_map/ppermute | solution.py:227
  130.5 24.6 %collective-permute-start.14 = (bf16[16,72,128]{2,1,0:T(8,128)(2,1)S(1)}, bf16[16,72,128]{2,1,0:T(8,128)(2,1)S(1)}, u32[]{:S(2)}, u32[]{:S(2)}) collective-permute-start(bf16[16,72,128]{2,1,0:T(8,128)(2,1)S(1)} %get-tuple-element.35), channel_id=1, source_target_pairs={{0,128},{64,192},{128,0},{192,64},{1,129},{65,193},{129,1},{193,65... | collective-permute-start | bytes 884744 | tf_op jit(solution)/shard_map/ppermute | solution.py:227
  135.1 20.0 %collective-permute-start.15 = (bf16[16,72,128]{2,1,0:T(8,128)(2,1)S(1)}, bf16[16,72,128]{2,1,0:T(8,128)(2,1)S(1)}, u32[]{:S(2)}, u32[]{:S(2)}) collective-permute-start(bf16[16,72,128]{2,1,0:T(8,128)(2,1)S(1)} %get-tuple-element.36), channel_id=1, source_target_pairs={{0,192},{64,0},{128,64},{192,128},{1,193},{65,1},{129,65},{193,129... | collective-permute-start | bytes 884744 | tf_op jit(solution)/shard_map/ppermute | solution.py:227
  (7 other events, 22.4 us)

commit v10 on v5

--- a/solution.py
+++ b/solution.py
@@ -151,30 +151,89 @@
     lax.fori_loop(0, shards // per, pack, 0)
 
 
-def base_kernel(tok_ref, cot_ref, w_ref, at_ref, up_ref, hid_ref, back_ref, keys_ref, grad_ref, acc_ref):
-    step = pl.program_id(0)
-
-    @pl.when(step == 0)
-    def _():
-        acc_ref[...] = adapter_scale * lax.dot_general(
-            hid_ref[...], up_ref[...], TN, preferred_element_type=f32
-        )
-
-    weight = w_ref[...]
-    acc_ref[...] += jnp.dot(tok_ref[...], weight, preferred_element_type=f32)
-    grad = lax.dot_general(cot_ref[...], weight, NT, preferred_element_type=f32)
-    grad += adapter_scale * lax.dot_general(
-        back_ref[...], at_ref[...], TN, preferred_element_type=f32
-    )
-    grad_ref[...] = grad.astype(grad_ref.dtype)
-
-    @pl.when(step == pl.num_programs(0) - 1)
-    def _():
-        keys_ref[...] = acc_ref[...].astype(keys_ref.dtype)
+def join_kernel(x0, x1, x2, x3, o_ref, sems):
+    copies = [
+        pltpu.make_async_copy(x, o_ref.at[k], sems.at[k]) for k, x in enumerate((x0, x1, x2, x3))
+    ]
+    for copy in copies:
+        copy.start()
+    for copy in copies:
+        copy.wait()
+
+
+def fetch(place_ref, core, sources, w_ref, sems):
+    wide, _, groups = w_ref.shape[:3]
+    for a, source in enumerate(sources):
+        for b in range(source.shape[0]):
+            back_y = jnp.where(core == 0, b, a)
+            back_g = jnp.where(core == 0, a, b)
+            y = lax.rem(place_ref[1] - back_y + wide, wide)
+            g = lax.rem(place_ref[0] - back_g + groups, groups)
+            pltpu.make_async_copy(source.at[b], w_ref.at[y, core, g], sems.at[y, core, g]).start()
+
+
+def base_kernel(
+    place_ref, tok_ref, cot_ref, s0, s1, s2, s3, t0, t1, t2, t3, adapter_ref, keys_ref, out_ref,
+    w_ref, grad_ref, acc_ref, sems, out_sems,
+):
+    wide, cores, groups, deep, _, key_columns = w_ref.shape
+    rows, depth = tok_ref.shape
+    width = depth + key_columns
+    core = place_ref[2]
+    fetch(place_ref, core, (s0, s1, s2, s3), w_ref, sems)
+    fetch(place_ref, 1 - core, (t0, t1, t2, t3), w_ref, sems)
+    hidden = adapter_ref[:, width : width + rows]
+    back = adapter_ref[:, width + rows :]
+    up = adapter_ref[:, depth:width]
+    acc_ref[...] = adapter_scale * lax.dot_general(hidden, up, TN, preferred_element_type=f32)
+    halves = 2
+    span = depth // (wide * halves)
+    stores = []
+    for y in range(wide):
+        for c in range(cores):
+            for g in range(groups):
+                pltpu.make_async_copy(s0.at[0], w_ref.at[y, c, g], sems.at[y, c, g]).wait()
+        for h in range(halves):
+            at = slice((y * halves + h) * span, (y * halves + h + 1) * span)
+            weight = jnp.concatenate(
+                [
+                    w_ref[y, c, g, z]
+                    for z in range(h * deep // halves, (h + 1) * deep // halves)
+                    for c in range(cores)
+                    for g in range(groups)
+                ],
+                axis=0,
+            )
+            acc_ref[...] += jnp.dot(tok_ref[:, at], weight, preferred_element_type=f32)
+            grad = lax.dot_general(cot_ref[...], weight, NT, preferred_element_type=f32)
+            grad += adapter_scale * lax.dot_general(
+                back, adapter_ref[:, at], TN, preferred_element_type=f32
+            )
+            grad_ref[:, at] = grad.astype(grad_ref.dtype)
+            stores.append(
+                pltpu.make_async_copy(
+                    grad_ref.at[:, at], out_ref.at[:, at], out_sems.at[y * halves + h]
+                )
+            )
+            stores[-1].start()
+    keys_ref[...] = acc_ref[...].astype(keys_ref.dtype)
+    for store in stores:
+        store.wait()
 
 
 def shift(x, by, groups):
     return lax.ppermute(x, "grp", [(i, (i + by) % groups) for i in range(groups)])
+
+
+def route(x, by, groups, wide, first):
+    pairs = []
+    for g in range(groups):
+        for y in range(wide):
+            for c in range(2):
+                along_y = (c == 0) == first
+                to = (g, (y + by) % wide) if along_y else ((g + by) % groups, y)
+                pairs.append(((g * wide + y) * 2 + c, (to[0] * wide + to[1]) * 2 + c))
+    return lax.ppermute(x, ("grp", "y", "core"), pairs)
 
 
 def whole(memory=pltpu.VMEM):
@@ -190,9 +249,27 @@
     packed_rows = row_count * rank // LANES
     width = depth + key_columns
     group = lax.axis_index("grp").reshape(1).astype(jnp.int32)
+    place = jnp.stack([lax.axis_index("grp"), lax.axis_index("y"), lax.axis_index("core")])
+    place = place.astype(jnp.int32)
     jobs = tile_job.reshape(-1)
 
-    weight = lax.all_gather(frozen_weight, SEQ, axis=0, tiled=True)
+    quarter = TILE_ROWS // groups
+    wide, deep = lax.axis_size("y"), lax.axis_size("z")
+    mine = lax.dynamic_slice_in_dim(frozen_weight, lax.axis_index("grp") * quarter, quarter, 0)
+    column = lax.all_to_all(
+        jnp.broadcast_to(mine, (deep,) + mine.shape), "z", split_axis=0, concat_axis=0, tiled=True
+    )
+    line = pl.pallas_call(
+        join_kernel,
+        out_shape=jax.ShapeDtypeStruct((wide,) + column.shape, bf16),
+        in_specs=[whole(pl.ANY)] * wide,
+        out_specs=whole(pl.ANY),
+        scratch_shapes=[pltpu.SemaphoreType.DMA((wide,))],
+        compiler_params=params(),
+        name="join",
+    )(column, *[route(column, k, groups, wide, True) for k in range(1, wide)])
+    halves = [line] + [route(line, k, groups, wide, False) for k in range(1, groups)]
+    others = [lax.ppermute(x, "core", [(0, 1), (1, 0)]) for x in halves]
 
     own = pl.pallas_call(
         pack_kernel,
@@ -227,6 +304,7 @@
         name="tile",
     )(arrived, tokens, cotangent)
     incoming = lax.all_to_all(terms, SEQ, split_axis=0, concat_axis=0, tiled=True)
+    incoming, others[0] = lax.optimization_barrier((incoming, others[0]))
     sums = pl.pallas_call(
         sum_kernel,
         out_shape=(jax.ShapeDtypeStruct((slot_count, packed_rows, LANES), f32),)
@@ -237,8 +315,9 @@
         compiler_params=params(),
         name="sum",
     )(group, jobs, job_slot, incoming)
-    last, weight = lax.optimization_barrier((sums[-1], weight))
-    sums = tuple(sums[:-1]) + (last,)
+    kept, halves[0] = lax.optimization_barrier((sums[0], halves[0]))
+    last, others = lax.optimization_barrier((sums[-1], others))
+    sums = (kept,) + tuple(sums[1:-1]) + (last,)
     owned = (sums[0],) + tuple(shift(sums[k], k, groups) for k in range(1, groups))
     grads = pl.pallas_call(
         unpack_kernel,
@@ -249,37 +328,30 @@
         name="unpack",
     )(*owned)
 
-    block = 1024
-    steps = depth // block
+    blocks = (wide, 2, groups, deep, quarter, key_columns)
     keys, token_gradient = pl.pallas_call(
         base_kernel,
-        grid=(steps,),
         out_shape=(
             jax.ShapeDtypeStruct((rows, key_columns), bf16),
             jax.ShapeDtypeStruct((rows, depth), bf16),
         ),
-        in_specs=[
-            pl.BlockSpec((rows, block), lambda i: (0, i)),
-            pl.BlockSpec((rows, key_columns), lambda i: (0, 0)),
-            pl.BlockSpec((block, key_columns), lambda i: (i, 0)),
-            pl.BlockSpec((rank, block), lambda i: (0, i)),
-            pl.BlockSpec((rank, key_columns), lambda i: (0, depth // key_columns)),
-            pl.BlockSpec((rank, rows), lambda i: (0, width // rows)),
-            pl.BlockSpec((rank, rows), lambda i: (0, width // rows + 1)),
+        in_specs=[smem, whole(), whole()] + [whole(pltpu.HBM)] * (2 * groups) + [whole()],
+        out_specs=(whole(), whole(pltpu.HBM)),
+        scratch_shapes=[
+            pltpu.VMEM(blocks, bf16),
+            pltpu.VMEM((rows, depth), bf16),
+            pltpu.VMEM((rows, key_columns), f32),
+            pltpu.SemaphoreType.DMA(blocks[:3]),
+            pltpu.SemaphoreType.DMA((2 * wide,)),
         ],
-        out_specs=(
-            pl.BlockSpec((rows, key_columns), lambda i: (0, 0)),
-            pl.BlockSpec((rows, block), lambda i: (0, i)),
-        ),
-        scratch_shapes=[pltpu.VMEM((rows, key_columns), f32)],
-        compiler_params=params(56),
+        compiler_params=params(50),
         cost_estimate=pl.CostEstimate(
             flops=4 * rows * depth * key_columns,
             bytes_accessed=2 * depth * key_columns + 4 * rows * width,
             transcendentals=0,
         ),
         name="base",
-    )(tokens, cotangent, weight, adapter, adapter, adapter, adapter)
+    )(place, tokens, cotangent, *halves, *others, adapter)
     return keys, token_gradient, jnp.swapaxes(grads, 1, 2)
 
 

time: 171 us -> 205 us (1.20)
  blocking collectives: 96.8 us -> 0 us
  Pallas kernels: 21.5 us -> 89.3 us
  starting transfers between devices: 7.91 us -> 54.6 us
  waiting for transfers between devices: 27.6 us -> 53 us
  between operations: 14.1 us -> 0.83 us
  local copies, waits for them, and re-layouts: 2.4 us -> 7.02 us
    all_to_all x2 -> x0, blocking collectives: 96.8 us -> none  [the longest x1 50.9 us: on_device(): lax.all_to_all(terms, SEQ, split_axis=0, concat_axis=0, tiled=True)]
    pallas_call x1 -> x2, Pallas kernels: 14.5 us -> 81.3 us  [the longest x1 64.7 us: on_device(): pl.pallas_call(join_kernel, out_shape=jax.ShapeDtypeStruct((wide,) + colu...]
    ppermute x0 -> x10, waiting for transfers between devices: none -> 38.6 us  [the longest x6 37.8 us: route(): return lax.ppermute(x, ('grp', 'y', 'core'), pairs)]
    all_to_all x0 -> x3, starting transfers between devices: none -> 30.2 us  [the longest x1 10.7 us: on_device(): lax.all_to_all(outgoing, SEQ, split_axis=0, concat_axis=0, tiled=True)]
    ppermute x6, waiting for transfers between devices: 15.6 us -> 0.02 us  [shift(): lax.ppermute(x, 'grp', [(i, (i + by) % groups) for i in range(groups)])]
    all_to_all x0 -> x3, waiting for transfers between devices: none -> 14.4 us  [the longest x1 14.2 us: on_device(): lax.all_to_all(jnp.broadcast_to(mine, (deep,) + mine.shape), 'z', split_a...]
    ppermute x0 -> x10, starting transfers between devices: none -> 12.6 us  [the longest x6 9.95 us: route(): return lax.ppermute(x, ('grp', 'y', 'core'), pairs)]
    all_gather x1 -> x0, waiting for transfers between devices: 11.3 us -> none  [on_device(): weight = lax.all_gather(frozen_weight, SEQ, axis=0, tiled=True)]
  transfers between devices with their start and end apart: 7 -> 19, of which waited for: 4 -> 5; matrix products, arithmetic and copies ran while one was open for 0% -> 0% of each run, Pallas kernels for 12% -> 43%
where the time goes in v10:
time: 205 us
  Pallas kernels  89.3 us (44%)
  starting transfers between devices  54.6 us (27%)
  waiting for transfers between devices  53 us (26%)
  local copies, waits for them, and re-layouts  7.02 us (3%)
    pallas_call x1, Pallas kernels, on_device(): pl.pallas_call(join_kernel, out_shape=jax.ShapeDtypeStruct((wide,) + colu...  64.7 us
    ppermute x6, waiting for transfers between devices, route(): return lax.ppermute(x, ('grp', 'y', 'core'), pairs)  37.8 us
    pallas_call x1, Pallas kernels, on_device(): pl.pallas_call(base_kernel, out_shape=(jax.ShapeDtypeStruct((rows, key_co...  16.6 us
    all_to_all x1, waiting for transfers between devices, on_device(): lax.all_to_all(jnp.broadcast_to(mine, (deep,) + mine.shape), 'z', split_a...  14.2 us
    ppermute x6, starting transfers between devices, shift(): lax.ppermute(x, 'grp', [(i, (i + by) % groups) for i in range(groups)])  11.8 us
    all_to_all x1, starting transfers between devices, on_device(): lax.all_to_all(outgoing, SEQ, split_axis=0, concat_axis=0, tiled=True)  10.7 us
    all_to_all x1, starting transfers between devices, on_device(): lax.all_to_all(terms, SEQ, split_axis=0, concat_axis=0, tiled=True)  10.4 us
    ppermute x6, starting transfers between devices, route(): return lax.ppermute(x, ('grp', 'y', 'core'), pairs)  9.95 us
  transfers between devices with their start and end apart: 19, of which 5 were waited for; matrix products, arithmetic and copies ran while one was open for 0% of the time, Pallas kernels for 43%

profile of v10, /device:TPU:1, one launch (start us, length us, event | category | flops | bytes accessed | tf_op | source)
XLA Modules:
  0.0 204.8 jit_solution(3419398498712740631)
XLA Ops:
  2.4 9.0 %all-to-all-start.2 = ((bf16[8,32,1024]{2,1,0:T(8,128)(2,1)}), bf16[8,32,1024]{2,1,0:T(8,128)(2,1)}, u32[]{:S(2)}, u32[]{:S(2)}) async-start(bf16[8,32,1024]{2,1,0:T(8,128)(2,1)} %broadcast_in_dim.3), calls=%async_computation.2 | async-start | bytes 1048576 | tf_op jit(solution)/shard_map/all_to_all | solution.py:259
  11.6 2.6 %collective-permute-start = (bf16[16,72,128]{2,1,0:T(8,128)(2,1)S(1)}, bf16[16,72,128]{2,1,0:T(8,128)(2,1)S(1)}, u32[]{:S(2)}, u32[]{:S(2)}) collective-permute-start(bf16[16,72,128]{2,1,0:T(8,128)(2,1)S(1)} %pack.1.refs_0_), channel_id=1, source_target_pairs={{0,192},{64,0},{128,64},{192,128},{1,193},{65,1},{129,65},{193,129... | collective-permute-start | bytes 884744 | tf_op jit(solution)/shard_map/ppermute | solution.py:225
  15.3 14.2 %all-to-all-done.2.x0 = bf16[8,32,1024]{2,1,0:T(8,128)(2,1)} async-done(((bf16[8,32,1024]{2,1,0:T(8,128)(2,1)}), bf16[8,32,1024]{2,1,0:T(8,128)(2,1)}, u32[]{:S(2)}, u32[]{:S(2)}) %all-to-all-start.2) | async-done | bytes 524320 | tf_op jit(solution)/shard_map/all_to_all | solution.py:259
  29.5 1.2 collective-permute-start.3
  30.7 2.5 %collective-permute-start.4 = (bf16[8,32,1024]{2,1,0:T(8,128)(2,1)}, bf16[8,32,1024]{2,1,0:T(8,128)(2,1)}, u32[]{:S(2)}, u32[]{:S(2)}) collective-permute-start(bf16[8,32,1024]{2,1,0:T(8,128)(2,1)} %all-to-all-done.2.x0), channel_id=1, source_target_pairs={{0,32},{1,129},{16,48},{17,145},{32,0},{33,161},{48,16},{49,177},{... | collective-permute-start | bytes 1572872 | tf_op jit(solution)/shard_map/ppermute | solution.py:236
  33.2 1.2 collective-permute-start.5
  34.4 1.9 pick.1
  36.3 10.7 %all-to-all-start = ((bf16[64,72,128]{2,1,0:T(8,128)(2,1)}), bf16[64,72,128]{2,1,0:T(8,128)(2,1)S(1)}, u32[]{:S(2)}, u32[]{:S(2)}) async-start(bf16[64,72,128]{2,1,0:T(8,128)(2,1)} %pick.1), calls=%async_computation | async-start | bytes 2359296 | tf_op jit(solution)/shard_map/all_to_all | solution.py:293
  47.1 64.7 %join.1.s0 = bf16[4,8,32,1024]{3,2,1,0:T(8,128)(2,1)} custom-call(bf16[8,32,1024]{2,1,0:T(8,128)(2,1)} %all-to-all-done.2.x0, bf16[8,32,1024]{2,1,0:T(8,128)(2,1)} %collective-permute-done.3.x1, bf16[8,32,1024]{2,1,0:T(8,128)(2,1)} %collective-permute-done.4.x2, bf16[8,32,1024]{2,1,0:T(8,128)(2,1)} %collective-permute-done.5.x3), custom_call_target="tpu_custom_call" | custom-call | tf_op jit(solution)/shard_map/join/pallas_call | solution.py:262
  111.7 1.5 collective-permute-start.7
  113.2 2.6 %collective-permute-start.8 = (bf16[4,8,32,1024]{3,2,1,0:T(8,128)(2,1)}, bf16[4,8,32,1024]{3,2,1,0:T(8,128)(2,1)}, u32[]{:S(2)}, u32[]{:S(2)}) collective-permute-start(bf16[4,8,32,1024]{3,2,1,0:T(8,128)(2,1)} %join.1.s0), channel_id=1, source_target_pairs={{0,128},{1,33},{16,144},{17,49},{32,160},{33,1},{48,176},{49,17},{... | collective-permute-start | bytes 6291464 | tf_op jit(solution)/shard_map/ppermute | solution.py:236
  115.8 1.1 collective-permute-start.9
  117.8 3.6 %tile.1 = (bf16[64,72,128]{2,1,0:T(8,128)(2,1)S(1)}, bf16[64,9472]{1,0:T(8,128)(2,1)S(1)}) custom-call(bf16[64,72,128]{2,1,0:T(8,128)(2,1)S(1)} %all-to-all-done.x_ref, bf16[128,8192]{1,0:T(8,128)(2,1)S(1)} %copy-done.1, bf16[128,1024]{1,0:T(8,128)(2,1)S(1)} %copy-done.5), custom_call_target="tpu_custom_call" | custom-call | tf_op jit(solution)/shard_map/tile/pallas_call | solution.py:294
  122.4 1.0 copy-done.4
  123.5 10.4 %all-to-all-start.1 = ((bf16[64,72,128]{2,1,0:T(8,128)(2,1)}), bf16[64,72,128]{2,1,0:T(8,128)(2,1)S(1)}, u32[]{:S(2)}, u32[]{:S(2)}) async-start(bf16[64,72,128]{2,1,0:T(8,128)(2,1)} %copy-done.4), calls=%async_computation.1 | async-start | bytes 2359296 | tf_op jit(solution)/shard_map/all_to_all | solution.py:306
  134.4 4.2 %collective-permute-done.7.s1 = bf16[4,8,32,1024]{3,2,1,0:T(8,128)(2,1)} collective-permute-done((bf16[4,8,32,1024]{3,2,1,0:T(8,128)(2,1)}, bf16[4,8,32,1024]{3,2,1,0:T(8,128)(2,1)}, u32[]{:S(2)}, u32[]{:S(2)}) %collective-permute-start.7) | collective-permute-done | bytes 2097184 | tf_op jit(solution)/shard_map/ppermute | solution.py:236
  138.7 1.6 collective-permute-start.10
  140.3 33.6 %collective-permute-done.8.s2 = bf16[4,8,32,1024]{3,2,1,0:T(8,128)(2,1)} collective-permute-done((bf16[4,8,32,1024]{3,2,1,0:T(8,128)(2,1)}, bf16[4,8,32,1024]{3,2,1,0:T(8,128)(2,1)}, u32[]{:S(2)}, u32[]{:S(2)}) %collective-permute-start.8) | collective-permute-done | bytes 2097184 | tf_op jit(solution)/shard_map/ppermute | solution.py:236
  174.6 1.3 sum.1
  176.0 4.6 %collective-permute-start.14 = (bf16[16,72,128]{2,1,0:T(8,128)(2,1)S(1)}, bf16[16,72,128]{2,1,0:T(8,128)(2,1)S(1)}, u32[]{:S(2)}, u32[]{:S(2)}) collective-permute-start(bf16[16,72,128]{2,1,0:T(8,128)(2,1)S(1)} %get-tuple-element.35), channel_id=1, source_target_pairs={{0,128},{64,192},{128,0},{192,64},{1,129},{65,193},{129,1},{193,65... | collective-permute-start | bytes 884744 | tf_op jit(solution)/shard_map/ppermute | solution.py:225
  181.4 3.4 %collective-permute-start.15 = (bf16[16,72,128]{2,1,0:T(8,128)(2,1)S(1)}, bf16[16,72,128]{2,1,0:T(8,128)(2,1)S(1)}, u32[]{:S(2)}, u32[]{:S(2)}) collective-permute-start(bf16[16,72,128]{2,1,0:T(8,128)(2,1)S(1)} %get-tuple-element.36), channel_id=1, source_target_pairs={{0,192},{64,0},{128,64},{192,128},{1,193},{65,1},{129,65},{193,129... | collective-permute-start | bytes 884744 | tf_op jit(solution)/shard_map/ppermute | solution.py:225
  184.8 1.3 copy-done.3
  187.0 16.6 %base.1 = (bf16[128,1024]{1,0:T(8,128)(2,1)}, bf16[128,8192]{1,0:T(8,128)(2,1)}) custom-call(s32[3]{0:T(128)S(1)} %pad_add_fusion.place_ref, bf16[128,8192]{1,0:T(8,128)(2,1)S(1)} %copy-done.1, bf16[128,1024]{1,0:T(8,128)(2,1)S(1)} %copy-done.6, bf16[4,8,32,1024]{3,2,1,0:T(8,128)(2,1)} %join.1.s0, bf16[4,8,32,1024]{3,2,1,0:T(8,128)(2,1)} %collective-permute-done.7.s1, ...), custom_call_target="tpu_custom_call" | custom-call | flops 4294967296 | bytes 21495808 | tf_op jit(solution)/shard_map/base/pallas_call | solution.py:332
  203.6 1.2 unpack.1
  (44 shorter events, 8.2 us)
Async XLA Ops:
  0.6 10.8 %copy-start.7 = (bf16[16,144,64]{1,2,0:T(8,128)(2,1)S(1)}, bf16[16,144,64]{1,2,0:T(8,128)(2,1)}, u32[]{:S(2)}) copy-start(bf16[16,144,64]{1,2,0:T(8,128)(2,1)} %param.9) | copy-start | bytes 884740
  0.7 33.7 %copy-start.8 = (s32[256,1]{0,1:T(1,128)S(1)}, s32[256,1]{0,1:T(1,128)}, u32[]{:S(2)}) copy-start(s32[256,1]{0,1:T(1,128)} %param.10) | copy-start | bytes 3076
  0.7 33.7 %copy-start.9 = (s32[64]{0:T(128)S(1)}, s32[64]{0:T(128)}, u32[]{:S(2)}) copy-start(s32[64]{0:T(128)} %slot_ref.3) | copy-start | bytes 772
  2.4 27.1 %all-to-all-start.2 = ((bf16[8,32,1024]{2,1,0:T(8,128)(2,1)}), bf16[8,32,1024]{2,1,0:T(8,128)(2,1)}, u32[]{:S(2)}, u32[]{:S(2)}) async-start(bf16[8,32,1024]{2,1,0:T(8,128)(2,1)} %broadcast_in_dim.3), calls=%async_computation.2 | async-start | bytes 1048576 | tf_op jit(solution)/shard_map/all_to_all | solution.py:259
  11.6 21.6 %collective-permute-start = (bf16[16,72,128]{2,1,0:T(8,128)(2,1)S(1)}, bf16[16,72,128]{2,1,0:T(8,128)(2,1)S(1)}, u32[]{:S(2)}, u32[]{:S(2)}) collective-permute-start(bf16[16,72,128]{2,1,0:T(8,128)(2,1)S(1)} %pack.1.refs_0_), channel_id=1, source_target_pairs={{0,192},{64,0},{128,64},{192,128},{1,193},{65,1},{129,65},{193,129... | collective-permute-start | bytes 884744 | tf_op jit(solution)/shard_map/ppermute | solution.py:225
  14.2 20.2 %collective-permute-start.1 = (bf16[16,72,128]{2,1,0:T(8,128)(2,1)S(1)}, bf16[16,72,128]{2,1,0:T(8,128)(2,1)S(1)}, u32[]{:S(2)}, u32[]{:S(2)}) collective-permute-start(bf16[16,72,128]{2,1,0:T(8,128)(2,1)S(1)} %pack.1.refs_0_), channel_id=1, source_target_pairs={{0,128},{64,192},{128,0},{192,64},{1,129},{65,193},{129,1},{193,65... | collective-permute-start | bytes 884744 | tf_op jit(solution)/shard_map/ppermute | solution.py:225
  14.7 19.7 %collective-permute-start.2 = (bf16[16,72,128]{2,1,0:T(8,128)(2,1)S(1)}, bf16[16,72,128]{2,1,0:T(8,128)(2,1)S(1)}, u32[]{:S(2)}, u32[]{:S(2)}) collective-permute-start(bf16[16,72,128]{2,1,0:T(8,128)(2,1)S(1)} %pack.1.refs_0_), channel_id=1, source_target_pairs={{0,64},{64,128},{128,192},{192,0},{1,65},{65,129},{129,193},{193,1... | collective-permute-start | bytes 884744 | tf_op jit(solution)/shard_map/ppermute | solution.py:225
  29.5 17.5 %collective-permute-start.3 = (bf16[8,32,1024]{2,1,0:T(8,128)(2,1)}, bf16[8,32,1024]{2,1,0:T(8,128)(2,1)}, u32[]{:S(2)}, u32[]{:S(2)}) collective-permute-start(bf16[8,32,1024]{2,1,0:T(8,128)(2,1)} %all-to-all-done.2.x0), channel_id=1, source_target_pairs={{0,16},{1,65},{16,32},{17,81},{32,48},{33,97},{48,0},{49,113},{64,... | collective-permute-start | bytes 1572872 | tf_op jit(solution)/shard_map/ppermute | solution.py:236
  30.7 16.3 %collective-permute-start.4 = (bf16[8,32,1024]{2,1,0:T(8,128)(2,1)}, bf16[8,32,1024]{2,1,0:T(8,128)(2,1)}, u32[]{:S(2)}, u32[]{:S(2)}) collective-permute-start(bf16[8,32,1024]{2,1,0:T(8,128)(2,1)} %all-to-all-done.2.x0), channel_id=1, source_target_pairs={{0,32},{1,129},{16,48},{17,145},{32,0},{33,161},{48,16},{49,177},{... | collective-permute-start | bytes 1572872 | tf_op jit(solution)/shard_map/ppermute | solution.py:236
  33.2 13.9 %collective-permute-start.5 = (bf16[8,32,1024]{2,1,0:T(8,128)(2,1)}, bf16[8,32,1024]{2,1,0:T(8,128)(2,1)}, u32[]{:S(2)}, u32[]{:S(2)}) collective-permute-start(bf16[8,32,1024]{2,1,0:T(8,128)(2,1)} %all-to-all-done.2.x0), channel_id=1, source_target_pairs={{0,48},{1,193},{16,0},{17,209},{32,16},{33,225},{48,32},{49,241},{... | collective-permute-start | bytes 1572872 | tf_op jit(solution)/shard_map/ppermute | solution.py:236
  36.3 80.6 %all-to-all-start = ((bf16[64,72,128]{2,1,0:T(8,128)(2,1)}), bf16[64,72,128]{2,1,0:T(8,128)(2,1)S(1)}, u32[]{:S(2)}, u32[]{:S(2)}) async-start(bf16[64,72,128]{2,1,0:T(8,128)(2,1)} %pick.1), calls=%async_computation | async-start | bytes 2359296 | tf_op jit(solution)/shard_map/all_to_all | solution.py:293
  47.0 69.9 %copy-start.1 = (bf16[128,8192]{1,0:T(8,128)(2,1)S(1)}, bf16[128,8192]{1,0:T(8,128)(2,1)}, u32[]{:S(2)}) copy-start(bf16[128,8192]{1,0:T(8,128)(2,1)} %tok_ref.3) | copy-start | bytes 6291460
  111.7 26.9 %collective-permute-start.7 = (bf16[4,8,32,1024]{3,2,1,0:T(8,128)(2,1)}, bf16[4,8,32,1024]{3,2,1,0:T(8,128)(2,1)}, u32[]{:S(2)}, u32[]{:S(2)}) collective-permute-start(bf16[4,8,32,1024]{3,2,1,0:T(8,128)(2,1)} %join.1.s0), channel_id=1, source_target_pairs={{0,64},{1,17},{16,80},{17,33},{32,96},{33,49},{48,112},{49,1},{64,... | collective-permute-start | bytes 6291464 | tf_op jit(solution)/shard_map/ppermute | solution.py:236
  113.2 60.6 %collective-permute-start.8 = (bf16[4,8,32,1024]{3,2,1,0:T(8,128)(2,1)}, bf16[4,8,32,1024]{3,2,1,0:T(8,128)(2,1)}, u32[]{:S(2)}, u32[]{:S(2)}) collective-permute-start(bf16[4,8,32,1024]{3,2,1,0:T(8,128)(2,1)} %join.1.s0), channel_id=1, source_target_pairs={{0,128},{1,33},{16,144},{17,49},{32,160},{33,1},{48,176},{49,17},{... | collective-permute-start | bytes 6291464 | tf_op jit(solution)/shard_map/ppermute | solution.py:236
  115.8 58.1 %collective-permute-start.9 = (bf16[4,8,32,1024]{3,2,1,0:T(8,128)(2,1)}, bf16[4,8,32,1024]{3,2,1,0:T(8,128)(2,1)}, u32[]{:S(2)}, u32[]{:S(2)}) collective-permute-start(bf16[4,8,32,1024]{3,2,1,0:T(8,128)(2,1)} %join.1.s0), channel_id=1, source_target_pairs={{0,192},{1,49},{16,208},{17,1},{32,224},{33,17},{48,240},{49,33},{... | collective-permute-start | bytes 6291464 | tf_op jit(solution)/shard_map/ppermute | solution.py:236
  123.5 51.2 %all-to-all-start.1 = ((bf16[64,72,128]{2,1,0:T(8,128)(2,1)}), bf16[64,72,128]{2,1,0:T(8,128)(2,1)S(1)}, u32[]{:S(2)}, u32[]{:S(2)}) async-start(bf16[64,72,128]{2,1,0:T(8,128)(2,1)} %copy-done.4), calls=%async_computation.1 | async-start | bytes 2359296 | tf_op jit(solution)/shard_map/all_to_all | solution.py:306
  133.9 40.5 %collective-permute-start.6 = (bf16[4,8,32,1024]{3,2,1,0:T(8,128)(2,1)}, bf16[4,8,32,1024]{3,2,1,0:T(8,128)(2,1)}, u32[]{:S(2)}, u32[]{:S(2)}) collective-permute-start(bf16[4,8,32,1024]{3,2,1,0:T(8,128)(2,1)} %join.1.s0), channel_id=1, source_target_pairs={{0,1},{1,0},{2,3},{3,2},{4,5},{5,4},{6,7},{7,6},{8,9},{9,8},{10,11... | collective-permute-start | bytes 6291464 | tf_op jit(solution)/shard_map/ppermute | solution.py:272
  138.7 41.9 %collective-permute-start.10 = (bf16[4,8,32,1024]{3,2,1,0:T(8,128)(2,1)}, bf16[4,8,32,1024]{3,2,1,0:T(8,128)(2,1)}, u32[]{:S(2)}, u32[]{:S(2)}) collective-permute-start(bf16[4,8,32,1024]{3,2,1,0:T(8,128)(2,1)} %collective-permute-done.7.s1), channel_id=1, source_target_pairs={{0,1},{1,0},{2,3},{3,2},{4,5},{5,4},{6,7},{7,6},{8,9},{9,8},{10,11... | collective-permute-start | bytes 6291464 | tf_op jit(solution)/shard_map/ppermute | solution.py:272
  173.9 6.7 %collective-permute-start.11 = (bf16[4,8,32,1024]{3,2,1,0:T(8,128)(2,1)}, bf16[4,8,32,1024]{3,2,1,0:T(8,128)(2,1)}, u32[]{:S(2)}, u32[]{:S(2)}) collective-permute-start(bf16[4,8,32,1024]{3,2,1,0:T(8,128)(2,1)} %collective-permute-done.8.s2), channel_id=1, source_target_pairs={{0,1},{1,0},{2,3},{3,2},{4,5},{5,4},{6,7},{7,6},{8,9},{9,8},{10,11... | collective-permute-start | bytes 6291464 | tf_op jit(solution)/shard_map/ppermute | solution.py:272
  173.9 7.5 %collective-permute-start.12 = (bf16[4,8,32,1024]{3,2,1,0:T(8,128)(2,1)}, bf16[4,8,32,1024]{3,2,1,0:T(8,128)(2,1)}, u32[]{:S(2)}, u32[]{:S(2)}) collective-permute-start(bf16[4,8,32,1024]{3,2,1,0:T(8,128)(2,1)} %collective-permute-done.9.s3), channel_id=1, source_target_pairs={{0,1},{1,0},{2,3},{3,2},{4,5},{5,4},{6,7},{7,6},{8,9},{9,8},{10,11... | collective-permute-start | bytes 6291464 | tf_op jit(solution)/shard_map/ppermute | solution.py:272
  175.9 27.7 %collective-permute-start.13 = (bf16[16,72,128]{2,1,0:T(8,128)(2,1)S(1)}, bf16[16,72,128]{2,1,0:T(8,128)(2,1)S(1)}, u32[]{:S(2)}, u32[]{:S(2)}) collective-permute-start(bf16[16,72,128]{2,1,0:T(8,128)(2,1)S(1)} %get-tuple-element.34), channel_id=1, source_target_pairs={{0,64},{64,128},{128,192},{192,0},{1,65},{65,129},{129,193},{193,1... | collective-permute-start | bytes 884744 | tf_op jit(solution)/shard_map/ppermute | solution.py:225
  176.0 27.6 %collective-permute-start.14 = (bf16[16,72,128]{2,1,0:T(8,128)(2,1)S(1)}, bf16[16,72,128]{2,1,0:T(8,128)(2,1)S(1)}, u32[]{:S(2)}, u32[]{:S(2)}) collective-permute-start(bf16[16,72,128]{2,1,0:T(8,128)(2,1)S(1)} %get-tuple-element.35), channel_id=1, source_target_pairs={{0,128},{64,192},{128,0},{192,64},{1,129},{65,193},{129,1},{193,65... | collective-permute-start | bytes 884744 | tf_op jit(solution)/shard_map/ppermute | solution.py:225
  181.4 22.3 %collective-permute-start.15 = (bf16[16,72,128]{2,1,0:T(8,128)(2,1)S(1)}, bf16[16,72,128]{2,1,0:T(8,128)(2,1)S(1)}, u32[]{:S(2)}, u32[]{:S(2)}) collective-permute-start(bf16[16,72,128]{2,1,0:T(8,128)(2,1)S(1)} %get-tuple-element.36), channel_id=1, source_target_pairs={{0,192},{64,0},{128,64},{192,128},{1,193},{65,1},{129,65},{193,129... | collective-permute-start | bytes 884744 | tf_op jit(solution)/shard_map/ppermute | solution.py:225
  184.8 1.3 copy-start.3
  (5 other events, 4.9 us)

commit v11 on v10

--- a/solution.py
+++ b/solution.py
@@ -73,7 +73,7 @@
             o_ref[s, 8 * b : 8 * b + 8, LANES:] = rest[:, tail * b : tail * (b + 1)]
 
 
-def tile_kernel(x_ref, tok_ref, cot_ref, terms_ref, at_ref, t_ref):
+def tile_kernel(x_ref, tok_ref, cot_ref, terms_out, at_out, t_ref, terms_ref, at_ref, sems):
     shards, _, _ = x_ref.shape
     rank = at_ref.shape[0]
     depth = tok_ref.shape[1]
@@ -125,6 +125,8 @@
     ).astype(bf16)
     at_ref[:, width : width + LANES] = hidden
     at_ref[:, width + LANES :] = back
+    at_copy = pltpu.make_async_copy(at_ref, at_out, sems.at[0])
+    at_copy.start()
     t_ref[:, :depth] = adapter_scale * jnp.dot(back, tok, preferred_element_type=f32)
     t_ref[:, depth:] = adapter_scale * jnp.dot(hidden, cot, preferred_element_type=f32)
 
@@ -148,7 +150,14 @@
             )
         return carry
 
-    lax.fori_loop(0, shards // per, pack, 0)
+    for a in range(shards // per):
+        pack(a, 0)
+        piece = slice(a * per, (a + 1) * per)
+        pltpu.make_async_copy(terms_ref.at[piece], terms_out.at[piece], sems.at[a + 1]).start()
+    for a in range(shards // per):
+        piece = slice(a * per, (a + 1) * per)
+        pltpu.make_async_copy(terms_ref.at[piece], terms_out.at[piece], sems.at[a + 1]).wait()
+    at_copy.wait()
 
 
 def join_kernel(x0, x1, x2, x3, o_ref, sems):
@@ -161,27 +170,41 @@
         copy.wait()
 
 
-def fetch(place_ref, core, sources, w_ref, sems):
-    wide, _, groups = w_ref.shape[:3]
-    for a, source in enumerate(sources):
-        for b in range(source.shape[0]):
-            back_y = jnp.where(core == 0, b, a)
-            back_g = jnp.where(core == 0, a, b)
-            y = lax.rem(place_ref[1] - back_y + wide, wide)
-            g = lax.rem(place_ref[0] - back_g + groups, groups)
-            pltpu.make_async_copy(source.at[b], w_ref.at[y, core, g], sems.at[y, core, g]).start()
-
-
 def base_kernel(
-    place_ref, tok_ref, cot_ref, s0, s1, s2, s3, t0, t1, t2, t3, adapter_ref, keys_ref, out_ref,
-    w_ref, grad_ref, acc_ref, sems, out_sems,
+    place_ref, tok_ref, cot_in, s0, s1, s2, s3, t0, t1, t2, t3, adapter_in, keys_ref, out_ref,
+    w_ref, grad_ref, acc_ref, cot_ref, adapter_ref, sems, out_sems, in_sems,
 ):
     wide, cores, groups, deep, _, key_columns = w_ref.shape
     rows, depth = tok_ref.shape
     width = depth + key_columns
     core = place_ref[2]
-    fetch(place_ref, core, (s0, s1, s2, s3), w_ref, sems)
-    fetch(place_ref, 1 - core, (t0, t1, t2, t3), w_ref, sems)
+    inputs = [
+        pltpu.make_async_copy(cot_in, cot_ref, in_sems.at[0]),
+        pltpu.make_async_copy(adapter_in, adapter_ref, in_sems.at[1]),
+    ]
+    for copy in inputs:
+        copy.start()
+
+    def fetch(source, back, c, k):
+        g = lax.rem(place_ref[0] - k + groups, groups)
+        pltpu.make_async_copy(source, w_ref.at[back, c, g], sems.at[back, c, g]).start()
+
+    def fetch_all(along_y_first, along_y_second):
+        for back in range(wide):
+            for k in range(groups):
+                fetch(along_y_first[k].at[back], back, 0, k)
+                fetch(along_y_second[back].at[k], back, 1, k)
+
+    @pl.when(core == 0)
+    def _():
+        fetch_all((s0, s1, s2, s3), (t0, t1, t2, t3))
+
+    @pl.when(core == 1)
+    def _():
+        fetch_all((t0, t1, t2, t3), (s0, s1, s2, s3))
+
+    for copy in inputs:
+        copy.wait()
     hidden = adapter_ref[:, width : width + rows]
     back = adapter_ref[:, width + rows :]
     up = adapter_ref[:, depth:width]
@@ -189,15 +212,16 @@
     halves = 2
     span = depth // (wide * halves)
     stores = []
-    for y in range(wide):
+    for step in range(wide):
+        y = lax.rem(place_ref[1] - step + wide, wide)
         for c in range(cores):
             for g in range(groups):
-                pltpu.make_async_copy(s0.at[0], w_ref.at[y, c, g], sems.at[y, c, g]).wait()
+                pltpu.make_async_copy(s0.at[0], w_ref.at[step, c, g], sems.at[step, c, g]).wait()
         for h in range(halves):
-            at = slice((y * halves + h) * span, (y * halves + h + 1) * span)
+            at = pl.ds(pl.multiple_of((y * halves + h) * span, span), span)
             weight = jnp.concatenate(
                 [
-                    w_ref[y, c, g, z]
+                    w_ref[step, c, g, z]
                     for z in range(h * deep // halves, (h + 1) * deep // halves)
                     for c in range(cores)
                     for g in range(groups)
@@ -210,12 +234,11 @@
                 back, adapter_ref[:, at], TN, preferred_element_type=f32
             )
             grad_ref[:, at] = grad.astype(grad_ref.dtype)
-            stores.append(
-                pltpu.make_async_copy(
-                    grad_ref.at[:, at], out_ref.at[:, at], out_sems.at[y * halves + h]
-                )
+            store = pltpu.make_async_copy(
+                grad_ref.at[:, at], out_ref.at[:, at], out_sems.at[step * halves + h]
             )
-            stores[-1].start()
+            store.start()
+            stores.append(store)
     keys_ref[...] = acc_ref[...].astype(keys_ref.dtype)
     for store in stores:
         store.wait()
@@ -262,8 +285,8 @@
     line = pl.pallas_call(
         join_kernel,
         out_shape=jax.ShapeDtypeStruct((wide,) + column.shape, bf16),
-        in_specs=[whole(pl.ANY)] * wide,
-        out_specs=whole(pl.ANY),
+        in_specs=[whole()] * wide,
+        out_specs=whole(pltpu.HBM),
         scratch_shapes=[pltpu.SemaphoreType.DMA((wide,))],
         compiler_params=params(),
         name="join",
@@ -298,9 +321,14 @@
             jax.ShapeDtypeStruct((rank, width + 2 * rows), bf16),
         ),
         in_specs=[whole()] * 3,
-        out_specs=(whole(),) * 2,
-        scratch_shapes=[pltpu.VMEM((rank, width), f32)],
-        compiler_params=params(),
+        out_specs=(whole(pltpu.HBM),) * 2,
+        scratch_shapes=[
+            pltpu.VMEM((rank, width), f32),
+            pltpu.VMEM((shards, packed_rows, LANES), bf16),
+            pltpu.VMEM((rank, width + 2 * rows), bf16),
+            pltpu.SemaphoreType.DMA((shards + 1,)),
+        ],
+        compiler_params=params(32),
         name="tile",
     )(arrived, tokens, cotangent)
     incoming = lax.all_to_all(terms, SEQ, split_axis=0, concat_axis=0, tiled=True)
@@ -335,16 +363,19 @@
             jax.ShapeDtypeStruct((rows, key_columns), bf16),
             jax.ShapeDtypeStruct((rows, depth), bf16),
         ),
-        in_specs=[smem, whole(), whole()] + [whole(pltpu.HBM)] * (2 * groups) + [whole()],
+        in_specs=[smem, whole()] + [whole(pltpu.HBM)] * (2 * groups + 2),
         out_specs=(whole(), whole(pltpu.HBM)),
         scratch_shapes=[
             pltpu.VMEM(blocks, bf16),
             pltpu.VMEM((rows, depth), bf16),
             pltpu.VMEM((rows, key_columns), f32),
+            pltpu.VMEM((rows, key_columns), bf16),
+            pltpu.VMEM((rank, width + 2 * rows), bf16),
             pltpu.SemaphoreType.DMA(blocks[:3]),
             pltpu.SemaphoreType.DMA((2 * wide,)),
+            pltpu.SemaphoreType.DMA((2,)),
         ],
-        compiler_params=params(50),
+        compiler_params=params(58),
         cost_estimate=pl.CostEstimate(
             flops=4 * rows * depth * key_columns,
             bytes_accessed=2 * depth * key_columns + 4 * rows * width,

time: 205 us -> 149 us (0.73)
  Pallas kernels: 89.3 us -> 28.5 us
  waiting for transfers between devices: 53 us -> 66.8 us
  starting transfers between devices: 54.6 us -> 47 us
  local copies, waits for them, and re-layouts: 7.02 us -> 4.79 us
    pallas_call x1, Pallas kernels: 64.7 us -> 3.05 us  [on_device(): pl.pallas_call(join_kernel, out_shape=jax.ShapeDtypeStruct((wide,) + colu...]
    all_to_all x1, waiting for transfers between devices: 0.01 us -> 23.1 us  [on_device(): lax.all_to_all(outgoing, SEQ, split_axis=0, concat_axis=0, tiled=True)]
    ppermute x6, waiting for transfers between devices: 37.8 us -> 26.9 us  [route(): return lax.ppermute(x, ('grp', 'y', 'core'), pairs)]
    all_to_all x1, starting transfers between devices: 10.4 us -> 6.28 us  [on_device(): lax.all_to_all(terms, SEQ, split_axis=0, concat_axis=0, tiled=True)]
    pallas_call x1, Pallas kernels: 3.58 us -> 6.14 us  [on_device(): pl.pallas_call(tile_kernel, out_shape=(jax.ShapeDtypeStruct((shards, pack...]
    all_to_all x1, waiting for transfers between devices: 0.19 us -> 2.55 us  [on_device(): lax.all_to_all(terms, SEQ, split_axis=0, concat_axis=0, tiled=True)]
    unnamed x20 -> x18, local copies, waits for them, and re-layouts: 6.16 us -> 3.93 us
    ppermute x6, starting transfers between devices: 11.8 us -> 9.64 us  [shift(): lax.ppermute(x, 'grp', [(i, (i + by) % groups) for i in range(groups)])]
  transfers between devices with their start and end apart: 19 -> 19, of which waited for: 5 -> 4; matrix products, arithmetic and copies ran while one was open for 0% -> 0% of each run, Pallas kernels for 43% -> 18%
where the time goes in v11:
time: 149 us
  waiting for transfers between devices  66.8 us (45%)
  starting transfers between devices  47 us (32%)
  Pallas kernels  28.5 us (19%)
  local copies, waits for them, and re-layouts  4.79 us (3%)
    ppermute x6, waiting for transfers between devices, route(): return lax.ppermute(x, ('grp', 'y', 'core'), pairs)  26.9 us
    all_to_all x1, waiting for transfers between devices, on_device(): lax.all_to_all(outgoing, SEQ, split_axis=0, concat_axis=0, tiled=True)  23.1 us
    pallas_call x1, Pallas kernels, on_device(): pl.pallas_call(base_kernel, out_shape=(jax.ShapeDtypeStruct((rows, key_co...  14.9 us
    all_to_all x1, waiting for transfers between devices, on_device(): lax.all_to_all(jnp.broadcast_to(mine, (deep,) + mine.shape), 'z', split_a...  14.2 us
    all_to_all x1, starting transfers between devices, on_device(): lax.all_to_all(outgoing, SEQ, split_axis=0, concat_axis=0, tiled=True)  10.7 us
    ppermute x6, starting transfers between devices, route(): return lax.ppermute(x, ('grp', 'y', 'core'), pairs)  9.95 us
    ppermute x6, starting transfers between devices, shift(): lax.ppermute(x, 'grp', [(i, (i + by) % groups) for i in range(groups)])  9.64 us
    all_to_all x1, starting transfers between devices, on_device(): lax.all_to_all(jnp.broadcast_to(mine, (deep,) + mine.shape), 'z', split_a...  9.01 us
  transfers between devices with their start and end apart: 19, of which 4 were waited for; matrix products, arithmetic and copies ran while one was open for 0% of the time, Pallas kernels for 18%

profile of v11, /device:TPU:1, one launch (start us, length us, event | category | flops | bytes accessed | tf_op | source)
XLA Modules:
  0.0 148.5 jit_solution(12413357027084351272)
XLA Ops:
  2.4 9.0 %all-to-all-start.2 = ((bf16[8,32,1024]{2,1,0:T(8,128)(2,1)}), bf16[8,32,1024]{2,1,0:T(8,128)(2,1)}, u32[]{:S(2)}, u32[]{:S(2)}) async-start(bf16[8,32,1024]{2,1,0:T(8,128)(2,1)} %broadcast_in_dim.3), calls=%async_computation.2 | async-start | bytes 1048576 | tf_op jit(solution)/shard_map/all_to_all | solution.py:282
  11.6 2.6 %collective-permute-start = (bf16[16,72,128]{2,1,0:T(8,128)(2,1)S(1)}, bf16[16,72,128]{2,1,0:T(8,128)(2,1)S(1)}, u32[]{:S(2)}, u32[]{:S(2)}) collective-permute-start(bf16[16,72,128]{2,1,0:T(8,128)(2,1)S(1)} %pack.1.refs_0_), channel_id=1, source_target_pairs={{0,192},{64,0},{128,64},{192,128},{1,193},{65,1},{129,65},{193,129... | collective-permute-start | bytes 884744 | tf_op jit(solution)/shard_map/ppermute | solution.py:248
  15.3 14.2 %all-to-all-done.2.x0 = bf16[8,32,1024]{2,1,0:T(8,128)(2,1)} async-done(((bf16[8,32,1024]{2,1,0:T(8,128)(2,1)}), bf16[8,32,1024]{2,1,0:T(8,128)(2,1)}, u32[]{:S(2)}, u32[]{:S(2)}) %all-to-all-start.2) | async-done | bytes 524320 | tf_op jit(solution)/shard_map/all_to_all | solution.py:282
  29.5 1.2 collective-permute-start.3
  30.7 2.5 %collective-permute-start.4 = (bf16[8,32,1024]{2,1,0:T(8,128)(2,1)}, bf16[8,32,1024]{2,1,0:T(8,128)(2,1)}, u32[]{:S(2)}, u32[]{:S(2)}) collective-permute-start(bf16[8,32,1024]{2,1,0:T(8,128)(2,1)} %all-to-all-done.2.x0), channel_id=1, source_target_pairs={{0,32},{1,129},{16,48},{17,145},{32,0},{33,161},{48,16},{49,177},{... | collective-permute-start | bytes 1572872 | tf_op jit(solution)/shard_map/ppermute | solution.py:259
  33.2 1.2 collective-permute-start.5
  34.4 1.9 %pick.1 = bf16[64,72,128]{2,1,0:T(8,128)(2,1)} custom-call(s32[1]{0:T(128)} %bitcast.group_ref, s32[256]{0:T(256)S(1)} %bitcast.7, s32[64]{0:T(128)S(1)} %copy-done.7, bf16[16,72,128]{2,1,0:T(8,128)(2,1)S(1)} %pack.1.refs_0_, bf16[16,72,128]{2,1,0:T(8,128)(2,1)S(1)} %collective-permute-done.refs_1_, bf16[16,72,128]{2,1,0:T(8,128)(2,1)S(1)} %collective-permute-done.1.refs_2_, ...), custom_call_target="tpu_custom_call" | custom-call | tf_op jit(solution)/shard_map/pick/pallas_call | solution.py:307
  36.3 10.7 %all-to-all-start = ((bf16[64,72,128]{2,1,0:T(8,128)(2,1)}), bf16[64,72,128]{2,1,0:T(8,128)(2,1)S(1)}, u32[]{:S(2)}, u32[]{:S(2)}) async-start(bf16[64,72,128]{2,1,0:T(8,128)(2,1)} %pick.1), calls=%async_computation | async-start | bytes 2359296 | tf_op jit(solution)/shard_map/all_to_all | solution.py:316
  47.1 3.0 %join.1.s0 = bf16[4,8,32,1024]{3,2,1,0:T(8,128)(2,1)} custom-call(bf16[8,32,1024]{2,1,0:T(8,128)(2,1)} %all-to-all-done.2.x0, bf16[8,32,1024]{2,1,0:T(8,128)(2,1)} %collective-permute-done.3.x1, bf16[8,32,1024]{2,1,0:T(8,128)(2,1)} %collective-permute-done.4.x2, bf16[8,32,1024]{2,1,0:T(8,128)(2,1)} %collective-permute-done.5.x3), custom_call_target="tpu_custom_call" | custom-call | tf_op jit(solution)/shard_map/join/pallas_call | solution.py:285
  50.1 1.5 collective-permute-start.7
  51.6 2.6 %collective-permute-start.8 = (bf16[4,8,32,1024]{3,2,1,0:T(8,128)(2,1)}, bf16[4,8,32,1024]{3,2,1,0:T(8,128)(2,1)}, u32[]{:S(2)}, u32[]{:S(2)}) collective-permute-start(bf16[4,8,32,1024]{3,2,1,0:T(8,128)(2,1)} %join.1.s0), channel_id=1, source_target_pairs={{0,128},{1,33},{16,144},{17,49},{32,160},{33,1},{48,176},{49,17},{... | collective-permute-start | bytes 6291464 | tf_op jit(solution)/shard_map/ppermute | solution.py:259
  54.2 1.1 collective-permute-start.9
  55.3 23.1 %all-to-all-done.x_ref = bf16[64,72,128]{2,1,0:T(8,128)(2,1)S(1)} async-done(((bf16[64,72,128]{2,1,0:T(8,128)(2,1)}), bf16[64,72,128]{2,1,0:T(8,128)(2,1)S(1)}, u32[]{:S(2)}, u32[]{:S(2)}) %all-to-all-start) | async-done | bytes 1179680 | tf_op jit(solution)/shard_map/all_to_all | solution.py:316
  79.3 6.1 %tile.1 = (bf16[64,72,128]{2,1,0:T(8,128)(2,1)S(1)}, bf16[64,9472]{1,0:T(8,128)(2,1)S(1)}) custom-call(bf16[64,72,128]{2,1,0:T(8,128)(2,1)S(1)} %all-to-all-done.x_ref, bf16[128,8192]{1,0:T(8,128)(2,1)S(1)} %copy-done.1, bf16[128,1024]{1,0:T(8,128)(2,1)S(1)} %copy-done.4), custom_call_target="tpu_custom_call" | custom-call | tf_op jit(solution)/shard_map/tile/pallas_call | solution.py:317
  85.5 1.0 copy-done.2
  86.5 1.0 copy-done.3
  87.5 6.3 %all-to-all-start.1 = ((bf16[64,72,128]{2,1,0:T(8,128)(2,1)}), bf16[64,72,128]{2,1,0:T(8,128)(2,1)S(1)}, u32[]{:S(2)}, u32[]{:S(2)}) async-start(bf16[64,72,128]{2,1,0:T(8,128)(2,1)} %copy-done.3), calls=%async_computation.1 | async-start | bytes 2359296 | tf_op jit(solution)/shard_map/all_to_all | solution.py:334
  94.7 26.9 %collective-permute-done.8.s2 = bf16[4,8,32,1024]{3,2,1,0:T(8,128)(2,1)} collective-permute-done((bf16[4,8,32,1024]{3,2,1,0:T(8,128)(2,1)}, bf16[4,8,32,1024]{3,2,1,0:T(8,128)(2,1)}, u32[]{:S(2)}, u32[]{:S(2)}) %collective-permute-start.8) | collective-permute-done | bytes 2097184 | tf_op jit(solution)/shard_map/ppermute | solution.py:259
  122.6 2.5 %all-to-all-done.1.x_ref = bf16[64,72,128]{2,1,0:T(8,128)(2,1)S(1)} async-done(((bf16[64,72,128]{2,1,0:T(8,128)(2,1)}), bf16[64,72,128]{2,1,0:T(8,128)(2,1)S(1)}, u32[]{:S(2)}, u32[]{:S(2)}) %all-to-all-start.1) | async-done | bytes 1179680 | tf_op jit(solution)/shard_map/all_to_all | solution.py:334
  125.2 1.3 sum.1
  126.5 4.6 %collective-permute-start.14 = (bf16[16,72,128]{2,1,0:T(8,128)(2,1)S(1)}, bf16[16,72,128]{2,1,0:T(8,128)(2,1)S(1)}, u32[]{:S(2)}, u32[]{:S(2)}) collective-permute-start(bf16[16,72,128]{2,1,0:T(8,128)(2,1)S(1)} %get-tuple-element.35), channel_id=1, source_target_pairs={{0,128},{64,192},{128,0},{192,64},{1,129},{65,193},{129,1},{193,65... | collective-permute-start | bytes 884744 | tf_op jit(solution)/shard_map/ppermute | solution.py:248
  131.1 1.3 collective-permute-start.15
  132.4 14.9 %base.1 = (bf16[128,1024]{1,0:T(8,128)(2,1)}, bf16[128,8192]{1,0:T(8,128)(2,1)}) custom-call(s32[3]{0:T(128)} %pad_add_fusion.place_ref, bf16[128,8192]{1,0:T(8,128)(2,1)} %tok_ref.3, bf16[128,1024]{1,0:T(8,128)(2,1)} %cot_in.1, bf16[4,8,32,1024]{3,2,1,0:T(8,128)(2,1)} %join.1.s0, bf16[4,8,32,1024]{3,2,1,0:T(8,128)(2,1)} %collective-permute-done.7.s1, ...), custom_call_target="tpu_custom_call" | custom-call | flops 4294967296 | bytes 21495808 | tf_op jit(solution)/shard_map/base/pallas_call | solution.py:360
  147.3 1.2 unpack.1
  (42 shorter events, 6.1 us)
Async XLA Ops:
  0.6 10.8 %copy-start.5 = (bf16[16,144,64]{1,2,0:T(8,128)(2,1)S(1)}, bf16[16,144,64]{1,2,0:T(8,128)(2,1)}, u32[]{:S(2)}) copy-start(bf16[16,144,64]{1,2,0:T(8,128)(2,1)} %param.9) | copy-start | bytes 884740
  0.7 33.7 %copy-start.6 = (s32[256,1]{0,1:T(1,128)S(1)}, s32[256,1]{0,1:T(1,128)}, u32[]{:S(2)}) copy-start(s32[256,1]{0,1:T(1,128)} %param.10) | copy-start | bytes 3076
  0.7 33.7 %copy-start.7 = (s32[64]{0:T(128)S(1)}, s32[64]{0:T(128)}, u32[]{:S(2)}) copy-start(s32[64]{0:T(128)} %slot_ref.3) | copy-start | bytes 772
  2.4 27.1 %all-to-all-start.2 = ((bf16[8,32,1024]{2,1,0:T(8,128)(2,1)}), bf16[8,32,1024]{2,1,0:T(8,128)(2,1)}, u32[]{:S(2)}, u32[]{:S(2)}) async-start(bf16[8,32,1024]{2,1,0:T(8,128)(2,1)} %broadcast_in_dim.3), calls=%async_computation.2 | async-start | bytes 1048576 | tf_op jit(solution)/shard_map/all_to_all | solution.py:282
  11.6 21.6 %collective-permute-start = (bf16[16,72,128]{2,1,0:T(8,128)(2,1)S(1)}, bf16[16,72,128]{2,1,0:T(8,128)(2,1)S(1)}, u32[]{:S(2)}, u32[]{:S(2)}) collective-permute-start(bf16[16,72,128]{2,1,0:T(8,128)(2,1)S(1)} %pack.1.refs_0_), channel_id=1, source_target_pairs={{0,192},{64,0},{128,64},{192,128},{1,193},{65,1},{129,65},{193,129... | collective-permute-start | bytes 884744 | tf_op jit(solution)/shard_map/ppermute | solution.py:248
  14.2 20.2 %collective-permute-start.1 = (bf16[16,72,128]{2,1,0:T(8,128)(2,1)S(1)}, bf16[16,72,128]{2,1,0:T(8,128)(2,1)S(1)}, u32[]{:S(2)}, u32[]{:S(2)}) collective-permute-start(bf16[16,72,128]{2,1,0:T(8,128)(2,1)S(1)} %pack.1.refs_0_), channel_id=1, source_target_pairs={{0,128},{64,192},{128,0},{192,64},{1,129},{65,193},{129,1},{193,65... | collective-permute-start | bytes 884744 | tf_op jit(solution)/shard_map/ppermute | solution.py:248
  14.7 19.7 %collective-permute-start.2 = (bf16[16,72,128]{2,1,0:T(8,128)(2,1)S(1)}, bf16[16,72,128]{2,1,0:T(8,128)(2,1)S(1)}, u32[]{:S(2)}, u32[]{:S(2)}) collective-permute-start(bf16[16,72,128]{2,1,0:T(8,128)(2,1)S(1)} %pack.1.refs_0_), channel_id=1, source_target_pairs={{0,64},{64,128},{128,192},{192,0},{1,65},{65,129},{129,193},{193,1... | collective-permute-start | bytes 884744 | tf_op jit(solution)/shard_map/ppermute | solution.py:248
  29.5 17.5 %collective-permute-start.3 = (bf16[8,32,1024]{2,1,0:T(8,128)(2,1)}, bf16[8,32,1024]{2,1,0:T(8,128)(2,1)}, u32[]{:S(2)}, u32[]{:S(2)}) collective-permute-start(bf16[8,32,1024]{2,1,0:T(8,128)(2,1)} %all-to-all-done.2.x0), channel_id=1, source_target_pairs={{0,16},{1,65},{16,32},{17,81},{32,48},{33,97},{48,0},{49,113},{64,... | collective-permute-start | bytes 1572872 | tf_op jit(solution)/shard_map/ppermute | solution.py:259
  30.7 16.3 %collective-permute-start.4 = (bf16[8,32,1024]{2,1,0:T(8,128)(2,1)}, bf16[8,32,1024]{2,1,0:T(8,128)(2,1)}, u32[]{:S(2)}, u32[]{:S(2)}) collective-permute-start(bf16[8,32,1024]{2,1,0:T(8,128)(2,1)} %all-to-all-done.2.x0), channel_id=1, source_target_pairs={{0,32},{1,129},{16,48},{17,145},{32,0},{33,161},{48,16},{49,177},{... | collective-permute-start | bytes 1572872 | tf_op jit(solution)/shard_map/ppermute | solution.py:259
  33.2 13.9 %collective-permute-start.5 = (bf16[8,32,1024]{2,1,0:T(8,128)(2,1)}, bf16[8,32,1024]{2,1,0:T(8,128)(2,1)}, u32[]{:S(2)}, u32[]{:S(2)}) collective-permute-start(bf16[8,32,1024]{2,1,0:T(8,128)(2,1)} %all-to-all-done.2.x0), channel_id=1, source_target_pairs={{0,48},{1,193},{16,0},{17,209},{32,16},{33,225},{48,32},{49,241},{... | collective-permute-start | bytes 1572872 | tf_op jit(solution)/shard_map/ppermute | solution.py:259
  36.3 42.1 %all-to-all-start = ((bf16[64,72,128]{2,1,0:T(8,128)(2,1)}), bf16[64,72,128]{2,1,0:T(8,128)(2,1)S(1)}, u32[]{:S(2)}, u32[]{:S(2)}) async-start(bf16[64,72,128]{2,1,0:T(8,128)(2,1)} %pick.1), calls=%async_computation | async-start | bytes 2359296 | tf_op jit(solution)/shard_map/all_to_all | solution.py:316
  47.0 31.4 %copy-start.1 = (bf16[128,8192]{1,0:T(8,128)(2,1)S(1)}, bf16[128,8192]{1,0:T(8,128)(2,1)}, u32[]{:S(2)}) copy-start(bf16[128,8192]{1,0:T(8,128)(2,1)} %tok_ref.3) | copy-start | bytes 6291460
  50.1 44.3 %collective-permute-start.7 = (bf16[4,8,32,1024]{3,2,1,0:T(8,128)(2,1)}, bf16[4,8,32,1024]{3,2,1,0:T(8,128)(2,1)}, u32[]{:S(2)}, u32[]{:S(2)}) collective-permute-start(bf16[4,8,32,1024]{3,2,1,0:T(8,128)(2,1)} %join.1.s0), channel_id=1, source_target_pairs={{0,64},{1,17},{16,80},{17,33},{32,96},{33,49},{48,112},{49,1},{64,... | collective-permute-start | bytes 6291464 | tf_op jit(solution)/shard_map/ppermute | solution.py:259
  51.6 69.9 %collective-permute-start.8 = (bf16[4,8,32,1024]{3,2,1,0:T(8,128)(2,1)}, bf16[4,8,32,1024]{3,2,1,0:T(8,128)(2,1)}, u32[]{:S(2)}, u32[]{:S(2)}) collective-permute-start(bf16[4,8,32,1024]{3,2,1,0:T(8,128)(2,1)} %join.1.s0), channel_id=1, source_target_pairs={{0,128},{1,33},{16,144},{17,49},{32,160},{33,1},{48,176},{49,17},{... | collective-permute-start | bytes 6291464 | tf_op jit(solution)/shard_map/ppermute | solution.py:259
  54.2 67.3 %collective-permute-start.9 = (bf16[4,8,32,1024]{3,2,1,0:T(8,128)(2,1)}, bf16[4,8,32,1024]{3,2,1,0:T(8,128)(2,1)}, u32[]{:S(2)}, u32[]{:S(2)}) collective-permute-start(bf16[4,8,32,1024]{3,2,1,0:T(8,128)(2,1)} %join.1.s0), channel_id=1, source_target_pairs={{0,192},{1,49},{16,208},{17,1},{32,224},{33,17},{48,240},{49,33},{... | collective-permute-start | bytes 6291464 | tf_op jit(solution)/shard_map/ppermute | solution.py:259
  87.5 37.6 %all-to-all-start.1 = ((bf16[64,72,128]{2,1,0:T(8,128)(2,1)}), bf16[64,72,128]{2,1,0:T(8,128)(2,1)S(1)}, u32[]{:S(2)}, u32[]{:S(2)}) async-start(bf16[64,72,128]{2,1,0:T(8,128)(2,1)} %copy-done.3), calls=%async_computation.1 | async-start | bytes 2359296 | tf_op jit(solution)/shard_map/all_to_all | solution.py:334
  93.8 28.8 %collective-permute-start.6 = (bf16[4,8,32,1024]{3,2,1,0:T(8,128)(2,1)}, bf16[4,8,32,1024]{3,2,1,0:T(8,128)(2,1)S(1)}, u32[]{:S(2)}, u32[]{:S(2)}) collective-permute-start(bf16[4,8,32,1024]{3,2,1,0:T(8,128)(2,1)} %join.1.s0), channel_id=1, source_target_pairs={{0,1},{1,0},{2,3},{3,2},{4,5},{5,4},{6,7},{7,6},{8,9},{9,8},{10,11... | collective-permute-start | bytes 6291464 | tf_op jit(solution)/shard_map/ppermute | solution.py:295
  94.4 36.8 %collective-permute-start.10 = (bf16[4,8,32,1024]{3,2,1,0:T(8,128)(2,1)}, bf16[4,8,32,1024]{3,2,1,0:T(8,128)(2,1)}, u32[]{:S(2)}, u32[]{:S(2)}) collective-permute-start(bf16[4,8,32,1024]{3,2,1,0:T(8,128)(2,1)} %collective-permute-done.7.s1), channel_id=1, source_target_pairs={{0,1},{1,0},{2,3},{3,2},{4,5},{5,4},{6,7},{7,6},{8,9},{9,8},{10,11... | collective-permute-start | bytes 6291464 | tf_op jit(solution)/shard_map/ppermute | solution.py:295
  121.5 9.6 %collective-permute-start.11 = (bf16[4,8,32,1024]{3,2,1,0:T(8,128)(2,1)}, bf16[4,8,32,1024]{3,2,1,0:T(8,128)(2,1)}, u32[]{:S(2)}, u32[]{:S(2)}) collective-permute-start(bf16[4,8,32,1024]{3,2,1,0:T(8,128)(2,1)} %collective-permute-done.8.s2), channel_id=1, source_target_pairs={{0,1},{1,0},{2,3},{3,2},{4,5},{5,4},{6,7},{7,6},{8,9},{9,8},{10,11... | collective-permute-start | bytes 6291464 | tf_op jit(solution)/shard_map/ppermute | solution.py:295
  121.5 9.6 %collective-permute-start.12 = (bf16[4,8,32,1024]{3,2,1,0:T(8,128)(2,1)}, bf16[4,8,32,1024]{3,2,1,0:T(8,128)(2,1)}, u32[]{:S(2)}, u32[]{:S(2)}) collective-permute-start(bf16[4,8,32,1024]{3,2,1,0:T(8,128)(2,1)} %collective-permute-done.9.s3), channel_id=1, source_target_pairs={{0,1},{1,0},{2,3},{3,2},{4,5},{5,4},{6,7},{7,6},{8,9},{9,8},{10,11... | collective-permute-start | bytes 6291464 | tf_op jit(solution)/shard_map/ppermute | solution.py:295
  122.6 9.8 %copy-start.8 = (bf16[4,8,32,1024]{3,2,1,0:T(8,128)(2,1)}, bf16[4,8,32,1024]{3,2,1,0:T(8,128)(2,1)S(1)}, u32[]{:S(2)}) copy-start(bf16[4,8,32,1024]{3,2,1,0:T(8,128)(2,1)S(1)} %collective-permute-done.6.t0) | copy-start | bytes 6291460
  126.5 20.9 %collective-permute-start.13 = (bf16[16,72,128]{2,1,0:T(8,128)(2,1)S(1)}, bf16[16,72,128]{2,1,0:T(8,128)(2,1)S(1)}, u32[]{:S(2)}, u32[]{:S(2)}) collective-permute-start(bf16[16,72,128]{2,1,0:T(8,128)(2,1)S(1)} %get-tuple-element.34), channel_id=1, source_target_pairs={{0,64},{64,128},{128,192},{192,0},{1,65},{65,129},{129,193},{193,1... | collective-permute-start | bytes 884744 | tf_op jit(solution)/shard_map/ppermute | solution.py:248
  126.5 20.8 %collective-permute-start.14 = (bf16[16,72,128]{2,1,0:T(8,128)(2,1)S(1)}, bf16[16,72,128]{2,1,0:T(8,128)(2,1)S(1)}, u32[]{:S(2)}, u32[]{:S(2)}) collective-permute-start(bf16[16,72,128]{2,1,0:T(8,128)(2,1)S(1)} %get-tuple-element.35), channel_id=1, source_target_pairs={{0,128},{64,192},{128,0},{192,64},{1,129},{65,193},{129,1},{193,65... | collective-permute-start | bytes 884744 | tf_op jit(solution)/shard_map/ppermute | solution.py:248
  131.1 16.2 %collective-permute-start.15 = (bf16[16,72,128]{2,1,0:T(8,128)(2,1)S(1)}, bf16[16,72,128]{2,1,0:T(8,128)(2,1)S(1)}, u32[]{:S(2)}, u32[]{:S(2)}) collective-permute-start(bf16[16,72,128]{2,1,0:T(8,128)(2,1)S(1)} %get-tuple-element.36), channel_id=1, source_target_pairs={{0,192},{64,0},{128,64},{192,128},{1,193},{65,1},{129,65},{193,129... | collective-permute-start | bytes 884744 | tf_op jit(solution)/shard_map/ppermute | solution.py:248
  (4 other events, 4.0 us)

commit v12 on v11

--- a/solution.py
+++ b/solution.py
@@ -73,7 +73,7 @@
             o_ref[s, 8 * b : 8 * b + 8, LANES:] = rest[:, tail * b : tail * (b + 1)]
 
 
-def tile_kernel(x_ref, tok_ref, cot_ref, terms_out, at_out, t_ref, terms_ref, at_ref, sems):
+def tile_kernel(x_ref, tok_ref, cot_ref, terms_ref, at_ref, t_ref):
     shards, _, _ = x_ref.shape
     rank = at_ref.shape[0]
     depth = tok_ref.shape[1]
@@ -125,8 +125,6 @@
     ).astype(bf16)
     at_ref[:, width : width + LANES] = hidden
     at_ref[:, width + LANES :] = back
-    at_copy = pltpu.make_async_copy(at_ref, at_out, sems.at[0])
-    at_copy.start()
     t_ref[:, :depth] = adapter_scale * jnp.dot(back, tok, preferred_element_type=f32)
     t_ref[:, depth:] = adapter_scale * jnp.dot(hidden, cot, preferred_element_type=f32)
 
@@ -150,14 +148,7 @@
             )
         return carry
 
-    for a in range(shards // per):
-        pack(a, 0)
-        piece = slice(a * per, (a + 1) * per)
-        pltpu.make_async_copy(terms_ref.at[piece], terms_out.at[piece], sems.at[a + 1]).start()
-    for a in range(shards // per):
-        piece = slice(a * per, (a + 1) * per)
-        pltpu.make_async_copy(terms_ref.at[piece], terms_out.at[piece], sems.at[a + 1]).wait()
-    at_copy.wait()
+    lax.fori_loop(0, shards // per, pack, 0)
 
 
 def join_kernel(x0, x1, x2, x3, o_ref, sems):
@@ -209,7 +200,7 @@
     back = adapter_ref[:, width + rows :]
     up = adapter_ref[:, depth:width]
     acc_ref[...] = adapter_scale * lax.dot_general(hidden, up, TN, preferred_element_type=f32)
-    halves = 2
+    halves = 1
     span = depth // (wide * halves)
     stores = []
     for step in range(wide):
@@ -229,11 +220,11 @@
                 axis=0,
             )
             acc_ref[...] += jnp.dot(tok_ref[:, at], weight, preferred_element_type=f32)
-            grad = lax.dot_general(cot_ref[...], weight, NT, preferred_element_type=f32)
+            grad = lax.dot_general(weight, cot_ref[...], NT, preferred_element_type=f32)
             grad += adapter_scale * lax.dot_general(
-                back, adapter_ref[:, at], TN, preferred_element_type=f32
+                adapter_ref[:, at], back, TN, preferred_element_type=f32
             )
-            grad_ref[:, at] = grad.astype(grad_ref.dtype)
+            grad_ref[:, at] = grad.T.astype(grad_ref.dtype)
             store = pltpu.make_async_copy(
                 grad_ref.at[:, at], out_ref.at[:, at], out_sems.at[step * halves + h]
             )
@@ -321,13 +312,8 @@
             jax.ShapeDtypeStruct((rank, width + 2 * rows), bf16),
         ),
         in_specs=[whole()] * 3,
-        out_specs=(whole(pltpu.HBM),) * 2,
-        scratch_shapes=[
-            pltpu.VMEM((rank, width), f32),
-            pltpu.VMEM((shards, packed_rows, LANES), bf16),
-            pltpu.VMEM((rank, width + 2 * rows), bf16),
-            pltpu.SemaphoreType.DMA((shards + 1,)),
-        ],
+        out_specs=(whole(),) * 2,
+        scratch_shapes=[pltpu.VMEM((rank, width), f32)],
         compiler_params=params(32),
         name="tile",
     )(arrived, tokens, cotangent)

time: 149 us -> 155 us (1.040)
  waiting for transfers between devices: 66.8 us -> 68.8 us
  starting transfers between devices: 47 us -> 48.9 us
  Pallas kernels: 28.5 us -> 30.2 us
    pallas_call x1, Pallas kernels: 14.9 us -> 19.1 us  [on_device(): pl.pallas_call(base_kernel, out_shape=(jax.ShapeDtypeStruct((rows, key_co...]
    ppermute x6, waiting for transfers between devices: 26.9 us -> 31 us  [route(): return lax.ppermute(x, ('grp', 'y', 'core'), pairs)]
    pallas_call x1, Pallas kernels: 6.14 us -> 3.57 us  [on_device(): pl.pallas_call(tile_kernel, out_shape=(jax.ShapeDtypeStruct((shards, pack...]
    all_to_all x1, waiting for transfers between devices: 2.55 us -> 0.01 us  [on_device(): lax.all_to_all(terms, SEQ, split_axis=0, concat_axis=0, tiled=True)]
    ppermute x6, starting transfers between devices: 9.64 us -> 11.8 us  [shift(): lax.ppermute(x, 'grp', [(i, (i + by) % groups) for i in range(groups)])]
  transfers between devices with their start and end apart: 19 -> 19, of which waited for: 4 -> 4; matrix products, arithmetic and copies ran while one was open for 0% -> 0% of each run, Pallas kernels for 18% -> 19%
where the time goes in v12:
time: 155 us; the launch traced here: 154 us
  waiting for transfers between devices  68.8 us (44%)
  starting transfers between devices  48.9 us (32%)
  Pallas kernels  30.2 us (19%)
  local copies, waits for them, and re-layouts  4.79 us (3%)
    ppermute x6, waiting for transfers between devices, route(): return lax.ppermute(x, ('grp', 'y', 'core'), pairs)  31 us
    all_to_all x1, waiting for transfers between devices, on_device(): lax.all_to_all(outgoing, SEQ, split_axis=0, concat_axis=0, tiled=True)  23.1 us
    pallas_call x1, Pallas kernels, on_device(): pl.pallas_call(base_kernel, out_shape=(jax.ShapeDtypeStruct((rows, key_co...  19.1 us
    all_to_all x1, waiting for transfers between devices, on_device(): lax.all_to_all(jnp.broadcast_to(mine, (deep,) + mine.shape), 'z', split_a...  14.2 us
    ppermute x6, starting transfers between devices, shift(): lax.ppermute(x, 'grp', [(i, (i + by) % groups) for i in range(groups)])  11.8 us
    all_to_all x1, starting transfers between devices, on_device(): lax.all_to_all(outgoing, SEQ, split_axis=0, concat_axis=0, tiled=True)  10.7 us
    ppermute x6, starting transfers between devices, route(): return lax.ppermute(x, ('grp', 'y', 'core'), pairs)  9.95 us
    all_to_all x1, starting transfers between devices, on_device(): lax.all_to_all(jnp.broadcast_to(mine, (deep,) + mine.shape), 'z', split_a...  9.01 us
  transfers between devices with their start and end apart: 19, of which 4 were waited for; matrix products, arithmetic and copies ran while one was open for 0% of the time, Pallas kernels for 19%

profile of v12, /device:TPU:1, one launch (start us, length us, event | category | flops | bytes accessed | tf_op | source)
XLA Modules:
  0.0 154.1 jit_solution(9300978877634600401)
XLA Ops:
  2.4 9.0 %all-to-all-start.2 = ((bf16[8,32,1024]{2,1,0:T(8,128)(2,1)}), bf16[8,32,1024]{2,1,0:T(8,128)(2,1)}, u32[]{:S(2)}, u32[]{:S(2)}) async-start(bf16[8,32,1024]{2,1,0:T(8,128)(2,1)} %broadcast_in_dim.3), calls=%async_computation.2 | async-start | bytes 1048576 | tf_op jit(solution)/shard_map/all_to_all | solution.py:273
  11.6 2.6 %collective-permute-start = (bf16[16,72,128]{2,1,0:T(8,128)(2,1)S(1)}, bf16[16,72,128]{2,1,0:T(8,128)(2,1)S(1)}, u32[]{:S(2)}, u32[]{:S(2)}) collective-permute-start(bf16[16,72,128]{2,1,0:T(8,128)(2,1)S(1)} %pack.1.refs_0_), channel_id=1, source_target_pairs={{0,192},{64,0},{128,64},{192,128},{1,193},{65,1},{129,65},{193,129... | collective-permute-start | bytes 884744 | tf_op jit(solution)/shard_map/ppermute | solution.py:239
  15.3 14.2 %all-to-all-done.2.x0 = bf16[8,32,1024]{2,1,0:T(8,128)(2,1)} async-done(((bf16[8,32,1024]{2,1,0:T(8,128)(2,1)}), bf16[8,32,1024]{2,1,0:T(8,128)(2,1)}, u32[]{:S(2)}, u32[]{:S(2)}) %all-to-all-start.2) | async-done | bytes 524320 | tf_op jit(solution)/shard_map/all_to_all | solution.py:273
  29.5 1.2 collective-permute-start.3
  30.7 2.5 %collective-permute-start.4 = (bf16[8,32,1024]{2,1,0:T(8,128)(2,1)}, bf16[8,32,1024]{2,1,0:T(8,128)(2,1)}, u32[]{:S(2)}, u32[]{:S(2)}) collective-permute-start(bf16[8,32,1024]{2,1,0:T(8,128)(2,1)} %all-to-all-done.2.x0), channel_id=1, source_target_pairs={{0,32},{1,129},{16,48},{17,145},{32,0},{33,161},{48,16},{49,177},{... | collective-permute-start | bytes 1572872 | tf_op jit(solution)/shard_map/ppermute | solution.py:250
  33.2 1.2 collective-permute-start.5
  34.4 1.9 %pick.1 = bf16[64,72,128]{2,1,0:T(8,128)(2,1)} custom-call(s32[1]{0:T(128)} %bitcast.group_ref, s32[256]{0:T(256)S(1)} %bitcast.7, s32[64]{0:T(128)S(1)} %copy-done.7, bf16[16,72,128]{2,1,0:T(8,128)(2,1)S(1)} %pack.1.refs_0_, bf16[16,72,128]{2,1,0:T(8,128)(2,1)S(1)} %collective-permute-done.refs_1_, bf16[16,72,128]{2,1,0:T(8,128)(2,1)S(1)} %collective-permute-done.1.refs_2_, ...), custom_call_target="tpu_custom_call" | custom-call | tf_op jit(solution)/shard_map/pick/pallas_call | solution.py:298
  36.3 10.7 %all-to-all-start = ((bf16[64,72,128]{2,1,0:T(8,128)(2,1)}), bf16[64,72,128]{2,1,0:T(8,128)(2,1)S(1)}, u32[]{:S(2)}, u32[]{:S(2)}) async-start(bf16[64,72,128]{2,1,0:T(8,128)(2,1)} %pick.1), calls=%async_computation | async-start | bytes 2359296 | tf_op jit(solution)/shard_map/all_to_all | solution.py:307
  47.1 3.0 %join.1.s0 = bf16[4,8,32,1024]{3,2,1,0:T(8,128)(2,1)} custom-call(bf16[8,32,1024]{2,1,0:T(8,128)(2,1)} %all-to-all-done.2.x0, bf16[8,32,1024]{2,1,0:T(8,128)(2,1)} %collective-permute-done.3.x1, bf16[8,32,1024]{2,1,0:T(8,128)(2,1)} %collective-permute-done.4.x2, bf16[8,32,1024]{2,1,0:T(8,128)(2,1)} %collective-permute-done.5.x3), custom_call_target="tpu_custom_call" | custom-call | tf_op jit(solution)/shard_map/join/pallas_call | solution.py:276
  50.1 1.5 collective-permute-start.7
  51.6 2.6 %collective-permute-start.8 = (bf16[4,8,32,1024]{3,2,1,0:T(8,128)(2,1)}, bf16[4,8,32,1024]{3,2,1,0:T(8,128)(2,1)}, u32[]{:S(2)}, u32[]{:S(2)}) collective-permute-start(bf16[4,8,32,1024]{3,2,1,0:T(8,128)(2,1)} %join.1.s0), channel_id=1, source_target_pairs={{0,128},{1,33},{16,144},{17,49},{32,160},{33,1},{48,176},{49,17},{... | collective-permute-start | bytes 6291464 | tf_op jit(solution)/shard_map/ppermute | solution.py:250
  54.2 1.1 collective-permute-start.9
  55.3 23.1 %all-to-all-done.x_ref = bf16[64,72,128]{2,1,0:T(8,128)(2,1)S(1)} async-done(((bf16[64,72,128]{2,1,0:T(8,128)(2,1)}), bf16[64,72,128]{2,1,0:T(8,128)(2,1)S(1)}, u32[]{:S(2)}, u32[]{:S(2)}) %all-to-all-start) | async-done | bytes 1179680 | tf_op jit(solution)/shard_map/all_to_all | solution.py:307
  78.4 0.9 copy-done.4
  79.3 3.6 %tile.1 = (bf16[64,72,128]{2,1,0:T(8,128)(2,1)S(1)}, bf16[64,9472]{1,0:T(8,128)(2,1)S(1)}) custom-call(bf16[64,72,128]{2,1,0:T(8,128)(2,1)S(1)} %all-to-all-done.x_ref, bf16[128,8192]{1,0:T(8,128)(2,1)S(1)} %copy-done.1, bf16[128,1024]{1,0:T(8,128)(2,1)S(1)} %copy-done.4), custom_call_target="tpu_custom_call" | custom-call | tf_op jit(solution)/shard_map/tile/pallas_call | solution.py:308
  82.9 1.0 copy-done.2
  84.0 1.0 copy-done.3
  85.0 6.3 %all-to-all-start.1 = ((bf16[64,72,128]{2,1,0:T(8,128)(2,1)}), bf16[64,72,128]{2,1,0:T(8,128)(2,1)S(1)}, u32[]{:S(2)}, u32[]{:S(2)}) async-start(bf16[64,72,128]{2,1,0:T(8,128)(2,1)} %copy-done.3), calls=%async_computation.1 | async-start | bytes 2359296 | tf_op jit(solution)/shard_map/all_to_all | solution.py:320
  91.9 31.0 %collective-permute-done.8.s2 = bf16[4,8,32,1024]{3,2,1,0:T(8,128)(2,1)} collective-permute-done((bf16[4,8,32,1024]{3,2,1,0:T(8,128)(2,1)}, bf16[4,8,32,1024]{3,2,1,0:T(8,128)(2,1)}, u32[]{:S(2)}, u32[]{:S(2)}) %collective-permute-start.8) | collective-permute-done | bytes 2097184 | tf_op jit(solution)/shard_map/ppermute | solution.py:250
  124.0 1.3 sum.1
  125.4 4.6 %collective-permute-start.14 = (bf16[16,72,128]{2,1,0:T(8,128)(2,1)S(1)}, bf16[16,72,128]{2,1,0:T(8,128)(2,1)S(1)}, u32[]{:S(2)}, u32[]{:S(2)}) collective-permute-start(bf16[16,72,128]{2,1,0:T(8,128)(2,1)S(1)} %get-tuple-element.35), channel_id=1, source_target_pairs={{0,128},{64,192},{128,0},{192,64},{1,129},{65,193},{129,1},{193,65... | collective-permute-start | bytes 884744 | tf_op jit(solution)/shard_map/ppermute | solution.py:239
  130.4 3.4 %collective-permute-start.15 = (bf16[16,72,128]{2,1,0:T(8,128)(2,1)S(1)}, bf16[16,72,128]{2,1,0:T(8,128)(2,1)S(1)}, u32[]{:S(2)}, u32[]{:S(2)}) collective-permute-start(bf16[16,72,128]{2,1,0:T(8,128)(2,1)S(1)} %get-tuple-element.36), channel_id=1, source_target_pairs={{0,192},{64,0},{128,64},{192,128},{1,193},{65,1},{129,65},{193,129... | collective-permute-start | bytes 884744 | tf_op jit(solution)/shard_map/ppermute | solution.py:239
  133.8 19.1 %base.1 = (bf16[128,1024]{1,0:T(8,128)(2,1)}, bf16[128,8192]{1,0:T(8,128)(2,1)}) custom-call(s32[3]{0:T(128)} %pad_add_fusion.place_ref, bf16[128,8192]{1,0:T(8,128)(2,1)} %tok_ref.3, bf16[128,1024]{1,0:T(8,128)(2,1)} %cot_in.1, bf16[4,8,32,1024]{3,2,1,0:T(8,128)(2,1)} %join.1.s0, bf16[4,8,32,1024]{3,2,1,0:T(8,128)(2,1)} %collective-permute-done.7.s1, ...), custom_call_target="tpu_custom_call" | custom-call | flops 4294967296 | bytes 21495808 | tf_op jit(solution)/shard_map/base/pallas_call | solution.py:346
  152.9 1.2 unpack.1
  (42 shorter events, 5.4 us)
Async XLA Ops:
  0.6 10.8 %copy-start.5 = (bf16[16,144,64]{1,2,0:T(8,128)(2,1)S(1)}, bf16[16,144,64]{1,2,0:T(8,128)(2,1)}, u32[]{:S(2)}) copy-start(bf16[16,144,64]{1,2,0:T(8,128)(2,1)} %param.9) | copy-start | bytes 884740
  0.7 33.7 %copy-start.6 = (s32[256,1]{0,1:T(1,128)S(1)}, s32[256,1]{0,1:T(1,128)}, u32[]{:S(2)}) copy-start(s32[256,1]{0,1:T(1,128)} %param.10) | copy-start | bytes 3076
  0.7 33.7 %copy-start.7 = (s32[64]{0:T(128)S(1)}, s32[64]{0:T(128)}, u32[]{:S(2)}) copy-start(s32[64]{0:T(128)} %slot_ref.3) | copy-start | bytes 772
  2.4 27.1 %all-to-all-start.2 = ((bf16[8,32,1024]{2,1,0:T(8,128)(2,1)}), bf16[8,32,1024]{2,1,0:T(8,128)(2,1)}, u32[]{:S(2)}, u32[]{:S(2)}) async-start(bf16[8,32,1024]{2,1,0:T(8,128)(2,1)} %broadcast_in_dim.3), calls=%async_computation.2 | async-start | bytes 1048576 | tf_op jit(solution)/shard_map/all_to_all | solution.py:273
  11.6 21.6 %collective-permute-start = (bf16[16,72,128]{2,1,0:T(8,128)(2,1)S(1)}, bf16[16,72,128]{2,1,0:T(8,128)(2,1)S(1)}, u32[]{:S(2)}, u32[]{:S(2)}) collective-permute-start(bf16[16,72,128]{2,1,0:T(8,128)(2,1)S(1)} %pack.1.refs_0_), channel_id=1, source_target_pairs={{0,192},{64,0},{128,64},{192,128},{1,193},{65,1},{129,65},{193,129... | collective-permute-start | bytes 884744 | tf_op jit(solution)/shard_map/ppermute | solution.py:239
  14.2 20.2 %collective-permute-start.1 = (bf16[16,72,128]{2,1,0:T(8,128)(2,1)S(1)}, bf16[16,72,128]{2,1,0:T(8,128)(2,1)S(1)}, u32[]{:S(2)}, u32[]{:S(2)}) collective-permute-start(bf16[16,72,128]{2,1,0:T(8,128)(2,1)S(1)} %pack.1.refs_0_), channel_id=1, source_target_pairs={{0,128},{64,192},{128,0},{192,64},{1,129},{65,193},{129,1},{193,65... | collective-permute-start | bytes 884744 | tf_op jit(solution)/shard_map/ppermute | solution.py:239
  14.7 19.7 %collective-permute-start.2 = (bf16[16,72,128]{2,1,0:T(8,128)(2,1)S(1)}, bf16[16,72,128]{2,1,0:T(8,128)(2,1)S(1)}, u32[]{:S(2)}, u32[]{:S(2)}) collective-permute-start(bf16[16,72,128]{2,1,0:T(8,128)(2,1)S(1)} %pack.1.refs_0_), channel_id=1, source_target_pairs={{0,64},{64,128},{128,192},{192,0},{1,65},{65,129},{129,193},{193,1... | collective-permute-start | bytes 884744 | tf_op jit(solution)/shard_map/ppermute | solution.py:239
  29.5 17.5 %collective-permute-start.3 = (bf16[8,32,1024]{2,1,0:T(8,128)(2,1)}, bf16[8,32,1024]{2,1,0:T(8,128)(2,1)}, u32[]{:S(2)}, u32[]{:S(2)}) collective-permute-start(bf16[8,32,1024]{2,1,0:T(8,128)(2,1)} %all-to-all-done.2.x0), channel_id=1, source_target_pairs={{0,16},{1,65},{16,32},{17,81},{32,48},{33,97},{48,0},{49,113},{64,... | collective-permute-start | bytes 1572872 | tf_op jit(solution)/shard_map/ppermute | solution.py:250
  30.7 16.3 %collective-permute-start.4 = (bf16[8,32,1024]{2,1,0:T(8,128)(2,1)}, bf16[8,32,1024]{2,1,0:T(8,128)(2,1)}, u32[]{:S(2)}, u32[]{:S(2)}) collective-permute-start(bf16[8,32,1024]{2,1,0:T(8,128)(2,1)} %all-to-all-done.2.x0), channel_id=1, source_target_pairs={{0,32},{1,129},{16,48},{17,145},{32,0},{33,161},{48,16},{49,177},{... | collective-permute-start | bytes 1572872 | tf_op jit(solution)/shard_map/ppermute | solution.py:250
  33.2 13.9 %collective-permute-start.5 = (bf16[8,32,1024]{2,1,0:T(8,128)(2,1)}, bf16[8,32,1024]{2,1,0:T(8,128)(2,1)}, u32[]{:S(2)}, u32[]{:S(2)}) collective-permute-start(bf16[8,32,1024]{2,1,0:T(8,128)(2,1)} %all-to-all-done.2.x0), channel_id=1, source_target_pairs={{0,48},{1,193},{16,0},{17,209},{32,16},{33,225},{48,32},{49,241},{... | collective-permute-start | bytes 1572872 | tf_op jit(solution)/shard_map/ppermute | solution.py:250
  36.3 42.1 %all-to-all-start = ((bf16[64,72,128]{2,1,0:T(8,128)(2,1)}), bf16[64,72,128]{2,1,0:T(8,128)(2,1)S(1)}, u32[]{:S(2)}, u32[]{:S(2)}) async-start(bf16[64,72,128]{2,1,0:T(8,128)(2,1)} %pick.1), calls=%async_computation | async-start | bytes 2359296 | tf_op jit(solution)/shard_map/all_to_all | solution.py:307
  47.0 31.4 %copy-start.1 = (bf16[128,8192]{1,0:T(8,128)(2,1)S(1)}, bf16[128,8192]{1,0:T(8,128)(2,1)}, u32[]{:S(2)}) copy-start(bf16[128,8192]{1,0:T(8,128)(2,1)} %tok_ref.3) | copy-start | bytes 6291460
  50.1 41.7 %collective-permute-start.7 = (bf16[4,8,32,1024]{3,2,1,0:T(8,128)(2,1)}, bf16[4,8,32,1024]{3,2,1,0:T(8,128)(2,1)}, u32[]{:S(2)}, u32[]{:S(2)}) collective-permute-start(bf16[4,8,32,1024]{3,2,1,0:T(8,128)(2,1)} %join.1.s0), channel_id=1, source_target_pairs={{0,64},{1,17},{16,80},{17,33},{32,96},{33,49},{48,112},{49,1},{64,... | collective-permute-start | bytes 6291464 | tf_op jit(solution)/shard_map/ppermute | solution.py:250
  51.6 71.3 %collective-permute-start.8 = (bf16[4,8,32,1024]{3,2,1,0:T(8,128)(2,1)}, bf16[4,8,32,1024]{3,2,1,0:T(8,128)(2,1)}, u32[]{:S(2)}, u32[]{:S(2)}) collective-permute-start(bf16[4,8,32,1024]{3,2,1,0:T(8,128)(2,1)} %join.1.s0), channel_id=1, source_target_pairs={{0,128},{1,33},{16,144},{17,49},{32,160},{33,1},{48,176},{49,17},{... | collective-permute-start | bytes 6291464 | tf_op jit(solution)/shard_map/ppermute | solution.py:250
  54.2 68.7 %collective-permute-start.9 = (bf16[4,8,32,1024]{3,2,1,0:T(8,128)(2,1)}, bf16[4,8,32,1024]{3,2,1,0:T(8,128)(2,1)}, u32[]{:S(2)}, u32[]{:S(2)}) collective-permute-start(bf16[4,8,32,1024]{3,2,1,0:T(8,128)(2,1)} %join.1.s0), channel_id=1, source_target_pairs={{0,192},{1,49},{16,208},{17,1},{32,224},{33,17},{48,240},{49,33},{... | collective-permute-start | bytes 6291464 | tf_op jit(solution)/shard_map/ppermute | solution.py:250
  85.0 39.0 %all-to-all-start.1 = ((bf16[64,72,128]{2,1,0:T(8,128)(2,1)}), bf16[64,72,128]{2,1,0:T(8,128)(2,1)S(1)}, u32[]{:S(2)}, u32[]{:S(2)}) async-start(bf16[64,72,128]{2,1,0:T(8,128)(2,1)} %copy-done.3), calls=%async_computation.1 | async-start | bytes 2359296 | tf_op jit(solution)/shard_map/all_to_all | solution.py:320
  91.3 32.7 %collective-permute-start.6 = (bf16[4,8,32,1024]{3,2,1,0:T(8,128)(2,1)}, bf16[4,8,32,1024]{3,2,1,0:T(8,128)(2,1)S(1)}, u32[]{:S(2)}, u32[]{:S(2)}) collective-permute-start(bf16[4,8,32,1024]{3,2,1,0:T(8,128)(2,1)} %join.1.s0), channel_id=1, source_target_pairs={{0,1},{1,0},{2,3},{3,2},{4,5},{5,4},{6,7},{7,6},{8,9},{9,8},{10,11... | collective-permute-start | bytes 6291464 | tf_op jit(solution)/shard_map/ppermute | solution.py:286
  91.8 38.2 %collective-permute-start.10 = (bf16[4,8,32,1024]{3,2,1,0:T(8,128)(2,1)}, bf16[4,8,32,1024]{3,2,1,0:T(8,128)(2,1)}, u32[]{:S(2)}, u32[]{:S(2)}) collective-permute-start(bf16[4,8,32,1024]{3,2,1,0:T(8,128)(2,1)} %collective-permute-done.7.s1), channel_id=1, source_target_pairs={{0,1},{1,0},{2,3},{3,2},{4,5},{5,4},{6,7},{7,6},{8,9},{9,8},{10,11... | collective-permute-start | bytes 6291464 | tf_op jit(solution)/shard_map/ppermute | solution.py:286
  122.9 7.1 %collective-permute-start.11 = (bf16[4,8,32,1024]{3,2,1,0:T(8,128)(2,1)}, bf16[4,8,32,1024]{3,2,1,0:T(8,128)(2,1)}, u32[]{:S(2)}, u32[]{:S(2)}) collective-permute-start(bf16[4,8,32,1024]{3,2,1,0:T(8,128)(2,1)} %collective-permute-done.8.s2), channel_id=1, source_target_pairs={{0,1},{1,0},{2,3},{3,2},{4,5},{5,4},{6,7},{7,6},{8,9},{9,8},{10,11... | collective-permute-start | bytes 6291464 | tf_op jit(solution)/shard_map/ppermute | solution.py:286
  122.9 7.5 %collective-permute-start.12 = (bf16[4,8,32,1024]{3,2,1,0:T(8,128)(2,1)}, bf16[4,8,32,1024]{3,2,1,0:T(8,128)(2,1)}, u32[]{:S(2)}, u32[]{:S(2)}) collective-permute-start(bf16[4,8,32,1024]{3,2,1,0:T(8,128)(2,1)} %collective-permute-done.9.s3), channel_id=1, source_target_pairs={{0,1},{1,0},{2,3},{3,2},{4,5},{5,4},{6,7},{7,6},{8,9},{9,8},{10,11... | collective-permute-start | bytes 6291464 | tf_op jit(solution)/shard_map/ppermute | solution.py:286
  124.0 9.8 %copy-start.8 = (bf16[4,8,32,1024]{3,2,1,0:T(8,128)(2,1)}, bf16[4,8,32,1024]{3,2,1,0:T(8,128)(2,1)S(1)}, u32[]{:S(2)}) copy-start(bf16[4,8,32,1024]{3,2,1,0:T(8,128)(2,1)S(1)} %collective-permute-done.6.t0) | copy-start | bytes 6291460
  125.3 27.6 %collective-permute-start.13 = (bf16[16,72,128]{2,1,0:T(8,128)(2,1)S(1)}, bf16[16,72,128]{2,1,0:T(8,128)(2,1)S(1)}, u32[]{:S(2)}, u32[]{:S(2)}) collective-permute-start(bf16[16,72,128]{2,1,0:T(8,128)(2,1)S(1)} %get-tuple-element.34), channel_id=1, source_target_pairs={{0,64},{64,128},{128,192},{192,0},{1,65},{65,129},{129,193},{193,1... | collective-permute-start | bytes 884744 | tf_op jit(solution)/shard_map/ppermute | solution.py:239
  125.4 27.6 %collective-permute-start.14 = (bf16[16,72,128]{2,1,0:T(8,128)(2,1)S(1)}, bf16[16,72,128]{2,1,0:T(8,128)(2,1)S(1)}, u32[]{:S(2)}, u32[]{:S(2)}) collective-permute-start(bf16[16,72,128]{2,1,0:T(8,128)(2,1)S(1)} %get-tuple-element.35), channel_id=1, source_target_pairs={{0,128},{64,192},{128,0},{192,64},{1,129},{65,193},{129,1},{193,65... | collective-permute-start | bytes 884744 | tf_op jit(solution)/shard_map/ppermute | solution.py:239
  130.4 22.5 %collective-permute-start.15 = (bf16[16,72,128]{2,1,0:T(8,128)(2,1)S(1)}, bf16[16,72,128]{2,1,0:T(8,128)(2,1)S(1)}, u32[]{:S(2)}, u32[]{:S(2)}) collective-permute-start(bf16[16,72,128]{2,1,0:T(8,128)(2,1)S(1)} %get-tuple-element.36), channel_id=1, source_target_pairs={{0,192},{64,0},{128,64},{192,128},{1,193},{65,1},{129,65},{193,129... | collective-permute-start | bytes 884744 | tf_op jit(solution)/shard_map/ppermute | solution.py:239
  (4 other events, 4.0 us)

commit v13 on v12

--- a/solution.py
+++ b/solution.py
@@ -200,7 +200,7 @@
     back = adapter_ref[:, width + rows :]
     up = adapter_ref[:, depth:width]
     acc_ref[...] = adapter_scale * lax.dot_general(hidden, up, TN, preferred_element_type=f32)
-    halves = 1
+    halves = 2
     span = depth // (wide * halves)
     stores = []
     for step in range(wide):
@@ -220,11 +220,11 @@
                 axis=0,
             )
             acc_ref[...] += jnp.dot(tok_ref[:, at], weight, preferred_element_type=f32)
-            grad = lax.dot_general(weight, cot_ref[...], NT, preferred_element_type=f32)
+            grad = lax.dot_general(cot_ref[...], weight, NT, preferred_element_type=f32)
             grad += adapter_scale * lax.dot_general(
-                adapter_ref[:, at], back, TN, preferred_element_type=f32
+                back, adapter_ref[:, at], TN, preferred_element_type=f32
             )
-            grad_ref[:, at] = grad.T.astype(grad_ref.dtype)
+            grad_ref[:, at] = grad.astype(grad_ref.dtype)
             store = pltpu.make_async_copy(
                 grad_ref.at[:, at], out_ref.at[:, at], out_sems.at[step * halves + h]
             )

time: 155 us -> 150 us (0.968)
  Pallas kernels: 30.2 us -> 26 us
    pallas_call x1, Pallas kernels: 19.1 us -> 14.9 us  [on_device(): pl.pallas_call(base_kernel, out_shape=(jax.ShapeDtypeStruct((rows, key_co...]
  transfers between devices with their start and end apart: 19 -> 19, of which waited for: 4 -> 4; matrix products, arithmetic and copies ran while one was open for 0% -> 0% of each run, Pallas kernels for 19% -> 17%
where the time goes in v13:
time: 150 us
  waiting for transfers between devices  68.8 us (46%)
  starting transfers between devices  48.9 us (33%)
  Pallas kernels  26 us (17%)
  local copies, waits for them, and re-layouts  4.79 us (3%)
    ppermute x6, waiting for transfers between devices, route(): return lax.ppermute(x, ('grp', 'y', 'core'), pairs)  31 us
    all_to_all x1, waiting for transfers between devices, on_device(): lax.all_to_all(outgoing, SEQ, split_axis=0, concat_axis=0, tiled=True)  23.1 us
    pallas_call x1, Pallas kernels, on_device(): pl.pallas_call(base_kernel, out_shape=(jax.ShapeDtypeStruct((rows, key_co...  14.9 us
    all_to_all x1, waiting for transfers between devices, on_device(): lax.all_to_all(jnp.broadcast_to(mine, (deep,) + mine.shape), 'z', split_a...  14.2 us
    ppermute x6, starting transfers between devices, shift(): lax.ppermute(x, 'grp', [(i, (i + by) % groups) for i in range(groups)])  11.8 us
    all_to_all x1, starting transfers between devices, on_device(): lax.all_to_all(outgoing, SEQ, split_axis=0, concat_axis=0, tiled=True)  10.7 us
    ppermute x6, starting transfers between devices, route(): return lax.ppermute(x, ('grp', 'y', 'core'), pairs)  9.95 us
    all_to_all x1, starting transfers between devices, on_device(): lax.all_to_all(jnp.broadcast_to(mine, (deep,) + mine.shape), 'z', split_a...  9.01 us
  transfers between devices with their start and end apart: 19, of which 4 were waited for; matrix products, arithmetic and copies ran while one was open for 0% of the time, Pallas kernels for 17%

profile of v13, /device:TPU:1, one launch (start us, length us, event | category | flops | bytes accessed | tf_op | source)
XLA Modules:
  0.0 149.9 jit_solution(7018672972183180935)
XLA Ops:
  2.4 9.0 %all-to-all-start.2 = ((bf16[8,32,1024]{2,1,0:T(8,128)(2,1)}), bf16[8,32,1024]{2,1,0:T(8,128)(2,1)}, u32[]{:S(2)}, u32[]{:S(2)}) async-start(bf16[8,32,1024]{2,1,0:T(8,128)(2,1)} %broadcast_in_dim.3), calls=%async_computation.2 | async-start | bytes 1048576 | tf_op jit(solution)/shard_map/all_to_all | solution.py:273
  11.6 2.6 %collective-permute-start = (bf16[16,72,128]{2,1,0:T(8,128)(2,1)S(1)}, bf16[16,72,128]{2,1,0:T(8,128)(2,1)S(1)}, u32[]{:S(2)}, u32[]{:S(2)}) collective-permute-start(bf16[16,72,128]{2,1,0:T(8,128)(2,1)S(1)} %pack.1.refs_0_), channel_id=1, source_target_pairs={{0,192},{64,0},{128,64},{192,128},{1,193},{65,1},{129,65},{193,129... | collective-permute-start | bytes 884744 | tf_op jit(solution)/shard_map/ppermute | solution.py:239
  15.3 14.2 %all-to-all-done.2.x0 = bf16[8,32,1024]{2,1,0:T(8,128)(2,1)} async-done(((bf16[8,32,1024]{2,1,0:T(8,128)(2,1)}), bf16[8,32,1024]{2,1,0:T(8,128)(2,1)}, u32[]{:S(2)}, u32[]{:S(2)}) %all-to-all-start.2) | async-done | bytes 524320 | tf_op jit(solution)/shard_map/all_to_all | solution.py:273
  29.5 1.2 collective-permute-start.3
  30.7 2.5 %collective-permute-start.4 = (bf16[8,32,1024]{2,1,0:T(8,128)(2,1)}, bf16[8,32,1024]{2,1,0:T(8,128)(2,1)}, u32[]{:S(2)}, u32[]{:S(2)}) collective-permute-start(bf16[8,32,1024]{2,1,0:T(8,128)(2,1)} %all-to-all-done.2.x0), channel_id=1, source_target_pairs={{0,32},{1,129},{16,48},{17,145},{32,0},{33,161},{48,16},{49,177},{... | collective-permute-start | bytes 1572872 | tf_op jit(solution)/shard_map/ppermute | solution.py:250
  33.2 1.2 collective-permute-start.5
  34.4 1.9 %pick.1 = bf16[64,72,128]{2,1,0:T(8,128)(2,1)} custom-call(s32[1]{0:T(128)} %bitcast.group_ref, s32[256]{0:T(256)S(1)} %bitcast.7, s32[64]{0:T(128)S(1)} %copy-done.7, bf16[16,72,128]{2,1,0:T(8,128)(2,1)S(1)} %pack.1.refs_0_, bf16[16,72,128]{2,1,0:T(8,128)(2,1)S(1)} %collective-permute-done.refs_1_, bf16[16,72,128]{2,1,0:T(8,128)(2,1)S(1)} %collective-permute-done.1.refs_2_, ...), custom_call_target="tpu_custom_call" | custom-call | tf_op jit(solution)/shard_map/pick/pallas_call | solution.py:298
  36.3 10.7 %all-to-all-start = ((bf16[64,72,128]{2,1,0:T(8,128)(2,1)}), bf16[64,72,128]{2,1,0:T(8,128)(2,1)S(1)}, u32[]{:S(2)}, u32[]{:S(2)}) async-start(bf16[64,72,128]{2,1,0:T(8,128)(2,1)} %pick.1), calls=%async_computation | async-start | bytes 2359296 | tf_op jit(solution)/shard_map/all_to_all | solution.py:307
  47.1 3.0 %join.1.s0 = bf16[4,8,32,1024]{3,2,1,0:T(8,128)(2,1)} custom-call(bf16[8,32,1024]{2,1,0:T(8,128)(2,1)} %all-to-all-done.2.x0, bf16[8,32,1024]{2,1,0:T(8,128)(2,1)} %collective-permute-done.3.x1, bf16[8,32,1024]{2,1,0:T(8,128)(2,1)} %collective-permute-done.4.x2, bf16[8,32,1024]{2,1,0:T(8,128)(2,1)} %collective-permute-done.5.x3), custom_call_target="tpu_custom_call" | custom-call | tf_op jit(solution)/shard_map/join/pallas_call | solution.py:276
  50.1 1.5 collective-permute-start.7
  51.6 2.6 %collective-permute-start.8 = (bf16[4,8,32,1024]{3,2,1,0:T(8,128)(2,1)}, bf16[4,8,32,1024]{3,2,1,0:T(8,128)(2,1)}, u32[]{:S(2)}, u32[]{:S(2)}) collective-permute-start(bf16[4,8,32,1024]{3,2,1,0:T(8,128)(2,1)} %join.1.s0), channel_id=1, source_target_pairs={{0,128},{1,33},{16,144},{17,49},{32,160},{33,1},{48,176},{49,17},{... | collective-permute-start | bytes 6291464 | tf_op jit(solution)/shard_map/ppermute | solution.py:250
  54.2 1.1 collective-permute-start.9
  55.3 23.1 %all-to-all-done.x_ref = bf16[64,72,128]{2,1,0:T(8,128)(2,1)S(1)} async-done(((bf16[64,72,128]{2,1,0:T(8,128)(2,1)}), bf16[64,72,128]{2,1,0:T(8,128)(2,1)S(1)}, u32[]{:S(2)}, u32[]{:S(2)}) %all-to-all-start) | async-done | bytes 1179680 | tf_op jit(solution)/shard_map/all_to_all | solution.py:307
  78.4 0.9 copy-done.4
  79.3 3.6 %tile.1 = (bf16[64,72,128]{2,1,0:T(8,128)(2,1)S(1)}, bf16[64,9472]{1,0:T(8,128)(2,1)S(1)}) custom-call(bf16[64,72,128]{2,1,0:T(8,128)(2,1)S(1)} %all-to-all-done.x_ref, bf16[128,8192]{1,0:T(8,128)(2,1)S(1)} %copy-done.1, bf16[128,1024]{1,0:T(8,128)(2,1)S(1)} %copy-done.4), custom_call_target="tpu_custom_call" | custom-call | tf_op jit(solution)/shard_map/tile/pallas_call | solution.py:308
  82.9 1.0 copy-done.2
  84.0 1.0 copy-done.3
  85.0 6.3 %all-to-all-start.1 = ((bf16[64,72,128]{2,1,0:T(8,128)(2,1)}), bf16[64,72,128]{2,1,0:T(8,128)(2,1)S(1)}, u32[]{:S(2)}, u32[]{:S(2)}) async-start(bf16[64,72,128]{2,1,0:T(8,128)(2,1)} %copy-done.3), calls=%async_computation.1 | async-start | bytes 2359296 | tf_op jit(solution)/shard_map/all_to_all | solution.py:320
  91.9 31.0 %collective-permute-done.8.s2 = bf16[4,8,32,1024]{3,2,1,0:T(8,128)(2,1)} collective-permute-done((bf16[4,8,32,1024]{3,2,1,0:T(8,128)(2,1)}, bf16[4,8,32,1024]{3,2,1,0:T(8,128)(2,1)}, u32[]{:S(2)}, u32[]{:S(2)}) %collective-permute-start.8) | collective-permute-done | bytes 2097184 | tf_op jit(solution)/shard_map/ppermute | solution.py:250
  124.0 1.3 sum.1
  125.4 4.6 %collective-permute-start.14 = (bf16[16,72,128]{2,1,0:T(8,128)(2,1)S(1)}, bf16[16,72,128]{2,1,0:T(8,128)(2,1)S(1)}, u32[]{:S(2)}, u32[]{:S(2)}) collective-permute-start(bf16[16,72,128]{2,1,0:T(8,128)(2,1)S(1)} %get-tuple-element.35), channel_id=1, source_target_pairs={{0,128},{64,192},{128,0},{192,64},{1,129},{65,193},{129,1},{193,65... | collective-permute-start | bytes 884744 | tf_op jit(solution)/shard_map/ppermute | solution.py:239
  130.4 3.4 %collective-permute-start.15 = (bf16[16,72,128]{2,1,0:T(8,128)(2,1)S(1)}, bf16[16,72,128]{2,1,0:T(8,128)(2,1)S(1)}, u32[]{:S(2)}, u32[]{:S(2)}) collective-permute-start(bf16[16,72,128]{2,1,0:T(8,128)(2,1)S(1)} %get-tuple-element.36), channel_id=1, source_target_pairs={{0,192},{64,0},{128,64},{192,128},{1,193},{65,1},{129,65},{193,129... | collective-permute-start | bytes 884744 | tf_op jit(solution)/shard_map/ppermute | solution.py:239
  133.8 14.9 %base.1 = (bf16[128,1024]{1,0:T(8,128)(2,1)}, bf16[128,8192]{1,0:T(8,128)(2,1)}) custom-call(s32[3]{0:T(128)} %pad_add_fusion.place_ref, bf16[128,8192]{1,0:T(8,128)(2,1)} %tok_ref.3, bf16[128,1024]{1,0:T(8,128)(2,1)} %cot_in.1, bf16[4,8,32,1024]{3,2,1,0:T(8,128)(2,1)} %join.1.s0, bf16[4,8,32,1024]{3,2,1,0:T(8,128)(2,1)} %collective-permute-done.7.s1, ...), custom_call_target="tpu_custom_call" | custom-call | flops 4294967296 | bytes 21495808 | tf_op jit(solution)/shard_map/base/pallas_call | solution.py:346
  148.7 1.2 unpack.1
  (42 shorter events, 5.4 us)
Async XLA Ops:
  0.6 10.8 %copy-start.5 = (bf16[16,144,64]{1,2,0:T(8,128)(2,1)S(1)}, bf16[16,144,64]{1,2,0:T(8,128)(2,1)}, u32[]{:S(2)}) copy-start(bf16[16,144,64]{1,2,0:T(8,128)(2,1)} %param.9) | copy-start | bytes 884740
  0.7 33.7 %copy-start.6 = (s32[256,1]{0,1:T(1,128)S(1)}, s32[256,1]{0,1:T(1,128)}, u32[]{:S(2)}) copy-start(s32[256,1]{0,1:T(1,128)} %param.10) | copy-start | bytes 3076
  0.7 33.7 %copy-start.7 = (s32[64]{0:T(128)S(1)}, s32[64]{0:T(128)}, u32[]{:S(2)}) copy-start(s32[64]{0:T(128)} %slot_ref.3) | copy-start | bytes 772
  2.4 27.1 %all-to-all-start.2 = ((bf16[8,32,1024]{2,1,0:T(8,128)(2,1)}), bf16[8,32,1024]{2,1,0:T(8,128)(2,1)}, u32[]{:S(2)}, u32[]{:S(2)}) async-start(bf16[8,32,1024]{2,1,0:T(8,128)(2,1)} %broadcast_in_dim.3), calls=%async_computation.2 | async-start | bytes 1048576 | tf_op jit(solution)/shard_map/all_to_all | solution.py:273
  11.6 21.6 %collective-permute-start = (bf16[16,72,128]{2,1,0:T(8,128)(2,1)S(1)}, bf16[16,72,128]{2,1,0:T(8,128)(2,1)S(1)}, u32[]{:S(2)}, u32[]{:S(2)}) collective-permute-start(bf16[16,72,128]{2,1,0:T(8,128)(2,1)S(1)} %pack.1.refs_0_), channel_id=1, source_target_pairs={{0,192},{64,0},{128,64},{192,128},{1,193},{65,1},{129,65},{193,129... | collective-permute-start | bytes 884744 | tf_op jit(solution)/shard_map/ppermute | solution.py:239
  14.2 20.2 %collective-permute-start.1 = (bf16[16,72,128]{2,1,0:T(8,128)(2,1)S(1)}, bf16[16,72,128]{2,1,0:T(8,128)(2,1)S(1)}, u32[]{:S(2)}, u32[]{:S(2)}) collective-permute-start(bf16[16,72,128]{2,1,0:T(8,128)(2,1)S(1)} %pack.1.refs_0_), channel_id=1, source_target_pairs={{0,128},{64,192},{128,0},{192,64},{1,129},{65,193},{129,1},{193,65... | collective-permute-start | bytes 884744 | tf_op jit(solution)/shard_map/ppermute | solution.py:239
  14.7 19.7 %collective-permute-start.2 = (bf16[16,72,128]{2,1,0:T(8,128)(2,1)S(1)}, bf16[16,72,128]{2,1,0:T(8,128)(2,1)S(1)}, u32[]{:S(2)}, u32[]{:S(2)}) collective-permute-start(bf16[16,72,128]{2,1,0:T(8,128)(2,1)S(1)} %pack.1.refs_0_), channel_id=1, source_target_pairs={{0,64},{64,128},{128,192},{192,0},{1,65},{65,129},{129,193},{193,1... | collective-permute-start | bytes 884744 | tf_op jit(solution)/shard_map/ppermute | solution.py:239
  29.5 17.5 %collective-permute-start.3 = (bf16[8,32,1024]{2,1,0:T(8,128)(2,1)}, bf16[8,32,1024]{2,1,0:T(8,128)(2,1)}, u32[]{:S(2)}, u32[]{:S(2)}) collective-permute-start(bf16[8,32,1024]{2,1,0:T(8,128)(2,1)} %all-to-all-done.2.x0), channel_id=1, source_target_pairs={{0,16},{1,65},{16,32},{17,81},{32,48},{33,97},{48,0},{49,113},{64,... | collective-permute-start | bytes 1572872 | tf_op jit(solution)/shard_map/ppermute | solution.py:250
  30.7 16.3 %collective-permute-start.4 = (bf16[8,32,1024]{2,1,0:T(8,128)(2,1)}, bf16[8,32,1024]{2,1,0:T(8,128)(2,1)}, u32[]{:S(2)}, u32[]{:S(2)}) collective-permute-start(bf16[8,32,1024]{2,1,0:T(8,128)(2,1)} %all-to-all-done.2.x0), channel_id=1, source_target_pairs={{0,32},{1,129},{16,48},{17,145},{32,0},{33,161},{48,16},{49,177},{... | collective-permute-start | bytes 1572872 | tf_op jit(solution)/shard_map/ppermute | solution.py:250
  33.2 13.9 %collective-permute-start.5 = (bf16[8,32,1024]{2,1,0:T(8,128)(2,1)}, bf16[8,32,1024]{2,1,0:T(8,128)(2,1)}, u32[]{:S(2)}, u32[]{:S(2)}) collective-permute-start(bf16[8,32,1024]{2,1,0:T(8,128)(2,1)} %all-to-all-done.2.x0), channel_id=1, source_target_pairs={{0,48},{1,193},{16,0},{17,209},{32,16},{33,225},{48,32},{49,241},{... | collective-permute-start | bytes 1572872 | tf_op jit(solution)/shard_map/ppermute | solution.py:250
  36.3 42.1 %all-to-all-start = ((bf16[64,72,128]{2,1,0:T(8,128)(2,1)}), bf16[64,72,128]{2,1,0:T(8,128)(2,1)S(1)}, u32[]{:S(2)}, u32[]{:S(2)}) async-start(bf16[64,72,128]{2,1,0:T(8,128)(2,1)} %pick.1), calls=%async_computation | async-start | bytes 2359296 | tf_op jit(solution)/shard_map/all_to_all | solution.py:307
  47.0 31.4 %copy-start.1 = (bf16[128,8192]{1,0:T(8,128)(2,1)S(1)}, bf16[128,8192]{1,0:T(8,128)(2,1)}, u32[]{:S(2)}) copy-start(bf16[128,8192]{1,0:T(8,128)(2,1)} %tok_ref.3) | copy-start | bytes 6291460
  50.1 41.7 %collective-permute-start.7 = (bf16[4,8,32,1024]{3,2,1,0:T(8,128)(2,1)}, bf16[4,8,32,1024]{3,2,1,0:T(8,128)(2,1)}, u32[]{:S(2)}, u32[]{:S(2)}) collective-permute-start(bf16[4,8,32,1024]{3,2,1,0:T(8,128)(2,1)} %join.1.s0), channel_id=1, source_target_pairs={{0,64},{1,17},{16,80},{17,33},{32,96},{33,49},{48,112},{49,1},{64,... | collective-permute-start | bytes 6291464 | tf_op jit(solution)/shard_map/ppermute | solution.py:250
  51.6 71.3 %collective-permute-start.8 = (bf16[4,8,32,1024]{3,2,1,0:T(8,128)(2,1)}, bf16[4,8,32,1024]{3,2,1,0:T(8,128)(2,1)}, u32[]{:S(2)}, u32[]{:S(2)}) collective-permute-start(bf16[4,8,32,1024]{3,2,1,0:T(8,128)(2,1)} %join.1.s0), channel_id=1, source_target_pairs={{0,128},{1,33},{16,144},{17,49},{32,160},{33,1},{48,176},{49,17},{... | collective-permute-start | bytes 6291464 | tf_op jit(solution)/shard_map/ppermute | solution.py:250
  54.2 68.7 %collective-permute-start.9 = (bf16[4,8,32,1024]{3,2,1,0:T(8,128)(2,1)}, bf16[4,8,32,1024]{3,2,1,0:T(8,128)(2,1)}, u32[]{:S(2)}, u32[]{:S(2)}) collective-permute-start(bf16[4,8,32,1024]{3,2,1,0:T(8,128)(2,1)} %join.1.s0), channel_id=1, source_target_pairs={{0,192},{1,49},{16,208},{17,1},{32,224},{33,17},{48,240},{49,33},{... | collective-permute-start | bytes 6291464 | tf_op jit(solution)/shard_map/ppermute | solution.py:250
  85.0 39.0 %all-to-all-start.1 = ((bf16[64,72,128]{2,1,0:T(8,128)(2,1)}), bf16[64,72,128]{2,1,0:T(8,128)(2,1)S(1)}, u32[]{:S(2)}, u32[]{:S(2)}) async-start(bf16[64,72,128]{2,1,0:T(8,128)(2,1)} %copy-done.3), calls=%async_computation.1 | async-start | bytes 2359296 | tf_op jit(solution)/shard_map/all_to_all | solution.py:320
  91.3 32.7 %collective-permute-start.6 = (bf16[4,8,32,1024]{3,2,1,0:T(8,128)(2,1)}, bf16[4,8,32,1024]{3,2,1,0:T(8,128)(2,1)S(1)}, u32[]{:S(2)}, u32[]{:S(2)}) collective-permute-start(bf16[4,8,32,1024]{3,2,1,0:T(8,128)(2,1)} %join.1.s0), channel_id=1, source_target_pairs={{0,1},{1,0},{2,3},{3,2},{4,5},{5,4},{6,7},{7,6},{8,9},{9,8},{10,11... | collective-permute-start | bytes 6291464 | tf_op jit(solution)/shard_map/ppermute | solution.py:286
  91.8 38.2 %collective-permute-start.10 = (bf16[4,8,32,1024]{3,2,1,0:T(8,128)(2,1)}, bf16[4,8,32,1024]{3,2,1,0:T(8,128)(2,1)}, u32[]{:S(2)}, u32[]{:S(2)}) collective-permute-start(bf16[4,8,32,1024]{3,2,1,0:T(8,128)(2,1)} %collective-permute-done.7.s1), channel_id=1, source_target_pairs={{0,1},{1,0},{2,3},{3,2},{4,5},{5,4},{6,7},{7,6},{8,9},{9,8},{10,11... | collective-permute-start | bytes 6291464 | tf_op jit(solution)/shard_map/ppermute | solution.py:286
  122.9 7.1 %collective-permute-start.11 = (bf16[4,8,32,1024]{3,2,1,0:T(8,128)(2,1)}, bf16[4,8,32,1024]{3,2,1,0:T(8,128)(2,1)}, u32[]{:S(2)}, u32[]{:S(2)}) collective-permute-start(bf16[4,8,32,1024]{3,2,1,0:T(8,128)(2,1)} %collective-permute-done.8.s2), channel_id=1, source_target_pairs={{0,1},{1,0},{2,3},{3,2},{4,5},{5,4},{6,7},{7,6},{8,9},{9,8},{10,11... | collective-permute-start | bytes 6291464 | tf_op jit(solution)/shard_map/ppermute | solution.py:286
  122.9 7.5 %collective-permute-start.12 = (bf16[4,8,32,1024]{3,2,1,0:T(8,128)(2,1)}, bf16[4,8,32,1024]{3,2,1,0:T(8,128)(2,1)}, u32[]{:S(2)}, u32[]{:S(2)}) collective-permute-start(bf16[4,8,32,1024]{3,2,1,0:T(8,128)(2,1)} %collective-permute-done.9.s3), channel_id=1, source_target_pairs={{0,1},{1,0},{2,3},{3,2},{4,5},{5,4},{6,7},{7,6},{8,9},{9,8},{10,11... | collective-permute-start | bytes 6291464 | tf_op jit(solution)/shard_map/ppermute | solution.py:286
  124.0 9.8 %copy-start.8 = (bf16[4,8,32,1024]{3,2,1,0:T(8,128)(2,1)}, bf16[4,8,32,1024]{3,2,1,0:T(8,128)(2,1)S(1)}, u32[]{:S(2)}) copy-start(bf16[4,8,32,1024]{3,2,1,0:T(8,128)(2,1)S(1)} %collective-permute-done.6.t0) | copy-start | bytes 6291460
  125.3 23.4 %collective-permute-start.13 = (bf16[16,72,128]{2,1,0:T(8,128)(2,1)S(1)}, bf16[16,72,128]{2,1,0:T(8,128)(2,1)S(1)}, u32[]{:S(2)}, u32[]{:S(2)}) collective-permute-start(bf16[16,72,128]{2,1,0:T(8,128)(2,1)S(1)} %get-tuple-element.34), channel_id=1, source_target_pairs={{0,64},{64,128},{128,192},{192,0},{1,65},{65,129},{129,193},{193,1... | collective-permute-start | bytes 884744 | tf_op jit(solution)/shard_map/ppermute | solution.py:239
  125.4 23.3 %collective-permute-start.14 = (bf16[16,72,128]{2,1,0:T(8,128)(2,1)S(1)}, bf16[16,72,128]{2,1,0:T(8,128)(2,1)S(1)}, u32[]{:S(2)}, u32[]{:S(2)}) collective-permute-start(bf16[16,72,128]{2,1,0:T(8,128)(2,1)S(1)} %get-tuple-element.35), channel_id=1, source_target_pairs={{0,128},{64,192},{128,0},{192,64},{1,129},{65,193},{129,1},{193,65... | collective-permute-start | bytes 884744 | tf_op jit(solution)/shard_map/ppermute | solution.py:239
  130.4 18.3 %collective-permute-start.15 = (bf16[16,72,128]{2,1,0:T(8,128)(2,1)S(1)}, bf16[16,72,128]{2,1,0:T(8,128)(2,1)S(1)}, u32[]{:S(2)}, u32[]{:S(2)}) collective-permute-start(bf16[16,72,128]{2,1,0:T(8,128)(2,1)S(1)} %get-tuple-element.36), channel_id=1, source_target_pairs={{0,192},{64,0},{128,64},{192,128},{1,193},{65,1},{129,65},{193,129... | collective-permute-start | bytes 884744 | tf_op jit(solution)/shard_map/ppermute | solution.py:239
  (4 other events, 4.0 us)

commit v14 on v13

--- a/solution.py
+++ b/solution.py
@@ -162,7 +162,7 @@
 
 
 def base_kernel(
-    place_ref, tok_ref, cot_in, s0, s1, s2, s3, t0, t1, t2, t3, adapter_in, keys_ref, out_ref,
+    place_ref, tok_ref, cot_in, s0, s1, s2, s2b, s3, t0, t1, t2, t2b, t3, adapter_in, keys_ref, out_ref,
     w_ref, grad_ref, acc_ref, cot_ref, adapter_ref, sems, out_sems, in_sems,
 ):
     wide, cores, groups, deep, _, key_columns = w_ref.shape
@@ -180,19 +180,28 @@
         g = lax.rem(place_ref[0] - k + groups, groups)
         pltpu.make_async_copy(source, w_ref.at[back, c, g], sems.at[back, c, g]).start()
 
+    def piece(sources, a, b):
+        first, second, low, high, last = sources
+        if a == 2:
+            cut = low.shape[0]
+            return low.at[b] if b < cut else high.at[b - cut]
+        return (first, second, None, last)[a].at[b]
+
     def fetch_all(along_y_first, along_y_second):
         for back in range(wide):
             for k in range(groups):
-                fetch(along_y_first[k].at[back], back, 0, k)
-                fetch(along_y_second[back].at[k], back, 1, k)
+                fetch(piece(along_y_first, k, back), back, 0, k)
+                fetch(piece(along_y_second, back, k), back, 1, k)
+
+    own, swapped = (s0, s1, s2, s2b, s3), (t0, t1, t2, t2b, t3)
 
     @pl.when(core == 0)
     def _():
-        fetch_all((s0, s1, s2, s3), (t0, t1, t2, t3))
+        fetch_all(own, swapped)
 
     @pl.when(core == 1)
     def _():
-        fetch_all((t0, t1, t2, t3), (s0, s1, s2, s3))
+        fetch_all(swapped, own)
 
     for copy in inputs:
         copy.wait()
@@ -282,7 +291,15 @@
         compiler_params=params(),
         name="join",
     )(column, *[route(column, k, groups, wide, True) for k in range(1, wide)])
-    halves = [line] + [route(line, k, groups, wide, False) for k in range(1, groups)]
+    before, after = route(line, 1, groups, wide, False), route(line, groups - 1, groups, wide, False)
+    cut = wide // 2
+    halves = [
+        line,
+        before,
+        route(before[:cut], 1, groups, wide, False),
+        route(after[cut:], groups - 1, groups, wide, False),
+        after,
+    ]
     others = [lax.ppermute(x, "core", [(0, 1), (1, 0)]) for x in halves]
 
     own = pl.pallas_call(
@@ -349,7 +366,7 @@
             jax.ShapeDtypeStruct((rows, key_columns), bf16),
             jax.ShapeDtypeStruct((rows, depth), bf16),
         ),
-        in_specs=[smem, whole()] + [whole(pltpu.HBM)] * (2 * groups + 2),
+        in_specs=[smem, whole()] + [whole(pltpu.HBM)] * (len(halves) + len(others) + 2),
         out_specs=(whole(), whole(pltpu.HBM)),
         scratch_shapes=[
             pltpu.VMEM(blocks, bf16),

time: 150 us -> 145 us (0.967)
  waiting for transfers between devices: 68.8 us -> 63.1 us
  local copies, waits for them, and re-layouts: 4.79 us -> 7.41 us
  starting transfers between devices: 48.9 us -> 46.7 us
    ppermute x6 -> x7, waiting for transfers between devices: 31 us -> 20 us  [route(): return lax.ppermute(x, ('grp', 'y', 'core'), pairs)]
    all_to_all x1, waiting for transfers between devices: 0.01 us -> 3.62 us  [on_device(): lax.all_to_all(terms, SEQ, split_axis=0, concat_axis=0, tiled=True)]
    ppermute x6, starting transfers between devices: 11.8 us -> 8.42 us  [shift(): lax.ppermute(x, 'grp', [(i, (i + by) % groups) for i in range(groups)])]
    slice x0 -> x2, local copies, waits for them, and re-layouts: none -> 2.63 us  [the longest x1 1.31 us: on_device(): before[:cut]]
    all_to_all x1, waiting for transfers between devices: 23.1 us -> 25.3 us  [on_device(): lax.all_to_all(outgoing, SEQ, split_axis=0, concat_axis=0, tiled=True)]
    ppermute x6 -> x7, starting transfers between devices: 9.95 us -> 10.7 us  [route(): return lax.ppermute(x, ('grp', 'y', 'core'), pairs)]
  transfers between devices with their start and end apart: 19 -> 21, of which waited for: 4 -> 5; matrix products, arithmetic and copies ran while one was open for 0% -> 2% of each run, Pallas kernels for 17% -> 17%
where the time goes in v14:
time: 145 us
  waiting for transfers between devices  63.1 us (44%)
  starting transfers between devices  46.7 us (32%)
  Pallas kernels  26 us (18%)
  local copies, waits for them, and re-layouts  7.41 us (5%)
    all_to_all x1, waiting for transfers between devices, on_device(): lax.all_to_all(outgoing, SEQ, split_axis=0, concat_axis=0, tiled=True)  25.3 us
    ppermute x7, waiting for transfers between devices, route(): return lax.ppermute(x, ('grp', 'y', 'core'), pairs)  20 us
    pallas_call x1, Pallas kernels, on_device(): pl.pallas_call(base_kernel, out_shape=(jax.ShapeDtypeStruct((rows, key_co...  14.9 us
    all_to_all x1, waiting for transfers between devices, on_device(): lax.all_to_all(jnp.broadcast_to(mine, (deep,) + mine.shape), 'z', split_a...  14.2 us
    all_to_all x1, starting transfers between devices, on_device(): lax.all_to_all(outgoing, SEQ, split_axis=0, concat_axis=0, tiled=True)  10.7 us
    ppermute x7, starting transfers between devices, route(): return lax.ppermute(x, ('grp', 'y', 'core'), pairs)  10.7 us
    all_to_all x1, starting transfers between devices, on_device(): lax.all_to_all(jnp.broadcast_to(mine, (deep,) + mine.shape), 'z', split_a...  9.01 us
    ppermute x6, starting transfers between devices, shift(): lax.ppermute(x, 'grp', [(i, (i + by) % groups) for i in range(groups)])  8.42 us
  transfers between devices with their start and end apart: 21, of which 5 were waited for; matrix products, arithmetic and copies ran while one was open for 2% of the time, Pallas kernels for 17%

profile of v14, /device:TPU:1, one launch (start us, length us, event | category | flops | bytes accessed | tf_op | source)
XLA Modules:
  0.0 144.8 jit_solution(8035351301301519712)
XLA Ops:
  2.4 9.0 %all-to-all-start.2 = ((bf16[8,32,1024]{2,1,0:T(8,128)(2,1)}), bf16[8,32,1024]{2,1,0:T(8,128)(2,1)}, u32[]{:S(2)}, u32[]{:S(2)}) async-start(bf16[8,32,1024]{2,1,0:T(8,128)(2,1)} %broadcast_in_dim.3), calls=%async_computation.2 | async-start | bytes 1048576 | tf_op jit(solution)/shard_map/all_to_all | solution.py:282
  11.6 2.6 %collective-permute-start = (bf16[16,72,128]{2,1,0:T(8,128)(2,1)S(1)}, bf16[16,72,128]{2,1,0:T(8,128)(2,1)S(1)}, u32[]{:S(2)}, u32[]{:S(2)}) collective-permute-start(bf16[16,72,128]{2,1,0:T(8,128)(2,1)S(1)} %pack.1.refs_0_), channel_id=1, source_target_pairs={{0,192},{64,0},{128,64},{192,128},{1,193},{65,1},{129,65},{193,129... | collective-permute-start | bytes 884744 | tf_op jit(solution)/shard_map/ppermute | solution.py:248
  15.3 14.2 %all-to-all-done.2.x0 = bf16[8,32,1024]{2,1,0:T(8,128)(2,1)} async-done(((bf16[8,32,1024]{2,1,0:T(8,128)(2,1)}), bf16[8,32,1024]{2,1,0:T(8,128)(2,1)}, u32[]{:S(2)}, u32[]{:S(2)}) %all-to-all-start.2) | async-done | bytes 524320 | tf_op jit(solution)/shard_map/all_to_all | solution.py:282
  29.5 1.2 collective-permute-start.3
  30.7 2.5 %collective-permute-start.4 = (bf16[8,32,1024]{2,1,0:T(8,128)(2,1)}, bf16[8,32,1024]{2,1,0:T(8,128)(2,1)}, u32[]{:S(2)}, u32[]{:S(2)}) collective-permute-start(bf16[8,32,1024]{2,1,0:T(8,128)(2,1)} %all-to-all-done.2.x0), channel_id=1, source_target_pairs={{0,32},{1,129},{16,48},{17,145},{32,0},{33,161},{48,16},{49,177},{... | collective-permute-start | bytes 1572872 | tf_op jit(solution)/shard_map/ppermute | solution.py:259
  33.2 1.2 collective-permute-start.5
  34.4 1.9 %pick.1 = bf16[64,72,128]{2,1,0:T(8,128)(2,1)} custom-call(s32[1]{0:T(128)} %bitcast.group_ref, s32[256]{0:T(256)S(1)} %bitcast.7, s32[64]{0:T(128)S(1)} %copy-done.7, bf16[16,72,128]{2,1,0:T(8,128)(2,1)S(1)} %pack.1.refs_0_, bf16[16,72,128]{2,1,0:T(8,128)(2,1)S(1)} %collective-permute-done.refs_1_, bf16[16,72,128]{2,1,0:T(8,128)(2,1)S(1)} %collective-permute-done.1.refs_2_, ...), custom_call_target="tpu_custom_call" | custom-call | tf_op jit(solution)/shard_map/pick/pallas_call | solution.py:315
  36.3 10.7 %all-to-all-start = ((bf16[64,72,128]{2,1,0:T(8,128)(2,1)}), bf16[64,72,128]{2,1,0:T(8,128)(2,1)S(1)}, u32[]{:S(2)}, u32[]{:S(2)}) async-start(bf16[64,72,128]{2,1,0:T(8,128)(2,1)} %pick.1), calls=%async_computation | async-start | bytes 2359296 | tf_op jit(solution)/shard_map/all_to_all | solution.py:324
  47.1 3.0 %join.1.s0 = bf16[4,8,32,1024]{3,2,1,0:T(8,128)(2,1)} custom-call(bf16[8,32,1024]{2,1,0:T(8,128)(2,1)} %all-to-all-done.2.x0, bf16[8,32,1024]{2,1,0:T(8,128)(2,1)} %collective-permute-done.3.x1, bf16[8,32,1024]{2,1,0:T(8,128)(2,1)} %collective-permute-done.4.x2, bf16[8,32,1024]{2,1,0:T(8,128)(2,1)} %collective-permute-done.5.x3), custom_call_target="tpu_custom_call" | custom-call | tf_op jit(solution)/shard_map/join/pallas_call | solution.py:285
  50.1 1.5 %collective-permute-start.7 = (bf16[4,8,32,1024]{3,2,1,0:T(8,128)(2,1)}, bf16[4,8,32,1024]{3,2,1,0:T(8,128)(2,1)}, u32[]{:S(2)}, u32[]{:S(2)}) collective-permute-start(bf16[4,8,32,1024]{3,2,1,0:T(8,128)(2,1)} %join.1.s0), channel_id=1, source_target_pairs={{0,64},{1,17},{16,80},{17,33},{32,96},{33,49},{48,112},{49,1},{64,... | collective-permute-start | bytes 6291464 | tf_op jit(solution)/shard_map/ppermute | solution.py:259
  51.6 1.5 %collective-permute-start.9 = (bf16[4,8,32,1024]{3,2,1,0:T(8,128)(2,1)}, bf16[4,8,32,1024]{3,2,1,0:T(8,128)(2,1)}, u32[]{:S(2)}, u32[]{:S(2)}) collective-permute-start(bf16[4,8,32,1024]{3,2,1,0:T(8,128)(2,1)} %join.1.s0), channel_id=1, source_target_pairs={{0,192},{1,49},{16,208},{17,1},{32,224},{33,17},{48,240},{49,33},{... | collective-permute-start | bytes 6291464 | tf_op jit(solution)/shard_map/ppermute | solution.py:259
  53.1 25.3 %all-to-all-done.x_ref = bf16[64,72,128]{2,1,0:T(8,128)(2,1)S(1)} async-done(((bf16[64,72,128]{2,1,0:T(8,128)(2,1)}), bf16[64,72,128]{2,1,0:T(8,128)(2,1)S(1)}, u32[]{:S(2)}, u32[]{:S(2)}) %all-to-all-start) | async-done | bytes 1179680 | tf_op jit(solution)/shard_map/all_to_all | solution.py:324
  79.3 3.6 %tile.1 = (bf16[64,72,128]{2,1,0:T(8,128)(2,1)S(1)}, bf16[64,9472]{1,0:T(8,128)(2,1)S(1)}) custom-call(bf16[64,72,128]{2,1,0:T(8,128)(2,1)S(1)} %all-to-all-done.x_ref, bf16[128,8192]{1,0:T(8,128)(2,1)S(1)} %copy-done.1, bf16[128,1024]{1,0:T(8,128)(2,1)S(1)} %copy-done.4), custom_call_target="tpu_custom_call" | custom-call | tf_op jit(solution)/shard_map/tile/pallas_call | solution.py:325
  85.0 6.3 %all-to-all-start.1 = ((bf16[64,72,128]{2,1,0:T(8,128)(2,1)}), bf16[64,72,128]{2,1,0:T(8,128)(2,1)S(1)}, u32[]{:S(2)}, u32[]{:S(2)}) async-start(bf16[64,72,128]{2,1,0:T(8,128)(2,1)} %copy-done.3), calls=%async_computation.1 | async-start | bytes 2359296 | tf_op jit(solution)/shard_map/all_to_all | solution.py:337
  91.8 1.3 slice.8
  93.1 1.4 collective-permute-start.8
  94.5 1.3 slice.9
  95.8 1.5 %collective-permute-start.10 = (bf16[2,8,32,1024]{3,2,1,0:T(8,128)(2,1)S(1)}, bf16[2,8,32,1024]{3,2,1,0:T(8,128)(2,1)}, u32[]{:S(2)}, u32[]{:S(2)}) collective-permute-start(bf16[2,8,32,1024]{3,2,1,0:T(8,128)(2,1)S(1)} %slice.9), channel_id=1, source_target_pairs={{0,192},{1,49},{16,208},{17,1},{32,224},{33,17},{48,240},{49,33},{... | collective-permute-start | bytes 3145736 | tf_op jit(solution)/shard_map/ppermute | solution.py:259
  98.4 19.2 %collective-permute-done.8.s2 = bf16[2,8,32,1024]{3,2,1,0:T(8,128)(2,1)} collective-permute-done((bf16[2,8,32,1024]{3,2,1,0:T(8,128)(2,1)S(1)}, bf16[2,8,32,1024]{3,2,1,0:T(8,128)(2,1)}, u32[]{:S(2)}, u32[]{:S(2)}) %collective-permute-start.8) | collective-permute-done | bytes 1048608 | tf_op jit(solution)/shard_map/ppermute | solution.py:259
  119.0 3.6 %all-to-all-done.1.x_ref = bf16[64,72,128]{2,1,0:T(8,128)(2,1)S(1)} async-done(((bf16[64,72,128]{2,1,0:T(8,128)(2,1)}), bf16[64,72,128]{2,1,0:T(8,128)(2,1)S(1)}, u32[]{:S(2)}, u32[]{:S(2)}) %all-to-all-start.1) | async-done | bytes 1179680 | tf_op jit(solution)/shard_map/all_to_all | solution.py:337
  122.6 1.3 sum.1
  124.0 4.6 %collective-permute-start.16 = (bf16[16,72,128]{2,1,0:T(8,128)(2,1)S(1)}, bf16[16,72,128]{2,1,0:T(8,128)(2,1)S(1)}, u32[]{:S(2)}, u32[]{:S(2)}) collective-permute-start(bf16[16,72,128]{2,1,0:T(8,128)(2,1)S(1)} %get-tuple-element.37), channel_id=1, source_target_pairs={{0,128},{64,192},{128,0},{192,64},{1,129},{65,193},{129,1},{193,65... | collective-permute-start | bytes 884744 | tf_op jit(solution)/shard_map/ppermute | solution.py:248
  128.7 14.9 %base.1 = (bf16[128,1024]{1,0:T(8,128)(2,1)}, bf16[128,8192]{1,0:T(8,128)(2,1)}) custom-call(s32[3]{0:T(128)} %pad_add_fusion.place_ref, bf16[128,8192]{1,0:T(8,128)(2,1)} %tok_ref.3, bf16[128,1024]{1,0:T(8,128)(2,1)} %cot_in.1, bf16[4,8,32,1024]{3,2,1,0:T(8,128)(2,1)} %join.1.s0, bf16[4,8,32,1024]{3,2,1,0:T(8,128)(2,1)} %collective-permute-done.7.s1, ...), custom_call_target="tpu_custom_call" | custom-call | flops 4294967296 | bytes 21495808 | tf_op jit(solution)/shard_map/base/pallas_call | solution.py:363
  143.6 1.2 unpack.1
  (48 shorter events, 9.3 us)
Async XLA Ops:
  0.7 33.7 %copy-start.6 = (s32[256,1]{0,1:T(1,128)S(1)}, s32[256,1]{0,1:T(1,128)}, u32[]{:S(2)}) copy-start(s32[256,1]{0,1:T(1,128)} %param.10) | copy-start | bytes 3076
  0.7 33.7 %copy-start.7 = (s32[64]{0:T(128)S(1)}, s32[64]{0:T(128)}, u32[]{:S(2)}) copy-start(s32[64]{0:T(128)} %slot_ref.3) | copy-start | bytes 772
  2.4 27.1 %all-to-all-start.2 = ((bf16[8,32,1024]{2,1,0:T(8,128)(2,1)}), bf16[8,32,1024]{2,1,0:T(8,128)(2,1)}, u32[]{:S(2)}, u32[]{:S(2)}) async-start(bf16[8,32,1024]{2,1,0:T(8,128)(2,1)} %broadcast_in_dim.3), calls=%async_computation.2 | async-start | bytes 1048576 | tf_op jit(solution)/shard_map/all_to_all | solution.py:282
  11.6 21.6 %collective-permute-start = (bf16[16,72,128]{2,1,0:T(8,128)(2,1)S(1)}, bf16[16,72,128]{2,1,0:T(8,128)(2,1)S(1)}, u32[]{:S(2)}, u32[]{:S(2)}) collective-permute-start(bf16[16,72,128]{2,1,0:T(8,128)(2,1)S(1)} %pack.1.refs_0_), channel_id=1, source_target_pairs={{0,192},{64,0},{128,64},{192,128},{1,193},{65,1},{129,65},{193,129... | collective-permute-start | bytes 884744 | tf_op jit(solution)/shard_map/ppermute | solution.py:248
  14.2 20.2 %collective-permute-start.1 = (bf16[16,72,128]{2,1,0:T(8,128)(2,1)S(1)}, bf16[16,72,128]{2,1,0:T(8,128)(2,1)S(1)}, u32[]{:S(2)}, u32[]{:S(2)}) collective-permute-start(bf16[16,72,128]{2,1,0:T(8,128)(2,1)S(1)} %pack.1.refs_0_), channel_id=1, source_target_pairs={{0,128},{64,192},{128,0},{192,64},{1,129},{65,193},{129,1},{193,65... | collective-permute-start | bytes 884744 | tf_op jit(solution)/shard_map/ppermute | solution.py:248
  14.7 19.7 %collective-permute-start.2 = (bf16[16,72,128]{2,1,0:T(8,128)(2,1)S(1)}, bf16[16,72,128]{2,1,0:T(8,128)(2,1)S(1)}, u32[]{:S(2)}, u32[]{:S(2)}) collective-permute-start(bf16[16,72,128]{2,1,0:T(8,128)(2,1)S(1)} %pack.1.refs_0_), channel_id=1, source_target_pairs={{0,64},{64,128},{128,192},{192,0},{1,65},{65,129},{129,193},{193,1... | collective-permute-start | bytes 884744 | tf_op jit(solution)/shard_map/ppermute | solution.py:248
  29.5 17.5 %collective-permute-start.3 = (bf16[8,32,1024]{2,1,0:T(8,128)(2,1)}, bf16[8,32,1024]{2,1,0:T(8,128)(2,1)}, u32[]{:S(2)}, u32[]{:S(2)}) collective-permute-start(bf16[8,32,1024]{2,1,0:T(8,128)(2,1)} %all-to-all-done.2.x0), channel_id=1, source_target_pairs={{0,16},{1,65},{16,32},{17,81},{32,48},{33,97},{48,0},{49,113},{64,... | collective-permute-start | bytes 1572872 | tf_op jit(solution)/shard_map/ppermute | solution.py:259
  30.7 16.3 %collective-permute-start.4 = (bf16[8,32,1024]{2,1,0:T(8,128)(2,1)}, bf16[8,32,1024]{2,1,0:T(8,128)(2,1)}, u32[]{:S(2)}, u32[]{:S(2)}) collective-permute-start(bf16[8,32,1024]{2,1,0:T(8,128)(2,1)} %all-to-all-done.2.x0), channel_id=1, source_target_pairs={{0,32},{1,129},{16,48},{17,145},{32,0},{33,161},{48,16},{49,177},{... | collective-permute-start | bytes 1572872 | tf_op jit(solution)/shard_map/ppermute | solution.py:259
  33.2 13.9 %collective-permute-start.5 = (bf16[8,32,1024]{2,1,0:T(8,128)(2,1)}, bf16[8,32,1024]{2,1,0:T(8,128)(2,1)}, u32[]{:S(2)}, u32[]{:S(2)}) collective-permute-start(bf16[8,32,1024]{2,1,0:T(8,128)(2,1)} %all-to-all-done.2.x0), channel_id=1, source_target_pairs={{0,48},{1,193},{16,0},{17,209},{32,16},{33,225},{48,32},{49,241},{... | collective-permute-start | bytes 1572872 | tf_op jit(solution)/shard_map/ppermute | solution.py:259
  36.3 42.1 %all-to-all-start = ((bf16[64,72,128]{2,1,0:T(8,128)(2,1)}), bf16[64,72,128]{2,1,0:T(8,128)(2,1)S(1)}, u32[]{:S(2)}, u32[]{:S(2)}) async-start(bf16[64,72,128]{2,1,0:T(8,128)(2,1)} %pick.1), calls=%async_computation | async-start | bytes 2359296 | tf_op jit(solution)/shard_map/all_to_all | solution.py:324
  47.0 31.4 %copy-start.1 = (bf16[128,8192]{1,0:T(8,128)(2,1)S(1)}, bf16[128,8192]{1,0:T(8,128)(2,1)}, u32[]{:S(2)}) copy-start(bf16[128,8192]{1,0:T(8,128)(2,1)} %tok_ref.3) | copy-start | bytes 6291460
  50.1 41.7 %collective-permute-start.7 = (bf16[4,8,32,1024]{3,2,1,0:T(8,128)(2,1)}, bf16[4,8,32,1024]{3,2,1,0:T(8,128)(2,1)}, u32[]{:S(2)}, u32[]{:S(2)}) collective-permute-start(bf16[4,8,32,1024]{3,2,1,0:T(8,128)(2,1)} %join.1.s0), channel_id=1, source_target_pairs={{0,64},{1,17},{16,80},{17,33},{32,96},{33,49},{48,112},{49,1},{64,... | collective-permute-start | bytes 6291464 | tf_op jit(solution)/shard_map/ppermute | solution.py:259
  51.6 42.9 %collective-permute-start.9 = (bf16[4,8,32,1024]{3,2,1,0:T(8,128)(2,1)}, bf16[4,8,32,1024]{3,2,1,0:T(8,128)(2,1)}, u32[]{:S(2)}, u32[]{:S(2)}) collective-permute-start(bf16[4,8,32,1024]{3,2,1,0:T(8,128)(2,1)} %join.1.s0), channel_id=1, source_target_pairs={{0,192},{1,49},{16,208},{17,1},{32,224},{33,17},{48,240},{49,33},{... | collective-permute-start | bytes 6291464 | tf_op jit(solution)/shard_map/ppermute | solution.py:259
  85.0 37.7 %all-to-all-start.1 = ((bf16[64,72,128]{2,1,0:T(8,128)(2,1)}), bf16[64,72,128]{2,1,0:T(8,128)(2,1)S(1)}, u32[]{:S(2)}, u32[]{:S(2)}) async-start(bf16[64,72,128]{2,1,0:T(8,128)(2,1)} %copy-done.3), calls=%async_computation.1 | async-start | bytes 2359296 | tf_op jit(solution)/shard_map/all_to_all | solution.py:337
  91.3 27.7 %collective-permute-start.6 = (bf16[4,8,32,1024]{3,2,1,0:T(8,128)(2,1)}, bf16[4,8,32,1024]{3,2,1,0:T(8,128)(2,1)S(1)}, u32[]{:S(2)}, u32[]{:S(2)}) collective-permute-start(bf16[4,8,32,1024]{3,2,1,0:T(8,128)(2,1)} %join.1.s0), channel_id=1, source_target_pairs={{0,1},{1,0},{2,3},{3,2},{4,5},{5,4},{6,7},{7,6},{8,9},{9,8},{10,11... | collective-permute-start | bytes 6291464 | tf_op jit(solution)/shard_map/ppermute | solution.py:303
  93.1 24.4 %collective-permute-start.8 = (bf16[2,8,32,1024]{3,2,1,0:T(8,128)(2,1)S(1)}, bf16[2,8,32,1024]{3,2,1,0:T(8,128)(2,1)}, u32[]{:S(2)}, u32[]{:S(2)}) collective-permute-start(bf16[2,8,32,1024]{3,2,1,0:T(8,128)(2,1)S(1)} %slice.8), channel_id=1, source_target_pairs={{0,64},{1,17},{16,80},{17,33},{32,96},{33,49},{48,112},{49,1},{64,... | collective-permute-start | bytes 3145736 | tf_op jit(solution)/shard_map/ppermute | solution.py:259
  95.8 22.5 %collective-permute-start.10 = (bf16[2,8,32,1024]{3,2,1,0:T(8,128)(2,1)S(1)}, bf16[2,8,32,1024]{3,2,1,0:T(8,128)(2,1)}, u32[]{:S(2)}, u32[]{:S(2)}) collective-permute-start(bf16[2,8,32,1024]{3,2,1,0:T(8,128)(2,1)S(1)} %slice.9), channel_id=1, source_target_pairs={{0,192},{1,49},{16,208},{17,1},{32,224},{33,17},{48,240},{49,33},{... | collective-permute-start | bytes 3145736 | tf_op jit(solution)/shard_map/ppermute | solution.py:259
  97.3 31.2 %collective-permute-start.11 = (bf16[4,8,32,1024]{3,2,1,0:T(8,128)(2,1)}, bf16[4,8,32,1024]{3,2,1,0:T(8,128)(2,1)}, u32[]{:S(2)}, u32[]{:S(2)}) collective-permute-start(bf16[4,8,32,1024]{3,2,1,0:T(8,128)(2,1)} %collective-permute-done.7.s1), channel_id=1, source_target_pairs={{0,1},{1,0},{2,3},{3,2},{4,5},{5,4},{6,7},{7,6},{8,9},{9,8},{10,11... | collective-permute-start | bytes 6291464 | tf_op jit(solution)/shard_map/ppermute | solution.py:303
  98.4 30.2 %collective-permute-start.14 = (bf16[4,8,32,1024]{3,2,1,0:T(8,128)(2,1)}, bf16[4,8,32,1024]{3,2,1,0:T(8,128)(2,1)}, u32[]{:S(2)}, u32[]{:S(2)}) collective-permute-start(bf16[4,8,32,1024]{3,2,1,0:T(8,128)(2,1)} %collective-permute-done.9.s3), channel_id=1, source_target_pairs={{0,1},{1,0},{2,3},{3,2},{4,5},{5,4},{6,7},{7,6},{8,9},{9,8},{10,11... | collective-permute-start | bytes 6291464 | tf_op jit(solution)/shard_map/ppermute | solution.py:303
  117.5 6.5 %collective-permute-start.12 = (bf16[2,8,32,1024]{3,2,1,0:T(8,128)(2,1)}, bf16[2,8,32,1024]{3,2,1,0:T(8,128)(2,1)}, u32[]{:S(2)}, u32[]{:S(2)}) collective-permute-start(bf16[2,8,32,1024]{3,2,1,0:T(8,128)(2,1)} %collective-permute-done.8.s2), channel_id=1, source_target_pairs={{0,1},{1,0},{2,3},{3,2},{4,5},{5,4},{6,7},{7,6},{8,9},{9,8},{10,11... | collective-permute-start | bytes 3145736 | tf_op jit(solution)/shard_map/ppermute | solution.py:303
  118.3 10.2 %collective-permute-start.13 = (bf16[2,8,32,1024]{3,2,1,0:T(8,128)(2,1)}, bf16[2,8,32,1024]{3,2,1,0:T(8,128)(2,1)}, u32[]{:S(2)}, u32[]{:S(2)}) collective-permute-start(bf16[2,8,32,1024]{3,2,1,0:T(8,128)(2,1)} %collective-permute-done.10.s2b), channel_id=1, source_target_pairs={{0,1},{1,0},{2,3},{3,2},{4,5},{5,4},{6,7},{7,6},{8,9},{9,8},{10,11... | collective-permute-start | bytes 3145736 | tf_op jit(solution)/shard_map/ppermute | solution.py:303
  123.9 19.7 %collective-permute-start.15 = (bf16[16,72,128]{2,1,0:T(8,128)(2,1)S(1)}, bf16[16,72,128]{2,1,0:T(8,128)(2,1)S(1)}, u32[]{:S(2)}, u32[]{:S(2)}) collective-permute-start(bf16[16,72,128]{2,1,0:T(8,128)(2,1)S(1)} %get-tuple-element.36), channel_id=1, source_target_pairs={{0,64},{64,128},{128,192},{192,0},{1,65},{65,129},{129,193},{193,1... | collective-permute-start | bytes 884744 | tf_op jit(solution)/shard_map/ppermute | solution.py:248
  124.0 19.6 %collective-permute-start.16 = (bf16[16,72,128]{2,1,0:T(8,128)(2,1)S(1)}, bf16[16,72,128]{2,1,0:T(8,128)(2,1)S(1)}, u32[]{:S(2)}, u32[]{:S(2)}) collective-permute-start(bf16[16,72,128]{2,1,0:T(8,128)(2,1)S(1)} %get-tuple-element.37), channel_id=1, source_target_pairs={{0,128},{64,192},{128,0},{192,64},{1,129},{65,193},{129,1},{193,65... | collective-permute-start | bytes 884744 | tf_op jit(solution)/shard_map/ppermute | solution.py:248
  128.6 15.0 %collective-permute-start.17 = (bf16[16,72,128]{2,1,0:T(8,128)(2,1)S(1)}, bf16[16,72,128]{2,1,0:T(8,128)(2,1)S(1)}, u32[]{:S(2)}, u32[]{:S(2)}) collective-permute-start(bf16[16,72,128]{2,1,0:T(8,128)(2,1)S(1)} %get-tuple-element.38), channel_id=1, source_target_pairs={{0,192},{64,0},{128,64},{192,128},{1,193},{65,1},{129,65},{193,129... | collective-permute-start | bytes 884744 | tf_op jit(solution)/shard_map/ppermute | solution.py:248
  (6 other events, 24.4 us)

commit v15 on v14

--- a/solution.py
+++ b/solution.py
@@ -73,7 +73,7 @@
             o_ref[s, 8 * b : 8 * b + 8, LANES:] = rest[:, tail * b : tail * (b + 1)]
 
 
-def tile_kernel(x_ref, tok_ref, cot_ref, terms_ref, at_ref, t_ref):
+def tile_kernel(x_ref, tok_ref, cot_ref, at_ref):
     shards, _, _ = x_ref.shape
     rank = at_ref.shape[0]
     depth = tok_ref.shape[1]
@@ -82,7 +82,6 @@
     per = LANES // tail
     group = per * (LANES + tail)
     lane = lax.broadcasted_iota(jnp.int32, (rank, LANES), 1)
-    lane8 = lax.broadcasted_iota(jnp.int32, (8, LANES), 1)
 
     def unpack(a, carry):
         before = None
@@ -125,8 +124,21 @@
     ).astype(bf16)
     at_ref[:, width : width + LANES] = hidden
     at_ref[:, width + LANES :] = back
-    t_ref[:, :depth] = adapter_scale * jnp.dot(back, tok, preferred_element_type=f32)
-    t_ref[:, depth:] = adapter_scale * jnp.dot(hidden, cot, preferred_element_type=f32)
+
+
+def terms_kernel(at_ref, tok_ref, cot_ref, terms_ref, t_ref):
+    shards = terms_ref.shape[0]
+    rank, width = t_ref.shape
+    depth = tok_ref.shape[1]
+    tail = width // shards - LANES
+    per = LANES // tail
+    group = per * (LANES + tail)
+    lane = lax.broadcasted_iota(jnp.int32, (rank, LANES), 1)
+    lane8 = lax.broadcasted_iota(jnp.int32, (8, LANES), 1)
+    hidden = at_ref[:, width : width + LANES]
+    back = at_ref[:, width + LANES :]
+    t_ref[:, :depth] = adapter_scale * jnp.dot(back, tok_ref[...], preferred_element_type=f32)
+    t_ref[:, depth:] = adapter_scale * jnp.dot(hidden, cot_ref[...], preferred_element_type=f32)
 
     def pack(a, carry):
         cols = [
@@ -322,18 +334,23 @@
         name="pick",
     )(group, jobs, job_slot, *every)
     arrived = lax.all_to_all(outgoing, SEQ, split_axis=0, concat_axis=0, tiled=True)
-    terms, adapter = pl.pallas_call(
+    adapter = pl.pallas_call(
         tile_kernel,
-        out_shape=(
-            jax.ShapeDtypeStruct((shards, packed_rows, LANES), bf16),
-            jax.ShapeDtypeStruct((rank, width + 2 * rows), bf16),
-        ),
+        out_shape=jax.ShapeDtypeStruct((rank, width + 2 * rows), bf16),
         in_specs=[whole()] * 3,
-        out_specs=(whole(),) * 2,
-        scratch_shapes=[pltpu.VMEM((rank, width), f32)],
-        compiler_params=params(32),
+        out_specs=whole(),
+        compiler_params=params(),
         name="tile",
     )(arrived, tokens, cotangent)
+    terms = pl.pallas_call(
+        terms_kernel,
+        out_shape=jax.ShapeDtypeStruct((shards, packed_rows, LANES), bf16),
+        in_specs=[whole()] * 3,
+        out_specs=whole(),
+        scratch_shapes=[pltpu.VMEM((rank, width), f32)],
+        compiler_params=params(),
+        name="terms",
+    )(adapter, tokens, cotangent)
     incoming = lax.all_to_all(terms, SEQ, split_axis=0, concat_axis=0, tiled=True)
     incoming, others[0] = lax.optimization_barrier((incoming, others[0]))
     sums = pl.pallas_call(

time: 145 us -> 145 us (level)
    unnamed x18 -> x16, local copies, waits for them, and re-layouts: 3.92 us -> 2.9 us
    pallas_call x1 -> x2, Pallas kernels: 3.57 us -> 4.56 us  [the longest x1 2.57 us: on_device(): pl.pallas_call(terms_kernel, out_shape=jax.ShapeDtypeStruct((shards, pack...]
  transfers between devices with their start and end apart: 21 -> 21, of which waited for: 5 -> 5; matrix products, arithmetic and copies ran while one was open for 2% -> 2% of each run, Pallas kernels for 17% -> 18%
where the time goes in v15:
time: 145 us
  waiting for transfers between devices  63.2 us (44%)
  starting transfers between devices  46.7 us (32%)
  Pallas kernels  27 us (19%)
  local copies, waits for them, and re-layouts  6.39 us (4%)
    all_to_all x1, waiting for transfers between devices, on_device(): lax.all_to_all(outgoing, SEQ, split_axis=0, concat_axis=0, tiled=True)  25.3 us
    ppermute x7, waiting for transfers between devices, route(): return lax.ppermute(x, ('grp', 'y', 'core'), pairs)  20 us
    pallas_call x1, Pallas kernels, on_device(): pl.pallas_call(base_kernel, out_shape=(jax.ShapeDtypeStruct((rows, key_co...  14.9 us
    all_to_all x1, waiting for transfers between devices, on_device(): lax.all_to_all(jnp.broadcast_to(mine, (deep,) + mine.shape), 'z', split_a...  14.2 us
    all_to_all x1, starting transfers between devices, on_device(): lax.all_to_all(outgoing, SEQ, split_axis=0, concat_axis=0, tiled=True)  10.7 us
    ppermute x7, starting transfers between devices, route(): return lax.ppermute(x, ('grp', 'y', 'core'), pairs)  10.7 us
    all_to_all x1, starting transfers between devices, on_device(): lax.all_to_all(jnp.broadcast_to(mine, (deep,) + mine.shape), 'z', split_a...  9.01 us
    ppermute x6, starting transfers between devices, shift(): lax.ppermute(x, 'grp', [(i, (i + by) % groups) for i in range(groups)])  8.42 us
  transfers between devices with their start and end apart: 21, of which 5 were waited for; matrix products, arithmetic and copies ran while one was open for 2% of the time, Pallas kernels for 18%

profile of v15, /device:TPU:1, one launch (start us, length us, event | category | flops | bytes accessed | tf_op | source)
XLA Modules:
  0.0 144.7 jit_solution(4894958938297604286)
XLA Ops:
  2.4 9.0 %all-to-all-start.2 = ((bf16[8,32,1024]{2,1,0:T(8,128)(2,1)}), bf16[8,32,1024]{2,1,0:T(8,128)(2,1)}, u32[]{:S(2)}, u32[]{:S(2)}) async-start(bf16[8,32,1024]{2,1,0:T(8,128)(2,1)} %broadcast_in_dim.3), calls=%async_computation.2 | async-start | bytes 1048576 | tf_op jit(solution)/shard_map/all_to_all | solution.py:294
  11.6 2.6 %collective-permute-start = (bf16[16,72,128]{2,1,0:T(8,128)(2,1)S(1)}, bf16[16,72,128]{2,1,0:T(8,128)(2,1)S(1)}, u32[]{:S(2)}, u32[]{:S(2)}) collective-permute-start(bf16[16,72,128]{2,1,0:T(8,128)(2,1)S(1)} %pack.1.refs_0_), channel_id=1, source_target_pairs={{0,192},{64,0},{128,64},{192,128},{1,193},{65,1},{129,65},{193,129... | collective-permute-start | bytes 884744 | tf_op jit(solution)/shard_map/ppermute | solution.py:260
  15.3 14.2 %all-to-all-done.2.x0 = bf16[8,32,1024]{2,1,0:T(8,128)(2,1)} async-done(((bf16[8,32,1024]{2,1,0:T(8,128)(2,1)}), bf16[8,32,1024]{2,1,0:T(8,128)(2,1)}, u32[]{:S(2)}, u32[]{:S(2)}) %all-to-all-start.2) | async-done | bytes 524320 | tf_op jit(solution)/shard_map/all_to_all | solution.py:294
  29.5 1.2 collective-permute-start.3
  30.7 2.5 %collective-permute-start.4 = (bf16[8,32,1024]{2,1,0:T(8,128)(2,1)}, bf16[8,32,1024]{2,1,0:T(8,128)(2,1)}, u32[]{:S(2)}, u32[]{:S(2)}) collective-permute-start(bf16[8,32,1024]{2,1,0:T(8,128)(2,1)} %all-to-all-done.2.x0), channel_id=1, source_target_pairs={{0,32},{1,129},{16,48},{17,145},{32,0},{33,161},{48,16},{49,177},{... | collective-permute-start | bytes 1572872 | tf_op jit(solution)/shard_map/ppermute | solution.py:271
  34.4 1.9 %pick.1 = bf16[64,72,128]{2,1,0:T(8,128)(2,1)} custom-call(s32[1]{0:T(128)} %bitcast.group_ref, s32[256]{0:T(256)S(1)} %bitcast.7, s32[64]{0:T(128)S(1)} %copy-done.6, bf16[16,72,128]{2,1,0:T(8,128)(2,1)S(1)} %pack.1.refs_0_, bf16[16,72,128]{2,1,0:T(8,128)(2,1)S(1)} %collective-permute-done.refs_1_, bf16[16,72,128]{2,1,0:T(8,128)(2,1)S(1)} %collective-permute-done.1.refs_2_, ...), custom_call_target="tpu_custom_call" | custom-call | tf_op jit(solution)/shard_map/pick/pallas_call | solution.py:327
  36.3 10.7 %all-to-all-start = ((bf16[64,72,128]{2,1,0:T(8,128)(2,1)}), bf16[64,72,128]{2,1,0:T(8,128)(2,1)S(1)}, u32[]{:S(2)}, u32[]{:S(2)}) async-start(bf16[64,72,128]{2,1,0:T(8,128)(2,1)} %pick.1), calls=%async_computation | async-start | bytes 2359296 | tf_op jit(solution)/shard_map/all_to_all | solution.py:336
  47.1 3.0 %join.1.s0 = bf16[4,8,32,1024]{3,2,1,0:T(8,128)(2,1)} custom-call(bf16[8,32,1024]{2,1,0:T(8,128)(2,1)} %all-to-all-done.2.x0, bf16[8,32,1024]{2,1,0:T(8,128)(2,1)} %collective-permute-done.3.x1, bf16[8,32,1024]{2,1,0:T(8,128)(2,1)} %collective-permute-done.4.x2, bf16[8,32,1024]{2,1,0:T(8,128)(2,1)} %collective-permute-done.5.x3), custom_call_target="tpu_custom_call" | custom-call | tf_op jit(solution)/shard_map/join/pallas_call | solution.py:297
  50.1 1.5 %collective-permute-start.7 = (bf16[4,8,32,1024]{3,2,1,0:T(8,128)(2,1)}, bf16[4,8,32,1024]{3,2,1,0:T(8,128)(2,1)}, u32[]{:S(2)}, u32[]{:S(2)}) collective-permute-start(bf16[4,8,32,1024]{3,2,1,0:T(8,128)(2,1)} %join.1.s0), channel_id=1, source_target_pairs={{0,64},{1,17},{16,80},{17,33},{32,96},{33,49},{48,112},{49,1},{64,... | collective-permute-start | bytes 6291464 | tf_op jit(solution)/shard_map/ppermute | solution.py:271
  51.6 1.5 %collective-permute-start.9 = (bf16[4,8,32,1024]{3,2,1,0:T(8,128)(2,1)}, bf16[4,8,32,1024]{3,2,1,0:T(8,128)(2,1)}, u32[]{:S(2)}, u32[]{:S(2)}) collective-permute-start(bf16[4,8,32,1024]{3,2,1,0:T(8,128)(2,1)} %join.1.s0), channel_id=1, source_target_pairs={{0,192},{1,49},{16,208},{17,1},{32,224},{33,17},{48,240},{49,33},{... | collective-permute-start | bytes 6291464 | tf_op jit(solution)/shard_map/ppermute | solution.py:271
  53.1 25.3 %all-to-all-done.x_ref = bf16[64,72,128]{2,1,0:T(8,128)(2,1)S(1)} async-done(((bf16[64,72,128]{2,1,0:T(8,128)(2,1)}), bf16[64,72,128]{2,1,0:T(8,128)(2,1)S(1)}, u32[]{:S(2)}, u32[]{:S(2)}) %all-to-all-start) | async-done | bytes 1179680 | tf_op jit(solution)/shard_map/all_to_all | solution.py:336
  79.3 2.0 %tile.1.at_ref.adapter_in = bf16[64,9472]{1,0:T(8,128)(2,1)S(1)} custom-call(bf16[64,72,128]{2,1,0:T(8,128)(2,1)S(1)} %all-to-all-done.x_ref, bf16[128,8192]{1,0:T(8,128)(2,1)S(1)} %copy-done.1, bf16[128,1024]{1,0:T(8,128)(2,1)S(1)} %copy-done.3), custom_call_target="tpu_custom_call" | custom-call | tf_op jit(solution)/shard_map/tile/pallas_call | solution.py:337
  81.3 2.6 %terms.1 = bf16[64,72,128]{2,1,0:T(8,128)(2,1)} custom-call(bf16[64,9472]{1,0:T(8,128)(2,1)S(1)} %tile.1.at_ref.adapter_in, bf16[128,8192]{1,0:T(8,128)(2,1)S(1)} %copy-done.1, bf16[128,1024]{1,0:T(8,128)(2,1)S(1)} %copy-done.3), custom_call_target="tpu_custom_call" | custom-call | tf_op jit(solution)/shard_map/terms/pallas_call | solution.py:345
  84.9 6.3 %all-to-all-start.1 = ((bf16[64,72,128]{2,1,0:T(8,128)(2,1)}), bf16[64,72,128]{2,1,0:T(8,128)(2,1)S(1)}, u32[]{:S(2)}, u32[]{:S(2)}) async-start(bf16[64,72,128]{2,1,0:T(8,128)(2,1)} %terms.1), calls=%async_computation.1 | async-start | bytes 2359296 | tf_op jit(solution)/shard_map/all_to_all | solution.py:354
  91.8 1.3 slice.8
  93.1 1.4 collective-permute-start.8
  94.5 1.3 slice.9
  95.8 1.5 %collective-permute-start.10 = (bf16[2,8,32,1024]{3,2,1,0:T(8,128)(2,1)S(1)}, bf16[2,8,32,1024]{3,2,1,0:T(8,128)(2,1)}, u32[]{:S(2)}, u32[]{:S(2)}) collective-permute-start(bf16[2,8,32,1024]{3,2,1,0:T(8,128)(2,1)S(1)} %slice.9), channel_id=1, source_target_pairs={{0,192},{1,49},{16,208},{17,1},{32,224},{33,17},{48,240},{49,33},{... | collective-permute-start | bytes 3145736 | tf_op jit(solution)/shard_map/ppermute | solution.py:271
  98.3 19.2 %collective-permute-done.8.s2 = bf16[2,8,32,1024]{3,2,1,0:T(8,128)(2,1)} collective-permute-done((bf16[2,8,32,1024]{3,2,1,0:T(8,128)(2,1)S(1)}, bf16[2,8,32,1024]{3,2,1,0:T(8,128)(2,1)}, u32[]{:S(2)}, u32[]{:S(2)}) %collective-permute-start.8) | collective-permute-done | bytes 1048608 | tf_op jit(solution)/shard_map/ppermute | solution.py:271
  118.9 3.7 %all-to-all-done.1.x_ref = bf16[64,72,128]{2,1,0:T(8,128)(2,1)S(1)} async-done(((bf16[64,72,128]{2,1,0:T(8,128)(2,1)}), bf16[64,72,128]{2,1,0:T(8,128)(2,1)S(1)}, u32[]{:S(2)}, u32[]{:S(2)}) %all-to-all-start.1) | async-done | bytes 1179680 | tf_op jit(solution)/shard_map/all_to_all | solution.py:354
  122.6 1.3 sum.1
  124.0 4.6 %collective-permute-start.16 = (bf16[16,72,128]{2,1,0:T(8,128)(2,1)S(1)}, bf16[16,72,128]{2,1,0:T(8,128)(2,1)S(1)}, u32[]{:S(2)}, u32[]{:S(2)}) collective-permute-start(bf16[16,72,128]{2,1,0:T(8,128)(2,1)S(1)} %get-tuple-element.33), channel_id=1, source_target_pairs={{0,128},{64,192},{128,0},{192,64},{1,129},{65,193},{129,1},{193,65... | collective-permute-start | bytes 884744 | tf_op jit(solution)/shard_map/ppermute | solution.py:260
  128.6 14.9 %base.1 = (bf16[128,1024]{1,0:T(8,128)(2,1)}, bf16[128,8192]{1,0:T(8,128)(2,1)}) custom-call(s32[3]{0:T(128)} %pad_add_fusion.place_ref, bf16[128,8192]{1,0:T(8,128)(2,1)} %tok_ref.5, bf16[128,1024]{1,0:T(8,128)(2,1)} %cot_in.1, bf16[4,8,32,1024]{3,2,1,0:T(8,128)(2,1)} %join.1.s0, bf16[4,8,32,1024]{3,2,1,0:T(8,128)(2,1)} %collective-permute-done.7.s1, ...), custom_call_target="tpu_custom_call" | custom-call | flops 4294967296 | bytes 21495808 | tf_op jit(solution)/shard_map/base/pallas_call | solution.py:380
  143.6 1.2 unpack.1
  (47 shorter events, 9.4 us)
Async XLA Ops:
  0.7 33.7 %copy-start.5 = (s32[256,1]{0,1:T(1,128)S(1)}, s32[256,1]{0,1:T(1,128)}, u32[]{:S(2)}) copy-start(s32[256,1]{0,1:T(1,128)} %param.10) | copy-start | bytes 3076
  0.7 33.7 %copy-start.6 = (s32[64]{0:T(128)S(1)}, s32[64]{0:T(128)}, u32[]{:S(2)}) copy-start(s32[64]{0:T(128)} %slot_ref.3) | copy-start | bytes 772
  2.4 27.1 %all-to-all-start.2 = ((bf16[8,32,1024]{2,1,0:T(8,128)(2,1)}), bf16[8,32,1024]{2,1,0:T(8,128)(2,1)}, u32[]{:S(2)}, u32[]{:S(2)}) async-start(bf16[8,32,1024]{2,1,0:T(8,128)(2,1)} %broadcast_in_dim.3), calls=%async_computation.2 | async-start | bytes 1048576 | tf_op jit(solution)/shard_map/all_to_all | solution.py:294
  11.6 21.6 %collective-permute-start = (bf16[16,72,128]{2,1,0:T(8,128)(2,1)S(1)}, bf16[16,72,128]{2,1,0:T(8,128)(2,1)S(1)}, u32[]{:S(2)}, u32[]{:S(2)}) collective-permute-start(bf16[16,72,128]{2,1,0:T(8,128)(2,1)S(1)} %pack.1.refs_0_), channel_id=1, source_target_pairs={{0,192},{64,0},{128,64},{192,128},{1,193},{65,1},{129,65},{193,129... | collective-permute-start | bytes 884744 | tf_op jit(solution)/shard_map/ppermute | solution.py:260
  14.2 20.2 %collective-permute-start.1 = (bf16[16,72,128]{2,1,0:T(8,128)(2,1)S(1)}, bf16[16,72,128]{2,1,0:T(8,128)(2,1)S(1)}, u32[]{:S(2)}, u32[]{:S(2)}) collective-permute-start(bf16[16,72,128]{2,1,0:T(8,128)(2,1)S(1)} %pack.1.refs_0_), channel_id=1, source_target_pairs={{0,128},{64,192},{128,0},{192,64},{1,129},{65,193},{129,1},{193,65... | collective-permute-start | bytes 884744 | tf_op jit(solution)/shard_map/ppermute | solution.py:260
  14.7 19.7 %collective-permute-start.2 = (bf16[16,72,128]{2,1,0:T(8,128)(2,1)S(1)}, bf16[16,72,128]{2,1,0:T(8,128)(2,1)S(1)}, u32[]{:S(2)}, u32[]{:S(2)}) collective-permute-start(bf16[16,72,128]{2,1,0:T(8,128)(2,1)S(1)} %pack.1.refs_0_), channel_id=1, source_target_pairs={{0,64},{64,128},{128,192},{192,0},{1,65},{65,129},{129,193},{193,1... | collective-permute-start | bytes 884744 | tf_op jit(solution)/shard_map/ppermute | solution.py:260
  29.5 17.5 %collective-permute-start.3 = (bf16[8,32,1024]{2,1,0:T(8,128)(2,1)}, bf16[8,32,1024]{2,1,0:T(8,128)(2,1)}, u32[]{:S(2)}, u32[]{:S(2)}) collective-permute-start(bf16[8,32,1024]{2,1,0:T(8,128)(2,1)} %all-to-all-done.2.x0), channel_id=1, source_target_pairs={{0,16},{1,65},{16,32},{17,81},{32,48},{33,97},{48,0},{49,113},{64,... | collective-permute-start | bytes 1572872 | tf_op jit(solution)/shard_map/ppermute | solution.py:271
  30.7 16.3 %collective-permute-start.4 = (bf16[8,32,1024]{2,1,0:T(8,128)(2,1)}, bf16[8,32,1024]{2,1,0:T(8,128)(2,1)}, u32[]{:S(2)}, u32[]{:S(2)}) collective-permute-start(bf16[8,32,1024]{2,1,0:T(8,128)(2,1)} %all-to-all-done.2.x0), channel_id=1, source_target_pairs={{0,32},{1,129},{16,48},{17,145},{32,0},{33,161},{48,16},{49,177},{... | collective-permute-start | bytes 1572872 | tf_op jit(solution)/shard_map/ppermute | solution.py:271
  33.2 13.9 %collective-permute-start.5 = (bf16[8,32,1024]{2,1,0:T(8,128)(2,1)}, bf16[8,32,1024]{2,1,0:T(8,128)(2,1)}, u32[]{:S(2)}, u32[]{:S(2)}) collective-permute-start(bf16[8,32,1024]{2,1,0:T(8,128)(2,1)} %all-to-all-done.2.x0), channel_id=1, source_target_pairs={{0,48},{1,193},{16,0},{17,209},{32,16},{33,225},{48,32},{49,241},{... | collective-permute-start | bytes 1572872 | tf_op jit(solution)/shard_map/ppermute | solution.py:271
  36.3 42.1 %all-to-all-start = ((bf16[64,72,128]{2,1,0:T(8,128)(2,1)}), bf16[64,72,128]{2,1,0:T(8,128)(2,1)S(1)}, u32[]{:S(2)}, u32[]{:S(2)}) async-start(bf16[64,72,128]{2,1,0:T(8,128)(2,1)} %pick.1), calls=%async_computation | async-start | bytes 2359296 | tf_op jit(solution)/shard_map/all_to_all | solution.py:336
  47.0 31.4 %copy-start.1 = (bf16[128,8192]{1,0:T(8,128)(2,1)S(1)}, bf16[128,8192]{1,0:T(8,128)(2,1)}, u32[]{:S(2)}) copy-start(bf16[128,8192]{1,0:T(8,128)(2,1)} %tok_ref.5) | copy-start | bytes 6291460
  50.1 41.6 %collective-permute-start.7 = (bf16[4,8,32,1024]{3,2,1,0:T(8,128)(2,1)}, bf16[4,8,32,1024]{3,2,1,0:T(8,128)(2,1)}, u32[]{:S(2)}, u32[]{:S(2)}) collective-permute-start(bf16[4,8,32,1024]{3,2,1,0:T(8,128)(2,1)} %join.1.s0), channel_id=1, source_target_pairs={{0,64},{1,17},{16,80},{17,33},{32,96},{33,49},{48,112},{49,1},{64,... | collective-permute-start | bytes 6291464 | tf_op jit(solution)/shard_map/ppermute | solution.py:271
  51.6 42.9 %collective-permute-start.9 = (bf16[4,8,32,1024]{3,2,1,0:T(8,128)(2,1)}, bf16[4,8,32,1024]{3,2,1,0:T(8,128)(2,1)}, u32[]{:S(2)}, u32[]{:S(2)}) collective-permute-start(bf16[4,8,32,1024]{3,2,1,0:T(8,128)(2,1)} %join.1.s0), channel_id=1, source_target_pairs={{0,192},{1,49},{16,208},{17,1},{32,224},{33,17},{48,240},{49,33},{... | collective-permute-start | bytes 6291464 | tf_op jit(solution)/shard_map/ppermute | solution.py:271
  84.9 37.7 %all-to-all-start.1 = ((bf16[64,72,128]{2,1,0:T(8,128)(2,1)}), bf16[64,72,128]{2,1,0:T(8,128)(2,1)S(1)}, u32[]{:S(2)}, u32[]{:S(2)}) async-start(bf16[64,72,128]{2,1,0:T(8,128)(2,1)} %terms.1), calls=%async_computation.1 | async-start | bytes 2359296 | tf_op jit(solution)/shard_map/all_to_all | solution.py:354
  91.2 27.7 %collective-permute-start.6 = (bf16[4,8,32,1024]{3,2,1,0:T(8,128)(2,1)}, bf16[4,8,32,1024]{3,2,1,0:T(8,128)(2,1)S(1)}, u32[]{:S(2)}, u32[]{:S(2)}) collective-permute-start(bf16[4,8,32,1024]{3,2,1,0:T(8,128)(2,1)} %join.1.s0), channel_id=1, source_target_pairs={{0,1},{1,0},{2,3},{3,2},{4,5},{5,4},{6,7},{7,6},{8,9},{9,8},{10,11... | collective-permute-start | bytes 6291464 | tf_op jit(solution)/shard_map/ppermute | solution.py:315
  93.1 24.4 %collective-permute-start.8 = (bf16[2,8,32,1024]{3,2,1,0:T(8,128)(2,1)S(1)}, bf16[2,8,32,1024]{3,2,1,0:T(8,128)(2,1)}, u32[]{:S(2)}, u32[]{:S(2)}) collective-permute-start(bf16[2,8,32,1024]{3,2,1,0:T(8,128)(2,1)S(1)} %slice.8), channel_id=1, source_target_pairs={{0,64},{1,17},{16,80},{17,33},{32,96},{33,49},{48,112},{49,1},{64,... | collective-permute-start | bytes 3145736 | tf_op jit(solution)/shard_map/ppermute | solution.py:271
  95.8 22.5 %collective-permute-start.10 = (bf16[2,8,32,1024]{3,2,1,0:T(8,128)(2,1)S(1)}, bf16[2,8,32,1024]{3,2,1,0:T(8,128)(2,1)}, u32[]{:S(2)}, u32[]{:S(2)}) collective-permute-start(bf16[2,8,32,1024]{3,2,1,0:T(8,128)(2,1)S(1)} %slice.9), channel_id=1, source_target_pairs={{0,192},{1,49},{16,208},{17,1},{32,224},{33,17},{48,240},{49,33},{... | collective-permute-start | bytes 3145736 | tf_op jit(solution)/shard_map/ppermute | solution.py:271
  97.3 31.2 %collective-permute-start.11 = (bf16[4,8,32,1024]{3,2,1,0:T(8,128)(2,1)}, bf16[4,8,32,1024]{3,2,1,0:T(8,128)(2,1)}, u32[]{:S(2)}, u32[]{:S(2)}) collective-permute-start(bf16[4,8,32,1024]{3,2,1,0:T(8,128)(2,1)} %collective-permute-done.7.s1), channel_id=1, source_target_pairs={{0,1},{1,0},{2,3},{3,2},{4,5},{5,4},{6,7},{7,6},{8,9},{9,8},{10,11... | collective-permute-start | bytes 6291464 | tf_op jit(solution)/shard_map/ppermute | solution.py:315
  98.3 30.2 %collective-permute-start.14 = (bf16[4,8,32,1024]{3,2,1,0:T(8,128)(2,1)}, bf16[4,8,32,1024]{3,2,1,0:T(8,128)(2,1)}, u32[]{:S(2)}, u32[]{:S(2)}) collective-permute-start(bf16[4,8,32,1024]{3,2,1,0:T(8,128)(2,1)} %collective-permute-done.9.s3), channel_id=1, source_target_pairs={{0,1},{1,0},{2,3},{3,2},{4,5},{5,4},{6,7},{7,6},{8,9},{9,8},{10,11... | collective-permute-start | bytes 6291464 | tf_op jit(solution)/shard_map/ppermute | solution.py:315
  117.5 6.5 %collective-permute-start.12 = (bf16[2,8,32,1024]{3,2,1,0:T(8,128)(2,1)}, bf16[2,8,32,1024]{3,2,1,0:T(8,128)(2,1)}, u32[]{:S(2)}, u32[]{:S(2)}) collective-permute-start(bf16[2,8,32,1024]{3,2,1,0:T(8,128)(2,1)} %collective-permute-done.8.s2), channel_id=1, source_target_pairs={{0,1},{1,0},{2,3},{3,2},{4,5},{5,4},{6,7},{7,6},{8,9},{9,8},{10,11... | collective-permute-start | bytes 3145736 | tf_op jit(solution)/shard_map/ppermute | solution.py:315
  118.3 10.2 %collective-permute-start.13 = (bf16[2,8,32,1024]{3,2,1,0:T(8,128)(2,1)}, bf16[2,8,32,1024]{3,2,1,0:T(8,128)(2,1)}, u32[]{:S(2)}, u32[]{:S(2)}) collective-permute-start(bf16[2,8,32,1024]{3,2,1,0:T(8,128)(2,1)} %collective-permute-done.10.s2b), channel_id=1, source_target_pairs={{0,1},{1,0},{2,3},{3,2},{4,5},{5,4},{6,7},{7,6},{8,9},{9,8},{10,11... | collective-permute-start | bytes 3145736 | tf_op jit(solution)/shard_map/ppermute | solution.py:315
  123.9 19.7 %collective-permute-start.15 = (bf16[16,72,128]{2,1,0:T(8,128)(2,1)S(1)}, bf16[16,72,128]{2,1,0:T(8,128)(2,1)S(1)}, u32[]{:S(2)}, u32[]{:S(2)}) collective-permute-start(bf16[16,72,128]{2,1,0:T(8,128)(2,1)S(1)} %get-tuple-element.32), channel_id=1, source_target_pairs={{0,64},{64,128},{128,192},{192,0},{1,65},{65,129},{129,193},{193,1... | collective-permute-start | bytes 884744 | tf_op jit(solution)/shard_map/ppermute | solution.py:260
  124.0 19.6 %collective-permute-start.16 = (bf16[16,72,128]{2,1,0:T(8,128)(2,1)S(1)}, bf16[16,72,128]{2,1,0:T(8,128)(2,1)S(1)}, u32[]{:S(2)}, u32[]{:S(2)}) collective-permute-start(bf16[16,72,128]{2,1,0:T(8,128)(2,1)S(1)} %get-tuple-element.33), channel_id=1, source_target_pairs={{0,128},{64,192},{128,0},{192,64},{1,129},{65,193},{129,1},{193,65... | collective-permute-start | bytes 884744 | tf_op jit(solution)/shard_map/ppermute | solution.py:260
  128.5 15.0 %collective-permute-start.17 = (bf16[16,72,128]{2,1,0:T(8,128)(2,1)S(1)}, bf16[16,72,128]{2,1,0:T(8,128)(2,1)S(1)}, u32[]{:S(2)}, u32[]{:S(2)}) collective-permute-start(bf16[16,72,128]{2,1,0:T(8,128)(2,1)S(1)} %get-tuple-element.34), channel_id=1, source_target_pairs={{0,192},{64,0},{128,64},{192,128},{1,193},{65,1},{129,65},{193,129... | collective-permute-start | bytes 884744 | tf_op jit(solution)/shard_map/ppermute | solution.py:260
  (5 other events, 23.5 us)
